TPU v7x, 32 devices: a whole 2x2x4 slice. The times are simulated.
32 devices in a mesh: design: 2 (over x), slab: 16 (over z, y, core).
Axes of the slice: x: 2, y: 2, z: 4, core: 2. Of those that a mesh axis runs over, the one named last changes fastest.
Arguments:
- e_start: float32 [3, 512, 64, 128], P(None, ('design', 'slab')), parts along dimension 1, may hold values from -6 to 6
- h_start: float32 [3, 512, 64, 128], P(None, ('design', 'slab')), parts along dimension 1, may hold values from -6 to 6
- material: int32 [512, 64, 128], P(('design', 'slab')), parts along dimension 0, may hold values from 0 to 3
- mat_permit: float32 [4], replicated, may hold values from 1 to 4
- mat_loss: float32 [4], replicated, may hold values from 0 to 0.2
- monitor_z: int32 [4], replicated, may hold values from 0 to 255, as said below
- monitor_span: int32 [4, 2], replicated, may hold values from 0 to 64, as said below
- freq_bins: int32 [128], P('slab'), may hold values from 1 to 255
Outputs:
- e_final: float32 [3, 512, 64, 128], P(None, ('design', 'slab')), parts along dimension 1
- h_final: float32 [3, 512, 64, 128], P(None, ('design', 'slab')), parts along dimension 1
- spectrum: float32 [256, 2, 4, 2, 64, 128], P(('design', 'slab')), parts along dimension 0
There are 2 independent parts, one for each index of `design`. A program takes and returns all parts, laid end to end along the dimension named above; an argument that names none is the same for every part. Nothing has to cross between parts.
Inputs may be any that keep to these rules, and one draw needn't show every extreme that they name: `monitor_z`: the 4 monitor planes have distinct z indices. `monitor_span`: each monitor's first row is at most a quarter of 64, and it records between half and three quarters of the rows.
All inputs are finite; a program needn't handle non-finite values.
Results may differ from a plain program's by a relative error of at most 0.000075.
Values sent between devices are 32-bit elements; how exact they have to be, the bound alone decides.
No kernel may reach another device: no remote copies, remote signals or barrier semaphores. Data moves between devices by JAX's collectives and lax.ppermute only.
A program may use at most 128 MiB of HBM per device.

v0:
```python
import functools
import math

import jax
import jax.numpy as jnp
from jax import lax
from jax.experimental import pallas as pl
from jax.experimental.pallas import tpu as pltpu
from jax.sharding import PartitionSpec as P

STEPS = 8
PERIOD = 512
ROUNDS = (4, 3, 1)
GHOST = max(ROUNDS)
COURANT = 0.5
VMEM = pl.BlockSpec(memory_space=pltpu.VMEM)
SMEM = pl.BlockSpec(memory_space=pltpu.SMEM)
ANY = pl.BlockSpec(memory_space=pl.ANY)
LIMIT = 48 * 1024 * 1024


def params():
    return pltpu.CompilerParams(vmem_limit_bytes=LIMIT)


def down_pieces(d, mats):
    pieces = [("e", 0, 2, 0, d)]
    if d > 1:
        pieces += [("e", 2, 1, 0, d - 1), ("h", 0, 3, 0, d - 1)]
    if mats:
        pieces += [("m", 0, 1, 0, mats)]
    return pieces


def up_pieces(d, mats, depth, first):
    pieces = [("e", 0, 3, depth - d, d)]
    if first:
        pieces += [("h", 0, 2, depth - d, d)]
        if d > 1:
            pieces += [("h", 2, 1, depth - d + 1, d - 1)]
    else:
        if d > 1:
            pieces += [("h", 0, 2, depth - d, d - 1)]
        if d > 2:
            pieces += [("h", 2, 1, depth - d + 1, d - 2)]
    if mats:
        pieces += [("m", 0, 1, depth - mats, mats)]
    return pieces


def size_of(pieces):
    return sum(p[2] * p[4] for p in pieces)


def message_size(d, mats, depth, first):
    return max(size_of(down_pieces(d, mats)), size_of(up_pieces(d, mats, depth, first)))


def spots(pieces):
    at = 0
    for name, comp, comps, plane, planes in pieces:
        for c in range(comp, comp + comps):
            yield name, c, plane, planes, at
            at += planes


def first_pack_kernel(d, mats, depth, info, e_ref, h_ref, m_ref, far_ref, near_ref, m_buf, sem):
    even = info[0] == 0

    def pack(down_ref, up_ref):
        copies = []
        for k, (pieces, out) in enumerate(
            ((down_pieces(d, mats), down_ref), (up_pieces(d, mats, depth, True), up_ref))
        ):
            for name, c, plane, planes, at in spots(pieces):
                target = out.at[pl.ds(at, planes)]
                if name == "m":
                    source, target = m_ref.at[pl.ds(plane, planes)], m_buf.at[k]
                else:
                    source = (e_ref if name == "e" else h_ref).at[c, pl.ds(plane, planes)]
                copy = pltpu.make_async_copy(source, target, sem.at[len(copies)])
                copy.start()
                copies.append(copy)
        for copy in copies:
            copy.wait()
        if mats:
            for k, (pieces, out) in enumerate(
                ((down_pieces(d, mats), down_ref), (up_pieces(d, mats, depth, True), up_ref))
            ):
                at = size_of(pieces) - mats
                out[pl.ds(at, mats)] = m_buf[k].astype(jnp.float32)

    @pl.when(even)
    def _():
        pack(far_ref, near_ref)

    @pl.when(jnp.logical_not(even))
    def _():
        pack(near_ref, far_ref)


def round_kernel(
    d, nxt, first, depth, monitors, rows, info, tables, *refs
):
    if first:
        e_in, h_in, m_in, far_in, near_in = refs[:5]
        refs = refs[5:]
    else:
        e_in, h_in, keep_in, drive_in, hb_in, far_in, near_in = refs[:7]
        refs = refs[7:]
    e_out, h_out = refs[:2]
    refs = refs[2:]
    mine_out, other_out = refs[:2]
    refs = refs[2:]
    if nxt:
        hb_out, far_out, near_out = refs[:3]
        refs = refs[3:]
    if first:
        keep_ref, drive_ref = refs[:2]
        refs = refs[2:]
    else:
        keep_ref, drive_ref = keep_in, drive_in
    e, h = refs
    height, width = e.shape[2], e.shape[3]
    mats = GHOST - 1
    even = info[0] == 0
    below, above = info[1], info[2]
    g = GHOST

    for c in range(3):
        e[c, pl.ds(g, depth)] = e_in[c]
        h[c, pl.ds(g, depth)] = h_in[c]

    def unpack(below_ref, above_ref):
        for shift, pieces, source in (
            (-depth, up_pieces(d, mats if first else 0, depth, first), below_ref),
            (depth, down_pieces(d, mats if first else 0), above_ref),
        ):
            for name, c, plane, planes, at in spots(pieces):
                value = source[pl.ds(at, planes)]
                where = g + plane + shift
                if name == "e":
                    e[c, pl.ds(where, planes)] = value
                elif name == "h":
                    h[c, pl.ds(where, planes)] = value
                else:
                    keep_ref[pl.ds(where - 1, planes)] = value

    @pl.when(even)
    def _():
        unpack(far_in, near_in)

    @pl.when(jnp.logical_not(even))
    def _():
        unpack(near_in, far_in)

    if first:
        loss = [jnp.full((1, width), tables[1, k], jnp.float32) for k in range(tables.shape[1])]
        permit = [jnp.full((1, width), tables[0, k], jnp.float32) for k in range(tables.shape[1])]
        keeps = [(1.0 - x) / (1.0 + x) for x in loss]
        drives = [COURANT / (p * (1.0 + x)) for p, x in zip(permit, loss)]

        def look_up(values, which):
            total = jnp.broadcast_to(values[0], which.shape)
            for k in range(1, len(values)):
                total = jnp.where(which == k, values[k], total)
            return total

        def own(z, _):
            which = m_in[z]
            keep_ref[z + mats] = look_up(keeps, which)
            drive_ref[z + mats] = look_up(drives, which)
            return 0

        lax.fori_loop(0, depth, own, 0)

        def ghosts(at, alive):
            which = keep_ref[at].astype(jnp.int32)
            keep_ref[at] = look_up(keeps, which) * alive
            drive_ref[at] = look_up(drives, which) * alive

        for k in range(mats):
            ghosts(k, below.astype(jnp.float32))
            ghosts(mats + depth + k, above.astype(jnp.float32))
    else:
        h[:, g - 1] = hb_in[...]

    row = lax.broadcasted_iota(jnp.int32, (height, width), 0)
    lane = lax.broadcasted_iota(jnp.int32, (height, width), 1)
    row_last, row_first = row == height - 1, row == 0
    lane_last, lane_first = lane == width - 1, lane == 0

    def fore_y(v):
        return jnp.where(row_last, 0.0, pltpu.roll(v, height - 1, 0)) - v

    def fore_x(v):
        return jnp.where(lane_last, 0.0, pltpu.roll(v, width - 1, 1)) - v

    def back_y(v):
        return v - jnp.where(row_first, 0.0, pltpu.roll(v, 1, 0))

    def back_x(v):
        return v - jnp.where(lane_first, 0.0, pltpu.roll(v, 1, 1))

    ghost_factor = COURANT * below.astype(jnp.float32)

    def step_h(at):
        factor = jnp.where(at < g, ghost_factor, COURANT)
        ex, ey, ez = e[0, at], e[1, at], e[2, at]
        hx = h[0, at] - factor * (fore_y(ez) - (e[1, at + 1] - ey))
        hy = h[1, at] - factor * ((e[0, at + 1] - ex) - fore_x(ez))
        hz = h[2, at] - factor * (fore_x(ey) - fore_y(ex))
        h[0, at] = hx
        h[1, at] = hy
        h[2, at] = hz
        return hx, hy, hz

    def step_both(at, _):
        hx, hy, hz = step_h(at)
        keep, drive = keep_ref[at - 1], drive_ref[at - 1]
        e[0, at] = keep * e[0, at] + drive * (back_y(hz) - (hy - h[1, at - 1]))
        e[1, at] = keep * e[1, at] + drive * ((hx - h[0, at - 1]) - back_x(hz))
        e[2, at] = keep * e[2, at] + drive * (back_x(hy) - back_y(hx))
        return 0

    mine, other = info[0], 1 - info[0]
    kept_row = lax.broadcasted_iota(jnp.int32, (rows, width), 0)
    for s in range(1, d + 1):
        low = g - (d - s)
        high = g + depth + (d - s)
        step_h(low - 1)
        lax.fori_loop(low, high, step_both, 0)
        for m in range(monitors):
            offset, start, extent = info[3 + m], info[3 + monitors + m], info[3 + 2 * monitors + m]
            held = jnp.logical_and(offset >= 0, offset < depth)
            spot = g + jnp.clip(offset, 0, depth - 1)
            taken = jnp.where(held, extent, 0)
            for out, c in ((mine_out, mine), (other_out, other)):
                plane = pltpu.roll(e[c, spot], height - start, 0)[:rows]
                out[s - 1, m] = jnp.where(kept_row < taken, plane, 0.0)

    for c in range(3):
        e_out[c] = e[c, pl.ds(g, depth)]
        h_out[c] = h[c, pl.ds(g, depth)]
    if nxt:
        hb_out[...] = h[:, g - 1]

        def pack(down_ref, up_ref):
            for pieces, out in (
                (down_pieces(nxt, 0), down_ref),
                (up_pieces(nxt, 0, depth, False), up_ref),
            ):
                for name, c, plane, planes, at in spots(pieces):
                    source = e if name == "e" else h
                    out[pl.ds(at, planes)] = source[c, pl.ds(g + plane, planes)]

        @pl.when(even)
        def _():
            pack(far_out, near_out)

        @pl.when(jnp.logical_not(even))
        def _():
            pack(near_out, far_out)


def spectrum_kernel(
    chunks, freqs, monitors, height, info, table, *refs
):
    samples = refs[: 2 * len(chunks)]
    out = refs[-1]
    rows, width = samples[0].shape[2:]
    f = pl.program_id(0)
    steps = sum(chunks)
    pad = jnp.zeros((height - rows, width), jnp.float32)
    for m in range(monitors):
        start = info[3 + monitors + m]
        for side in range(2):
            c = info[0] if side == 0 else 1 - info[0]
            planes = [
                samples[2 * k + side][t, m] for k in range(len(chunks)) for t in range(chunks[k])
            ]
            for part in range(2):
                total = planes[0] * table[f, part * steps]
                for t in range(1, steps):
                    total = total + planes[t] * table[f, part * steps + t]
                placed = pltpu.roll(jnp.concatenate([total, pad], 0), start, 0)
                out[0, part, m, c] = placed


def per_device(
    slabs, e_start, h_start, material, mat_permit, mat_loss, monitor_z, monitor_span, freq_bins
):
    depth, height, width = e_start.shape[1:]
    monitors = monitor_z.shape[0]
    freqs = freq_bins.shape[0]
    rows = 3 * height // 4
    mats = GHOST - 1
    me = lax.axis_index("slab")
    info = jnp.concatenate(
        [
            jnp.stack([me % 2, (me > 0).astype(jnp.int32), (me < slabs - 1).astype(jnp.int32)]),
            monitor_z - me * depth,
            monitor_span[:, 0],
            monitor_span[:, 1] - monitor_span[:, 0],
        ]
    ).astype(jnp.int32)
    tables = jnp.stack([mat_permit, mat_loss])
    moments = jnp.arange(1, STEPS + 1, dtype=jnp.int32)
    phase_turns = freq_bins[:, None] * moments[None, :] % PERIOD
    angles = phase_turns.astype(jnp.float32) * jnp.float32(2.0 * math.pi / PERIOD)
    phase_table = jnp.concatenate([jnp.cos(angles), -jnp.sin(angles)], 1)

    far_pairs = []
    for i in range(1, slabs - 1, 2):
        far_pairs += [(i, i + 1), (i + 1, i)]
    near_pairs = [(i, i ^ 1) for i in range(slabs)]

    def exchange(far, near):
        return lax.ppermute(far, "slab", far_pairs), lax.ppermute(near, "slab", near_pairs)

    def f32(*shape):
        return jax.ShapeDtypeStruct(shape, jnp.float32)

    d = ROUNDS[0]
    size = message_size(d, mats, depth, True)
    copies = sum(1 for _ in spots(down_pieces(d, mats))) + sum(
        1 for _ in spots(up_pieces(d, mats, depth, True))
    )
    with jax.named_scope("first_pack"):
        far, near = pl.pallas_call(
            functools.partial(first_pack_kernel, d, mats, depth),
            out_shape=[f32(size, height, width)] * 2,
            in_specs=[SMEM, ANY, ANY, ANY],
            out_specs=[VMEM] * 2,
            scratch_shapes=[
                pltpu.VMEM((2, mats, height, width), jnp.int32),
                pltpu.SemaphoreType.DMA((copies,)),
            ],
            compiler_params=params(),
        )(info, e_start, h_start, material)

    e, h = e_start, h_start
    keep = drive = hb = None
    chunks = []
    for k, d in enumerate(ROUNDS):
        first = k == 0
        nxt = ROUNDS[k + 1] if k + 1 < len(ROUNDS) else 0
        far, near = exchange(far, near)
        if first:
            operands = (e, h, material, far, near)
        else:
            operands = (e, h, keep, drive, hb, far, near)
        outs = [f32(*e.shape), f32(*h.shape)] + [f32(d, monitors, rows, width)] * 2
        if nxt:
            size = message_size(nxt, 0, depth, False)
            outs += [f32(3, height, width)] + [f32(size, height, width)] * 2
        if first:
            outs += [f32(depth + 2 * mats, height, width)] * 2
        extended = (3, depth + 2 * GHOST, height, width)
        with jax.named_scope(f"round{k}"):
            results = pl.pallas_call(
                functools.partial(round_kernel, d, nxt, first, depth, monitors, rows),
                out_shape=outs,
                in_specs=[SMEM, SMEM] + [VMEM] * len(operands),
                out_specs=[VMEM] * len(outs),
                scratch_shapes=[pltpu.VMEM(extended, jnp.float32)] * 2,
                compiler_params=params(),
            )(info, tables, *operands)
        e, h, mine, other = results[:4]
        results = results[4:]
        if nxt:
            hb, far, near = results[:3]
            results = results[3:]
        if first:
            keep, drive = results
        total = mine + lax.ppermute(other, "slab", near_pairs)
        stride = 2
        while stride < slabs:
            total = total + lax.ppermute(
                total, "slab", [(i, i ^ stride) for i in range(slabs)]
            )
            stride *= 2
        partner = lax.ppermute(total, "slab", near_pairs)
        chunks += [total, partner]

    with jax.named_scope("spectrum"):
        block = (1, 2, monitors, 2, height, width)
        spectrum = pl.pallas_call(
            functools.partial(spectrum_kernel, ROUNDS, freqs, monitors, height),
            out_shape=f32(freqs, *block[1:]),
            grid=(freqs,),
            in_specs=[SMEM, SMEM] + [VMEM] * len(chunks),
            out_specs=pl.BlockSpec(block, lambda f: (f, 0, 0, 0, 0, 0)),
            compiler_params=params(),
        )(info, phase_table, *chunks)
    return e, h, spectrum


def solution(mesh):
    slabs = mesh.shape["slab"]
    in_specs = (
        P(None, ("design", "slab"), None, None),
        P(None, ("design", "slab"), None, None),
        P(("design", "slab"), None, None),
        P(),
        P(),
        P(),
        P(),
        P("slab"),
    )
    out_specs = (
        P(None, ("design", "slab"), None, None),
        P(None, ("design", "slab"), None, None),
        P(("design", "slab"), None, None, None, None, None),
    )
    return jax.shard_map(
        functools.partial(per_device, slabs),
        mesh=mesh,
        in_specs=in_specs,
        out_specs=out_specs,
        check_vma=False,
    )
```

profile of v0, /device:TPU:0, one launch (start us, length us, event | category | flops | bytes accessed | tf_op | source)
XLA Modules:
  0.0 149.9 jit_solution(5855999365208990866)
XLA Ops:
  0.6 0.7 slice_bitcast_fusion
  1.3 0.8 bitcast_subtract_fusion
  2.1 0.1 concatenate.6.info
  2.2 1.4 copy-done
  3.6 1.4 copy-done.1
  5.0 1.0 copy-done.2
  6.0 2.8 %first_pack.1 = (f32[26,64,128]{2,1,0:T(8,128)S(1)}, f32[26,64,128]{2,1,0:T(8,128)S(1)}) custom-call(s32[15]{0:T(128)S(1)} %concatenate.6.info, f32[3,16,64,128]{3,2,1,0:T(8,128)S(1)} %copy-done, f32[3,16,64,128]{3,2,1,0:T(8,128)S(1)} %copy-done.1, s32[16,64,128]{2,1,0:T(8,128)S(1)} %copy-done.2), custom_call_target="tpu_custom_call" | custom-call | tf_op jit(solution)/shard_map/first_pack/pallas_call | solution.py:330
  8.8 0.7 collective-permute-start
  9.5 4.3 %collective-permute-start.1 = (f32[26,64,128]{2,1,0:T(8,128)S(1)}, f32[26,64,128]{2,1,0:T(8,128)S(1)}, u32[]{:S(2)}, u32[]{:S(2)}) collective-permute-start(f32[26,64,128]{2,1,0:T(8,128)S(1)} %get-tuple-element.26), channel_id=1, source_target_pairs={{0,1},{1,0},{2,3},{3,2},{4,5},{5,4},{6,7},{7,6},{8,9},{9,8},{10,11... | collective-permute-start | bytes 2555912 | tf_op jit(solution)/shard_map/ppermute | solution.py:319
  13.9 0.0 copy-done.6
  13.9 0.0 copy-done.7
  13.9 0.0 collective-permute-done.refs_3_
  13.9 2.0 %collective-permute-done.1.refs_4_ = f32[26,64,128]{2,1,0:T(8,128)S(1)} collective-permute-done((f32[26,64,128]{2,1,0:T(8,128)S(1)}, f32[26,64,128]{2,1,0:T(8,128)S(1)}, u32[]{:S(2)}, u32[]{:S(2)}) %collective-permute-start.1) | collective-permute-done | bytes 852000 | tf_op jit(solution)/shard_map/ppermute | solution.py:319
  15.9 0.0 copy-done.3
  15.9 17.8 %round0.1 = (f32[3,16,64,128]{3,2,1,0:T(8,128)}, f32[3,16,64,128]{3,2,1,0:T(8,128)}, f32[4,4,48,128]{3,2,1,0:T(8,128)S(1)}, f32[4,4,48,128]{3,2,1,0:T(8,128)S(1)...) custom-call(s32[15]{0:T(128)S(1)} %concatenate.6.info, ...), custom_call_target="tpu_custom_call" | custom-call | tf_op jit(solution)/shard_map/round0/pallas_call | solution.py:361
  33.7 16.7 %collective-permute-start.6 = (f32[4,4,48,128]{3,2,1,0:T(8,128)S(1)}, f32[4,4,48,128]{3,2,1,0:T(8,128)S(1)}, u32[]{:S(2)}, u32[]{:S(2)}) collective-permute-start(f32[4,4,48,128]{3,2,1,0:T(8,128)S(1)} %get-tuple-element.42), channel_id=1, source_target_pairs={{0,1},{1,0},{2,3},{3,2},{4,5},{5,4},{6,7},{7,6},{8,9},{9,8},{10,11... | collective-permute-start | bytes 1179656 | tf_op jit(solution)/shard_map/ppermute | solution.py:376
  50.3 0.7 collective-permute-start.2
  51.0 3.8 %collective-permute-start.3 = (f32[14,64,128]{2,1,0:T(8,128)S(1)}, f32[14,64,128]{2,1,0:T(8,128)S(1)}, u32[]{:S(2)}, u32[]{:S(2)}) collective-permute-start(f32[14,64,128]{2,1,0:T(8,128)S(1)} %get-tuple-element.33), channel_id=1, source_target_pairs={{0,1},{1,0},{2,3},{3,2},{4,5},{5,4},{6,7},{7,6},{8,9},{9,8},{10,11... | collective-permute-start | bytes 1376264 | tf_op jit(solution)/shard_map/ppermute | solution.py:319
  54.8 0.0 collective-permute-done.6
  54.8 0.1 add.56
  54.9 1.5 collective-permute-start.7
  56.3 0.0 collective-permute-done.2.refs_5_
  56.3 0.0 collective-permute-done.3.refs_6_
  56.3 13.0 %round1.1 = (f32[3,16,64,128]{3,2,1,0:T(8,128)S(1)}, f32[3,16,64,128]{3,2,1,0:T(8,128)}, f32[3,4,48,128]{3,2,1,0:T(8,128)S(1)}, f32[3,4,48,128]{3,2,1,0:T(8,128)...) custom-call(s32[15]{0:T(128)S(1)} %concatenate.6.info, ...), custom_call_target="tpu_custom_call" | custom-call | tf_op jit(solution)/shard_map/round1/pallas_call | solution.py:361
  69.3 11.9 %collective-permute-start.11 = (f32[3,4,48,128]{3,2,1,0:T(8,128)S(1)}, f32[3,4,48,128]{3,2,1,0:T(8,128)S(1)}, u32[]{:S(2)}, u32[]{:S(2)}) collective-permute-start(f32[3,4,48,128]{3,2,1,0:T(8,128)S(1)} %get-tuple-element.44), channel_id=1, source_target_pairs={{0,1},{1,0},{2,3},{3,2},{4,5},{5,4},{6,7},{7,6},{8,9},{9,8},{10,11... | collective-permute-start | bytes 884744 | tf_op jit(solution)/shard_map/ppermute | solution.py:376
  81.2 0.0 collective-permute-done.7
  81.2 0.1 add.57
  81.3 0.0 copy-start.4
  81.3 3.3 %collective-permute-start.8 = (f32[4,4,48,128]{3,2,1,0:T(8,128)S(1)}, f32[4,4,48,128]{3,2,1,0:T(8,128)S(1)}, u32[]{:S(2)}, u32[]{:S(2)}) collective-permute-start(f32[4,4,48,128]{3,2,1,0:T(8,128)S(1)} %add.57), channel_id=1, source_target_pairs={{0,4},{1,5},{2,6},{3,7},{4,0},{5,1},{6,2},{7,3},{8,12},{9,13},{10,... | collective-permute-start | bytes 1179656 | tf_op jit(solution)/shard_map/ppermute | solution.py:379
  84.5 0.0 collective-permute-done.11
  84.6 0.8 collective-permute-start.12
  85.4 7.9 %collective-permute-done.12 = f32[3,4,48,128]{3,2,1,0:T(8,128)S(1)} collective-permute-done((f32[3,4,48,128]{3,2,1,0:T(8,128)S(1)}, f32[3,4,48,128]{3,2,1,0:T(8,128)S(1)}, u32[]{:S(2)}, u32[]{:S(2)}) %collective-permute-start.12) | collective-permute-done | bytes 294944 | tf_op jit(solution)/shard_map/ppermute | solution.py:379
  93.3 1.8 %collective-permute-start.13 = (f32[3,4,48,128]{3,2,1,0:T(8,128)S(1)}, f32[3,4,48,128]{3,2,1,0:T(8,128)S(1)}, u32[]{:S(2)}, u32[]{:S(2)}) collective-permute-start(f32[3,4,48,128]{3,2,1,0:T(8,128)S(1)} %add.61), channel_id=1, source_target_pairs={{0,4},{1,5},{2,6},{3,7},{4,0},{5,1},{6,2},{7,3},{8,12},{9,13},{10,... | collective-permute-start | bytes 884744 | tf_op jit(solution)/shard_map/ppermute | solution.py:379
  95.1 0.0 collective-permute-done.8
  95.2 2.6 %collective-permute-start.9 = (f32[4,4,48,128]{3,2,1,0:T(8,128)S(1)}, f32[4,4,48,128]{3,2,1,0:T(8,128)S(1)}, u32[]{:S(2)}, u32[]{:S(2)}) collective-permute-start(f32[4,4,48,128]{3,2,1,0:T(8,128)S(1)} %add.58), channel_id=1, source_target_pairs={{0,8},{1,9},{2,10},{3,11},{4,12},{5,13},{6,14},{7,15},{8,0},{9,1},... | collective-permute-start | bytes 1179656 | tf_op jit(solution)/shard_map/ppermute | solution.py:379
  97.8 0.7 collective-permute-start.4
  98.5 1.7 %collective-permute-start.5 = (f32[3,64,128]{2,1,0:T(8,128)S(1)}, f32[3,64,128]{2,1,0:T(8,128)S(1)}, u32[]{:S(2)}, u32[]{:S(2)}) collective-permute-start(f32[3,64,128]{2,1,0:T(8,128)S(1)} %get-tuple-element.38), channel_id=1, source_target_pairs={{0,1},{1,0},{2,3},{3,2},{4,5},{5,4},{6,7},{7,6},{8,9},{9,8},{10,11... | collective-permute-start | bytes 294920 | tf_op jit(solution)/shard_map/ppermute | solution.py:319
  100.2 0.0 collective-permute-done.4.refs_5_
  100.2 0.9 collective-permute-done.5.refs_6_
  101.1 0.0 copy-done.4
  101.1 5.4 %round2.1 = (f32[3,16,64,128]{3,2,1,0:T(8,128)}, f32[3,16,64,128]{3,2,1,0:T(8,128)}, f32[1,4,48,128]{3,2,1,0:T(8,128)S(1)}, f32[1,4,48,128]{3,2,1,0:T(8,128)S(1)}) custom-call(s32[15]{0:T(128)S(1)} %concatenate.6.info, f32[2,4]{1,0:T(2,128)S(1)} %pad_maximum_fusion.1.tables, f32[3,16,64,128]{3,2,1,0:T(8,128)S(1)} %get-tuple-element.34.refs_0_, ...), custom_call_target="tpu_custom_call" | custom-call | tf_op jit(solution)/shard_map/round2/pallas_call | solution.py:361
  106.6 1.9 %collective-permute-start.16 = (f32[1,4,48,128]{3,2,1,0:T(8,128)S(1)}, f32[1,4,48,128]{3,2,1,0:T(8,128)S(1)}, u32[]{:S(2)}, u32[]{:S(2)}) collective-permute-start(f32[1,4,48,128]{3,2,1,0:T(8,128)S(1)} %get-tuple-element.46), channel_id=1, source_target_pairs={{0,1},{1,0},{2,3},{3,2},{4,5},{5,4},{6,7},{7,6},{8,9},{9,8},{10,11... | collective-permute-start | bytes 294920 | tf_op jit(solution)/shard_map/ppermute | solution.py:376
  108.5 0.0 collective-permute-done.13
  108.5 0.0 copy-start.5
  108.5 13.8 %collective-permute-start.14 = (f32[3,4,48,128]{3,2,1,0:T(8,128)S(1)}, f32[3,4,48,128]{3,2,1,0:T(8,128)S(1)}, u32[]{:S(2)}, u32[]{:S(2)}) collective-permute-start(f32[3,4,48,128]{3,2,1,0:T(8,128)S(1)} %add.62), channel_id=1, source_target_pairs={{0,8},{1,9},{2,10},{3,11},{4,12},{5,13},{6,14},{7,15},{8,0},{9,1},... | collective-permute-start | bytes 884744 | tf_op jit(solution)/shard_map/ppermute | solution.py:379
  122.3 0.0 collective-permute-done.16
  122.3 0.1 collective-permute-start.17
  122.4 4.9 %collective-permute-done.17 = f32[1,4,48,128]{3,2,1,0:T(8,128)S(1)} collective-permute-done((f32[1,4,48,128]{3,2,1,0:T(8,128)S(1)}, f32[1,4,48,128]{3,2,1,0:T(8,128)S(1)}, u32[]{:S(2)}, u32[]{:S(2)}) %collective-permute-start.17) | collective-permute-done | bytes 98336 | tf_op jit(solution)/shard_map/ppermute | solution.py:379
  127.3 0.3 collective-permute-start.18
  127.7 0.0 collective-permute-done.9
  127.7 0.1 collective-permute-start.10
  127.8 8.5 %collective-permute-done.18 = f32[1,4,48,128]{3,2,1,0:T(8,128)S(1)} collective-permute-done((f32[1,4,48,128]{3,2,1,0:T(8,128)S(1)}, f32[1,4,48,128]{3,2,1,0:T(8,128)S(1)}, u32[]{:S(2)}, u32[]{:S(2)}) %collective-permute-start.18) | collective-permute-done | bytes 98336 | tf_op jit(solution)/shard_map/ppermute | solution.py:379
  136.3 0.1 collective-permute-start.19
  136.3 0.0 collective-permute-done.14
  136.4 0.1 collective-permute-start.15
  136.5 0.0 copy-done.5
  136.5 0.1 fusion.3
  136.6 6.4 %collective-permute-done.19 = f32[1,4,48,128]{3,2,1,0:T(8,128)S(1)} collective-permute-done((f32[1,4,48,128]{3,2,1,0:T(8,128)S(1)}, f32[1,4,48,128]{3,2,1,0:T(8,128)S(1)}, u32[]{:S(2)}, u32[]{:S(2)}) %collective-permute-start.19) | collective-permute-done | bytes 98336 | tf_op jit(solution)/shard_map/ppermute | solution.py:379
  143.0 0.1 collective-permute-start.20
  143.1 0.1 pad_maximum_fusion.table
  143.2 1.2 collective-permute-done.20.refs_5_
  144.4 0.0 collective-permute-done.15.refs_3_
  144.4 0.0 collective-permute-done.10.refs_1_
  144.4 5.5 %spectrum.1 = f32[8,2,4,2,64,128]{5,4,3,2,1,0:T(8,128)} custom-call(s32[15]{0:T(128)S(1)} %concatenate.6.info, f32[8,16]{1,0:T(8,128)S(1)} %pad_maximum_fusion.table, f32[4,4,48,128]{3,2,1,0:T(8,128)S(1)} %add.59.refs_0_, f32[4,4,48,128]{3,2,1,0:T(8,128)S(1)} %collective-permute-done.10.refs_1_, f32[3,4,48,128]{3,2,1,0:T(8,128)S(1)} %add.63.refs_2_, ...), custom_call_target="tpu_custom_call" | custom-call | tf_op jit(solution)/shard_map/spectrum/pallas_call | solution.py:388
  (18 shorter events, 0.3 us)
Async XLA Ops:
  2.2 1.4 copy-start
  3.6 1.4 copy-start.1
  5.0 1.0 copy-start.2
  6.0 7.9 %copy-start.6 = (f32[4]{0:T(128)S(1)}, f32[4]{0:T(128)}, u32[]{:S(2)}) copy-start(f32[4]{0:T(128)} %param.12) | copy-start | bytes 52
  6.0 7.9 %copy-start.7 = (f32[4]{0:T(128)S(1)}, f32[4]{0:T(128)}, u32[]{:S(2)}) copy-start(f32[4]{0:T(128)} %param.11) | copy-start | bytes 52
  6.0 9.9 %copy-start.3 = (s32[16,64,128]{2,1,0:T(8,128)S(1)}, s32[16,64,128]{2,1,0:T(8,128)}, u32[]{:S(2)}) copy-start(s32[16,64,128]{2,1,0:T(8,128)} %refs_2_.1) | copy-start | bytes 1572868
  8.8 5.1 %collective-permute-start = (f32[26,64,128]{2,1,0:T(8,128)S(1)}, f32[26,64,128]{2,1,0:T(8,128)S(1)}, u32[]{:S(2)}, u32[]{:S(2)}) collective-permute-start(f32[26,64,128]{2,1,0:T(8,128)S(1)} %get-tuple-element.25), channel_id=1, source_target_pairs={{1,2},{2,1},{3,4},{4,3},{5,6},{6,5},{7,8},{8,7},{9,10},{10,9},{11,... | collective-permute-start | bytes 2555912 | tf_op jit(solution)/shard_map/ppermute | solution.py:319
  9.5 6.3 %collective-permute-start.1 = (f32[26,64,128]{2,1,0:T(8,128)S(1)}, f32[26,64,128]{2,1,0:T(8,128)S(1)}, u32[]{:S(2)}, u32[]{:S(2)}) collective-permute-start(f32[26,64,128]{2,1,0:T(8,128)S(1)} %get-tuple-element.26), channel_id=1, source_target_pairs={{0,1},{1,0},{2,3},{3,2},{4,5},{5,4},{6,7},{7,6},{8,9},{9,8},{10,11... | collective-permute-start | bytes 2555912 | tf_op jit(solution)/shard_map/ppermute | solution.py:319
  33.7 21.1 %collective-permute-start.6 = (f32[4,4,48,128]{3,2,1,0:T(8,128)S(1)}, f32[4,4,48,128]{3,2,1,0:T(8,128)S(1)}, u32[]{:S(2)}, u32[]{:S(2)}) collective-permute-start(f32[4,4,48,128]{3,2,1,0:T(8,128)S(1)} %get-tuple-element.42), channel_id=1, source_target_pairs={{0,1},{1,0},{2,3},{3,2},{4,5},{5,4},{6,7},{7,6},{8,9},{9,8},{10,11... | collective-permute-start | bytes 1179656 | tf_op jit(solution)/shard_map/ppermute | solution.py:376
  50.3 6.0 %collective-permute-start.2 = (f32[14,64,128]{2,1,0:T(8,128)S(1)}, f32[14,64,128]{2,1,0:T(8,128)S(1)}, u32[]{:S(2)}, u32[]{:S(2)}) collective-permute-start(f32[14,64,128]{2,1,0:T(8,128)S(1)} %get-tuple-element.32), channel_id=1, source_target_pairs={{1,2},{2,1},{3,4},{4,3},{5,6},{6,5},{7,8},{8,7},{9,10},{10,9},{11,... | collective-permute-start | bytes 1376264 | tf_op jit(solution)/shard_map/ppermute | solution.py:319
  51.0 5.3 %collective-permute-start.3 = (f32[14,64,128]{2,1,0:T(8,128)S(1)}, f32[14,64,128]{2,1,0:T(8,128)S(1)}, u32[]{:S(2)}, u32[]{:S(2)}) collective-permute-start(f32[14,64,128]{2,1,0:T(8,128)S(1)} %get-tuple-element.33), channel_id=1, source_target_pairs={{0,1},{1,0},{2,3},{3,2},{4,5},{5,4},{6,7},{7,6},{8,9},{9,8},{10,11... | collective-permute-start | bytes 1376264 | tf_op jit(solution)/shard_map/ppermute | solution.py:319
  54.9 26.4 %collective-permute-start.7 = (f32[4,4,48,128]{3,2,1,0:T(8,128)S(1)}, f32[4,4,48,128]{3,2,1,0:T(8,128)S(1)}, u32[]{:S(2)}, u32[]{:S(2)}) collective-permute-start(f32[4,4,48,128]{3,2,1,0:T(8,128)S(1)} %add.56), channel_id=1, source_target_pairs={{0,2},{1,3},{2,0},{3,1},{4,6},{5,7},{6,4},{7,5},{8,10},{9,11},{10,... | collective-permute-start | bytes 1179656 | tf_op jit(solution)/shard_map/ppermute | solution.py:379
  69.3 15.2 %collective-permute-start.11 = (f32[3,4,48,128]{3,2,1,0:T(8,128)S(1)}, f32[3,4,48,128]{3,2,1,0:T(8,128)S(1)}, u32[]{:S(2)}, u32[]{:S(2)}) collective-permute-start(f32[3,4,48,128]{3,2,1,0:T(8,128)S(1)} %get-tuple-element.44), channel_id=1, source_target_pairs={{0,1},{1,0},{2,3},{3,2},{4,5},{5,4},{6,7},{7,6},{8,9},{9,8},{10,11... | collective-permute-start | bytes 884744 | tf_op jit(solution)/shard_map/ppermute | solution.py:376
  81.3 19.9 %copy-start.4 = (f32[3,16,64,128]{3,2,1,0:T(8,128)S(1)}, f32[3,16,64,128]{3,2,1,0:T(8,128)}, u32[]{:S(2)}) copy-start(f32[3,16,64,128]{3,2,1,0:T(8,128)} %get-tuple-element.35.refs_1_) | copy-start | bytes 4718596
  81.3 13.8 %collective-permute-start.8 = (f32[4,4,48,128]{3,2,1,0:T(8,128)S(1)}, f32[4,4,48,128]{3,2,1,0:T(8,128)S(1)}, u32[]{:S(2)}, u32[]{:S(2)}) collective-permute-start(f32[4,4,48,128]{3,2,1,0:T(8,128)S(1)} %add.57), channel_id=1, source_target_pairs={{0,4},{1,5},{2,6},{3,7},{4,0},{5,1},{6,2},{7,3},{8,12},{9,13},{10,... | collective-permute-start | bytes 1179656 | tf_op jit(solution)/shard_map/ppermute | solution.py:379
  84.6 8.7 %collective-permute-start.12 = (f32[3,4,48,128]{3,2,1,0:T(8,128)S(1)}, f32[3,4,48,128]{3,2,1,0:T(8,128)S(1)}, u32[]{:S(2)}, u32[]{:S(2)}) collective-permute-start(f32[3,4,48,128]{3,2,1,0:T(8,128)S(1)} %add.60), channel_id=1, source_target_pairs={{0,2},{1,3},{2,0},{3,1},{4,6},{5,7},{6,4},{7,5},{8,10},{9,11},{10,... | collective-permute-start | bytes 884744 | tf_op jit(solution)/shard_map/ppermute | solution.py:379
  93.3 15.1 %collective-permute-start.13 = (f32[3,4,48,128]{3,2,1,0:T(8,128)S(1)}, f32[3,4,48,128]{3,2,1,0:T(8,128)S(1)}, u32[]{:S(2)}, u32[]{:S(2)}) collective-permute-start(f32[3,4,48,128]{3,2,1,0:T(8,128)S(1)} %add.61), channel_id=1, source_target_pairs={{0,4},{1,5},{2,6},{3,7},{4,0},{5,1},{6,2},{7,3},{8,12},{9,13},{10,... | collective-permute-start | bytes 884744 | tf_op jit(solution)/shard_map/ppermute | solution.py:379
  95.2 32.5 %collective-permute-start.9 = (f32[4,4,48,128]{3,2,1,0:T(8,128)S(1)}, f32[4,4,48,128]{3,2,1,0:T(8,128)S(1)}, u32[]{:S(2)}, u32[]{:S(2)}) collective-permute-start(f32[4,4,48,128]{3,2,1,0:T(8,128)S(1)} %add.58), channel_id=1, source_target_pairs={{0,8},{1,9},{2,10},{3,11},{4,12},{5,13},{6,14},{7,15},{8,0},{9,1},... | collective-permute-start | bytes 1179656 | tf_op jit(solution)/shard_map/ppermute | solution.py:379
  97.8 2.4 %collective-permute-start.4 = (f32[3,64,128]{2,1,0:T(8,128)S(1)}, f32[3,64,128]{2,1,0:T(8,128)S(1)}, u32[]{:S(2)}, u32[]{:S(2)}) collective-permute-start(f32[3,64,128]{2,1,0:T(8,128)S(1)} %get-tuple-element.37), channel_id=1, source_target_pairs={{1,2},{2,1},{3,4},{4,3},{5,6},{6,5},{7,8},{8,7},{9,10},{10,9},{11,... | collective-permute-start | bytes 294920 | tf_op jit(solution)/shard_map/ppermute | solution.py:319
  98.5 2.7 %collective-permute-start.5 = (f32[3,64,128]{2,1,0:T(8,128)S(1)}, f32[3,64,128]{2,1,0:T(8,128)S(1)}, u32[]{:S(2)}, u32[]{:S(2)}) collective-permute-start(f32[3,64,128]{2,1,0:T(8,128)S(1)} %get-tuple-element.38), channel_id=1, source_target_pairs={{0,1},{1,0},{2,3},{3,2},{4,5},{5,4},{6,7},{7,6},{8,9},{9,8},{10,11... | collective-permute-start | bytes 294920 | tf_op jit(solution)/shard_map/ppermute | solution.py:319
  106.6 15.8 %collective-permute-start.16 = (f32[1,4,48,128]{3,2,1,0:T(8,128)S(1)}, f32[1,4,48,128]{3,2,1,0:T(8,128)S(1)}, u32[]{:S(2)}, u32[]{:S(2)}) collective-permute-start(f32[1,4,48,128]{3,2,1,0:T(8,128)S(1)} %get-tuple-element.46), channel_id=1, source_target_pairs={{0,1},{1,0},{2,3},{3,2},{4,5},{5,4},{6,7},{7,6},{8,9},{9,8},{10,11... | collective-permute-start | bytes 294920 | tf_op jit(solution)/shard_map/ppermute | solution.py:376
  108.5 28.0 %copy-start.5 = (s32[8]{0:T(128)S(1)}, s32[8]{0:T(128)}, u32[]{:S(2)}) copy-start(s32[8]{0:T(128)} %param.15) | copy-start | bytes 100
  108.5 27.8 %collective-permute-start.14 = (f32[3,4,48,128]{3,2,1,0:T(8,128)S(1)}, f32[3,4,48,128]{3,2,1,0:T(8,128)S(1)}, u32[]{:S(2)}, u32[]{:S(2)}) collective-permute-start(f32[3,4,48,128]{3,2,1,0:T(8,128)S(1)} %add.62), channel_id=1, source_target_pairs={{0,8},{1,9},{2,10},{3,11},{4,12},{5,13},{6,14},{7,15},{8,0},{9,1},... | collective-permute-start | bytes 884744 | tf_op jit(solution)/shard_map/ppermute | solution.py:379
  122.3 5.0 %collective-permute-start.17 = (f32[1,4,48,128]{3,2,1,0:T(8,128)S(1)}, f32[1,4,48,128]{3,2,1,0:T(8,128)S(1)}, u32[]{:S(2)}, u32[]{:S(2)}) collective-permute-start(f32[1,4,48,128]{3,2,1,0:T(8,128)S(1)} %add.64), channel_id=1, source_target_pairs={{0,2},{1,3},{2,0},{3,1},{4,6},{5,7},{6,4},{7,5},{8,10},{9,11},{10,... | collective-permute-start | bytes 294920 | tf_op jit(solution)/shard_map/ppermute | solution.py:379
  127.3 8.9 %collective-permute-start.18 = (f32[1,4,48,128]{3,2,1,0:T(8,128)S(1)}, f32[1,4,48,128]{3,2,1,0:T(8,128)S(1)}, u32[]{:S(2)}, u32[]{:S(2)}) collective-permute-start(f32[1,4,48,128]{3,2,1,0:T(8,128)S(1)} %add.65), channel_id=1, source_target_pairs={{0,4},{1,5},{2,6},{3,7},{4,0},{5,1},{6,2},{7,3},{8,12},{9,13},{10,... | collective-permute-start | bytes 294920 | tf_op jit(solution)/shard_map/ppermute | solution.py:379
  127.7 16.7 %collective-permute-start.10 = (f32[4,4,48,128]{3,2,1,0:T(8,128)S(1)}, f32[4,4,48,128]{3,2,1,0:T(8,128)S(1)}, u32[]{:S(2)}, u32[]{:S(2)}) collective-permute-start(f32[4,4,48,128]{3,2,1,0:T(8,128)S(1)} %add.59.refs_0_), channel_id=1, source_target_pairs={{0,1},{1,0},{2,3},{3,2},{4,5},{5,4},{6,7},{7,6},{8,9},{9,8},{10,11... | collective-permute-start | bytes 1179656 | tf_op jit(solution)/shard_map/ppermute | solution.py:383
  136.3 6.8 %collective-permute-start.19 = (f32[1,4,48,128]{3,2,1,0:T(8,128)S(1)}, f32[1,4,48,128]{3,2,1,0:T(8,128)S(1)}, u32[]{:S(2)}, u32[]{:S(2)}) collective-permute-start(f32[1,4,48,128]{3,2,1,0:T(8,128)S(1)} %add.66), channel_id=1, source_target_pairs={{0,8},{1,9},{2,10},{3,11},{4,12},{5,13},{6,14},{7,15},{8,0},{9,1},... | collective-permute-start | bytes 294920 | tf_op jit(solution)/shard_map/ppermute | solution.py:379
  136.4 8.0 %collective-permute-start.15 = (f32[3,4,48,128]{3,2,1,0:T(8,128)S(1)}, f32[3,4,48,128]{3,2,1,0:T(8,128)S(1)}, u32[]{:S(2)}, u32[]{:S(2)}) collective-permute-start(f32[3,4,48,128]{3,2,1,0:T(8,128)S(1)} %add.63.refs_2_), channel_id=1, source_target_pairs={{0,1},{1,0},{2,3},{3,2},{4,5},{5,4},{6,7},{7,6},{8,9},{9,8},{10,11... | collective-permute-start | bytes 884744 | tf_op jit(solution)/shard_map/ppermute | solution.py:383
  143.0 1.4 collective-permute-start.20
where the time goes:
time: 150 us
  starting transfers between devices  66.8 us (45%)
  Pallas kernels  44.4 us (30%)
  waiting for transfers between devices  31.8 us (21%)
  local copies, waits for them, and re-layouts  4.65 us (3%)
    pallas_call x3, Pallas kernels, per_device(): pl.pallas_call(functools.partial(round_kernel, d, nxt, first, depth, moni...  36.2 us
    ppermute x3, starting transfers between devices, per_device(): total = mine + lax.ppermute(other, 'slab', near_pairs)  30.4 us
    ppermute x9, waiting for transfers between devices, per_device(): lax.ppermute(total, 'slab', [(i, i ^ stride) for i in range(slabs)])  27.7 us
    ppermute x9, starting transfers between devices, per_device(): lax.ppermute(total, 'slab', [(i, i ^ stride) for i in range(slabs)])  24.2 us
    ppermute x3, starting transfers between devices, exchange(): lax.ppermute(near, 'slab', near_pairs)  9.82 us
    pallas_call x1, Pallas kernels, per_device(): pl.pallas_call(functools.partial(spectrum_kernel, ROUNDS, freqs, monitors...  5.47 us
    unnamed x16, local copies, waits for them, and re-layouts  3.89 us
  transfers between devices with their start and end apart: 21, of which 7 were waited for; matrix products, arithmetic and copies ran while one was open for 0% of the time, Pallas kernels for 12%

commit v1 on v0

v1 whole, which is shorter than its diff:
```python
import functools
import math

import jax
import jax.numpy as jnp
from jax import lax
from jax.experimental import pallas as pl
from jax.experimental.pallas import tpu as pltpu
from jax.sharding import PartitionSpec as P

STEPS = 8
PERIOD = 512
ROUNDS = (4, 4)
SCATTER = (True, True)
GHOST = max(ROUNDS)
COURANT = 0.5
VMEM = pl.BlockSpec(memory_space=pltpu.VMEM)
SMEM = pl.BlockSpec(memory_space=pltpu.SMEM)
ANY = pl.BlockSpec(memory_space=pl.ANY)
HBM = pl.BlockSpec(memory_space=pltpu.HBM)
LIMIT = 24 * 1024 * 1024
PAD = 8


def params():
    return pltpu.CompilerParams(vmem_limit_bytes=LIMIT)


def cost(microseconds):
    return pl.CostEstimate(
        flops=0, bytes_accessed=int(microseconds * 3.0e6), transcendentals=0
    )


def down_pieces(d, mats):
    pieces = [("e", 0, 2, 0, d)]
    if d > 1:
        pieces += [("e", 2, 1, 0, d - 1), ("h", 0, 3, 0, d - 1)]
    if mats:
        pieces += [("m", 0, 1, 0, mats)]
    return pieces


def up_pieces(d, mats, depth, first):
    pieces = [("e", 0, 3, depth - d, d)]
    if first:
        pieces += [("h", 0, 2, depth - d, d)]
        if d > 1:
            pieces += [("h", 2, 1, depth - d + 1, d - 1)]
    else:
        if d > 1:
            pieces += [("h", 0, 2, depth - d, d - 1)]
        if d > 2:
            pieces += [("h", 2, 1, depth - d + 1, d - 2)]
    if mats:
        pieces += [("m", 0, 1, depth - mats, mats)]
    return pieces


def size_of(pieces):
    return sum(p[2] * p[4] for p in pieces)


def message_size(d, mats, depth, first):
    return max(size_of(down_pieces(d, mats)), size_of(up_pieces(d, mats, depth, first)))


def spots(pieces):
    at = 0
    for name, comp, comps, plane, planes in pieces:
        for c in range(comp, comp + comps):
            yield name, c, plane, planes, at
            at += planes


def start_all(pairs, sem):
    copies = [pltpu.make_async_copy(a, b, sem.at[k]) for k, (a, b) in enumerate(pairs)]
    for copy in copies:
        copy.start()
    return copies


def first_pack_kernel(d, mats, depth, e_ref, h_ref, m_ref, far_ref, near_ref, m_buf, sem):
    even = lax.rem(lax.axis_index("slab"), 2) == 0

    def pack(down_ref, up_ref):
        sides = (
            (down_pieces(d, mats), down_ref),
            (up_pieces(d, mats, depth, True), up_ref),
        )
        moves = []
        for k, (pieces, out) in enumerate(sides):
            for name, c, plane, planes, at in spots(pieces):
                if name == "m":
                    moves.append((m_ref.at[pl.ds(plane, planes)], m_buf.at[k]))
                else:
                    source = e_ref if name == "e" else h_ref
                    moves.append((source.at[c, pl.ds(plane, planes)], out.at[pl.ds(at, planes)]))
        for copy in start_all(moves, sem):
            copy.wait()
        if mats:
            for k, (pieces, out) in enumerate(sides):
                out[pl.ds(size_of(pieces) - mats, mats)] = m_buf[k].astype(jnp.float32)

    @pl.when(even)
    def _():
        pack(far_ref, near_ref)

    @pl.when(jnp.logical_not(even))
    def _():
        pack(near_ref, far_ref)


class Yee:
    def __init__(self, e, h, coefs, height, width, first_plane, below):
        self.e, self.h, self.coefs = e, h, coefs
        self.first_plane, self.width = first_plane, width
        self.own = pl.ds(PAD, height)
        self.next_row, self.last_row = pl.ds(PAD + 1, height), pl.ds(PAD - 1, height)
        lane = lax.broadcasted_iota(jnp.int32, (height, width), 1)
        self.lane_last, self.lane_first = lane == width - 1, lane == 0
        self.ghost_factor = None if below is None else COURANT * below.astype(jnp.float32)
        planes = e.shape[1]
        e[:, :, pl.ds(PAD + height, PAD)] = jnp.zeros((3, planes, PAD, width), jnp.float32)
        h[:, :, pl.ds(0, PAD)] = jnp.zeros((3, planes, PAD, width), jnp.float32)

    def fore_x(self, v):
        return jnp.where(self.lane_last, 0.0, pltpu.roll(v, self.width - 1, 1)) - v

    def back_x(self, v):
        return v - jnp.where(self.lane_first, 0.0, pltpu.roll(v, 1, 1))

    def step_h(self, z, ghost=False):
        e, h, own, up = self.e, self.h, self.own, self.next_row
        at = self.first_plane + z
        factor = self.ghost_factor if ghost else COURANT
        ex, ey, ez = e[0, at, own], e[1, at, own], e[2, at, own]
        h[0, at, own] = h[0, at, own] - factor * ((e[2, at, up] - ez) - (e[1, at + 1, own] - ey))
        h[1, at, own] = h[1, at, own] - factor * ((e[0, at + 1, own] - ex) - self.fore_x(ez))
        h[2, at, own] = h[2, at, own] - factor * (self.fore_x(ey) - (e[0, at, up] - ex))

    def step_e(self, z):
        e, h, own, down = self.e, self.h, self.own, self.last_row
        at = self.first_plane + z
        hx, hy, hz = h[0, at, own], h[1, at, own], h[2, at, own]
        keep, drive = self.coefs[0, at], self.coefs[1, at]
        e[0, at, own] = keep * e[0, at, own] + drive * (
            (hz - h[2, at, down]) - (hy - h[1, at - 1, own])
        )
        e[1, at, own] = keep * e[1, at, own] + drive * (
            (hx - h[0, at - 1, own]) - self.back_x(hz)
        )
        e[2, at, own] = keep * e[2, at, own] + drive * (self.back_x(hy) - (hx - h[0, at, down]))


def material_tables(tables, width):
    loss = [jnp.full((1, width), tables[1, k], jnp.float32) for k in range(tables.shape[1])]
    permit = [jnp.full((1, width), tables[0, k], jnp.float32) for k in range(tables.shape[1])]
    keeps = [(1.0 - x) / (1.0 + x) for x in loss]
    drives = [COURANT / (p * (1.0 + x)) for p, x in zip(permit, loss)]
    return keeps, drives


def look_up(values, which):
    total = jnp.broadcast_to(values[0], which.shape)
    for k in range(1, len(values)):
        total = jnp.where(which == k, values[k], total)
    return total


def monitor_info(info, m, monitors):
    return info[4 + m], info[4 + monitors + m], info[4 + 2 * monitors + m]


def take_sample(e, c, spot, start, extent, rows):
    height, width = e.shape[2] - 2 * PAD, e.shape[3]
    plane = pltpu.roll(e[c, spot, pl.ds(PAD, height)], height - start, 0)[:rows]
    return jnp.where(lax.broadcasted_iota(jnp.int32, (rows, width), 0) < extent, plane, 0.0)


def inner_kernel(d, first, depth, monitors, rows, info, *refs):
    if first:
        tables, e_in, h_in, m_in, e_out, h_out, coefs_out, mine_out, other_out = refs[:9]
        e, h, coefs, m_buf, sem = refs[9:]
    else:
        e_in, h_in, coefs_in, e_out, h_out, mine_out, other_out = refs[:7]
        e, h, coefs, sem = refs[7:]
    height, width = e_in.shape[2:]
    g = 1
    own, inside = pl.ds(g, depth), pl.ds(PAD, height)
    moves = [(e_in.at[c], e.at[c, own, inside]) for c in range(3)]
    moves += [(h_in.at[c], h.at[c, own, inside]) for c in range(3)]
    if first:
        moves.append((m_in, m_buf))
    else:
        moves += [(coefs_in.at[k], coefs.at[k, own]) for k in range(2)]
    copies = start_all(moves, sem)
    yee = Yee(e, h, coefs, height, width, g, None)
    if first:
        copies.pop().wait()
        keeps, drives = material_tables(tables, width)

        def fill(z, _):
            which = m_buf[z]
            coefs[0, g + z] = look_up(keeps, which)
            coefs[1, g + z] = look_up(drives, which)
            return 0

        lax.fori_loop(0, depth, fill, 0)
    for copy in copies:
        copy.wait()

    mine, other = info[0], 1 - info[0]
    group = 4
    for s in range(1, d + 1):
        low, high = s, depth - s
        yee.step_h(low - 1)

        def chunk(base, planes):
            for u in range(planes):
                yee.step_h(base + u)
            for u in range(planes):
                yee.step_e(base + u)

        whole = (high - low) // group

        def body(k, _):
            chunk(low + group * k, group)
            return 0

        lax.fori_loop(0, whole, body, 0)
        if low + group * whole < high:
            chunk(low + group * whole, high - low - group * whole)
        for m in range(monitors):
            offset, start, extent = monitor_info(info, m, monitors)
            held = jnp.logical_and(offset >= low, offset < high)
            taken = jnp.where(held, extent, 0)
            spot = g + jnp.clip(offset, 0, depth - 1)
            mine_out[m, s - 1] = take_sample(e, mine, spot, start, taken, rows)
            other_out[m, s - 1] = take_sample(e, other, spot, start, taken, rows)

    moves = [(e.at[c, own, inside], e_out.at[c]) for c in range(3)]
    moves += [(h.at[c, own, inside], h_out.at[c]) for c in range(3)]
    if first:
        moves += [(coefs.at[k, own], coefs_out.at[k]) for k in range(2)]
    for copy in start_all(moves, sem):
        copy.wait()


def edge_kernel(d, nxt, first, depth, monitors, rows, info, *refs):
    e_in, h_in, coefs_in, mine_in, other_in, far_in, near_in = refs[:7]
    refs = refs[7:]
    mats = GHOST - 1
    if first:
        tables, refs = refs[0], refs[1:]
    else:
        ghosts_in, below_in, refs = refs[0], refs[1], refs[2:]
    e_out, h_out, mine_out, other_out, refs = *refs[:4], refs[4:]
    if nxt:
        below_out, far_out, near_out, refs = *refs[:3], refs[3:]
        if first:
            ghosts_out, refs = refs[0], refs[1:]
    e, h, coefs, sem = refs
    height, width = e_in.shape[2:]
    g = GHOST
    inside = pl.ds(PAD, height)
    even = info[0] == 0
    below, above = info[1], info[2]

    moves = []
    for plane, planes in ((0, d), (depth - 1 - d, d + 1)):
        for c in range(3):
            part, place = pl.ds(plane, planes), pl.ds(g + plane, planes)
            moves.append((e_in.at[c, part], e.at[c, place, inside]))
            moves.append((h_in.at[c, part], h.at[c, place, inside]))
    for plane in (0, depth - d):
        for k in range(2):
            moves.append((coefs_in.at[k, pl.ds(plane, d)], coefs.at[k, pl.ds(g + plane, d)]))
    copies = start_all(moves, sem)
    yee = Yee(e, h, coefs, height, width, g, below)

    sides = (
        (-depth, up_pieces(d, mats if first else 0, depth, first)),
        (depth, down_pieces(d, mats if first else 0)),
    )

    def unpack(below_ref, above_ref):
        for (shift, pieces), source in zip(sides, (below_ref, above_ref)):
            for name, c, plane, planes, at in spots(pieces):
                where = pl.ds(g + plane + shift, planes)
                value = source[pl.ds(at, planes)]
                if name == "e":
                    e[c, where, inside] = value
                elif name == "h":
                    h[c, where, inside] = value
                else:
                    coefs[0, where] = value

    @pl.when(even)
    def _():
        unpack(far_in, near_in)

    @pl.when(jnp.logical_not(even))
    def _():
        unpack(near_in, far_in)

    ghost_planes = list(range(g - mats, g)) + list(range(g + depth, g + depth + mats))
    if first:
        keeps, drives = material_tables(tables, width)
        for at in ghost_planes:
            alive = (below if at < g else above).astype(jnp.float32)
            which = coefs[0, at].astype(jnp.int32)
            coefs[0, at] = look_up(keeps, which) * alive
            coefs[1, at] = look_up(drives, which) * alive
        if nxt:
            for k, at in enumerate(ghost_planes):
                ghosts_out[:, k] = coefs[:, at]
    else:
        for k, at in enumerate(ghost_planes):
            coefs[:, at] = ghosts_in[:, k]
        h[:, g - 1, inside] = below_in[...]
    for copy in copies:
        copy.wait()

    mine, other = info[0], 1 - info[0]
    for s in range(1, d + 1):
        lower = list(range(s - d, s))
        upper = list(range(depth - s, depth + d - s))
        for z in lower:
            yee.step_h(z - 1, z - 1 < 0)
        for z in upper:
            yee.step_h(z)
        for z in lower + upper:
            yee.step_e(z)
        for m in range(monitors):
            offset, start, extent = monitor_info(info, m, monitors)
            held = jnp.logical_or(
                jnp.logical_and(offset >= 0, offset < s),
                jnp.logical_and(offset >= depth - s, offset < depth),
            )
            spot = g + jnp.clip(offset, 0, depth - 1)
            for out, before, c in ((mine_out, mine_in, mine), (other_out, other_in, other)):
                fresh = take_sample(e, c, spot, start, extent, rows)
                out[m, s - 1] = jnp.where(held, fresh, before[m, s - 1])

    moves = []
    for plane in (0, depth - d):
        part, place = pl.ds(plane, d), pl.ds(g + plane, d)
        for c in range(3):
            moves.append((e.at[c, place, inside], e_out.at[c, part]))
            moves.append((h.at[c, place, inside], h_out.at[c, part]))
    copies = start_all(moves, sem)
    if nxt:
        below_out[...] = h[:, g - 1, inside]

        def pack(down_ref, up_ref):
            for pieces, out in (
                (down_pieces(nxt, 0), down_ref),
                (up_pieces(nxt, 0, depth, False), up_ref),
            ):
                for name, c, plane, planes, at in spots(pieces):
                    source = e if name == "e" else h
                    out[pl.ds(at, planes)] = source[c, pl.ds(g + plane, planes), inside]

        @pl.when(even)
        def _():
            pack(far_out, near_out)

        @pl.when(jnp.logical_not(even))
        def _():
            pack(near_out, far_out)

    for copy in copies:
        copy.wait()


def spectrum_kernel(chunks, scattered, monitors, height, info, table, *refs):
    samples = refs[: 2 * len(chunks)]
    out = refs[-1]
    rows, width = samples[0].shape[2:]
    f = pl.program_id(0)
    steps = sum(chunks)
    pad = jnp.zeros((height - rows, width), jnp.float32)
    for m in range(monitors):
        start = monitor_info(info, m, monitors)[1]
        for side in range(2):
            c = info[0] if side == 0 else 1 - info[0]
            planes = []
            for k, d in enumerate(chunks):
                at = jnp.bitwise_xor(m, info[3]) if scattered[k] else m
                planes += [samples[2 * k + side][at, t] for t in range(d)]
            for part in range(2):
                total = planes[0] * table[f, part * steps]
                for t in range(1, steps):
                    total = total + planes[t] * table[f, part * steps + t]
                out[0, part, m, c] = pltpu.roll(jnp.concatenate([total, pad], 0), start, 0)


def share(total, slabs, scatter):
    def swap(block, stride):
        return lax.ppermute(block, "slab", [(i, i ^ stride) for i in range(slabs)])

    strides = [2**k for k in range(1, slabs.bit_length() - 1)]
    if not scatter:
        for stride in strides:
            total = total + swap(total, stride)
        return total
    quarter = lax.axis_index("slab") // 4 % 4
    pieces = [
        swap(lax.dynamic_index_in_dim(total, quarter ^ x, 0, keepdims=False), 4 * x)
        for x in (1, 2, 3)
    ]
    part = lax.dynamic_index_in_dim(total, quarter, 0, keepdims=False)
    for piece in pieces:
        part = part + piece
    for stride in strides:
        if stride not in (4, 8):
            part = part + swap(part, stride)
    return jnp.stack([part] + [swap(part, 4 * x) for x in (1, 2, 3)])


def per_device(
    slabs, e_start, h_start, material, mat_permit, mat_loss, monitor_z, monitor_span, freq_bins
):
    depth, height, width = e_start.shape[1:]
    monitors = monitor_z.shape[0]
    freqs = freq_bins.shape[0]
    rows = 3 * height // 4
    mats = GHOST - 1
    me = lax.axis_index("slab")
    info = jnp.concatenate(
        [
            jnp.stack(
                [
                    me % 2,
                    (me > 0).astype(jnp.int32),
                    (me < slabs - 1).astype(jnp.int32),
                    me // 4 % 4,
                ]
            ),
            monitor_z - me * depth,
            monitor_span[:, 0],
            monitor_span[:, 1] - monitor_span[:, 0],
        ]
    ).astype(jnp.int32)
    tables = jnp.stack([mat_permit, mat_loss])
    moments = jnp.arange(1, STEPS + 1, dtype=jnp.int32)
    phase_turns = freq_bins[:, None] * moments[None, :] % PERIOD
    angles = phase_turns.astype(jnp.float32) * jnp.float32(2.0 * math.pi / PERIOD)
    phase_table = jnp.concatenate([jnp.cos(angles), -jnp.sin(angles)], 1)

    far_pairs = []
    for i in range(1, slabs - 1, 2):
        far_pairs += [(i, i + 1), (i + 1, i)]
    near_pairs = [(i, i ^ 1) for i in range(slabs)]

    def near_swap(block):
        return lax.ppermute(block, "slab", near_pairs)

    def f32(*shape):
        return jax.ShapeDtypeStruct(shape, jnp.float32)

    def scratch(ghosts):
        planes = depth + 2 * ghosts
        padded = (3, planes, height + 2 * PAD, width)
        return [pltpu.VMEM(padded, jnp.float32)] * 2 + [
            pltpu.VMEM((2, planes, height, width), jnp.float32)
        ]

    d = ROUNDS[0]
    size = message_size(d, mats, depth, True)
    copies = sum(1 for _ in spots(down_pieces(d, mats))) + sum(
        1 for _ in spots(up_pieces(d, mats, depth, True))
    )
    with jax.named_scope("first_pack"):
        far, near = pl.pallas_call(
            functools.partial(first_pack_kernel, d, mats, depth),
            out_shape=[f32(size, height, width)] * 2,
            in_specs=[HBM] * 3,
            out_specs=[VMEM] * 2,
            scratch_shapes=[
                pltpu.VMEM((2, mats, height, width), jnp.int32),
                pltpu.SemaphoreType.DMA((copies,)),
            ],
            compiler_params=params(),
            cost_estimate=cost(2),
        )(e_start, h_start, material)

    state = [f32(*e_start.shape), f32(*h_start.shape)]
    e, h = e_start, h_start
    coefs = ghosts = below = None
    chunks = []
    for k, d in enumerate(ROUNDS):
        first = k == 0
        nxt = ROUNDS[k + 1] if k + 1 < len(ROUNDS) else 0
        far = lax.ppermute(far, "slab", far_pairs)
        near = near_swap(near)
        samples = [f32(monitors, d, rows, width)] * 2
        with jax.named_scope(f"inner{k}"):
            kernel = functools.partial(inner_kernel, d, first, depth, monitors, rows)
            if first:
                e, h, coefs, mine, other = pl.pallas_call(
                    kernel,
                    out_shape=state + [f32(2, depth, height, width)] + samples,
                    in_specs=[SMEM, SMEM, HBM, HBM, HBM],
                    out_specs=[ANY] * 3 + [VMEM] * 2,
                    scratch_shapes=scratch(1)
                    + [
                        pltpu.VMEM((depth, height, width), jnp.int32),
                        pltpu.SemaphoreType.DMA((8,)),
                    ],
                    compiler_params=params(),
                    cost_estimate=cost(5),
                )(info, tables, e, h, material)
            else:
                e, h, mine, other = pl.pallas_call(
                    kernel,
                    out_shape=state + samples,
                    in_specs=[SMEM] + [ANY] * 3,
                    out_specs=[ANY] * 2 + [VMEM] * 2,
                    input_output_aliases={1: 0, 2: 1},
                    scratch_shapes=scratch(1) + [pltpu.SemaphoreType.DMA((8,))],
                    compiler_params=params(),
                    cost_estimate=cost(5),
                )(info, e, h, coefs)
        operands = [info, e, h, coefs, mine, other, far, near]
        specs = [SMEM] + [ANY] * 3 + [VMEM] * 4
        if first:
            operands += [tables]
            specs += [SMEM]
        else:
            operands += [ghosts, below]
            specs += [VMEM] * 2
        outs = state + samples
        if nxt:
            size = message_size(nxt, 0, depth, False)
            outs = outs + [f32(3, height, width)] + [f32(size, height, width)] * 2
            if first:
                outs = outs + [f32(2, 2 * mats, height, width)]
        with jax.named_scope(f"edge{k}"):
            results = pl.pallas_call(
                functools.partial(edge_kernel, d, nxt, first, depth, monitors, rows),
                out_shape=outs,
                in_specs=specs,
                out_specs=[ANY] * 2 + [VMEM] * (len(outs) - 2),
                input_output_aliases={1: 0, 2: 1},
                scratch_shapes=scratch(GHOST) + [pltpu.SemaphoreType.DMA((16,))],
                compiler_params=params(),
                cost_estimate=cost(4),
            )(*operands)
        e, h, mine, other = results[:4]
        if nxt:
            below, far, near = results[4:7]
            if first:
                ghosts = results[7]
        total = share(mine + near_swap(other), slabs, SCATTER[k])
        chunks += [total, near_swap(total)]

    with jax.named_scope("spectrum"):
        block = (1, 2, monitors, 2, height, width)
        spectrum = pl.pallas_call(
            functools.partial(spectrum_kernel, ROUNDS, SCATTER, monitors, height),
            out_shape=f32(freqs, *block[1:]),
            grid=(freqs,),
            in_specs=[SMEM, SMEM] + [VMEM] * len(chunks),
            out_specs=pl.BlockSpec(block, lambda f: (f, 0, 0, 0, 0, 0)),
            compiler_params=params(),
            cost_estimate=cost(5),
        )(info, phase_table, *chunks)
    return e, h, spectrum


def solution(mesh):
    slabs = mesh.shape["slab"]
    in_specs = (
        P(None, ("design", "slab"), None, None),
        P(None, ("design", "slab"), None, None),
        P(("design", "slab"), None, None),
        P(),
        P(),
        P(),
        P(),
        P("slab"),
    )
    out_specs = (
        P(None, ("design", "slab"), None, None),
        P(None, ("design", "slab"), None, None),
        P(("design", "slab"), None, None, None, None, None),
    )
    return jax.shard_map(
        functools.partial(per_device, slabs),
        mesh=mesh,
        in_specs=in_specs,
        out_specs=out_specs,
        check_vma=False,
    )
```

time: 150 us -> 107 us (0.71)
  starting transfers between devices: 66.8 us -> 44.8 us
  Pallas kernels: 44.4 us -> 33.5 us
  waiting for transfers between devices: 31.8 us -> 22 us
    ppermute x21 -> x22, starting transfers between devices: 66.8 us -> 44.8 us  [the longest x14 22 us: swap(): return lax.ppermute(block, 'slab', [(i, i ^ stride) for i in range(slabs)])]
    pallas_call x4 -> x5, Pallas kernels: 41.7 us -> 30 us  [the longest x2 11.8 us: per_device(): pl.pallas_call(functools.partial(edge_kernel, d, nxt, first, depth, monit...]
    ppermute x21 -> x22, waiting for transfers between devices: 31.8 us -> 22 us  [the longest x14 20.5 us: swap(): return lax.ppermute(block, 'slab', [(i, i ^ stride) for i in range(slabs)])]
    unnamed x16 -> x22, local copies, waits for them, and re-layouts: 3.89 us -> 4.92 us
  transfers between devices with their start and end apart: 21 -> 22, of which waited for: 7 -> 5; matrix products, arithmetic and copies ran while one was open for 0% -> 1% of each run, Pallas kernels for 12% -> 17%
where the time goes in v1:
time: 107 us
  starting transfers between devices  44.8 us (42%)
  Pallas kernels  33.5 us (31%)
  waiting for transfers between devices  22 us (21%)
  local copies, waits for them, and re-layouts  5.06 us (5%)
    ppermute x14, starting transfers between devices, swap(): return lax.ppermute(block, 'slab', [(i, i ^ stride) for i in range(slabs)])  22 us
    ppermute x6, starting transfers between devices, near_swap(): return lax.ppermute(block, 'slab', near_pairs)  20.6 us
    ppermute x14, waiting for transfers between devices, swap(): return lax.ppermute(block, 'slab', [(i, i ^ stride) for i in range(slabs)])  20.5 us
    pallas_call x2, Pallas kernels, per_device(): pl.pallas_call(functools.partial(edge_kernel, d, nxt, first, depth, monit...  11.8 us
    pallas_call x1, Pallas kernels, per_device(): pl.pallas_call(kernel, out_shape=state + samples, in_specs=[SMEM] + [ANY]...  7.03 us
    pallas_call x1, Pallas kernels, per_device(): pl.pallas_call(kernel, out_shape=state + [f32(2, depth, height, width)] +...  5.75 us
    pallas_call x1, Pallas kernels, per_device(): pl.pallas_call(functools.partial(spectrum_kernel, ROUNDS, SCATTER, monito...  5.46 us
    unnamed x22, local copies, waits for them, and re-layouts  4.92 us
  transfers between devices with their start and end apart: 22, of which 5 were waited for; matrix products, arithmetic and copies ran while one was open for 1% of the time, Pallas kernels for 17%

profile of v1, /device:TPU:0, one launch (start us, length us, event | category | flops | bytes accessed | tf_op | source)
XLA Modules:
  0.0 106.6 jit_solution(2929293730960864621)
XLA Ops:
  0.6 0.0 copy-start
  0.6 1.4 %copy-done = f32[3,16,64,128]{3,2,1,0:T(8,128)S(1)} copy-done((f32[3,16,64,128]{3,2,1,0:T(8,128)S(1)}, f32[3,16,64,128]{3,2,1,0:T(8,128)}, u32[]{:S(2)}) %copy-start) | copy-done | bytes 1572888
  2.0 1.4 %copy-done.2 = f32[3,16,64,128]{3,2,1,0:T(8,128)S(1)} copy-done((f32[3,16,64,128]{3,2,1,0:T(8,128)S(1)}, f32[3,16,64,128]{3,2,1,0:T(8,128)}, u32[]{:S(2)}) %copy-start.2) | copy-done | bytes 1572888
  3.5 1.0 copy-done.4
  4.5 0.0 copy-start.1
  4.5 0.0 copy-start.3
  4.5 3.4 %first_pack.1 = (f32[26,64,128]{2,1,0:T(8,128)}, f32[26,64,128]{2,1,0:T(8,128)}) custom-call(f32[3,16,64,128]{3,2,1,0:T(8,128)S(1)} %copy-done, f32[3,16,64,128]{3,2,1,0:T(8,128)S(1)} %copy-done.2, s32[16,64,128]{2,1,0:T(8,128)S(1)} %copy-done.4), custom_call_target="tpu_custom_call" | custom-call | bytes 6000000 | tf_op jit(solution)/shard_map/first_pack/pallas_call | solution.py:476
  8.0 1.6 %collective-permute-start = (f32[26,64,128]{2,1,0:T(8,128)}, f32[26,64,128]{2,1,0:T(8,128)}, u32[]{:S(2)}, u32[]{:S(2)}) collective-permute-start(f32[26,64,128]{2,1,0:T(8,128)} %get-tuple-element.31), channel_id=1, source_target_pairs={{1,2},{2,1},{3,4},{4,3},{5,6},{6,5},{7,8},{8,7},{9,10},{10,9},{11,... | collective-permute-start | bytes 2555912 | tf_op jit(solution)/shard_map/ppermute | solution.py:496
  9.6 3.5 %collective-permute-start.1 = (f32[26,64,128]{2,1,0:T(8,128)}, f32[26,64,128]{2,1,0:T(8,128)}, u32[]{:S(2)}, u32[]{:S(2)}) collective-permute-start(f32[26,64,128]{2,1,0:T(8,128)} %get-tuple-element.32), channel_id=1, source_target_pairs={{0,1},{1,0},{2,3},{3,2},{4,5},{5,4},{6,7},{7,6},{8,9},{9,8},{10,11... | collective-permute-start | bytes 2555912 | tf_op jit(solution)/shard_map/ppermute | solution.py:458
  13.0 0.0 copy-done.6
  13.1 0.1 concatenate.6.info
  13.1 0.0 copy-done.10
  13.2 0.0 copy-start.5
  13.2 1.0 copy-done.5
  14.2 5.8 %inner0.1 = (f32[3,16,64,128]{3,2,1,0:T(8,128)}, f32[3,16,64,128]{3,2,1,0:T(8,128)}, f32[2,16,64,128]{3,2,1,0:T(8,128)S(1)}, f32[4,4,48,128]{3,2,1,0:T(8,128)S(1)}, f32[4,4,48,128]{3,2,1,0:T(8,128)S(1)}) custom-call(s32[16]{0:T(128)S(1)} %concatenate.6.info, f32[2,4]{1,0:T(2,128)S(1)} %pad_maximum_fusion.3.refs_0_.refs_7_, f32[3,16,64,128]{3,2,1,0:T(8,128)S(1)} %copy-done.1, ...), custom_call_target="tpu_custom_call" | custom-call | bytes 15000000 | tf_op jit(solution)/shard_map/inner0/pallas_call | solution.py:502
  20.0 0.0 collective-permute-done.refs_5_
  20.0 0.0 collective-permute-done.1.refs_6_
  20.0 6.4 %edge0.1 = (f32[3,16,64,128]{3,2,1,0:T(8,128)}, f32[3,16,64,128]{3,2,1,0:T(8,128)}, f32[4,4,48,128]{3,2,1,0:T(8,128)S(1)}, f32[4,4,48,128]{3,2,1,0:T(8,128)S(1)}...) custom-call(s32[16]{0:T(128)S(1)} %concatenate.6.info, ...), custom_call_target="tpu_custom_call", output_to_operand_aliasing={{0}: (1, {}), {1}: (2, {})} | custom-call | bytes 12000000 | tf_op jit(solution)/shard_map/edge0/pallas_call | solution.py:541
  26.4 0.7 collective-permute-start.2
  27.1 15.8 %collective-permute-start.3 = (f32[20,64,128]{2,1,0:T(8,128)S(1)}, f32[20,64,128]{2,1,0:T(8,128)S(1)}, u32[]{:S(2)}, u32[]{:S(2)}) collective-permute-start(f32[20,64,128]{2,1,0:T(8,128)S(1)} %get-tuple-element.40), channel_id=1, source_target_pairs={{0,1},{1,0},{2,3},{3,2},{4,5},{5,4},{6,7},{7,6},{8,9},{9,8},{10,11... | collective-permute-start | bytes 1966088 | tf_op jit(solution)/shard_map/ppermute | solution.py:458
  42.9 0.1 collective-permute-start.4
  42.9 7.0 %inner1.1 = (f32[3,16,64,128]{3,2,1,0:T(8,128)}, f32[3,16,64,128]{3,2,1,0:T(8,128)}, f32[4,4,48,128]{3,2,1,0:T(8,128)S(1)}, f32[4,4,48,128]{3,2,1,0:T(8,128)S(1)}) custom-call(s32[16]{0:T(128)S(1)} %concatenate.6.info, f32[3,16,64,128]{3,2,1,0:T(8,128)} %get-tuple-element.33.refs_0_, ...), custom_call_target="tpu_custom_call", output_to_operand_aliasing={{0}: (1, {}), {1}: (2, {})} | custom-call | bytes 15000000 | tf_op jit(solution)/shard_map/inner1/pallas_call | solution.py:516
  50.0 0.0 collective-permute-done.2.refs_5_
  50.0 0.0 collective-permute-done.3.refs_6_
  50.0 5.4 %edge1.1 = (f32[3,16,64,128]{3,2,1,0:T(8,128)}, f32[3,16,64,128]{3,2,1,0:T(8,128)}, f32[4,4,48,128]{3,2,1,0:T(8,128)S(1)}, f32[4,4,48,128]{3,2,1,0:T(8,128)S(1)}) custom-call(s32[16]{0:T(128)S(1)} %concatenate.6.info, f32[3,16,64,128]{3,2,1,0:T(8,128)} %get-tuple-element.35.refs_0_, ...), custom_call_target="tpu_custom_call", output_to_operand_aliasing={{0}: (1, {}), {1}: (2, {})} | custom-call | bytes 12000000 | tf_op jit(solution)/shard_map/edge1/pallas_call | solution.py:541
  55.4 1.1 %collective-permute-start.13 = (f32[4,4,48,128]{3,2,1,0:T(8,128)S(1)}, f32[4,4,48,128]{3,2,1,0:T(8,128)S(1)}, u32[]{:S(2)}, u32[]{:S(2)}) collective-permute-start(f32[4,4,48,128]{3,2,1,0:T(8,128)S(1)} %get-tuple-element.48), channel_id=1, source_target_pairs={{0,1},{1,0},{2,3},{3,2},{4,5},{5,4},{6,7},{7,6},{8,9},{9,8},{10,11... | collective-permute-start | bytes 1179656 | tf_op jit(solution)/shard_map/ppermute | solution.py:458
  56.5 0.0 collective-permute-done.4
  56.6 1.6 %collective-permute-start.5 = (f32[4,48,128]{2,1,0:T(8,128)S(1)}, f32[4,48,128]{2,1,0:T(8,128)S(1)}, u32[]{:S(2)}, u32[]{:S(2)}) collective-permute-start(f32[4,48,128]{2,1,0:T(8,128)S(1)} %get-tuple-element.52), channel_id=1, source_target_pairs={{0,4},{1,5},{2,6},{3,7},{4,0},{5,1},{6,2},{7,3},{8,12},{9,13},{10,... | collective-permute-start | bytes 294920 | tf_op jit(solution)/shard_map/ppermute | solution.py:401
  58.2 2.6 %collective-permute-start.6 = (f32[4,48,128]{2,1,0:T(8,128)S(1)}, f32[4,48,128]{2,1,0:T(8,128)S(1)}, u32[]{:S(2)}, u32[]{:S(2)}) collective-permute-start(f32[4,48,128]{2,1,0:T(8,128)S(1)} %get-tuple-element.54), channel_id=1, source_target_pairs={{0,8},{1,9},{2,10},{3,11},{4,12},{5,13},{6,14},{7,15},{8,0},{9,1},... | collective-permute-start | bytes 294920 | tf_op jit(solution)/shard_map/ppermute | solution.py:401
  60.8 0.2 collective-permute-start.7
  61.1 0.0 collective-permute-done.13
  61.1 0.7 collective-permute-start.14
  61.9 3.5 %collective-permute-start.15 = (f32[4,48,128]{2,1,0:T(8,128)S(1)}, f32[4,48,128]{2,1,0:T(8,128)S(1)}, u32[]{:S(2)}, u32[]{:S(2)}) collective-permute-start(f32[4,48,128]{2,1,0:T(8,128)S(1)} %get-tuple-element.51), channel_id=1, source_target_pairs={{0,8},{1,9},{2,10},{3,11},{4,12},{5,13},{6,14},{7,15},{8,0},{9,1},... | collective-permute-start | bytes 294920 | tf_op jit(solution)/shard_map/ppermute | solution.py:401
  65.4 0.0 collective-permute-done.5
  65.4 0.7 collective-permute-start.16
  66.1 2.8 %collective-permute-done.6 = f32[4,48,128]{2,1,0:T(8,128)S(1)} collective-permute-done((f32[4,48,128]{2,1,0:T(8,128)S(1)}, f32[4,48,128]{2,1,0:T(8,128)S(1)}, u32[]{:S(2)}, u32[]{:S(2)}) %collective-permute-start.6) | collective-permute-done | bytes 98336 | tf_op jit(solution)/shard_map/ppermute | solution.py:401
  68.9 0.0 collective-permute-done.7
  68.9 1.8 %collective-permute-start.8 = (f32[4,48,128]{2,1,0:T(8,128)S(1)}, f32[4,48,128]{2,1,0:T(8,128)S(1)}, u32[]{:S(2)}, u32[]{:S(2)}) collective-permute-start(f32[4,48,128]{2,1,0:T(8,128)S(1)} %fusion.3), channel_id=1, source_target_pairs={{0,2},{1,3},{2,0},{3,1},{4,6},{5,7},{6,4},{7,5},{8,10},{9,11},{10,... | collective-permute-start | bytes 294920 | tf_op jit(solution)/shard_map/ppermute | solution.py:401
  70.8 0.0 collective-permute-done.14
  70.8 6.6 %collective-permute-done.15 = f32[4,48,128]{2,1,0:T(8,128)S(1)} collective-permute-done((f32[4,48,128]{2,1,0:T(8,128)S(1)}, f32[4,48,128]{2,1,0:T(8,128)S(1)}, u32[]{:S(2)}, u32[]{:S(2)}) %collective-permute-start.15) | collective-permute-done | bytes 98336 | tf_op jit(solution)/shard_map/ppermute | solution.py:401
  77.3 0.0 collective-permute-done.16
  77.4 1.8 %collective-permute-start.17 = (f32[4,48,128]{2,1,0:T(8,128)S(1)}, f32[4,48,128]{2,1,0:T(8,128)S(1)}, u32[]{:S(2)}, u32[]{:S(2)}) collective-permute-start(f32[4,48,128]{2,1,0:T(8,128)S(1)} %fusion.1), channel_id=1, source_target_pairs={{0,2},{1,3},{2,0},{3,1},{4,6},{5,7},{6,4},{7,5},{8,10},{9,11},{10,... | collective-permute-start | bytes 294920 | tf_op jit(solution)/shard_map/ppermute | solution.py:401
  79.2 0.0 collective-permute-done.8
  79.2 2.0 %collective-permute-start.9 = (f32[4,48,128]{2,1,0:T(8,128)S(1)}, f32[4,48,128]{2,1,0:T(8,128)S(1)}, u32[]{:S(2)}, u32[]{:S(2)}) collective-permute-start(f32[4,48,128]{2,1,0:T(8,128)S(1)} %add.82), channel_id=1, source_target_pairs={{0,4},{1,5},{2,6},{3,7},{4,0},{5,1},{6,2},{7,3},{8,12},{9,13},{10,... | collective-permute-start | bytes 294920 | tf_op jit(solution)/shard_map/ppermute | solution.py:401
  81.2 1.1 %collective-permute-start.10 = (f32[4,48,128]{2,1,0:T(8,128)S(1)}, f32[4,48,128]{2,1,0:T(8,128)S(1)}, u32[]{:S(2)}, u32[]{:S(2)}) collective-permute-start(f32[4,48,128]{2,1,0:T(8,128)S(1)} %add.82), channel_id=1, source_target_pairs={{0,8},{1,9},{2,10},{3,11},{4,12},{5,13},{6,14},{7,15},{8,0},{9,1},... | collective-permute-start | bytes 294920 | tf_op jit(solution)/shard_map/ppermute | solution.py:401
  82.3 1.4 %collective-permute-start.11 = (f32[4,48,128]{2,1,0:T(8,128)S(1)}, f32[4,48,128]{2,1,0:T(8,128)S(1)}, u32[]{:S(2)}, u32[]{:S(2)}) collective-permute-start(f32[4,48,128]{2,1,0:T(8,128)S(1)} %add.82), channel_id=1, source_target_pairs={{0,12},{1,13},{2,14},{3,15},{4,8},{5,9},{6,10},{7,11},{8,4},{9,5},... | collective-permute-start | bytes 294920 | tf_op jit(solution)/shard_map/ppermute | solution.py:401
  83.7 0.0 collective-permute-done.17
  83.7 1.0 collective-permute-start.18
  84.8 2.0 %collective-permute-start.19 = (f32[4,48,128]{2,1,0:T(8,128)S(1)}, f32[4,48,128]{2,1,0:T(8,128)S(1)}, u32[]{:S(2)}, u32[]{:S(2)}) collective-permute-start(f32[4,48,128]{2,1,0:T(8,128)S(1)} %add.87), channel_id=1, source_target_pairs={{0,8},{1,9},{2,10},{3,11},{4,12},{5,13},{6,14},{7,15},{8,0},{9,1},... | collective-permute-start | bytes 294920 | tf_op jit(solution)/shard_map/ppermute | solution.py:401
  86.8 0.0 collective-permute-done.9
  86.8 1.4 %collective-permute-start.20 = (f32[4,48,128]{2,1,0:T(8,128)S(1)}, f32[4,48,128]{2,1,0:T(8,128)S(1)}, u32[]{:S(2)}, u32[]{:S(2)}) collective-permute-start(f32[4,48,128]{2,1,0:T(8,128)S(1)} %add.87), channel_id=1, source_target_pairs={{0,12},{1,13},{2,14},{3,15},{4,8},{5,9},{6,10},{7,11},{8,4},{9,5},... | collective-permute-start | bytes 294920 | tf_op jit(solution)/shard_map/ppermute | solution.py:401
  88.2 3.8 %collective-permute-done.10 = f32[4,48,128]{2,1,0:T(8,128)S(1)} collective-permute-done((f32[4,48,128]{2,1,0:T(8,128)S(1)}, f32[4,48,128]{2,1,0:T(8,128)S(1)}, u32[]{:S(2)}, u32[]{:S(2)}) %collective-permute-start.10) | collective-permute-done | bytes 98336 | tf_op jit(solution)/shard_map/ppermute | solution.py:401
  92.0 0.0 collective-permute-done.11
  92.0 0.1 collective-permute-start.12
  92.1 0.0 collective-permute-done.18
  92.1 7.3 %collective-permute-done.19 = f32[4,48,128]{2,1,0:T(8,128)S(1)} collective-permute-done((f32[4,48,128]{2,1,0:T(8,128)S(1)}, f32[4,48,128]{2,1,0:T(8,128)S(1)}, u32[]{:S(2)}, u32[]{:S(2)}) %collective-permute-start.19) | collective-permute-done | bytes 98336 | tf_op jit(solution)/shard_map/ppermute | solution.py:401
  99.3 0.0 collective-permute-done.20
  99.4 0.1 collective-permute-start.21
  99.5 0.0 copy-done.7
  99.5 0.1 fusion.7
  99.6 0.1 pad_maximum_fusion.2.table
  99.7 0.0 collective-permute-done.12.refs_1_
  99.7 1.5 %collective-permute-done.21.refs_3_ = f32[4,4,48,128]{3,2,1,0:T(8,128)S(1)} collective-permute-done((f32[4,4,48,128]{3,2,1,0:T(8,128)S(1)}, f32[4,4,48,128]{3,2,1,0:T(8,128)S(1)}, u32[]{:S(2)}, u32[]{:S(2)}) %collective-permute-start.21) | collective-permute-done | bytes 393248 | tf_op jit(solution)/shard_map/ppermute | solution.py:458
  101.2 5.5 %spectrum.1 = f32[8,2,4,2,64,128]{5,4,3,2,1,0:T(8,128)} custom-call(s32[16]{0:T(128)S(1)} %concatenate.6.info, f32[8,16]{1,0:T(8,128)S(1)} %pad_maximum_fusion.2.table, f32[4,4,48,128]{3,2,1,0:T(8,128)S(1)} %pad_maximum_fusion.refs_0_, f32[4,4,48,128]{3,2,1,0:T(8,128)S(1)} %collective-permute-done.12.refs_1_, ...), custom_call_target="tpu_custom_call" | custom-call | bytes 15000000 | tf_op jit(solution)/shard_map/spectrum/pallas_call | solution.py:561
  (25 shorter events, 0.3 us)
Async XLA Ops:
  0.6 1.4 %copy-start = (f32[3,16,64,128]{3,2,1,0:T(8,128)S(1)}, f32[3,16,64,128]{3,2,1,0:T(8,128)}, u32[]{:S(2)}) copy-start(f32[3,16,64,128]{3,2,1,0:T(8,128)} %e_ref.1) | copy-start | bytes 4718596
  2.0 1.4 %copy-start.2 = (f32[3,16,64,128]{3,2,1,0:T(8,128)S(1)}, f32[3,16,64,128]{3,2,1,0:T(8,128)}, u32[]{:S(2)}) copy-start(f32[3,16,64,128]{3,2,1,0:T(8,128)} %h_ref.1) | copy-start | bytes 4718596
  3.4 1.0 copy-start.4
  4.5 8.5 %copy-start.6 = (s32[4,2]{0,1:T(2,128)S(1)}, s32[4,2]{0,1:T(2,128)}, u32[]{:S(2)}) copy-start(s32[4,2]{0,1:T(2,128)} %param.14) | copy-start | bytes 100
  4.5 8.6 %copy-start.8 = (s32[4]{0:T(128)S(1)}, s32[4]{0:T(128)}, u32[]{:S(2)}) copy-start(s32[4]{0:T(128)} %param.13) | copy-start | bytes 52
  4.5 8.6 %copy-start.9 = (f32[4]{0:T(128)S(1)}, f32[4]{0:T(128)}, u32[]{:S(2)}) copy-start(f32[4]{0:T(128)} %param.12) | copy-start | bytes 52
  4.5 8.6 %copy-start.10 = (f32[4]{0:T(128)S(1)}, f32[4]{0:T(128)}, u32[]{:S(2)}) copy-start(f32[4]{0:T(128)} %param.11) | copy-start | bytes 52
  4.5 8.7 %copy-start.1 = (f32[3,16,64,128]{3,2,1,0:T(8,128)S(1)}, f32[3,16,64,128]{3,2,1,0:T(8,128)}, u32[]{:S(2)}) copy-start(f32[3,16,64,128]{3,2,1,0:T(8,128)} %e_ref.1) | copy-start | bytes 4718596
  4.5 8.7 %copy-start.3 = (f32[3,16,64,128]{3,2,1,0:T(8,128)S(1)}, f32[3,16,64,128]{3,2,1,0:T(8,128)}, u32[]{:S(2)}) copy-start(f32[3,16,64,128]{3,2,1,0:T(8,128)} %h_ref.1) | copy-start | bytes 4718596
  8.0 12.0 %collective-permute-start = (f32[26,64,128]{2,1,0:T(8,128)}, f32[26,64,128]{2,1,0:T(8,128)}, u32[]{:S(2)}, u32[]{:S(2)}) collective-permute-start(f32[26,64,128]{2,1,0:T(8,128)} %get-tuple-element.31), channel_id=1, source_target_pairs={{1,2},{2,1},{3,4},{4,3},{5,6},{6,5},{7,8},{8,7},{9,10},{10,9},{11,... | collective-permute-start | bytes 2555912 | tf_op jit(solution)/shard_map/ppermute | solution.py:496
  9.6 10.4 %collective-permute-start.1 = (f32[26,64,128]{2,1,0:T(8,128)}, f32[26,64,128]{2,1,0:T(8,128)}, u32[]{:S(2)}, u32[]{:S(2)}) collective-permute-start(f32[26,64,128]{2,1,0:T(8,128)} %get-tuple-element.32), channel_id=1, source_target_pairs={{0,1},{1,0},{2,3},{3,2},{4,5},{5,4},{6,7},{7,6},{8,9},{9,8},{10,11... | collective-permute-start | bytes 2555912 | tf_op jit(solution)/shard_map/ppermute | solution.py:458
  13.2 1.0 copy-start.5
  26.4 23.6 %collective-permute-start.2 = (f32[20,64,128]{2,1,0:T(8,128)S(1)}, f32[20,64,128]{2,1,0:T(8,128)S(1)}, u32[]{:S(2)}, u32[]{:S(2)}) collective-permute-start(f32[20,64,128]{2,1,0:T(8,128)S(1)} %get-tuple-element.39), channel_id=1, source_target_pairs={{1,2},{2,1},{3,4},{4,3},{5,6},{6,5},{7,8},{8,7},{9,10},{10,9},{11,... | collective-permute-start | bytes 1966088 | tf_op jit(solution)/shard_map/ppermute | solution.py:496
  27.1 22.9 %collective-permute-start.3 = (f32[20,64,128]{2,1,0:T(8,128)S(1)}, f32[20,64,128]{2,1,0:T(8,128)S(1)}, u32[]{:S(2)}, u32[]{:S(2)}) collective-permute-start(f32[20,64,128]{2,1,0:T(8,128)S(1)} %get-tuple-element.40), channel_id=1, source_target_pairs={{0,1},{1,0},{2,3},{3,2},{4,5},{5,4},{6,7},{7,6},{8,9},{9,8},{10,11... | collective-permute-start | bytes 1966088 | tf_op jit(solution)/shard_map/ppermute | solution.py:458
  42.9 13.6 %collective-permute-start.4 = (f32[4,4,48,128]{3,2,1,0:T(8,128)S(1)}, f32[4,4,48,128]{3,2,1,0:T(8,128)S(1)}, u32[]{:S(2)}, u32[]{:S(2)}) collective-permute-start(f32[4,4,48,128]{3,2,1,0:T(8,128)S(1)} %get-tuple-element.46), channel_id=1, source_target_pairs={{0,1},{1,0},{2,3},{3,2},{4,5},{5,4},{6,7},{7,6},{8,9},{9,8},{10,11... | collective-permute-start | bytes 1179656 | tf_op jit(solution)/shard_map/ppermute | solution.py:458
  55.4 5.7 %collective-permute-start.13 = (f32[4,4,48,128]{3,2,1,0:T(8,128)S(1)}, f32[4,4,48,128]{3,2,1,0:T(8,128)S(1)}, u32[]{:S(2)}, u32[]{:S(2)}) collective-permute-start(f32[4,4,48,128]{3,2,1,0:T(8,128)S(1)} %get-tuple-element.48), channel_id=1, source_target_pairs={{0,1},{1,0},{2,3},{3,2},{4,5},{5,4},{6,7},{7,6},{8,9},{9,8},{10,11... | collective-permute-start | bytes 1179656 | tf_op jit(solution)/shard_map/ppermute | solution.py:458
  56.6 8.8 %collective-permute-start.5 = (f32[4,48,128]{2,1,0:T(8,128)S(1)}, f32[4,48,128]{2,1,0:T(8,128)S(1)}, u32[]{:S(2)}, u32[]{:S(2)}) collective-permute-start(f32[4,48,128]{2,1,0:T(8,128)S(1)} %get-tuple-element.52), channel_id=1, source_target_pairs={{0,4},{1,5},{2,6},{3,7},{4,0},{5,1},{6,2},{7,3},{8,12},{9,13},{10,... | collective-permute-start | bytes 294920 | tf_op jit(solution)/shard_map/ppermute | solution.py:401
  58.2 10.6 %collective-permute-start.6 = (f32[4,48,128]{2,1,0:T(8,128)S(1)}, f32[4,48,128]{2,1,0:T(8,128)S(1)}, u32[]{:S(2)}, u32[]{:S(2)}) collective-permute-start(f32[4,48,128]{2,1,0:T(8,128)S(1)} %get-tuple-element.54), channel_id=1, source_target_pairs={{0,8},{1,9},{2,10},{3,11},{4,12},{5,13},{6,14},{7,15},{8,0},{9,1},... | collective-permute-start | bytes 294920 | tf_op jit(solution)/shard_map/ppermute | solution.py:401
  60.8 8.1 %collective-permute-start.7 = (f32[4,48,128]{2,1,0:T(8,128)S(1)}, f32[4,48,128]{2,1,0:T(8,128)S(1)}, u32[]{:S(2)}, u32[]{:S(2)}) collective-permute-start(f32[4,48,128]{2,1,0:T(8,128)S(1)} %get-tuple-element.53), channel_id=1, source_target_pairs={{0,12},{1,13},{2,14},{3,15},{4,8},{5,9},{6,10},{7,11},{8,4},{9,5},... | collective-permute-start | bytes 294920 | tf_op jit(solution)/shard_map/ppermute | solution.py:401
  61.1 9.6 %collective-permute-start.14 = (f32[4,48,128]{2,1,0:T(8,128)S(1)}, f32[4,48,128]{2,1,0:T(8,128)S(1)}, u32[]{:S(2)}, u32[]{:S(2)}) collective-permute-start(f32[4,48,128]{2,1,0:T(8,128)S(1)} %get-tuple-element.49), channel_id=1, source_target_pairs={{0,4},{1,5},{2,6},{3,7},{4,0},{5,1},{6,2},{7,3},{8,12},{9,13},{10,... | collective-permute-start | bytes 294920 | tf_op jit(solution)/shard_map/ppermute | solution.py:401
  61.9 15.4 %collective-permute-start.15 = (f32[4,48,128]{2,1,0:T(8,128)S(1)}, f32[4,48,128]{2,1,0:T(8,128)S(1)}, u32[]{:S(2)}, u32[]{:S(2)}) collective-permute-start(f32[4,48,128]{2,1,0:T(8,128)S(1)} %get-tuple-element.51), channel_id=1, source_target_pairs={{0,8},{1,9},{2,10},{3,11},{4,12},{5,13},{6,14},{7,15},{8,0},{9,1},... | collective-permute-start | bytes 294920 | tf_op jit(solution)/shard_map/ppermute | solution.py:401
  65.4 34.1 %copy-start.7 = (s32[8]{0:T(128)S(1)}, s32[8]{0:T(128)}, u32[]{:S(2)}) copy-start(s32[8]{0:T(128)} %param.15) | copy-start | bytes 100
  65.4 11.9 %collective-permute-start.16 = (f32[4,48,128]{2,1,0:T(8,128)S(1)}, f32[4,48,128]{2,1,0:T(8,128)S(1)}, u32[]{:S(2)}, u32[]{:S(2)}) collective-permute-start(f32[4,48,128]{2,1,0:T(8,128)S(1)} %get-tuple-element.50), channel_id=1, source_target_pairs={{0,12},{1,13},{2,14},{3,15},{4,8},{5,9},{6,10},{7,11},{8,4},{9,5},... | collective-permute-start | bytes 294920 | tf_op jit(solution)/shard_map/ppermute | solution.py:401
  68.9 10.3 %collective-permute-start.8 = (f32[4,48,128]{2,1,0:T(8,128)S(1)}, f32[4,48,128]{2,1,0:T(8,128)S(1)}, u32[]{:S(2)}, u32[]{:S(2)}) collective-permute-start(f32[4,48,128]{2,1,0:T(8,128)S(1)} %fusion.3), channel_id=1, source_target_pairs={{0,2},{1,3},{2,0},{3,1},{4,6},{5,7},{6,4},{7,5},{8,10},{9,11},{10,... | collective-permute-start | bytes 294920 | tf_op jit(solution)/shard_map/ppermute | solution.py:401
  77.4 6.3 %collective-permute-start.17 = (f32[4,48,128]{2,1,0:T(8,128)S(1)}, f32[4,48,128]{2,1,0:T(8,128)S(1)}, u32[]{:S(2)}, u32[]{:S(2)}) collective-permute-start(f32[4,48,128]{2,1,0:T(8,128)S(1)} %fusion.1), channel_id=1, source_target_pairs={{0,2},{1,3},{2,0},{3,1},{4,6},{5,7},{6,4},{7,5},{8,10},{9,11},{10,... | collective-permute-start | bytes 294920 | tf_op jit(solution)/shard_map/ppermute | solution.py:401
  79.2 7.6 %collective-permute-start.9 = (f32[4,48,128]{2,1,0:T(8,128)S(1)}, f32[4,48,128]{2,1,0:T(8,128)S(1)}, u32[]{:S(2)}, u32[]{:S(2)}) collective-permute-start(f32[4,48,128]{2,1,0:T(8,128)S(1)} %add.82), channel_id=1, source_target_pairs={{0,4},{1,5},{2,6},{3,7},{4,0},{5,1},{6,2},{7,3},{8,12},{9,13},{10,... | collective-permute-start | bytes 294920 | tf_op jit(solution)/shard_map/ppermute | solution.py:401
  81.2 10.8 %collective-permute-start.10 = (f32[4,48,128]{2,1,0:T(8,128)S(1)}, f32[4,48,128]{2,1,0:T(8,128)S(1)}, u32[]{:S(2)}, u32[]{:S(2)}) collective-permute-start(f32[4,48,128]{2,1,0:T(8,128)S(1)} %add.82), channel_id=1, source_target_pairs={{0,8},{1,9},{2,10},{3,11},{4,12},{5,13},{6,14},{7,15},{8,0},{9,1},... | collective-permute-start | bytes 294920 | tf_op jit(solution)/shard_map/ppermute | solution.py:401
  82.3 9.6 %collective-permute-start.11 = (f32[4,48,128]{2,1,0:T(8,128)S(1)}, f32[4,48,128]{2,1,0:T(8,128)S(1)}, u32[]{:S(2)}, u32[]{:S(2)}) collective-permute-start(f32[4,48,128]{2,1,0:T(8,128)S(1)} %add.82), channel_id=1, source_target_pairs={{0,12},{1,13},{2,14},{3,15},{4,8},{5,9},{6,10},{7,11},{8,4},{9,5},... | collective-permute-start | bytes 294920 | tf_op jit(solution)/shard_map/ppermute | solution.py:401
  83.7 8.4 %collective-permute-start.18 = (f32[4,48,128]{2,1,0:T(8,128)S(1)}, f32[4,48,128]{2,1,0:T(8,128)S(1)}, u32[]{:S(2)}, u32[]{:S(2)}) collective-permute-start(f32[4,48,128]{2,1,0:T(8,128)S(1)} %add.87), channel_id=1, source_target_pairs={{0,4},{1,5},{2,6},{3,7},{4,0},{5,1},{6,2},{7,3},{8,12},{9,13},{10,... | collective-permute-start | bytes 294920 | tf_op jit(solution)/shard_map/ppermute | solution.py:401
  84.8 14.6 %collective-permute-start.19 = (f32[4,48,128]{2,1,0:T(8,128)S(1)}, f32[4,48,128]{2,1,0:T(8,128)S(1)}, u32[]{:S(2)}, u32[]{:S(2)}) collective-permute-start(f32[4,48,128]{2,1,0:T(8,128)S(1)} %add.87), channel_id=1, source_target_pairs={{0,8},{1,9},{2,10},{3,11},{4,12},{5,13},{6,14},{7,15},{8,0},{9,1},... | collective-permute-start | bytes 294920 | tf_op jit(solution)/shard_map/ppermute | solution.py:401
  86.8 12.6 %collective-permute-start.20 = (f32[4,48,128]{2,1,0:T(8,128)S(1)}, f32[4,48,128]{2,1,0:T(8,128)S(1)}, u32[]{:S(2)}, u32[]{:S(2)}) collective-permute-start(f32[4,48,128]{2,1,0:T(8,128)S(1)} %add.87), channel_id=1, source_target_pairs={{0,12},{1,13},{2,14},{3,15},{4,8},{5,9},{6,10},{7,11},{8,4},{9,5},... | collective-permute-start | bytes 294920 | tf_op jit(solution)/shard_map/ppermute | solution.py:401
  92.0 7.7 %collective-permute-start.12 = (f32[4,4,48,128]{3,2,1,0:T(8,128)S(1)}, f32[4,4,48,128]{3,2,1,0:T(8,128)S(1)}, u32[]{:S(2)}, u32[]{:S(2)}) collective-permute-start(f32[4,4,48,128]{3,2,1,0:T(8,128)S(1)} %pad_maximum_fusion.refs_0_), channel_id=1, source_target_pairs={{0,1},{1,0},{2,3},{3,2},{4,5},{5,4},{6,7},{7,6},{8,9},{9,8},{10,11... | collective-permute-start | bytes 1179656 | tf_op jit(solution)/shard_map/ppermute | solution.py:458
  99.4 1.8 %collective-permute-start.21 = (f32[4,4,48,128]{3,2,1,0:T(8,128)S(1)}, f32[4,4,48,128]{3,2,1,0:T(8,128)S(1)}, u32[]{:S(2)}, u32[]{:S(2)}) collective-permute-start(f32[4,4,48,128]{3,2,1,0:T(8,128)S(1)} %pad_maximum_fusion.1.refs_2_), channel_id=1, source_target_pairs={{0,1},{1,0},{2,3},{3,2},{4,5},{5,4},{6,7},{7,6},{8,9},{9,8},{10,11... | collective-permute-start | bytes 1179656 | tf_op jit(solution)/shard_map/ppermute | solution.py:458

commit v2 on v1

--- a/solution.py
+++ b/solution.py
@@ -19,11 +19,12 @@
 ANY = pl.BlockSpec(memory_space=pl.ANY)
 HBM = pl.BlockSpec(memory_space=pltpu.HBM)
 LIMIT = 24 * 1024 * 1024
+PACK_LIMIT = 60 * 1024 * 1024
 PAD = 8
 
 
-def params():
-    return pltpu.CompilerParams(vmem_limit_bytes=LIMIT)
+def params(limit=LIMIT):
+    return pltpu.CompilerParams(vmem_limit_bytes=limit)
 
 
 def cost(microseconds):
@@ -80,7 +81,7 @@
     return copies
 
 
-def first_pack_kernel(d, mats, depth, e_ref, h_ref, m_ref, far_ref, near_ref, m_buf, sem):
+def first_pack_kernel(d, mats, depth, e_ref, h_ref, m_ref, far_ref, near_ref, m_in, m_out, sem):
     even = lax.rem(lax.axis_index("slab"), 2) == 0
 
     def pack(down_ref, up_ref):
@@ -88,19 +89,24 @@
             (down_pieces(d, mats), down_ref),
             (up_pieces(d, mats, depth, True), up_ref),
         )
-        moves = []
+        reads, moves, writes = [], [], []
         for k, (pieces, out) in enumerate(sides):
             for name, c, plane, planes, at in spots(pieces):
+                target = out.at[pl.ds(at, planes)]
                 if name == "m":
-                    moves.append((m_ref.at[pl.ds(plane, planes)], m_buf.at[k]))
+                    reads.append((m_ref.at[pl.ds(plane, planes)], m_in.at[k]))
+                    writes.append((m_out.at[k], target))
                 else:
                     source = e_ref if name == "e" else h_ref
-                    moves.append((source.at[c, pl.ds(plane, planes)], out.at[pl.ds(at, planes)]))
-        for copy in start_all(moves, sem):
+                    moves.append((source.at[c, pl.ds(plane, planes)], target))
+        copies = start_all(reads + moves, sem)
+        for copy in copies[: len(reads)]:
             copy.wait()
-        if mats:
-            for k, (pieces, out) in enumerate(sides):
-                out[pl.ds(size_of(pieces) - mats, mats)] = m_buf[k].astype(jnp.float32)
+        for k in range(len(reads)):
+            m_out[k] = m_in[k].astype(jnp.float32)
+        copies = copies[len(reads) :] + start_all(writes, sem)
+        for copy in copies:
+            copy.wait()
 
     @pl.when(even)
     def _():
@@ -178,21 +184,34 @@
     return jnp.where(lax.broadcasted_iota(jnp.int32, (rows, width), 0) < extent, plane, 0.0)
 
 
-def inner_kernel(d, first, depth, monitors, rows, info, *refs):
+def inner_kernel(d, before, depth, monitors, rows, info, *refs):
+    first = not before
     if first:
-        tables, e_in, h_in, m_in, e_out, h_out, coefs_out, mine_out, other_out = refs[:9]
-        e, h, coefs, m_buf, sem = refs[9:]
+        tables, e_in, h_in, m_in, *refs = refs
     else:
-        e_in, h_in, coefs_in, e_out, h_out, mine_out, other_out = refs[:7]
-        e, h, coefs, sem = refs[7:]
+        e_in, h_in, coefs_in, fresh_in, *refs = refs
+    e_out, h_out, mine_out, other_out, edge_out, *refs = refs
+    if first:
+        coefs_out, e, h, coefs, m_buf, sem = refs
+    else:
+        e, h, coefs, sem = refs
     height, width = e_in.shape[2:]
     g = 1
     own, inside = pl.ds(g, depth), pl.ds(PAD, height)
-    moves = [(e_in.at[c], e.at[c, own, inside]) for c in range(3)]
-    moves += [(h_in.at[c], h.at[c, own, inside]) for c in range(3)]
+    fields = ((e_in, e), (h_in, h))
     if first:
+        moves = [(x_in.at[c], x.at[c, own, inside]) for x_in, x in fields for c in range(3)]
         moves.append((m_in, m_buf))
     else:
+        middle = depth - 2 * before
+        moves = []
+        for k, (x_in, x) in enumerate(fields):
+            for source, planes, at in (
+                (x_in.at[:, pl.ds(before, middle)], middle, before),
+                (fresh_in.at[k, :, pl.ds(0, before)], before, 0),
+                (fresh_in.at[k, :, pl.ds(before, before)], before, depth - before),
+            ):
+                moves.append((source, x.at[:, pl.ds(g + at, planes), inside]))
         moves += [(coefs_in.at[k], coefs.at[k, own]) for k in range(2)]
     copies = start_all(moves, sem)
     yee = Yee(e, h, coefs, height, width, g, None)
@@ -239,8 +258,13 @@
             mine_out[m, s - 1] = take_sample(e, mine, spot, start, taken, rows)
             other_out[m, s - 1] = take_sample(e, other, spot, start, taken, rows)
 
-    moves = [(e.at[c, own, inside], e_out.at[c]) for c in range(3)]
-    moves += [(h.at[c, own, inside], h_out.at[c]) for c in range(3)]
+    moves = []
+    for k, (x, x_out) in enumerate(((e, e_out), (h, h_out))):
+        moves.append((x.at[:, pl.ds(g, d), inside], edge_out.at[k, :, pl.ds(0, d)]))
+        moves.append(
+            (x.at[:, pl.ds(g + depth - 1 - d, d + 1), inside], edge_out.at[k, :, pl.ds(d, d + 1)])
+        )
+        moves += [(x.at[c, own, inside], x_out.at[c]) for c in range(3)]
     if first:
         moves += [(coefs.at[k, own], coefs_out.at[k]) for k in range(2)]
     for copy in start_all(moves, sem):
@@ -248,34 +272,34 @@
 
 
 def edge_kernel(d, nxt, first, depth, monitors, rows, info, *refs):
-    e_in, h_in, coefs_in, mine_in, other_in, far_in, near_in = refs[:7]
-    refs = refs[7:]
+    edge_in, coefs_in, mine_in, other_in, far_in, near_in, *refs = refs
     mats = GHOST - 1
     if first:
-        tables, refs = refs[0], refs[1:]
+        tables, *refs = refs
     else:
-        ghosts_in, below_in, refs = refs[0], refs[1], refs[2:]
-    e_out, h_out, mine_out, other_out, refs = *refs[:4], refs[4:]
+        ghosts_in, below_in, _, *refs = refs
+    fresh_out, mine_out, *refs = refs
     if nxt:
-        below_out, far_out, near_out, refs = *refs[:3], refs[3:]
+        below_out, far_out, near_out, *refs = refs
         if first:
-            ghosts_out, refs = refs[0], refs[1:]
+            ghosts_out, *refs = refs
+    else:
+        other_out, *refs = refs
     e, h, coefs, sem = refs
-    height, width = e_in.shape[2:]
+    height, width = edge_in.shape[3:]
     g = GHOST
     inside = pl.ds(PAD, height)
     even = info[0] == 0
     below, above = info[1], info[2]
 
     moves = []
-    for plane, planes in ((0, d), (depth - 1 - d, d + 1)):
-        for c in range(3):
-            part, place = pl.ds(plane, planes), pl.ds(g + plane, planes)
-            moves.append((e_in.at[c, part], e.at[c, place, inside]))
-            moves.append((h_in.at[c, part], h.at[c, place, inside]))
+    for k, x in enumerate((e, h)):
+        for source, planes, at in ((0, d, 0), (d, d + 1, depth - 1 - d)):
+            moves.append(
+                (edge_in.at[k, :, pl.ds(source, planes)], x.at[:, pl.ds(g + at, planes), inside])
+            )
     for plane in (0, depth - d):
-        for k in range(2):
-            moves.append((coefs_in.at[k, pl.ds(plane, d)], coefs.at[k, pl.ds(g + plane, d)]))
+        moves.append((coefs_in.at[:, pl.ds(plane, d)], coefs.at[:, pl.ds(g + plane, d)]))
     copies = start_all(moves, sem)
     yee = Yee(e, h, coefs, height, width, g, below)
 
@@ -288,7 +312,8 @@
         for (shift, pieces), source in zip(sides, (below_ref, above_ref)):
             for name, c, plane, planes, at in spots(pieces):
                 where = pl.ds(g + plane + shift, planes)
-                value = source[pl.ds(at, planes)]
+                value = source[pl.ds(at * height, planes * height)]
+                value = value.reshape(planes, height, width)
                 if name == "e":
                     e[c, where, inside] = value
                 elif name == "h":
@@ -339,16 +364,24 @@
                 jnp.logical_and(offset >= depth - s, offset < depth),
             )
             spot = g + jnp.clip(offset, 0, depth - 1)
-            for out, before, c in ((mine_out, mine_in, mine), (other_out, other_in, other)):
-                fresh = take_sample(e, c, spot, start, extent, rows)
-                out[m, s - 1] = jnp.where(held, fresh, before[m, s - 1])
+            mine_out[m, s - 1] = jnp.where(
+                held, take_sample(e, mine, spot, start, extent, rows), mine_in[m, s - 1]
+            )
+            fresh = jnp.where(
+                held, take_sample(e, other, spot, start, extent, rows), other_in[m, s - 1]
+            )
+            if nxt:
+                at = near_out.shape[0] - (monitors * d - m * d - s + 1) * rows
+                near_out[pl.ds(at, rows)] = fresh
+            else:
+                other_out[m, s - 1] = fresh
 
     moves = []
-    for plane in (0, depth - d):
-        part, place = pl.ds(plane, d), pl.ds(g + plane, d)
-        for c in range(3):
-            moves.append((e.at[c, place, inside], e_out.at[c, part]))
-            moves.append((h.at[c, place, inside], h_out.at[c, part]))
+    for k, x in enumerate((e, h)):
+        for j, plane in enumerate((0, depth - d)):
+            moves.append(
+                (x.at[:, pl.ds(g + plane, d), inside], fresh_out.at[k, :, pl.ds(j * d, d)])
+            )
     copies = start_all(moves, sem)
     if nxt:
         below_out[...] = h[:, g - 1, inside]
@@ -360,7 +393,8 @@
             ):
                 for name, c, plane, planes, at in spots(pieces):
                     source = e if name == "e" else h
-                    out[pl.ds(at, planes)] = source[c, pl.ds(g + plane, planes), inside]
+                    value = source[c, pl.ds(g + plane, planes), inside]
+                    out[pl.ds(at * height, planes * height)] = value.reshape(-1, width)
 
         @pl.when(even)
         def _():
@@ -374,26 +408,57 @@
         copy.wait()
 
 
-def spectrum_kernel(chunks, scattered, monitors, height, info, table, *refs):
-    samples = refs[: 2 * len(chunks)]
-    out = refs[-1]
-    rows, width = samples[0].shape[2:]
+def merge_kernel(d, depth, e_in, h_in, fresh, e_out, h_out, sem):
+    moves = []
+    for k, x_out in enumerate((e_out, h_out)):
+        for j, plane in enumerate((0, depth - d)):
+            moves.append((fresh.at[k, :, pl.ds(j * d, d)], x_out.at[:, pl.ds(plane, d)]))
+    for copy in start_all(moves, sem):
+        copy.wait()
+
+
+def partial_kernel(d, at_step, scattered, monitors, info, table, mine, other, out):
     f = pl.program_id(0)
-    steps = sum(chunks)
+    steps = table.shape[1] // 2
+    for m in range(monitors):
+        at = jnp.bitwise_xor(m, info[3]) if scattered else m
+        for side, samples in enumerate((mine, other)):
+            planes = [samples[at, t] for t in range(d)]
+            for part in range(2):
+                total = planes[0] * table[f, part * steps + at_step]
+                for t in range(1, d):
+                    total = total + planes[t] * table[f, part * steps + at_step + t]
+                out[f, part, m, side] = total
+
+
+def spectrum_kernel(
+    d, at_step, scattered, monitors, freqs, info, table, before, mine, other, out, blocks, sem
+):
+    rows, width = mine.shape[2:]
+    height = blocks.shape[4]
+    steps = table.shape[1] // 2
     pad = jnp.zeros((height - rows, width), jnp.float32)
-    for m in range(monitors):
-        start = monitor_info(info, m, monitors)[1]
-        for side in range(2):
-            c = info[0] if side == 0 else 1 - info[0]
-            planes = []
-            for k, d in enumerate(chunks):
-                at = jnp.bitwise_xor(m, info[3]) if scattered[k] else m
-                planes += [samples[2 * k + side][at, t] for t in range(d)]
-            for part in range(2):
-                total = planes[0] * table[f, part * steps]
-                for t in range(1, steps):
-                    total = total + planes[t] * table[f, part * steps + t]
-                out[0, part, m, c] = pltpu.roll(jnp.concatenate([total, pad], 0), start, 0)
+
+    def body(f, _):
+        for m in range(monitors):
+            start = monitor_info(info, m, monitors)[1]
+            at = jnp.bitwise_xor(m, info[3]) if scattered else m
+            for side, samples in enumerate((mine, other)):
+                c = info[0] if side == 0 else 1 - info[0]
+                planes = [samples[at, t] for t in range(d)]
+                for part in range(2):
+                    total = before[f, part, m, side]
+                    for t in range(d):
+                        total = total + planes[t] * table[f, part * steps + at_step + t]
+                    blocks[f, part, m, c] = pltpu.roll(
+                        jnp.concatenate([total, pad], 0), start, 0
+                    )
+        pltpu.make_async_copy(blocks.at[f], out.at[f], sem.at[f]).start()
+        return 0
+
+    lax.fori_loop(0, freqs, body, 0)
+    for f in range(freqs):
+        pltpu.make_async_copy(blocks.at[f], out.at[f], sem.at[f]).wait()
 
 
 def share(total, slabs, scatter):
@@ -402,9 +467,15 @@
 
     strides = [2**k for k in range(1, slabs.bit_length() - 1)]
     if not scatter:
-        for stride in strides:
-            total = total + swap(total, stride)
-        return total
+        total = total + swap(total, strides[0])
+
+        def rest():
+            result = total
+            for stride in strides[1:]:
+                result = result + swap(result, stride)
+            return result
+
+        return total, rest
     quarter = lax.axis_index("slab") // 4 % 4
     pieces = [
         swap(lax.dynamic_index_in_dim(total, quarter ^ x, 0, keepdims=False), 4 * x)
@@ -413,10 +484,15 @@
     part = lax.dynamic_index_in_dim(total, quarter, 0, keepdims=False)
     for piece in pieces:
         part = part + piece
-    for stride in strides:
-        if stride not in (4, 8):
-            part = part + swap(part, stride)
-    return jnp.stack([part] + [swap(part, 4 * x) for x in (1, 2, 3)])
+
+    def rest():
+        result = part
+        for stride in strides:
+            if stride not in (4, 8):
+                result = result + swap(result, stride)
+        return jnp.stack([result] + [swap(result, 4 * x) for x in (1, 2, 3)])
+
+    return part, rest
 
 
 def per_device(
@@ -477,96 +553,142 @@
             functools.partial(first_pack_kernel, d, mats, depth),
             out_shape=[f32(size, height, width)] * 2,
             in_specs=[HBM] * 3,
-            out_specs=[VMEM] * 2,
+            out_specs=[HBM] * 2,
             scratch_shapes=[
                 pltpu.VMEM((2, mats, height, width), jnp.int32),
+                pltpu.VMEM((2, mats, height, width), jnp.float32),
                 pltpu.SemaphoreType.DMA((copies,)),
             ],
-            compiler_params=params(),
+            compiler_params=params(PACK_LIMIT),
             cost_estimate=cost(2),
         )(e_start, h_start, material)
+    far, near = far.reshape(-1, width), near.reshape(-1, width)
 
     state = [f32(*e_start.shape), f32(*h_start.shape)]
     e, h = e_start, h_start
-    coefs = ghosts = below = None
+    coefs = ghosts = below = fresh = None
     chunks = []
+    mine = None
     for k, d in enumerate(ROUNDS):
         first = k == 0
         nxt = ROUNDS[k + 1] if k + 1 < len(ROUNDS) else 0
+        extra = near.shape[0] - far.shape[0]
         far = lax.ppermute(far, "slab", far_pairs)
         near = near_swap(near)
+        if not first:
+            theirs = near[-extra:].reshape(mine.shape)
+            part, rest = share(mine + theirs, slabs, SCATTER[k - 1])
         samples = [f32(monitors, d, rows, width)] * 2
+        edge = f32(2, 3, 2 * d + 1, height, width)
         with jax.named_scope(f"inner{k}"):
-            kernel = functools.partial(inner_kernel, d, first, depth, monitors, rows)
+            kernel = functools.partial(
+                inner_kernel, d, 0 if first else ROUNDS[k - 1], depth, monitors, rows
+            )
             if first:
-                e, h, coefs, mine, other = pl.pallas_call(
+                e, h, mine, other, edge, coefs = pl.pallas_call(
                     kernel,
-                    out_shape=state + [f32(2, depth, height, width)] + samples,
+                    out_shape=state + samples + [edge, f32(2, depth, height, width)],
                     in_specs=[SMEM, SMEM, HBM, HBM, HBM],
-                    out_specs=[ANY] * 3 + [VMEM] * 2,
+                    out_specs=[ANY] * 2 + [VMEM] * 3 + [ANY],
                     scratch_shapes=scratch(1)
                     + [
                         pltpu.VMEM((depth, height, width), jnp.int32),
-                        pltpu.SemaphoreType.DMA((8,)),
+                        pltpu.SemaphoreType.DMA((12,)),
                     ],
                     compiler_params=params(),
                     cost_estimate=cost(5),
                 )(info, tables, e, h, material)
             else:
-                e, h, mine, other = pl.pallas_call(
+                e, h, mine, other, edge = pl.pallas_call(
                     kernel,
-                    out_shape=state + samples,
-                    in_specs=[SMEM] + [ANY] * 3,
-                    out_specs=[ANY] * 2 + [VMEM] * 2,
-                    input_output_aliases={1: 0, 2: 1},
-                    scratch_shapes=scratch(1) + [pltpu.SemaphoreType.DMA((8,))],
+                    out_shape=state + samples + [edge],
+                    in_specs=[SMEM] + [ANY] * 3 + [VMEM],
+                    out_specs=[ANY] * 2 + [VMEM] * 3,
+                    scratch_shapes=scratch(1) + [pltpu.SemaphoreType.DMA((12,))],
                     compiler_params=params(),
                     cost_estimate=cost(5),
-                )(info, e, h, coefs)
-        operands = [info, e, h, coefs, mine, other, far, near]
-        specs = [SMEM] + [ANY] * 3 + [VMEM] * 4
+                )(info, e, h, coefs, fresh)
+        operands = [info, edge, coefs, mine, other, far, near]
+        specs = [SMEM, VMEM, ANY] + [VMEM] * 4
         if first:
             operands += [tables]
             specs += [SMEM]
         else:
-            operands += [ghosts, below]
-            specs += [VMEM] * 2
-        outs = state + samples
+            operands += [ghosts, below, part]
+            specs += [VMEM] * 2 + [ANY]
+        outs = [f32(2, 3, 2 * d, height, width), samples[0]]
         if nxt:
-            size = message_size(nxt, 0, depth, False)
-            outs = outs + [f32(3, height, width)] + [f32(size, height, width)] * 2
+            size = message_size(nxt, 0, depth, False) * height
+            extra = monitors * d * rows
+            outs += [f32(3, height, width), f32(size, width), f32(size + extra, width)]
             if first:
-                outs = outs + [f32(2, 2 * mats, height, width)]
+                outs += [f32(2, 2 * mats, height, width)]
+        else:
+            outs += [samples[0]]
         with jax.named_scope(f"edge{k}"):
             results = pl.pallas_call(
                 functools.partial(edge_kernel, d, nxt, first, depth, monitors, rows),
                 out_shape=outs,
                 in_specs=specs,
-                out_specs=[ANY] * 2 + [VMEM] * (len(outs) - 2),
-                input_output_aliases={1: 0, 2: 1},
-                scratch_shapes=scratch(GHOST) + [pltpu.SemaphoreType.DMA((16,))],
+                out_specs=[VMEM] * len(outs),
+                scratch_shapes=scratch(GHOST) + [pltpu.SemaphoreType.DMA((8,))],
                 compiler_params=params(),
                 cost_estimate=cost(4),
             )(*operands)
-        e, h, mine, other = results[:4]
+        fresh, mine = results[:2]
         if nxt:
-            below, far, near = results[4:7]
+            below, far, near = results[2:5]
             if first:
-                ghosts = results[7]
-        total = share(mine + near_swap(other), slabs, SCATTER[k])
-        chunks += [total, near_swap(total)]
-
+                ghosts = results[5]
+        else:
+            other = results[2]
+        if not first:
+            total = rest()
+            chunks.append((total, near_swap(total)))
+    with jax.named_scope("merge"):
+        e, h = pl.pallas_call(
+            functools.partial(merge_kernel, d, depth),
+            out_shape=state,
+            in_specs=[ANY, ANY, VMEM],
+            out_specs=[ANY, ANY],
+            input_output_aliases={0: 0, 1: 1},
+            scratch_shapes=[pltpu.SemaphoreType.DMA((4,))],
+            compiler_params=params(),
+            cost_estimate=cost(1),
+        )(e, h, fresh)
+    total = share(mine + near_swap(other), slabs, SCATTER[-1])[1]()
+    chunks.append((total, near_swap(total)))
+
+    done = 0
+    sums = None
+    for k, d in enumerate(ROUNDS[:-1]):
+        with jax.named_scope(f"partial{k}"):
+            sums = pl.pallas_call(
+                functools.partial(partial_kernel, d, done, SCATTER[k], monitors),
+                out_shape=f32(freqs, 2, monitors, 2, rows, width),
+                grid=(freqs,),
+                in_specs=[SMEM, SMEM] + [VMEM] * 2,
+                out_specs=VMEM,
+                compiler_params=params(),
+                cost_estimate=cost(3),
+            )(info, phase_table, *chunks[k])
+        done += d
     with jax.named_scope("spectrum"):
-        block = (1, 2, monitors, 2, height, width)
+        block = (2, monitors, 2, height, width)
         spectrum = pl.pallas_call(
-            functools.partial(spectrum_kernel, ROUNDS, SCATTER, monitors, height),
-            out_shape=f32(freqs, *block[1:]),
-            grid=(freqs,),
-            in_specs=[SMEM, SMEM] + [VMEM] * len(chunks),
-            out_specs=pl.BlockSpec(block, lambda f: (f, 0, 0, 0, 0, 0)),
+            functools.partial(
+                spectrum_kernel, ROUNDS[-1], done, SCATTER[-1], monitors, freqs
+            ),
+            out_shape=f32(freqs, *block),
+            in_specs=[SMEM, SMEM] + [VMEM] * 3,
+            out_specs=HBM,
+            scratch_shapes=[
+                pltpu.VMEM((freqs, *block), jnp.float32),
+                pltpu.SemaphoreType.DMA((freqs,)),
+            ],
             compiler_params=params(),
-            cost_estimate=cost(5),
-        )(info, phase_table, *chunks)
+            cost_estimate=cost(4),
+        )(info, phase_table, sums, *chunks[-1])
     return e, h, spectrum
 
 

time: 107 us -> 145 us (1.36)
  Pallas kernels: 33.5 us -> 69.3 us
  starting transfers between devices: 44.8 us -> 36.7 us
  local copies, waits for them, and re-layouts: 5.06 us -> 11.3 us
  waiting for transfers between devices: 22 us -> 24.6 us
    pallas_call x1, Pallas kernels: 3.44 us -> 43.9 us  [per_device(): pl.pallas_call(functools.partial(first_pack_kernel, d, mats, depth), out_...]
    ppermute x6 -> x5, starting transfers between devices: 20.6 us -> 14.2 us  [near_swap(): return lax.ppermute(block, 'slab', near_pairs)]
    unnamed x22 -> x34, local copies, waits for them, and re-layouts: 4.92 us -> 10.4 us
    pallas_call x2, Pallas kernels: 11.8 us -> 8.99 us  [per_device(): pl.pallas_call(functools.partial(edge_kernel, d, nxt, first, depth, monit...]
    ppermute x6 -> x5, waiting for transfers between devices: 1.5 us -> 3.5 us  [near_swap(): return lax.ppermute(block, 'slab', near_pairs)]
    pallas_call x3 -> x5, Pallas kernels: 18.2 us -> 16.4 us  [the longest x1 5.71 us: per_device(): pl.pallas_call(kernel, out_shape=state + samples + [edge], in_specs=[SMEM...]
    ppermute x14, starting transfers between devices: 22 us -> 20.3 us  [swap(): return lax.ppermute(block, 'slab', [(i, i ^ stride) for i in range(slabs)])]
  transfers between devices with their start and end apart: 22 -> 21, of which waited for: 5 -> 8; matrix products, arithmetic and copies ran while one was open for 1% -> 1% of each run, Pallas kernels for 17% -> 9%
where the time goes in v2:
time: 145 us; the launch traced here: 144 us
  Pallas kernels  69.3 us (48%)
  starting transfers between devices  36.7 us (25%)
  waiting for transfers between devices  24.6 us (17%)
  local copies, waits for them, and re-layouts  11.3 us (8%)
    pallas_call x1, Pallas kernels, per_device(): pl.pallas_call(functools.partial(first_pack_kernel, d, mats, depth), out_...  43.9 us
    ppermute x14, waiting for transfers between devices, swap(): return lax.ppermute(block, 'slab', [(i, i ^ stride) for i in range(slabs)])  21.1 us
    ppermute x14, starting transfers between devices, swap(): return lax.ppermute(block, 'slab', [(i, i ^ stride) for i in range(slabs)])  20.3 us
    ppermute x5, starting transfers between devices, near_swap(): return lax.ppermute(block, 'slab', near_pairs)  14.2 us
    unnamed x34, local copies, waits for them, and re-layouts  10.4 us
    pallas_call x2, Pallas kernels, per_device(): pl.pallas_call(functools.partial(edge_kernel, d, nxt, first, depth, monit...  8.99 us
    pallas_call x1, Pallas kernels, per_device(): pl.pallas_call(kernel, out_shape=state + samples + [edge], in_specs=[SMEM...  5.71 us
    pallas_call x1, Pallas kernels, per_device(): pl.pallas_call(kernel, out_shape=state + samples + [edge, f32(2, depth, h...  4.61 us
  transfers between devices with their start and end apart: 21, of which 8 were waited for; matrix products, arithmetic and copies ran while one was open for 1% of the time, Pallas kernels for 9%

profile of v2, /device:TPU:0, one launch (start us, length us, event | category | flops | bytes accessed | tf_op | source)
XLA Modules:
  0.0 144.4 jit_solution(1732505467284889287)
XLA Ops:
  0.7 43.9 %first_pack.1 = (f32[26,64,128]{2,1,0:T(8,128)}, f32[26,64,128]{2,1,0:T(8,128)}) custom-call(f32[3,16,64,128]{3,2,1,0:T(8,128)} %e_ref.1, f32[3,16,64,128]{3,2,1,0:T(8,128)} %h_ref.1, s32[16,64,128]{2,1,0:T(8,128)} %m_ref.1), custom_call_target="tpu_custom_call" | custom-call | bytes 6000000 | tf_op jit(solution)/shard_map/first_pack/pallas_call | solution.py:552
  44.6 1.6 %collective-permute-start = (f32[1664,128]{1,0:T(8,128)}, f32[1664,128]{1,0:T(8,128)}, u32[]{:S(2)}, u32[]{:S(2)}) collective-permute-start(f32[1664,128]{1,0:T(8,128)} %bitcast.59), channel_id=1, source_target_pairs={{1,2},{2,1},{3,4},{4,3},{5,6},{6,5},{7,8},{8,7},{9,10},{10,9},{11,... | collective-permute-start | bytes 2555912 | tf_op jit(solution)/shard_map/ppermute | solution.py:576
  46.2 3.5 %collective-permute-start.1 = (f32[1664,128]{1,0:T(8,128)}, f32[1664,128]{1,0:T(8,128)}, u32[]{:S(2)}, u32[]{:S(2)}) collective-permute-start(f32[1664,128]{1,0:T(8,128)} %bitcast.58), channel_id=1, source_target_pairs={{0,1},{1,0},{2,3},{3,2},{4,5},{5,4},{6,7},{7,6},{8,9},{9,8},{10,11... | collective-permute-start | bytes 2555912 | tf_op jit(solution)/shard_map/ppermute | solution.py:534
  49.7 0.1 concatenate.6.info
  49.8 0.0 copy-done.15
  49.8 0.0 copy-start.1
  49.8 1.4 copy-done.1
  51.2 4.6 %inner0.1 = (f32[3,16,64,128]{3,2,1,0:T(8,128)S(1)}, f32[3,16,64,128]{3,2,1,0:T(8,128)S(1)}, f32[4,4,48,128]{3,2,1,0:T(8,128)S(1)}, f32[4,4,48,128]{3,2,1,0:T(8,...) custom-call(s32[16]{0:T(128)S(1)} %concatenate.6.info, ...), custom_call_target="tpu_custom_call" | custom-call | bytes 15000000 | tf_op jit(solution)/shard_map/inner0/pallas_call | solution.py:588
  55.9 0.0 copy-start.3
  55.9 1.1 copy-done.3
  57.0 1.1 copy-done.5
  58.2 5.6 %edge0.1 = (f32[2,3,8,64,128]{4,3,2,1,0:T(8,128)S(1)}, f32[4,4,48,128]{3,2,1,0:T(8,128)S(1)}, f32[3,64,128]{2,1,0:T(8,128)S(1)}, f32[1280,128]{1,0:T(8,128)}, f3...) custom-call(s32[16]{0:T(128)S(1)} %concatenate.6.info, f32[2,3,9,64,128]{4,3,2,1,0:T(8,128)S(1)} %get-tuple-element.30.refs_0_, ...), custom_call_target="tpu_custom_call" | custom-call | bytes 12000000 | tf_op jit(solution)/shard_map/edge0/pallas_call | solution.py:629
  63.8 0.0 copy-start.7
  63.8 1.1 copy-done.7
  64.9 0.6 copy-done.9
  65.5 10.5 %collective-permute-start.3 = (f32[2048,128]{1,0:T(8,128)}, f32[2048,128]{1,0:T(8,128)S(1)}, u32[]{:S(2)}, u32[]{:S(2)}) collective-permute-start(f32[2048,128]{1,0:T(8,128)} %get-tuple-element.42), channel_id=1, source_target_pairs={{0,1},{1,0},{2,3},{3,2},{4,5},{5,4},{6,7},{7,6},{8,9},{9,8},{10,11... | collective-permute-start | bytes 3145736 | tf_op jit(solution)/shard_map/ppermute | solution.py:534
  76.0 0.7 collective-permute-start.2
  76.8 1.8 %collective-permute-done.3.refs_5_ = f32[2048,128]{1,0:T(8,128)S(1)} collective-permute-done((f32[2048,128]{1,0:T(8,128)}, f32[2048,128]{1,0:T(8,128)S(1)}, u32[]{:S(2)}, u32[]{:S(2)}) %collective-permute-start.3) | collective-permute-done | bytes 1048608 | tf_op jit(solution)/shard_map/ppermute | solution.py:534
  78.6 0.1 add.72
  78.6 0.7 copy-done.11
  79.4 0.7 dynamic-slice_bitcast_fusion.5
  80.1 3.4 %collective-permute-start.4 = (f32[4,48,128]{2,1,0:T(8,128)}, f32[4,48,128]{2,1,0:T(8,128)S(1)}, u32[]{:S(2)}, u32[]{:S(2)}) collective-permute-start(f32[4,48,128]{2,1,0:T(8,128)} %get-tuple-element.54), channel_id=1, source_target_pairs={{0,4},{1,5},{2,6},{3,7},{4,0},{5,1},{6,2},{7,3},{8,12},{9,13},{10,... | collective-permute-start | bytes 294920 | tf_op jit(solution)/shard_map/ppermute | solution.py:466
  83.5 2.6 %collective-permute-start.5 = (f32[4,48,128]{2,1,0:T(8,128)}, f32[4,48,128]{2,1,0:T(8,128)S(1)}, u32[]{:S(2)}, u32[]{:S(2)}) collective-permute-start(f32[4,48,128]{2,1,0:T(8,128)} %get-tuple-element.56), channel_id=1, source_target_pairs={{0,8},{1,9},{2,10},{3,11},{4,12},{5,13},{6,14},{7,15},{8,0},{9,1},... | collective-permute-start | bytes 294920 | tf_op jit(solution)/shard_map/ppermute | solution.py:466
  86.1 1.4 copy-done.4
  87.5 1.4 copy-done.6
  88.9 1.4 copy-done.8
  90.3 5.7 %inner1.1 = (f32[3,16,64,128]{3,2,1,0:T(8,128)}, f32[3,16,64,128]{3,2,1,0:T(8,128)}, f32[4,4,48,128]{3,2,1,0:T(8,128)S(1)}, f32[4,4,48,128]{3,2,1,0:T(8,128)S(1)}, f32[2,3,9,64,128]{4,3,2,1,0:T(8,128)S(1)}) custom-call(s32[16]{0:T(128)S(1)} %concatenate.6.info, f32[3,16,64,128]{3,2,1,0:T(8,128)S(1)} %copy-done.4, f32[3,16,64,128]{3,2,1,0:T(8,128)S(1)} %copy-done.6, ...), custom_call_target="tpu_custom_call" | custom-call | bytes 15000000 | tf_op jit(solution)/shard_map/inner1/pallas_call | solution.py:602
  96.0 0.0 collective-permute-done.4
  96.0 1.0 collective-permute-done.5
  97.0 2.2 %collective-permute-done.6 = f32[4,48,128]{2,1,0:T(8,128)S(1)} collective-permute-done((f32[4,48,128]{2,1,0:T(8,128)S(1)}, f32[4,48,128]{2,1,0:T(8,128)S(1)}, u32[]{:S(2)}, u32[]{:S(2)}) %collective-permute-start.6) | collective-permute-done | bytes 98336 | tf_op jit(solution)/shard_map/ppermute | solution.py:466
  99.1 0.9 fusion.3.refs_8_
  100.1 0.0 collective-permute-done.2.refs_4_
  100.1 3.4 %edge1.1 = (f32[2,3,8,64,128]{4,3,2,1,0:T(8,128)S(1)}, f32[4,4,48,128]{3,2,1,0:T(8,128)S(1)}, f32[4,4,48,128]{3,2,1,0:T(8,128)S(1)}) custom-call(s32[16]{0:T(128)S(1)} %concatenate.6.info, f32[2,3,9,64,128]{4,3,2,1,0:T(8,128)S(1)} %get-tuple-element.38.refs_0_, f32[2,16,64,128]{3,2,1,0:T(8,128)S(1)} %get-tuple-element.29.refs_1_.refs_2_, ...), custom_call_target="tpu_custom_call" | custom-call | bytes 12000000 | tf_op jit(solution)/shard_map/edge1/pallas_call | solution.py:629
  103.5 0.1 collective-permute-start.12
  103.6 1.7 %collective-permute-done.12 = f32[4,4,48,128]{3,2,1,0:T(8,128)S(1)} collective-permute-done((f32[4,4,48,128]{3,2,1,0:T(8,128)S(1)}, f32[4,4,48,128]{3,2,1,0:T(8,128)S(1)}, u32[]{:S(2)}, u32[]{:S(2)}) %collective-permute-start.12) | collective-permute-done | bytes 393248 | tf_op jit(solution)/shard_map/ppermute | solution.py:534
  105.3 0.0 copy-start.13
  105.4 1.6 %collective-permute-start.13 = (f32[4,48,128]{2,1,0:T(8,128)S(1)}, f32[4,48,128]{2,1,0:T(8,128)S(1)}, u32[]{:S(2)}, u32[]{:S(2)}) collective-permute-start(f32[4,48,128]{2,1,0:T(8,128)S(1)} %get-tuple-element.51), channel_id=1, source_target_pairs={{0,4},{1,5},{2,6},{3,7},{4,0},{5,1},{6,2},{7,3},{8,12},{9,13},{10,... | collective-permute-start | bytes 294920 | tf_op jit(solution)/shard_map/ppermute | solution.py:466
  107.0 0.0 collective-permute-start.14
  107.0 2.8 %collective-permute-start.15 = (f32[4,48,128]{2,1,0:T(8,128)S(1)}, f32[4,48,128]{2,1,0:T(8,128)S(1)}, u32[]{:S(2)}, u32[]{:S(2)}) collective-permute-start(f32[4,48,128]{2,1,0:T(8,128)S(1)} %get-tuple-element.52), channel_id=1, source_target_pairs={{0,12},{1,13},{2,14},{3,15},{4,8},{5,9},{6,10},{7,11},{8,4},{9,5},... | collective-permute-start | bytes 294920 | tf_op jit(solution)/shard_map/ppermute | solution.py:466
  109.8 0.0 collective-permute-start.7
  109.8 0.4 collective-permute-done.13
  110.3 6.4 %collective-permute-done.14 = f32[4,48,128]{2,1,0:T(8,128)S(1)} collective-permute-done((f32[4,48,128]{2,1,0:T(8,128)S(1)}, f32[4,48,128]{2,1,0:T(8,128)S(1)}, u32[]{:S(2)}, u32[]{:S(2)}) %collective-permute-start.14) | collective-permute-done | bytes 98336 | tf_op jit(solution)/shard_map/ppermute | solution.py:466
  116.7 0.0 collective-permute-done.15
  116.7 0.1 collective-permute-start.16
  116.8 2.6 %collective-permute-start.8 = (f32[4,48,128]{2,1,0:T(8,128)S(1)}, f32[4,48,128]{2,1,0:T(8,128)S(1)}, u32[]{:S(2)}, u32[]{:S(2)}) collective-permute-start(f32[4,48,128]{2,1,0:T(8,128)S(1)} %add.82), channel_id=1, source_target_pairs={{0,4},{1,5},{2,6},{3,7},{4,0},{5,1},{6,2},{7,3},{8,12},{9,13},{10,... | collective-permute-start | bytes 294920 | tf_op jit(solution)/shard_map/ppermute | solution.py:466
  119.4 0.5 collective-permute-start.9
  119.9 2.0 %collective-permute-start.10 = (f32[4,48,128]{2,1,0:T(8,128)S(1)}, f32[4,48,128]{2,1,0:T(8,128)S(1)}, u32[]{:S(2)}, u32[]{:S(2)}) collective-permute-start(f32[4,48,128]{2,1,0:T(8,128)S(1)} %add.82), channel_id=1, source_target_pairs={{0,12},{1,13},{2,14},{3,15},{4,8},{5,9},{6,10},{7,11},{8,4},{9,5},... | collective-permute-start | bytes 294920 | tf_op jit(solution)/shard_map/ppermute | solution.py:466
  121.9 0.0 collective-permute-done.16
  121.9 2.2 %collective-permute-start.17 = (f32[4,48,128]{2,1,0:T(8,128)S(1)}, f32[4,48,128]{2,1,0:T(8,128)S(1)}, u32[]{:S(2)}, u32[]{:S(2)}) collective-permute-start(f32[4,48,128]{2,1,0:T(8,128)S(1)} %add.87), channel_id=1, source_target_pairs={{0,4},{1,5},{2,6},{3,7},{4,0},{5,1},{6,2},{7,3},{8,12},{9,13},{10,... | collective-permute-start | bytes 294920 | tf_op jit(solution)/shard_map/ppermute | solution.py:466
  124.1 0.3 collective-permute-start.18
  124.4 0.0 collective-permute-done.8
  124.4 2.2 %collective-permute-start.19 = (f32[4,48,128]{2,1,0:T(8,128)S(1)}, f32[4,48,128]{2,1,0:T(8,128)S(1)}, u32[]{:S(2)}, u32[]{:S(2)}) collective-permute-start(f32[4,48,128]{2,1,0:T(8,128)S(1)} %add.87), channel_id=1, source_target_pairs={{0,12},{1,13},{2,14},{3,15},{4,8},{5,9},{6,10},{7,11},{8,4},{9,5},... | collective-permute-start | bytes 294920 | tf_op jit(solution)/shard_map/ppermute | solution.py:466
  126.6 3.7 %collective-permute-done.9 = f32[4,48,128]{2,1,0:T(8,128)S(1)} collective-permute-done((f32[4,48,128]{2,1,0:T(8,128)S(1)}, f32[4,48,128]{2,1,0:T(8,128)S(1)}, u32[]{:S(2)}, u32[]{:S(2)}) %collective-permute-start.9) | collective-permute-done | bytes 98336 | tf_op jit(solution)/shard_map/ppermute | solution.py:466
  130.3 0.1 collective-permute-start.11
  130.4 0.0 collective-permute-done.17
  130.4 7.4 %collective-permute-done.18 = f32[4,48,128]{2,1,0:T(8,128)S(1)} collective-permute-done((f32[4,48,128]{2,1,0:T(8,128)S(1)}, f32[4,48,128]{2,1,0:T(8,128)S(1)}, u32[]{:S(2)}, u32[]{:S(2)}) %collective-permute-start.18) | collective-permute-done | bytes 98336 | tf_op jit(solution)/shard_map/ppermute | solution.py:466
  137.8 0.0 collective-permute-done.19
  137.8 0.1 collective-permute-start.20
  137.9 0.1 fusion.7
  138.1 0.1 pad_maximum_fusion.2.table
  138.1 1.2 merge.1
  139.3 0.0 collective-permute-done.11.other
  139.3 1.6 %partial0.1.before = f32[8,2,4,2,48,128]{5,4,3,2,1,0:T(8,128)S(1)} custom-call(s32[16]{0:T(128)S(1)} %concatenate.6.info, f32[8,16]{1,0:T(8,128)S(1)} %pad_maximum_fusion.2.table, f32[4,4,48,128]{3,2,1,0:T(8,128)S(1)} %pad_maximum_fusion.mine, f32[4,4,48,128]{3,2,1,0:T(8,128)S(1)} %collective-permute-done.11.other), custom_call_target="tpu_custom_call" | custom-call | bytes 9000000 | tf_op jit(solution)/shard_map/partial0/pallas_call | solution.py:666
  141.0 3.3 %spectrum.1 = f32[8,2,4,2,64,128]{5,4,3,2,1,0:T(8,128)} custom-call(s32[16]{0:T(128)S(1)} %concatenate.6.info, f32[8,16]{1,0:T(8,128)S(1)} %pad_maximum_fusion.2.table, f32[8,2,4,2,48,128]{5,4,3,2,1,0:T(8,128)S(1)} %partial0.1.before, f32[4,4,48,128]{3,2,1,0:T(8,128)S(1)} %pad_maximum_fusion.1.mine, f32[4,4,48,128]{3,2,1,0:T(8,128)S(1)} %collective-permute-done.20.other), custom_call_target="tpu_custom_call" | custom-call | bytes 12000000 | tf_op jit(solution)/shard_map/spectrum/pallas_call | solution.py:678
  (38 shorter events, 0.3 us)
Async XLA Ops:
  0.6 49.2 %copy-start.2 = (s32[16,64,128]{2,1,0:T(8,128)S(1)}, s32[16,64,128]{2,1,0:T(8,128)}, u32[]{:S(2)}) copy-start(s32[16,64,128]{2,1,0:T(8,128)} %m_ref.1) | copy-start | bytes 1572868
  0.6 49.2 %copy-start = (f32[3,16,64,128]{3,2,1,0:T(8,128)S(1)}, f32[3,16,64,128]{3,2,1,0:T(8,128)}, u32[]{:S(2)}) copy-start(f32[3,16,64,128]{3,2,1,0:T(8,128)} %e_ref.1) | copy-start | bytes 4718596
  0.7 49.0 %copy-start.12 = (s32[4,2]{0,1:T(2,128)S(1)}, s32[4,2]{0,1:T(2,128)}, u32[]{:S(2)}) copy-start(s32[4,2]{0,1:T(2,128)} %param.14) | copy-start | bytes 100
  0.7 49.0 %copy-start.14 = (s32[4]{0:T(128)S(1)}, s32[4]{0:T(128)}, u32[]{:S(2)}) copy-start(s32[4]{0:T(128)} %param.13) | copy-start | bytes 52
  0.7 49.1 %copy-start.16 = (f32[4]{0:T(128)S(1)}, f32[4]{0:T(128)}, u32[]{:S(2)}) copy-start(f32[4]{0:T(128)} %param.11) | copy-start | bytes 52
  0.7 49.1 %copy-start.15 = (f32[4]{0:T(128)S(1)}, f32[4]{0:T(128)}, u32[]{:S(2)}) copy-start(f32[4]{0:T(128)} %param.12) | copy-start | bytes 52
  44.6 13.5 %collective-permute-start = (f32[1664,128]{1,0:T(8,128)}, f32[1664,128]{1,0:T(8,128)}, u32[]{:S(2)}, u32[]{:S(2)}) collective-permute-start(f32[1664,128]{1,0:T(8,128)} %bitcast.59), channel_id=1, source_target_pairs={{1,2},{2,1},{3,4},{4,3},{5,6},{6,5},{7,8},{8,7},{9,10},{10,9},{11,... | collective-permute-start | bytes 2555912 | tf_op jit(solution)/shard_map/ppermute | solution.py:576
  46.2 12.0 %collective-permute-start.1 = (f32[1664,128]{1,0:T(8,128)}, f32[1664,128]{1,0:T(8,128)}, u32[]{:S(2)}, u32[]{:S(2)}) collective-permute-start(f32[1664,128]{1,0:T(8,128)} %bitcast.58), channel_id=1, source_target_pairs={{0,1},{1,0},{2,3},{3,2},{4,5},{5,4},{6,7},{7,6},{8,9},{9,8},{10,11... | collective-permute-start | bytes 2555912 | tf_op jit(solution)/shard_map/ppermute | solution.py:534
  49.8 1.4 copy-start.1
  55.9 1.1 copy-start.3
  57.0 1.1 copy-start.5
  63.8 1.1 copy-start.7
  64.9 0.6 copy-start.9
  65.5 13.0 %collective-permute-start.3 = (f32[2048,128]{1,0:T(8,128)}, f32[2048,128]{1,0:T(8,128)S(1)}, u32[]{:S(2)}, u32[]{:S(2)}) collective-permute-start(f32[2048,128]{1,0:T(8,128)} %get-tuple-element.42), channel_id=1, source_target_pairs={{0,1},{1,0},{2,3},{3,2},{4,5},{5,4},{6,7},{7,6},{8,9},{9,8},{10,11... | collective-permute-start | bytes 3145736 | tf_op jit(solution)/shard_map/ppermute | solution.py:534
  76.0 24.0 %collective-permute-start.2 = (f32[1280,128]{1,0:T(8,128)}, f32[1280,128]{1,0:T(8,128)S(1)}, u32[]{:S(2)}, u32[]{:S(2)}) collective-permute-start(f32[1280,128]{1,0:T(8,128)} %get-tuple-element.41), channel_id=1, source_target_pairs={{1,2},{2,1},{3,4},{4,3},{5,6},{6,5},{7,8},{8,7},{9,10},{10,9},{11,... | collective-permute-start | bytes 1966088 | tf_op jit(solution)/shard_map/ppermute | solution.py:576
  78.6 0.7 copy-start.11
  80.1 15.9 %collective-permute-start.4 = (f32[4,48,128]{2,1,0:T(8,128)}, f32[4,48,128]{2,1,0:T(8,128)S(1)}, u32[]{:S(2)}, u32[]{:S(2)}) collective-permute-start(f32[4,48,128]{2,1,0:T(8,128)} %get-tuple-element.54), channel_id=1, source_target_pairs={{0,4},{1,5},{2,6},{3,7},{4,0},{5,1},{6,2},{7,3},{8,12},{9,13},{10,... | collective-permute-start | bytes 294920 | tf_op jit(solution)/shard_map/ppermute | solution.py:466
  83.5 13.5 %collective-permute-start.5 = (f32[4,48,128]{2,1,0:T(8,128)}, f32[4,48,128]{2,1,0:T(8,128)S(1)}, u32[]{:S(2)}, u32[]{:S(2)}) collective-permute-start(f32[4,48,128]{2,1,0:T(8,128)} %get-tuple-element.56), channel_id=1, source_target_pairs={{0,8},{1,9},{2,10},{3,11},{4,12},{5,13},{6,14},{7,15},{8,0},{9,1},... | collective-permute-start | bytes 294920 | tf_op jit(solution)/shard_map/ppermute | solution.py:466
  86.0 13.1 %collective-permute-start.6 = (f32[4,48,128]{2,1,0:T(8,128)S(1)}, f32[4,48,128]{2,1,0:T(8,128)S(1)}, u32[]{:S(2)}, u32[]{:S(2)}) collective-permute-start(f32[4,48,128]{2,1,0:T(8,128)S(1)} %get-tuple-element.55), channel_id=1, source_target_pairs={{0,12},{1,13},{2,14},{3,15},{4,8},{5,9},{6,10},{7,11},{8,4},{9,5},... | collective-permute-start | bytes 294920 | tf_op jit(solution)/shard_map/ppermute | solution.py:466
  86.0 1.4 copy-start.4
  87.5 1.4 copy-start.6
  88.9 1.4 copy-start.8
  90.3 9.8 %copy-start.10 = (f32[3,64,128]{2,1,0:T(8,128)S(1)}, f32[3,64,128]{2,1,0:T(8,128)}, u32[]{:S(2)}) copy-start(f32[3,64,128]{2,1,0:T(8,128)} %copy-done.9) | copy-start | bytes 294916
  103.5 1.8 %collective-permute-start.12 = (f32[4,4,48,128]{3,2,1,0:T(8,128)S(1)}, f32[4,4,48,128]{3,2,1,0:T(8,128)S(1)}, u32[]{:S(2)}, u32[]{:S(2)}) collective-permute-start(f32[4,4,48,128]{3,2,1,0:T(8,128)S(1)} %get-tuple-element.50), channel_id=1, source_target_pairs={{0,1},{1,0},{2,3},{3,2},{4,5},{5,4},{6,7},{7,6},{8,9},{9,8},{10,11... | collective-permute-start | bytes 1179656 | tf_op jit(solution)/shard_map/ppermute | solution.py:534
  105.3 32.6 %copy-start.13 = (s32[8]{0:T(128)S(1)}, s32[8]{0:T(128)}, u32[]{:S(2)}) copy-start(s32[8]{0:T(128)} %param.15) | copy-start | bytes 100
  105.4 4.9 %collective-permute-start.13 = (f32[4,48,128]{2,1,0:T(8,128)S(1)}, f32[4,48,128]{2,1,0:T(8,128)S(1)}, u32[]{:S(2)}, u32[]{:S(2)}) collective-permute-start(f32[4,48,128]{2,1,0:T(8,128)S(1)} %get-tuple-element.51), channel_id=1, source_target_pairs={{0,4},{1,5},{2,6},{3,7},{4,0},{5,1},{6,2},{7,3},{8,12},{9,13},{10,... | collective-permute-start | bytes 294920 | tf_op jit(solution)/shard_map/ppermute | solution.py:466
  107.0 9.7 %collective-permute-start.14 = (f32[4,48,128]{2,1,0:T(8,128)S(1)}, f32[4,48,128]{2,1,0:T(8,128)S(1)}, u32[]{:S(2)}, u32[]{:S(2)}) collective-permute-start(f32[4,48,128]{2,1,0:T(8,128)S(1)} %get-tuple-element.53), channel_id=1, source_target_pairs={{0,8},{1,9},{2,10},{3,11},{4,12},{5,13},{6,14},{7,15},{8,0},{9,1},... | collective-permute-start | bytes 294920 | tf_op jit(solution)/shard_map/ppermute | solution.py:466
  107.0 9.7 %collective-permute-start.15 = (f32[4,48,128]{2,1,0:T(8,128)S(1)}, f32[4,48,128]{2,1,0:T(8,128)S(1)}, u32[]{:S(2)}, u32[]{:S(2)}) collective-permute-start(f32[4,48,128]{2,1,0:T(8,128)S(1)} %get-tuple-element.52), channel_id=1, source_target_pairs={{0,12},{1,13},{2,14},{3,15},{4,8},{5,9},{6,10},{7,11},{8,4},{9,5},... | collective-permute-start | bytes 294920 | tf_op jit(solution)/shard_map/ppermute | solution.py:466
  109.8 6.9 %collective-permute-start.7 = (f32[4,48,128]{2,1,0:T(8,128)S(1)}, f32[4,48,128]{2,1,0:T(8,128)S(1)}, u32[]{:S(2)}, u32[]{:S(2)}) collective-permute-start(f32[4,48,128]{2,1,0:T(8,128)S(1)} %fusion.3.refs_8_), channel_id=1, source_target_pairs={{0,2},{1,3},{2,0},{3,1},{4,6},{5,7},{6,4},{7,5},{8,10},{9,11},{10,... | collective-permute-start | bytes 294920 | tf_op jit(solution)/shard_map/ppermute | solution.py:466
  116.7 5.2 %collective-permute-start.16 = (f32[4,48,128]{2,1,0:T(8,128)S(1)}, f32[4,48,128]{2,1,0:T(8,128)S(1)}, u32[]{:S(2)}, u32[]{:S(2)}) collective-permute-start(f32[4,48,128]{2,1,0:T(8,128)S(1)} %fusion.1), channel_id=1, source_target_pairs={{0,2},{1,3},{2,0},{3,1},{4,6},{5,7},{6,4},{7,5},{8,10},{9,11},{10,... | collective-permute-start | bytes 294920 | tf_op jit(solution)/shard_map/ppermute | solution.py:466
  116.8 7.6 %collective-permute-start.8 = (f32[4,48,128]{2,1,0:T(8,128)S(1)}, f32[4,48,128]{2,1,0:T(8,128)S(1)}, u32[]{:S(2)}, u32[]{:S(2)}) collective-permute-start(f32[4,48,128]{2,1,0:T(8,128)S(1)} %add.82), channel_id=1, source_target_pairs={{0,4},{1,5},{2,6},{3,7},{4,0},{5,1},{6,2},{7,3},{8,12},{9,13},{10,... | collective-permute-start | bytes 294920 | tf_op jit(solution)/shard_map/ppermute | solution.py:466
  119.4 10.8 %collective-permute-start.9 = (f32[4,48,128]{2,1,0:T(8,128)S(1)}, f32[4,48,128]{2,1,0:T(8,128)S(1)}, u32[]{:S(2)}, u32[]{:S(2)}) collective-permute-start(f32[4,48,128]{2,1,0:T(8,128)S(1)} %add.82), channel_id=1, source_target_pairs={{0,8},{1,9},{2,10},{3,11},{4,12},{5,13},{6,14},{7,15},{8,0},{9,1},... | collective-permute-start | bytes 294920 | tf_op jit(solution)/shard_map/ppermute | solution.py:466
  119.9 10.4 %collective-permute-start.10 = (f32[4,48,128]{2,1,0:T(8,128)S(1)}, f32[4,48,128]{2,1,0:T(8,128)S(1)}, u32[]{:S(2)}, u32[]{:S(2)}) collective-permute-start(f32[4,48,128]{2,1,0:T(8,128)S(1)} %add.82), channel_id=1, source_target_pairs={{0,12},{1,13},{2,14},{3,15},{4,8},{5,9},{6,10},{7,11},{8,4},{9,5},... | collective-permute-start | bytes 294920 | tf_op jit(solution)/shard_map/ppermute | solution.py:466
  121.9 8.5 %collective-permute-start.17 = (f32[4,48,128]{2,1,0:T(8,128)S(1)}, f32[4,48,128]{2,1,0:T(8,128)S(1)}, u32[]{:S(2)}, u32[]{:S(2)}) collective-permute-start(f32[4,48,128]{2,1,0:T(8,128)S(1)} %add.87), channel_id=1, source_target_pairs={{0,4},{1,5},{2,6},{3,7},{4,0},{5,1},{6,2},{7,3},{8,12},{9,13},{10,... | collective-permute-start | bytes 294920 | tf_op jit(solution)/shard_map/ppermute | solution.py:466
  124.1 13.7 %collective-permute-start.18 = (f32[4,48,128]{2,1,0:T(8,128)S(1)}, f32[4,48,128]{2,1,0:T(8,128)S(1)}, u32[]{:S(2)}, u32[]{:S(2)}) collective-permute-start(f32[4,48,128]{2,1,0:T(8,128)S(1)} %add.87), channel_id=1, source_target_pairs={{0,8},{1,9},{2,10},{3,11},{4,12},{5,13},{6,14},{7,15},{8,0},{9,1},... | collective-permute-start | bytes 294920 | tf_op jit(solution)/shard_map/ppermute | solution.py:466
  124.4 13.4 %collective-permute-start.19 = (f32[4,48,128]{2,1,0:T(8,128)S(1)}, f32[4,48,128]{2,1,0:T(8,128)S(1)}, u32[]{:S(2)}, u32[]{:S(2)}) collective-permute-start(f32[4,48,128]{2,1,0:T(8,128)S(1)} %add.87), channel_id=1, source_target_pairs={{0,12},{1,13},{2,14},{3,15},{4,8},{5,9},{6,10},{7,11},{8,4},{9,5},... | collective-permute-start | bytes 294920 | tf_op jit(solution)/shard_map/ppermute | solution.py:466
  130.3 9.0 %collective-permute-start.11 = (f32[4,4,48,128]{3,2,1,0:T(8,128)S(1)}, f32[4,4,48,128]{3,2,1,0:T(8,128)S(1)}, u32[]{:S(2)}, u32[]{:S(2)}) collective-permute-start(f32[4,4,48,128]{3,2,1,0:T(8,128)S(1)} %pad_maximum_fusion.mine), channel_id=1, source_target_pairs={{0,1},{1,0},{2,3},{3,2},{4,5},{5,4},{6,7},{7,6},{8,9},{9,8},{10,11... | collective-permute-start | bytes 1179656 | tf_op jit(solution)/shard_map/ppermute | solution.py:534
  137.8 3.1 %collective-permute-start.20 = (f32[4,4,48,128]{3,2,1,0:T(8,128)S(1)}, f32[4,4,48,128]{3,2,1,0:T(8,128)S(1)}, u32[]{:S(2)}, u32[]{:S(2)}) collective-permute-start(f32[4,4,48,128]{3,2,1,0:T(8,128)S(1)} %pad_maximum_fusion.1.mine), channel_id=1, source_target_pairs={{0,1},{1,0},{2,3},{3,2},{4,5},{5,4},{6,7},{7,6},{8,9},{9,8},{10,11... | collective-permute-start | bytes 1179656 | tf_op jit(solution)/shard_map/ppermute | solution.py:534

commit v3 on v2

--- a/solution.py
+++ b/solution.py
@@ -11,15 +11,15 @@
 STEPS = 8
 PERIOD = 512
 ROUNDS = (4, 4)
-SCATTER = (True, True)
+DEEP = (False, False)
 GHOST = max(ROUNDS)
 COURANT = 0.5
 VMEM = pl.BlockSpec(memory_space=pltpu.VMEM)
 SMEM = pl.BlockSpec(memory_space=pltpu.SMEM)
 ANY = pl.BlockSpec(memory_space=pl.ANY)
 HBM = pl.BlockSpec(memory_space=pltpu.HBM)
-LIMIT = 24 * 1024 * 1024
-PACK_LIMIT = 60 * 1024 * 1024
+LIMIT = 12 * 1024 * 1024
+PACK_LIMIT = 58 * 1024 * 1024
 PAD = 8
 
 
@@ -81,7 +81,7 @@
     return copies
 
 
-def first_pack_kernel(d, mats, depth, e_ref, h_ref, m_ref, far_ref, near_ref, m_in, m_out, sem):
+def first_pack_kernel(d, mats, depth, e_ref, h_ref, m_ref, far_ref, near_ref, m_in, sem):
     even = lax.rem(lax.axis_index("slab"), 2) == 0
 
     def pack(down_ref, up_ref):
@@ -89,24 +89,19 @@
             (down_pieces(d, mats), down_ref),
             (up_pieces(d, mats, depth, True), up_ref),
         )
-        reads, moves, writes = [], [], []
+        moves, mats_at = [], []
         for k, (pieces, out) in enumerate(sides):
             for name, c, plane, planes, at in spots(pieces):
-                target = out.at[pl.ds(at, planes)]
                 if name == "m":
-                    reads.append((m_ref.at[pl.ds(plane, planes)], m_in.at[k]))
-                    writes.append((m_out.at[k], target))
+                    moves.append((m_ref.at[pl.ds(plane, planes)], m_in.at[k]))
+                    mats_at.append((k, out, at))
                 else:
                     source = e_ref if name == "e" else h_ref
-                    moves.append((source.at[c, pl.ds(plane, planes)], target))
-        copies = start_all(reads + moves, sem)
-        for copy in copies[: len(reads)]:
+                    moves.append((source.at[c, pl.ds(plane, planes)], out.at[pl.ds(at, planes)]))
+        for copy in start_all(moves, sem):
             copy.wait()
-        for k in range(len(reads)):
-            m_out[k] = m_in[k].astype(jnp.float32)
-        copies = copies[len(reads) :] + start_all(writes, sem)
-        for copy in copies:
-            copy.wait()
+        for k, out, at in mats_at:
+            out[pl.ds(at, mats)] = m_in[k].astype(jnp.float32)
 
     @pl.when(even)
     def _():
@@ -184,12 +179,11 @@
     return jnp.where(lax.broadcasted_iota(jnp.int32, (rows, width), 0) < extent, plane, 0.0)
 
 
-def inner_kernel(d, before, depth, monitors, rows, info, *refs):
-    first = not before
+def inner_kernel(d, first, depth, monitors, rows, info, *refs):
     if first:
         tables, e_in, h_in, m_in, *refs = refs
     else:
-        e_in, h_in, coefs_in, fresh_in, *refs = refs
+        e_in, h_in, coefs_in, *refs = refs
     e_out, h_out, mine_out, other_out, edge_out, *refs = refs
     if first:
         coefs_out, e, h, coefs, m_buf, sem = refs
@@ -199,19 +193,10 @@
     g = 1
     own, inside = pl.ds(g, depth), pl.ds(PAD, height)
     fields = ((e_in, e), (h_in, h))
+    moves = [(x_in.at[c], x.at[c, own, inside]) for x_in, x in fields for c in range(3)]
     if first:
-        moves = [(x_in.at[c], x.at[c, own, inside]) for x_in, x in fields for c in range(3)]
         moves.append((m_in, m_buf))
     else:
-        middle = depth - 2 * before
-        moves = []
-        for k, (x_in, x) in enumerate(fields):
-            for source, planes, at in (
-                (x_in.at[:, pl.ds(before, middle)], middle, before),
-                (fresh_in.at[k, :, pl.ds(0, before)], before, 0),
-                (fresh_in.at[k, :, pl.ds(before, before)], before, depth - before),
-            ):
-                moves.append((source, x.at[:, pl.ds(g + at, planes), inside]))
         moves += [(coefs_in.at[k], coefs.at[k, own]) for k in range(2)]
     copies = start_all(moves, sem)
     yee = Yee(e, h, coefs, height, width, g, None)
@@ -277,14 +262,13 @@
     if first:
         tables, *refs = refs
     else:
-        ghosts_in, below_in, _, *refs = refs
-    fresh_out, mine_out, *refs = refs
+        ghosts_in, below_in, *refs = refs
     if nxt:
-        below_out, far_out, near_out, *refs = refs
+        _, _, e_out, h_out, mine_out, other_out, below_out, far_out, near_out, *refs = refs
         if first:
             ghosts_out, *refs = refs
     else:
-        other_out, *refs = refs
+        fresh_out, mine_out, other_out, *refs = refs
     e, h, coefs, sem = refs
     height, width = edge_in.shape[3:]
     g = GHOST
@@ -300,6 +284,8 @@
             )
     for plane in (0, depth - d):
         moves.append((coefs_in.at[:, pl.ds(plane, d)], coefs.at[:, pl.ds(g + plane, d)]))
+    if not first:
+        moves.append((below_in, h.at[:, g - 1, inside]))
     copies = start_all(moves, sem)
     yee = Yee(e, h, coefs, height, width, g, below)
 
@@ -343,7 +329,6 @@
     else:
         for k, at in enumerate(ghost_planes):
             coefs[:, at] = ghosts_in[:, k]
-        h[:, g - 1, inside] = below_in[...]
     for copy in copies:
         copy.wait()
 
@@ -370,21 +355,20 @@
             fresh = jnp.where(
                 held, take_sample(e, other, spot, start, extent, rows), other_in[m, s - 1]
             )
-            if nxt:
-                at = near_out.shape[0] - (monitors * d - m * d - s + 1) * rows
-                near_out[pl.ds(at, rows)] = fresh
-            else:
-                other_out[m, s - 1] = fresh
+            other_out[m, s - 1] = fresh
 
     moves = []
     for k, x in enumerate((e, h)):
         for j, plane in enumerate((0, depth - d)):
-            moves.append(
-                (x.at[:, pl.ds(g + plane, d), inside], fresh_out.at[k, :, pl.ds(j * d, d)])
-            )
+            source = x.at[:, pl.ds(g + plane, d), inside]
+            if nxt:
+                moves.append((source, (e_out, h_out)[k].at[:, pl.ds(plane, d)]))
+            else:
+                moves.append((source, fresh_out.at[k, :, pl.ds(j * d, d)]))
+    if nxt:
+        moves.append((h.at[:, g - 1, inside], below_out))
     copies = start_all(moves, sem)
     if nxt:
-        below_out[...] = h[:, g - 1, inside]
 
         def pack(down_ref, up_ref):
             for pieces, out in (
@@ -417,11 +401,11 @@
         copy.wait()
 
 
-def partial_kernel(d, at_step, scattered, monitors, info, table, mine, other, out):
+def partial_kernel(d, at_step, monitors, info, table, mine, other, out):
     f = pl.program_id(0)
     steps = table.shape[1] // 2
     for m in range(monitors):
-        at = jnp.bitwise_xor(m, info[3]) if scattered else m
+        at = jnp.bitwise_xor(m, info[3])
         for side, samples in enumerate((mine, other)):
             planes = [samples[at, t] for t in range(d)]
             for part in range(2):
@@ -432,7 +416,7 @@
 
 
 def spectrum_kernel(
-    d, at_step, scattered, monitors, freqs, info, table, before, mine, other, out, blocks, sem
+    d, at_step, monitors, freqs, info, table, before, mine, other, out, blocks, sem
 ):
     rows, width = mine.shape[2:]
     height = blocks.shape[4]
@@ -442,7 +426,7 @@
     def body(f, _):
         for m in range(monitors):
             start = monitor_info(info, m, monitors)[1]
-            at = jnp.bitwise_xor(m, info[3]) if scattered else m
+            at = jnp.bitwise_xor(m, info[3])
             for side, samples in enumerate((mine, other)):
                 c = info[0] if side == 0 else 1 - info[0]
                 planes = [samples[at, t] for t in range(d)]
@@ -461,38 +445,68 @@
         pltpu.make_async_copy(blocks.at[f], out.at[f], sem.at[f]).wait()
 
 
-def share(total, slabs, scatter):
-    def swap(block, stride):
-        return lax.ppermute(block, "slab", [(i, i ^ stride) for i in range(slabs)])
-
-    strides = [2**k for k in range(1, slabs.bit_length() - 1)]
-    if not scatter:
-        total = total + swap(total, strides[0])
-
-        def rest():
-            result = total
-            for stride in strides[1:]:
-                result = result + swap(result, stride)
-            return result
-
-        return total, rest
-    quarter = lax.axis_index("slab") // 4 % 4
-    pieces = [
-        swap(lax.dynamic_index_in_dim(total, quarter ^ x, 0, keepdims=False), 4 * x)
-        for x in (1, 2, 3)
-    ]
-    part = lax.dynamic_index_in_dim(total, quarter, 0, keepdims=False)
-    for piece in pieces:
-        part = part + piece
-
-    def rest():
-        result = part
-        for stride in strides:
-            if stride not in (4, 8):
-                result = result + swap(result, stride)
-        return jnp.stack([result] + [swap(result, 4 * x) for x in (1, 2, 3)])
-
-    return part, rest
+class Sharing:
+    def __init__(self, slabs, deep):
+        self.slabs, self.deep = slabs, deep
+        me = lax.axis_index("slab")
+        self.low, self.high = me // 4 % 2, me // 8 % 2
+        self.others = [
+            2**k for k in range(1, slabs.bit_length() - 1) if 2**k not in (4, 8)
+        ]
+
+    def swap(self, block, stride):
+        return lax.ppermute(block, "slab", [(i, i ^ stride) for i in range(self.slabs)])
+
+    def scatter(self, total, hold):
+        if self.deep:
+            total = total.reshape(2, 2, *total.shape[1:])
+            sent = lax.dynamic_index_in_dim(total, 1 - self.low, 0, keepdims=False)
+            total = lax.dynamic_index_in_dim(total, self.low, 0, keepdims=False)
+            total = total + self.swap(sent, 4)
+            sent = lax.dynamic_index_in_dim(total, 1 - self.high, 0, keepdims=False)
+            total = lax.dynamic_index_in_dim(total, self.high, 0, keepdims=False)
+            return add(total, self.swap(sent, 8), hold=hold)
+        quarter = 2 * self.low + self.high
+        pieces = [
+            lax.dynamic_index_in_dim(total, quarter ^ x, 0, keepdims=False) for x in range(4)
+        ]
+        pieces = pieces[:1] + [self.swap(pieces[x], s) for x, s in ((1, 8), (2, 4), (3, 12))]
+        return add(*pieces, hold=hold)
+
+    def spread(self, part, hold):
+        for stride in self.others:
+            part = add(part, self.swap(part, stride), hold=hold)
+        return part
+
+    def gather_near(self, part):
+        return jnp.stack([part, self.swap(part, 8)]) if self.deep else part
+
+    def gather_far(self, part):
+        if self.deep:
+            return jnp.concatenate([part, self.swap(part, 4)])
+        return jnp.stack([part] + [self.swap(part, stride) for stride in (8, 4, 12)])
+
+
+def add_kernel(*refs):
+    *ins, _, out = refs
+    total = ins[0][...]
+    for more in ins[1:]:
+        total = total + more[...]
+    out[...] = total
+
+
+def add(*blocks, hold):
+    if hold is None:
+        return sum(blocks[1:], blocks[0])
+    with jax.named_scope("add"):
+        return pl.pallas_call(
+            add_kernel,
+            out_shape=jax.ShapeDtypeStruct(blocks[0].shape, jnp.float32),
+            in_specs=[VMEM] * len(blocks) + [ANY],
+            out_specs=VMEM,
+            compiler_params=params(),
+            cost_estimate=cost(0.3),
+        )(*blocks, hold)
 
 
 def per_device(
@@ -511,7 +525,7 @@
                     me % 2,
                     (me > 0).astype(jnp.int32),
                     (me < slabs - 1).astype(jnp.int32),
-                    me // 4 % 4,
+                    2 * (me // 4 % 2) + me // 8 % 2,
                 ]
             ),
             monitor_z - me * depth,
@@ -553,10 +567,9 @@
             functools.partial(first_pack_kernel, d, mats, depth),
             out_shape=[f32(size, height, width)] * 2,
             in_specs=[HBM] * 3,
-            out_specs=[HBM] * 2,
+            out_specs=[VMEM] * 2,
             scratch_shapes=[
                 pltpu.VMEM((2, mats, height, width), jnp.int32),
-                pltpu.VMEM((2, mats, height, width), jnp.float32),
                 pltpu.SemaphoreType.DMA((copies,)),
             ],
             compiler_params=params(PACK_LIMIT),
@@ -567,29 +580,25 @@
     state = [f32(*e_start.shape), f32(*h_start.shape)]
     e, h = e_start, h_start
     coefs = ghosts = below = fresh = None
-    chunks = []
     mine = None
     for k, d in enumerate(ROUNDS):
         first = k == 0
         nxt = ROUNDS[k + 1] if k + 1 < len(ROUNDS) else 0
-        extra = near.shape[0] - far.shape[0]
         far = lax.ppermute(far, "slab", far_pairs)
         near = near_swap(near)
         if not first:
-            theirs = near[-extra:].reshape(mine.shape)
-            part, rest = share(mine + theirs, slabs, SCATTER[k - 1])
+            early = Sharing(slabs, DEEP[k - 1])
+            part = early.scatter(mine + near_swap(other), None)
         samples = [f32(monitors, d, rows, width)] * 2
         edge = f32(2, 3, 2 * d + 1, height, width)
         with jax.named_scope(f"inner{k}"):
-            kernel = functools.partial(
-                inner_kernel, d, 0 if first else ROUNDS[k - 1], depth, monitors, rows
-            )
+            kernel = functools.partial(inner_kernel, d, first, depth, monitors, rows)
             if first:
                 e, h, mine, other, edge, coefs = pl.pallas_call(
                     kernel,
                     out_shape=state + samples + [edge, f32(2, depth, height, width)],
                     in_specs=[SMEM, SMEM, HBM, HBM, HBM],
-                    out_specs=[ANY] * 2 + [VMEM] * 3 + [ANY],
+                    out_specs=[HBM] * 2 + [VMEM] * 3 + [ANY],
                     scratch_shapes=scratch(1)
                     + [
                         pltpu.VMEM((depth, height, width), jnp.int32),
@@ -602,49 +611,52 @@
                 e, h, mine, other, edge = pl.pallas_call(
                     kernel,
                     out_shape=state + samples + [edge],
-                    in_specs=[SMEM] + [ANY] * 3 + [VMEM],
-                    out_specs=[ANY] * 2 + [VMEM] * 3,
+                    in_specs=[SMEM, HBM, HBM, ANY],
+                    out_specs=[HBM] * 2 + [VMEM] * 3,
+                    input_output_aliases={1: 0, 2: 1},
                     scratch_shapes=scratch(1) + [pltpu.SemaphoreType.DMA((12,))],
                     compiler_params=params(),
                     cost_estimate=cost(5),
-                )(info, e, h, coefs, fresh)
+                )(info, e, h, coefs)
         operands = [info, edge, coefs, mine, other, far, near]
         specs = [SMEM, VMEM, ANY] + [VMEM] * 4
         if first:
             operands += [tables]
             specs += [SMEM]
         else:
-            operands += [ghosts, below, part]
-            specs += [VMEM] * 2 + [ANY]
-        outs = [f32(2, 3, 2 * d, height, width), samples[0]]
+            operands += [ghosts, below]
+            specs += [VMEM, HBM]
+        outs = [f32(2, 3, 2 * d, height, width)] + samples
+        kinds = [VMEM] * 3
+        aliases = {}
         if nxt:
+            outs = state + samples
+            kinds = [HBM] * 2 + [VMEM] * 2
+            aliases = {len(operands): 0, len(operands) + 1: 1}
+            operands += [e, h]
+            specs += [HBM] * 2
             size = message_size(nxt, 0, depth, False) * height
-            extra = monitors * d * rows
-            outs += [f32(3, height, width), f32(size, width), f32(size + extra, width)]
+            outs += [f32(3, height, width), f32(size, width), f32(size, width)]
+            kinds += [HBM]
             if first:
                 outs += [f32(2, 2 * mats, height, width)]
-        else:
-            outs += [samples[0]]
         with jax.named_scope(f"edge{k}"):
             results = pl.pallas_call(
                 functools.partial(edge_kernel, d, nxt, first, depth, monitors, rows),
                 out_shape=outs,
                 in_specs=specs,
-                out_specs=[VMEM] * len(outs),
+                out_specs=kinds + [VMEM] * (len(outs) - len(kinds)),
+                input_output_aliases=aliases,
                 scratch_shapes=scratch(GHOST) + [pltpu.SemaphoreType.DMA((8,))],
                 compiler_params=params(),
                 cost_estimate=cost(4),
             )(*operands)
-        fresh, mine = results[:2]
         if nxt:
-            below, far, near = results[2:5]
+            e, h, mine, other, below, far, near = results[:7]
             if first:
-                ghosts = results[5]
+                ghosts = results[7]
         else:
-            other = results[2]
-        if not first:
-            total = rest()
-            chunks.append((total, near_swap(total)))
+            fresh, mine, other = results
     with jax.named_scope("merge"):
         e, h = pl.pallas_call(
             functools.partial(merge_kernel, d, depth),
@@ -656,7 +668,11 @@
             compiler_params=params(),
             cost_estimate=cost(1),
         )(e, h, fresh)
-    total = share(mine + near_swap(other), slabs, SCATTER[-1])[1]()
+    late = Sharing(slabs, DEEP[-1])
+    part = early.gather_far(early.gather_near(early.spread(part, None)))
+    chunks = [(part, near_swap(part))]
+    total = late.spread(late.scatter(mine + near_swap(other), None), None)
+    total = late.gather_far(late.gather_near(total))
     chunks.append((total, near_swap(total)))
 
     done = 0
@@ -664,7 +680,7 @@
     for k, d in enumerate(ROUNDS[:-1]):
         with jax.named_scope(f"partial{k}"):
             sums = pl.pallas_call(
-                functools.partial(partial_kernel, d, done, SCATTER[k], monitors),
+                functools.partial(partial_kernel, d, done, monitors),
                 out_shape=f32(freqs, 2, monitors, 2, rows, width),
                 grid=(freqs,),
                 in_specs=[SMEM, SMEM] + [VMEM] * 2,
@@ -676,9 +692,7 @@
     with jax.named_scope("spectrum"):
         block = (2, monitors, 2, height, width)
         spectrum = pl.pallas_call(
-            functools.partial(
-                spectrum_kernel, ROUNDS[-1], done, SCATTER[-1], monitors, freqs
-            ),
+            functools.partial(spectrum_kernel, ROUNDS[-1], done, monitors, freqs),
             out_shape=f32(freqs, *block),
             in_specs=[SMEM, SMEM] + [VMEM] * 3,
             out_specs=HBM,

time: 145 us -> 96.2 us (0.66)
  Pallas kernels: 69.3 us -> 30.9 us
  local copies, waits for them, and re-layouts: 11.3 us -> 1.21 us
  waiting for transfers between devices: 24.6 us -> 16.5 us
  starting transfers between devices: 36.7 us -> 44.8 us
    pallas_call x1, Pallas kernels: 43.9 us -> 2.94 us  [per_device(): pl.pallas_call(functools.partial(first_pack_kernel, d, mats, depth), out_...]
    unnamed x34 -> x16, local copies, waits for them, and re-layouts: 10.4 us -> 1.07 us
    ppermute x5 -> x6, starting transfers between devices: 14.2 us -> 20.3 us  [near_swap(): return lax.ppermute(block, 'slab', near_pairs)]
    ppermute x14, waiting for transfers between devices: 21.1 us -> 16.5 us  [swap(): lax.ppermute(block, 'slab', [(i, i ^ stride) for i in range(self.slabs)])]
    ppermute x5 -> x6, waiting for transfers between devices: 3.5 us -> 0.02 us  [near_swap(): return lax.ppermute(block, 'slab', near_pairs)]
    ppermute x14, starting transfers between devices: 20.3 us -> 22.2 us  [swap(): lax.ppermute(block, 'slab', [(i, i ^ stride) for i in range(self.slabs)])]
    pallas_call x1, Pallas kernels: 5.71 us -> 7.19 us  [per_device(): pl.pallas_call(kernel, out_shape=state + samples + [edge], in_specs=[SMEM...]
  transfers between devices with their start and end apart: 21 -> 22, of which waited for: 8 -> 4; matrix products, arithmetic and copies ran while one was open for 1% -> 2% of each run, Pallas kernels for 9% -> 20%
where the time goes in v3:
time: 96.2 us; the launch traced here: 95.9 us
  starting transfers between devices  44.8 us (47%)
  Pallas kernels  30.9 us (32%)
  waiting for transfers between devices  16.5 us (17%)
  other arithmetic  1.44 us (1%)
  local copies, waits for them, and re-layouts  1.21 us (1%)
  between operations  1.09 us (1%)
    ppermute x14, starting transfers between devices, swap(): lax.ppermute(block, 'slab', [(i, i ^ stride) for i in range(self.slabs)])  22.2 us
    ppermute x6, starting transfers between devices, near_swap(): return lax.ppermute(block, 'slab', near_pairs)  20.3 us
    ppermute x14, waiting for transfers between devices, swap(): lax.ppermute(block, 'slab', [(i, i ^ stride) for i in range(self.slabs)])  16.5 us
    pallas_call x2, Pallas kernels, per_device(): pl.pallas_call(functools.partial(edge_kernel, d, nxt, first, depth, monit...  8.73 us
    pallas_call x1, Pallas kernels, per_device(): pl.pallas_call(kernel, out_shape=state + samples + [edge], in_specs=[SMEM...  7.19 us
    pallas_call x1, Pallas kernels, per_device(): pl.pallas_call(kernel, out_shape=state + samples + [edge, f32(2, depth, h...  5.91 us
    pallas_call x1, Pallas kernels, per_device(): pl.pallas_call(functools.partial(spectrum_kernel, ROUNDS[-1], done, monit...  3.3 us
    pallas_call x1, Pallas kernels, per_device(): pl.pallas_call(functools.partial(first_pack_kernel, d, mats, depth), out_...  2.94 us
  transfers between devices with their start and end apart: 22, of which 4 were waited for; matrix products, arithmetic and copies ran while one was open for 2% of the time, Pallas kernels for 20%

profile of v3, /device:TPU:0, one launch (start us, length us, event | category | flops | bytes accessed | tf_op | source)
XLA Modules:
  0.0 95.9 jit_solution(5986581220699255908)
XLA Ops:
  0.6 0.0 copy-start
  0.6 0.0 copy-start.1
  0.7 2.9 %first_pack.1 = (f32[26,64,128]{2,1,0:T(8,128)}, f32[26,64,128]{2,1,0:T(8,128)}) custom-call(f32[3,16,64,128]{3,2,1,0:T(8,128)} %e_ref.1, f32[3,16,64,128]{3,2,1,0:T(8,128)} %h_ref.1, s32[16,64,128]{2,1,0:T(8,128)} %m_ref.1), custom_call_target="tpu_custom_call" | custom-call | bytes 6000000 | tf_op jit(solution)/shard_map/first_pack/pallas_call | solution.py:566
  3.6 1.6 %collective-permute-start = (f32[1664,128]{1,0:T(8,128)}, f32[1664,128]{1,0:T(8,128)}, u32[]{:S(2)}, u32[]{:S(2)}) collective-permute-start(f32[1664,128]{1,0:T(8,128)} %bitcast.57), channel_id=1, source_target_pairs={{1,2},{2,1},{3,4},{4,3},{5,6},{6,5},{7,8},{8,7},{9,10},{10,9},{11,... | collective-permute-start | bytes 2555912 | tf_op jit(solution)/shard_map/ppermute | solution.py:587
  5.2 3.5 %collective-permute-start.1 = (f32[1664,128]{1,0:T(8,128)}, f32[1664,128]{1,0:T(8,128)}, u32[]{:S(2)}, u32[]{:S(2)}) collective-permute-start(f32[1664,128]{1,0:T(8,128)} %bitcast.56), channel_id=1, source_target_pairs={{0,1},{1,0},{2,3},{3,2},{4,5},{5,4},{6,7},{7,6},{8,9},{9,8},{10,11... | collective-permute-start | bytes 2555912 | tf_op jit(solution)/shard_map/ppermute | solution.py:548
  8.7 0.1 concatenate.6.info
  8.8 0.0 copy-done.6
  8.8 0.0 copy-done
  8.8 0.0 copy-done.1
  8.9 0.0 copy-start.2
  8.9 1.0 %copy-done.2 = s32[16,64,128]{2,1,0:T(8,128)S(1)} copy-done((s32[16,64,128]{2,1,0:T(8,128)S(1)}, s32[16,64,128]{2,1,0:T(8,128)}, u32[]{:S(2)}) %copy-start.2) | copy-done | bytes 524312
  9.9 5.9 %inner0.1 = (f32[3,16,64,128]{3,2,1,0:T(8,128)}, f32[3,16,64,128]{3,2,1,0:T(8,128)}, f32[4,4,48,128]{3,2,1,0:T(8,128)S(1)}, f32[4,4,48,128]{3,2,1,0:T(8,128)S(1)...) custom-call(s32[16]{0:T(128)S(1)} %concatenate.6.info, ...), custom_call_target="tpu_custom_call" | custom-call | bytes 15000000 | tf_op jit(solution)/shard_map/inner0/pallas_call | solution.py:597
  15.8 0.0 collective-permute-done.refs_4_
  15.8 0.0 collective-permute-done.1.refs_5_
  15.8 5.3 %edge0.1 = (f32[3,16,64,128]{3,2,1,0:T(8,128)}, f32[3,16,64,128]{3,2,1,0:T(8,128)}, f32[4,4,48,128]{3,2,1,0:T(8,128)S(1)}, f32[4,4,48,128]{3,2,1,0:T(8,128)S(1)}...) custom-call(s32[16]{0:T(128)S(1)} %concatenate.6.info, ...), custom_call_target="tpu_custom_call", output_to_operand_aliasing={{0}: (8, {}), {1}: (9, {})} | custom-call | bytes 12000000 | tf_op jit(solution)/shard_map/edge0/pallas_call | solution.py:644
  21.1 0.7 collective-permute-start.2
  21.8 15.6 %collective-permute-start.3 = (f32[1280,128]{1,0:T(8,128)S(1)}, f32[1280,128]{1,0:T(8,128)S(1)}, u32[]{:S(2)}, u32[]{:S(2)}) collective-permute-start(f32[1280,128]{1,0:T(8,128)S(1)} %get-tuple-element.45), channel_id=1, source_target_pairs={{0,1},{1,0},{2,3},{3,2},{4,5},{5,4},{6,7},{7,6},{8,9},{9,8},{10,11... | collective-permute-start | bytes 1966088 | tf_op jit(solution)/shard_map/ppermute | solution.py:548
  37.5 0.1 collective-permute-start.4
  37.5 7.2 %inner1.1 = (f32[3,16,64,128]{3,2,1,0:T(8,128)}, f32[3,16,64,128]{3,2,1,0:T(8,128)}, f32[4,4,48,128]{3,2,1,0:T(8,128)S(1)}, f32[4,4,48,128]{3,2,1,0:T(8,128)S(1)}, f32[2,3,9,64,128]{4,3,2,1,0:T(8,128)S(1)}) custom-call(s32[16]{0:T(128)S(1)} %concatenate.6.info, ...), custom_call_target="tpu_custom_call", output_to_operand_aliasing={{0}: (1, {}), {1}: (2, {})} | custom-call | bytes 15000000 | tf_op jit(solution)/shard_map/inner1/pallas_call | solution.py:611
  44.7 0.0 collective-permute-done.2.refs_4_
  44.7 0.0 collective-permute-done.3.refs_5_
  44.7 3.4 %edge1.1 = (f32[2,3,8,64,128]{4,3,2,1,0:T(8,128)S(1)}, f32[4,4,48,128]{3,2,1,0:T(8,128)S(1)}, f32[4,4,48,128]{3,2,1,0:T(8,128)S(1)}) custom-call(s32[16]{0:T(128)S(1)} %concatenate.6.info, f32[2,3,9,64,128]{4,3,2,1,0:T(8,128)S(1)} %get-tuple-element.41.refs_0_, f32[2,16,64,128]{3,2,1,0:T(8,128)S(1)} %get-tuple-element.30.refs_1_.refs_2_, ...), custom_call_target="tpu_custom_call" | custom-call | bytes 12000000 | tf_op jit(solution)/shard_map/edge1/pallas_call | solution.py:644
  48.2 1.0 collective-permute-start.13
  49.2 0.0 collective-permute-done.4
  49.2 0.1 add.87
  49.3 2.7 %collective-permute-start.5 = (f32[4,48,128]{2,1,0:T(8,128)S(1)}, f32[4,48,128]{2,1,0:T(8,128)S(1)}, u32[]{:S(2)}, u32[]{:S(2)}) collective-permute-start(f32[4,48,128]{2,1,0:T(8,128)S(1)} %get-tuple-element.58), channel_id=1, source_target_pairs={{0,8},{1,9},{2,10},{3,11},{4,12},{5,13},{6,14},{7,15},{8,0},{9,1},... | collective-permute-start | bytes 294920 | tf_op jit(solution)/shard_map/ppermute | solution.py:458
  51.9 1.6 %collective-permute-start.6 = (f32[4,48,128]{2,1,0:T(8,128)S(1)}, f32[4,48,128]{2,1,0:T(8,128)S(1)}, u32[]{:S(2)}, u32[]{:S(2)}) collective-permute-start(f32[4,48,128]{2,1,0:T(8,128)S(1)} %get-tuple-element.60), channel_id=1, source_target_pairs={{0,4},{1,5},{2,6},{3,7},{4,0},{5,1},{6,2},{7,3},{8,12},{9,13},{10,... | collective-permute-start | bytes 294920 | tf_op jit(solution)/shard_map/ppermute | solution.py:458
  53.5 0.2 collective-permute-start.7
  53.7 0.0 collective-permute-done.13
  53.7 1.0 %add.96 = f32[4,4,48,128]{3,2,1,0:T(8,128)S(1)} add(f32[4,4,48,128]{3,2,1,0:T(8,128)S(1)} %get-tuple-element.53, f32[4,4,48,128]{3,2,1,0:T(8,128)} %collective-permute-done.13) | non-fusion elementwise | flops 98304 | bytes 1179648 | tf_op jit(solution)/shard_map/add | solution.py:674
  54.8 1.8 %collective-permute-start.14 = (f32[4,48,128]{2,1,0:T(8,128)S(1)}, f32[4,48,128]{2,1,0:T(8,128)S(1)}, u32[]{:S(2)}, u32[]{:S(2)}) collective-permute-start(f32[4,48,128]{2,1,0:T(8,128)S(1)} %get-tuple-element.55), channel_id=1, source_target_pairs={{0,8},{1,9},{2,10},{3,11},{4,12},{5,13},{6,14},{7,15},{8,0},{9,1},... | collective-permute-start | bytes 294920 | tf_op jit(solution)/shard_map/ppermute | solution.py:458
  56.5 2.5 %collective-permute-start.15 = (f32[4,48,128]{2,1,0:T(8,128)S(1)}, f32[4,48,128]{2,1,0:T(8,128)S(1)}, u32[]{:S(2)}, u32[]{:S(2)}) collective-permute-start(f32[4,48,128]{2,1,0:T(8,128)S(1)} %get-tuple-element.57), channel_id=1, source_target_pairs={{0,4},{1,5},{2,6},{3,7},{4,0},{5,1},{6,2},{7,3},{8,12},{9,13},{10,... | collective-permute-start | bytes 294920 | tf_op jit(solution)/shard_map/ppermute | solution.py:458
  59.0 0.0 collective-permute-done.5
  59.0 2.5 %collective-permute-start.16 = (f32[4,48,128]{2,1,0:T(8,128)S(1)}, f32[4,48,128]{2,1,0:T(8,128)S(1)}, u32[]{:S(2)}, u32[]{:S(2)}) collective-permute-start(f32[4,48,128]{2,1,0:T(8,128)S(1)} %get-tuple-element.56), channel_id=1, source_target_pairs={{0,12},{1,13},{2,14},{3,15},{4,8},{5,9},{6,10},{7,11},{8,4},{9,5},... | collective-permute-start | bytes 294920 | tf_op jit(solution)/shard_map/ppermute | solution.py:458
  61.5 0.0 collective-permute-done.6
  61.5 0.0 collective-permute-done.7
  61.5 1.4 %collective-permute-start.8 = (f32[4,48,128]{2,1,0:T(8,128)S(1)}, f32[4,48,128]{2,1,0:T(8,128)S(1)}, u32[]{:S(2)}, u32[]{:S(2)}) collective-permute-start(f32[4,48,128]{2,1,0:T(8,128)S(1)} %fusion.3), channel_id=1, source_target_pairs={{0,2},{1,3},{2,0},{3,1},{4,6},{5,7},{6,4},{7,5},{8,10},{9,11},{10,... | collective-permute-start | bytes 294920 | tf_op jit(solution)/shard_map/ppermute | solution.py:458
  62.9 5.5 %collective-permute-done.14 = f32[4,48,128]{2,1,0:T(8,128)S(1)} collective-permute-done((f32[4,48,128]{2,1,0:T(8,128)S(1)}, f32[4,48,128]{2,1,0:T(8,128)S(1)}, u32[]{:S(2)}, u32[]{:S(2)}) %collective-permute-start.14) | collective-permute-done | bytes 98336 | tf_op jit(solution)/shard_map/ppermute | solution.py:458
  68.5 0.0 collective-permute-done.15
  68.5 0.0 collective-permute-done.16
  68.5 1.7 %collective-permute-start.17 = (f32[4,48,128]{2,1,0:T(8,128)S(1)}, f32[4,48,128]{2,1,0:T(8,128)S(1)}, u32[]{:S(2)}, u32[]{:S(2)}) collective-permute-start(f32[4,48,128]{2,1,0:T(8,128)S(1)} %fusion.1), channel_id=1, source_target_pairs={{0,2},{1,3},{2,0},{3,1},{4,6},{5,7},{6,4},{7,5},{8,10},{9,11},{10,... | collective-permute-start | bytes 294920 | tf_op jit(solution)/shard_map/ppermute | solution.py:458
  70.2 0.0 collective-permute-done.8
  70.2 2.7 %collective-permute-start.9 = (f32[4,48,128]{2,1,0:T(8,128)S(1)}, f32[4,48,128]{2,1,0:T(8,128)S(1)}, u32[]{:S(2)}, u32[]{:S(2)}) collective-permute-start(f32[4,48,128]{2,1,0:T(8,128)S(1)} %add.95), channel_id=1, source_target_pairs={{0,8},{1,9},{2,10},{3,11},{4,12},{5,13},{6,14},{7,15},{8,0},{9,1},... | collective-permute-start | bytes 294920 | tf_op jit(solution)/shard_map/ppermute | solution.py:458
  73.0 0.0 collective-permute-start.10
  73.0 1.9 %collective-permute-start.11 = (f32[4,48,128]{2,1,0:T(8,128)S(1)}, f32[4,48,128]{2,1,0:T(8,128)S(1)}, u32[]{:S(2)}, u32[]{:S(2)}) collective-permute-start(f32[4,48,128]{2,1,0:T(8,128)S(1)} %add.95), channel_id=1, source_target_pairs={{0,12},{1,13},{2,14},{3,15},{4,8},{5,9},{6,10},{7,11},{8,4},{9,5},... | collective-permute-start | bytes 294920 | tf_op jit(solution)/shard_map/ppermute | solution.py:458
  74.9 0.0 collective-permute-done.17
  74.9 2.3 %collective-permute-start.18 = (f32[4,48,128]{2,1,0:T(8,128)S(1)}, f32[4,48,128]{2,1,0:T(8,128)S(1)}, u32[]{:S(2)}, u32[]{:S(2)}) collective-permute-start(f32[4,48,128]{2,1,0:T(8,128)S(1)} %add.100), channel_id=1, source_target_pairs={{0,8},{1,9},{2,10},{3,11},{4,12},{5,13},{6,14},{7,15},{8,0},{9,1},... | collective-permute-start | bytes 294920 | tf_op jit(solution)/shard_map/ppermute | solution.py:458
  77.2 0.2 collective-permute-start.19
  77.4 2.5 %collective-permute-done.9 = f32[4,48,128]{2,1,0:T(8,128)S(1)} collective-permute-done((f32[4,48,128]{2,1,0:T(8,128)S(1)}, f32[4,48,128]{2,1,0:T(8,128)S(1)}, u32[]{:S(2)}, u32[]{:S(2)}) %collective-permute-start.9) | collective-permute-done | bytes 98336 | tf_op jit(solution)/shard_map/ppermute | solution.py:458
  80.0 0.8 collective-permute-start.20
  80.8 0.0 collective-permute-done.10
  80.8 2.1 %collective-permute-done.11 = f32[4,48,128]{2,1,0:T(8,128)S(1)} collective-permute-done((f32[4,48,128]{2,1,0:T(8,128)S(1)}, f32[4,48,128]{2,1,0:T(8,128)S(1)}, u32[]{:S(2)}, u32[]{:S(2)}) %collective-permute-start.11) | collective-permute-done | bytes 98336 | tf_op jit(solution)/shard_map/ppermute | solution.py:458
  82.9 0.1 collective-permute-start.12
  83.0 6.3 %collective-permute-done.18 = f32[4,48,128]{2,1,0:T(8,128)S(1)} collective-permute-done((f32[4,48,128]{2,1,0:T(8,128)S(1)}, f32[4,48,128]{2,1,0:T(8,128)S(1)}, u32[]{:S(2)}, u32[]{:S(2)}) %collective-permute-start.18) | collective-permute-done | bytes 98336 | tf_op jit(solution)/shard_map/ppermute | solution.py:458
  89.3 0.0 collective-permute-done.19
  89.3 0.0 collective-permute-done.20
  89.3 0.1 collective-permute-start.21
  89.4 0.1 fusion.7
  89.6 0.1 pad_maximum_fusion.2.table
  89.6 1.2 %merge.1 = (f32[3,16,64,128]{3,2,1,0:T(8,128)}, f32[3,16,64,128]{3,2,1,0:T(8,128)}) custom-call(f32[3,16,64,128]{3,2,1,0:T(8,128)} %get-tuple-element.39.e_in, f32[3,16,64,128]{3,2,1,0:T(8,128)} %get-tuple-element.40.h_in, f32[2,3,8,64,128]{4,3,2,1,0:T(8,128)S(1)} %get-tuple-element.48.fresh), custom_call_target="tpu_custom_call", output_to_operand_aliasing={{0}: (0, {}), {1}: (1, {})} | custom-call | bytes 3000000 | tf_op jit(solution)/shard_map/merge/pallas_call | solution.py:661
  90.8 0.0 collective-permute-done.12.other
  90.8 1.6 %partial0.1.before = f32[8,2,4,2,48,128]{5,4,3,2,1,0:T(8,128)S(1)} custom-call(s32[16]{0:T(128)S(1)} %concatenate.6.info, f32[8,16]{1,0:T(8,128)S(1)} %pad_maximum_fusion.2.table, f32[4,4,48,128]{3,2,1,0:T(8,128)S(1)} %pad_maximum_fusion.mine, f32[4,4,48,128]{3,2,1,0:T(8,128)S(1)} %collective-permute-done.12.other), custom_call_target="tpu_custom_call" | custom-call | bytes 9000000 | tf_op jit(solution)/shard_map/partial0/pallas_call | solution.py:682
  92.5 0.0 collective-permute-done.21.other
  92.5 3.3 %spectrum.1 = f32[8,2,4,2,64,128]{5,4,3,2,1,0:T(8,128)} custom-call(s32[16]{0:T(128)S(1)} %concatenate.6.info, f32[8,16]{1,0:T(8,128)S(1)} %pad_maximum_fusion.2.table, f32[8,2,4,2,48,128]{5,4,3,2,1,0:T(8,128)S(1)} %partial0.1.before, f32[4,4,48,128]{3,2,1,0:T(8,128)S(1)} %pad_maximum_fusion.1.mine, f32[4,4,48,128]{3,2,1,0:T(8,128)S(1)} %collective-permute-done.21.other), custom_call_target="tpu_custom_call" | custom-call | bytes 12000000 | tf_op jit(solution)/shard_map/spectrum/pallas_call | solution.py:694
  (21 shorter events, 0.2 us)
Async XLA Ops:
  0.6 8.2 %copy-start = (f32[3,16,64,128]{3,2,1,0:T(8,128)S(1)}, f32[3,16,64,128]{3,2,1,0:T(8,128)}, u32[]{:S(2)}) copy-start(f32[3,16,64,128]{3,2,1,0:T(8,128)} %e_ref.1) | copy-start | bytes 4718596
  0.6 8.2 %copy-start.1 = (f32[3,16,64,128]{3,2,1,0:T(8,128)S(1)}, f32[3,16,64,128]{3,2,1,0:T(8,128)}, u32[]{:S(2)}) copy-start(f32[3,16,64,128]{3,2,1,0:T(8,128)} %h_ref.1) | copy-start | bytes 4718596
  0.7 8.1 %copy-start.3 = (s32[4,2]{0,1:T(2,128)S(1)}, s32[4,2]{0,1:T(2,128)}, u32[]{:S(2)}) copy-start(s32[4,2]{0,1:T(2,128)} %param.14) | copy-start | bytes 100
  0.7 8.1 %copy-start.5 = (s32[4]{0:T(128)S(1)}, s32[4]{0:T(128)}, u32[]{:S(2)}) copy-start(s32[4]{0:T(128)} %param.13) | copy-start | bytes 52
  0.7 8.1 %copy-start.7 = (f32[4]{0:T(128)S(1)}, f32[4]{0:T(128)}, u32[]{:S(2)}) copy-start(f32[4]{0:T(128)} %param.11) | copy-start | bytes 52
  0.7 8.1 %copy-start.6 = (f32[4]{0:T(128)S(1)}, f32[4]{0:T(128)}, u32[]{:S(2)}) copy-start(f32[4]{0:T(128)} %param.12) | copy-start | bytes 52
  3.6 12.2 %collective-permute-start = (f32[1664,128]{1,0:T(8,128)}, f32[1664,128]{1,0:T(8,128)}, u32[]{:S(2)}, u32[]{:S(2)}) collective-permute-start(f32[1664,128]{1,0:T(8,128)} %bitcast.57), channel_id=1, source_target_pairs={{1,2},{2,1},{3,4},{4,3},{5,6},{6,5},{7,8},{8,7},{9,10},{10,9},{11,... | collective-permute-start | bytes 2555912 | tf_op jit(solution)/shard_map/ppermute | solution.py:587
  5.2 10.6 %collective-permute-start.1 = (f32[1664,128]{1,0:T(8,128)}, f32[1664,128]{1,0:T(8,128)}, u32[]{:S(2)}, u32[]{:S(2)}) collective-permute-start(f32[1664,128]{1,0:T(8,128)} %bitcast.56), channel_id=1, source_target_pairs={{0,1},{1,0},{2,3},{3,2},{4,5},{5,4},{6,7},{7,6},{8,9},{9,8},{10,11... | collective-permute-start | bytes 2555912 | tf_op jit(solution)/shard_map/ppermute | solution.py:548
  8.9 1.0 %copy-start.2 = (s32[16,64,128]{2,1,0:T(8,128)S(1)}, s32[16,64,128]{2,1,0:T(8,128)}, u32[]{:S(2)}) copy-start(s32[16,64,128]{2,1,0:T(8,128)} %m_ref.1) | copy-start | bytes 1572868
  21.1 23.6 %collective-permute-start.2 = (f32[1280,128]{1,0:T(8,128)S(1)}, f32[1280,128]{1,0:T(8,128)S(1)}, u32[]{:S(2)}, u32[]{:S(2)}) collective-permute-start(f32[1280,128]{1,0:T(8,128)S(1)} %get-tuple-element.44), channel_id=1, source_target_pairs={{1,2},{2,1},{3,4},{4,3},{5,6},{6,5},{7,8},{8,7},{9,10},{10,9},{11,... | collective-permute-start | bytes 1966088 | tf_op jit(solution)/shard_map/ppermute | solution.py:587
  21.8 22.9 %collective-permute-start.3 = (f32[1280,128]{1,0:T(8,128)S(1)}, f32[1280,128]{1,0:T(8,128)S(1)}, u32[]{:S(2)}, u32[]{:S(2)}) collective-permute-start(f32[1280,128]{1,0:T(8,128)S(1)} %get-tuple-element.45), channel_id=1, source_target_pairs={{0,1},{1,0},{2,3},{3,2},{4,5},{5,4},{6,7},{7,6},{8,9},{9,8},{10,11... | collective-permute-start | bytes 1966088 | tf_op jit(solution)/shard_map/ppermute | solution.py:548
  37.5 11.7 %collective-permute-start.4 = (f32[4,4,48,128]{3,2,1,0:T(8,128)S(1)}, f32[4,4,48,128]{3,2,1,0:T(8,128)S(1)}, u32[]{:S(2)}, u32[]{:S(2)}) collective-permute-start(f32[4,4,48,128]{3,2,1,0:T(8,128)S(1)} %get-tuple-element.52), channel_id=1, source_target_pairs={{0,1},{1,0},{2,3},{3,2},{4,5},{5,4},{6,7},{7,6},{8,9},{9,8},{10,11... | collective-permute-start | bytes 1179656 | tf_op jit(solution)/shard_map/ppermute | solution.py:548
  48.2 5.5 %collective-permute-start.13 = (f32[4,4,48,128]{3,2,1,0:T(8,128)S(1)}, f32[4,4,48,128]{3,2,1,0:T(8,128)}, u32[]{:S(2)}, u32[]{:S(2)}) collective-permute-start(f32[4,4,48,128]{3,2,1,0:T(8,128)S(1)} %get-tuple-element.54), channel_id=1, source_target_pairs={{0,1},{1,0},{2,3},{3,2},{4,5},{5,4},{6,7},{7,6},{8,9},{9,8},{10,11... | collective-permute-start | bytes 1179656 | tf_op jit(solution)/shard_map/ppermute | solution.py:548
  49.3 9.8 %collective-permute-start.5 = (f32[4,48,128]{2,1,0:T(8,128)S(1)}, f32[4,48,128]{2,1,0:T(8,128)S(1)}, u32[]{:S(2)}, u32[]{:S(2)}) collective-permute-start(f32[4,48,128]{2,1,0:T(8,128)S(1)} %get-tuple-element.58), channel_id=1, source_target_pairs={{0,8},{1,9},{2,10},{3,11},{4,12},{5,13},{6,14},{7,15},{8,0},{9,1},... | collective-permute-start | bytes 294920 | tf_op jit(solution)/shard_map/ppermute | solution.py:458
  51.9 9.6 %collective-permute-start.6 = (f32[4,48,128]{2,1,0:T(8,128)S(1)}, f32[4,48,128]{2,1,0:T(8,128)S(1)}, u32[]{:S(2)}, u32[]{:S(2)}) collective-permute-start(f32[4,48,128]{2,1,0:T(8,128)S(1)} %get-tuple-element.60), channel_id=1, source_target_pairs={{0,4},{1,5},{2,6},{3,7},{4,0},{5,1},{6,2},{7,3},{8,12},{9,13},{10,... | collective-permute-start | bytes 294920 | tf_op jit(solution)/shard_map/ppermute | solution.py:458
  53.5 8.0 %collective-permute-start.7 = (f32[4,48,128]{2,1,0:T(8,128)S(1)}, f32[4,48,128]{2,1,0:T(8,128)S(1)}, u32[]{:S(2)}, u32[]{:S(2)}) collective-permute-start(f32[4,48,128]{2,1,0:T(8,128)S(1)} %get-tuple-element.59), channel_id=1, source_target_pairs={{0,12},{1,13},{2,14},{3,15},{4,8},{5,9},{6,10},{7,11},{8,4},{9,5},... | collective-permute-start | bytes 294920 | tf_op jit(solution)/shard_map/ppermute | solution.py:458
  54.8 13.7 %collective-permute-start.14 = (f32[4,48,128]{2,1,0:T(8,128)S(1)}, f32[4,48,128]{2,1,0:T(8,128)S(1)}, u32[]{:S(2)}, u32[]{:S(2)}) collective-permute-start(f32[4,48,128]{2,1,0:T(8,128)S(1)} %get-tuple-element.55), channel_id=1, source_target_pairs={{0,8},{1,9},{2,10},{3,11},{4,12},{5,13},{6,14},{7,15},{8,0},{9,1},... | collective-permute-start | bytes 294920 | tf_op jit(solution)/shard_map/ppermute | solution.py:458
  56.5 11.9 %collective-permute-start.15 = (f32[4,48,128]{2,1,0:T(8,128)S(1)}, f32[4,48,128]{2,1,0:T(8,128)S(1)}, u32[]{:S(2)}, u32[]{:S(2)}) collective-permute-start(f32[4,48,128]{2,1,0:T(8,128)S(1)} %get-tuple-element.57), channel_id=1, source_target_pairs={{0,4},{1,5},{2,6},{3,7},{4,0},{5,1},{6,2},{7,3},{8,12},{9,13},{10,... | collective-permute-start | bytes 294920 | tf_op jit(solution)/shard_map/ppermute | solution.py:458
  59.0 30.4 %copy-start.4 = (s32[8]{0:T(128)S(1)}, s32[8]{0:T(128)}, u32[]{:S(2)}) copy-start(s32[8]{0:T(128)} %param.15) | copy-start | bytes 100
  59.0 9.5 %collective-permute-start.16 = (f32[4,48,128]{2,1,0:T(8,128)S(1)}, f32[4,48,128]{2,1,0:T(8,128)S(1)}, u32[]{:S(2)}, u32[]{:S(2)}) collective-permute-start(f32[4,48,128]{2,1,0:T(8,128)S(1)} %get-tuple-element.56), channel_id=1, source_target_pairs={{0,12},{1,13},{2,14},{3,15},{4,8},{5,9},{6,10},{7,11},{8,4},{9,5},... | collective-permute-start | bytes 294920 | tf_op jit(solution)/shard_map/ppermute | solution.py:458
  61.5 8.7 %collective-permute-start.8 = (f32[4,48,128]{2,1,0:T(8,128)S(1)}, f32[4,48,128]{2,1,0:T(8,128)S(1)}, u32[]{:S(2)}, u32[]{:S(2)}) collective-permute-start(f32[4,48,128]{2,1,0:T(8,128)S(1)} %fusion.3), channel_id=1, source_target_pairs={{0,2},{1,3},{2,0},{3,1},{4,6},{5,7},{6,4},{7,5},{8,10},{9,11},{10,... | collective-permute-start | bytes 294920 | tf_op jit(solution)/shard_map/ppermute | solution.py:458
  68.5 6.4 %collective-permute-start.17 = (f32[4,48,128]{2,1,0:T(8,128)S(1)}, f32[4,48,128]{2,1,0:T(8,128)S(1)}, u32[]{:S(2)}, u32[]{:S(2)}) collective-permute-start(f32[4,48,128]{2,1,0:T(8,128)S(1)} %fusion.1), channel_id=1, source_target_pairs={{0,2},{1,3},{2,0},{3,1},{4,6},{5,7},{6,4},{7,5},{8,10},{9,11},{10,... | collective-permute-start | bytes 294920 | tf_op jit(solution)/shard_map/ppermute | solution.py:458
  70.2 9.7 %collective-permute-start.9 = (f32[4,48,128]{2,1,0:T(8,128)S(1)}, f32[4,48,128]{2,1,0:T(8,128)S(1)}, u32[]{:S(2)}, u32[]{:S(2)}) collective-permute-start(f32[4,48,128]{2,1,0:T(8,128)S(1)} %add.95), channel_id=1, source_target_pairs={{0,8},{1,9},{2,10},{3,11},{4,12},{5,13},{6,14},{7,15},{8,0},{9,1},... | collective-permute-start | bytes 294920 | tf_op jit(solution)/shard_map/ppermute | solution.py:458
  73.0 7.8 %collective-permute-start.10 = (f32[4,48,128]{2,1,0:T(8,128)S(1)}, f32[4,48,128]{2,1,0:T(8,128)S(1)}, u32[]{:S(2)}, u32[]{:S(2)}) collective-permute-start(f32[4,48,128]{2,1,0:T(8,128)S(1)} %add.95), channel_id=1, source_target_pairs={{0,4},{1,5},{2,6},{3,7},{4,0},{5,1},{6,2},{7,3},{8,12},{9,13},{10,... | collective-permute-start | bytes 294920 | tf_op jit(solution)/shard_map/ppermute | solution.py:458
  73.0 9.9 %collective-permute-start.11 = (f32[4,48,128]{2,1,0:T(8,128)S(1)}, f32[4,48,128]{2,1,0:T(8,128)S(1)}, u32[]{:S(2)}, u32[]{:S(2)}) collective-permute-start(f32[4,48,128]{2,1,0:T(8,128)S(1)} %add.95), channel_id=1, source_target_pairs={{0,12},{1,13},{2,14},{3,15},{4,8},{5,9},{6,10},{7,11},{8,4},{9,5},... | collective-permute-start | bytes 294920 | tf_op jit(solution)/shard_map/ppermute | solution.py:458
  74.9 14.4 %collective-permute-start.18 = (f32[4,48,128]{2,1,0:T(8,128)S(1)}, f32[4,48,128]{2,1,0:T(8,128)S(1)}, u32[]{:S(2)}, u32[]{:S(2)}) collective-permute-start(f32[4,48,128]{2,1,0:T(8,128)S(1)} %add.100), channel_id=1, source_target_pairs={{0,8},{1,9},{2,10},{3,11},{4,12},{5,13},{6,14},{7,15},{8,0},{9,1},... | collective-permute-start | bytes 294920 | tf_op jit(solution)/shard_map/ppermute | solution.py:458
  77.2 12.1 %collective-permute-start.19 = (f32[4,48,128]{2,1,0:T(8,128)S(1)}, f32[4,48,128]{2,1,0:T(8,128)S(1)}, u32[]{:S(2)}, u32[]{:S(2)}) collective-permute-start(f32[4,48,128]{2,1,0:T(8,128)S(1)} %add.100), channel_id=1, source_target_pairs={{0,4},{1,5},{2,6},{3,7},{4,0},{5,1},{6,2},{7,3},{8,12},{9,13},{10,... | collective-permute-start | bytes 294920 | tf_op jit(solution)/shard_map/ppermute | solution.py:458
  80.0 9.3 %collective-permute-start.20 = (f32[4,48,128]{2,1,0:T(8,128)S(1)}, f32[4,48,128]{2,1,0:T(8,128)S(1)}, u32[]{:S(2)}, u32[]{:S(2)}) collective-permute-start(f32[4,48,128]{2,1,0:T(8,128)S(1)} %add.100), channel_id=1, source_target_pairs={{0,12},{1,13},{2,14},{3,15},{4,8},{5,9},{6,10},{7,11},{8,4},{9,5},... | collective-permute-start | bytes 294920 | tf_op jit(solution)/shard_map/ppermute | solution.py:458
  82.9 7.9 %collective-permute-start.12 = (f32[4,4,48,128]{3,2,1,0:T(8,128)S(1)}, f32[4,4,48,128]{3,2,1,0:T(8,128)S(1)}, u32[]{:S(2)}, u32[]{:S(2)}) collective-permute-start(f32[4,4,48,128]{3,2,1,0:T(8,128)S(1)} %pad_maximum_fusion.mine), channel_id=1, source_target_pairs={{0,1},{1,0},{2,3},{3,2},{4,5},{5,4},{6,7},{7,6},{8,9},{9,8},{10,11... | collective-permute-start | bytes 1179656 | tf_op jit(solution)/shard_map/ppermute | solution.py:548
  89.3 3.1 %collective-permute-start.21 = (f32[4,4,48,128]{3,2,1,0:T(8,128)S(1)}, f32[4,4,48,128]{3,2,1,0:T(8,128)S(1)}, u32[]{:S(2)}, u32[]{:S(2)}) collective-permute-start(f32[4,4,48,128]{3,2,1,0:T(8,128)S(1)} %pad_maximum_fusion.1.mine), channel_id=1, source_target_pairs={{0,1},{1,0},{2,3},{3,2},{4,5},{5,4},{6,7},{7,6},{8,9},{9,8},{10,11... | collective-permute-start | bytes 1179656 | tf_op jit(solution)/shard_map/ppermute | solution.py:548

commit v4 on v3

--- a/solution.py
+++ b/solution.py
@@ -11,7 +11,7 @@
 STEPS = 8
 PERIOD = 512
 ROUNDS = (4, 4)
-DEEP = (False, False)
+ROWS_WHEN = ("", "before")
 GHOST = max(ROUNDS)
 COURANT = 0.5
 VMEM = pl.BlockSpec(memory_space=pltpu.VMEM)
@@ -262,13 +262,13 @@
     if first:
         tables, *refs = refs
     else:
-        ghosts_in, below_in, *refs = refs
+        ghosts_in, below_in, _, _, *refs = refs
     if nxt:
         _, _, e_out, h_out, mine_out, other_out, below_out, far_out, near_out, *refs = refs
         if first:
             ghosts_out, *refs = refs
     else:
-        fresh_out, mine_out, other_out, *refs = refs
+        fresh_out, mine_out, other_out, _, _, *refs = refs
     e, h, coefs, sem = refs
     height, width = edge_in.shape[3:]
     g = GHOST
@@ -446,67 +446,49 @@
 
 
 class Sharing:
-    def __init__(self, slabs, deep):
-        self.slabs, self.deep = slabs, deep
+    def __init__(self, slabs, rows_when):
+        self.slabs, self.rows_when = slabs, rows_when
         me = lax.axis_index("slab")
-        self.low, self.high = me // 4 % 2, me // 8 % 2
-        self.others = [
-            2**k for k in range(1, slabs.bit_length() - 1) if 2**k not in (4, 8)
-        ]
+        self.quarter = 2 * (me // 4 % 2) + me // 8 % 2
+        self.half = me // 2 % 2
+        self.others = [2**k for k in range(1, slabs.bit_length() - 1)]
+        self.others = [k for k in self.others if k not in ((4, 8) if not rows_when else (2, 4, 8))]
 
     def swap(self, block, stride):
         return lax.ppermute(block, "slab", [(i, i ^ stride) for i in range(self.slabs)])
 
-    def scatter(self, total, hold):
-        if self.deep:
-            total = total.reshape(2, 2, *total.shape[1:])
-            sent = lax.dynamic_index_in_dim(total, 1 - self.low, 0, keepdims=False)
-            total = lax.dynamic_index_in_dim(total, self.low, 0, keepdims=False)
-            total = total + self.swap(sent, 4)
-            sent = lax.dynamic_index_in_dim(total, 1 - self.high, 0, keepdims=False)
-            total = lax.dynamic_index_in_dim(total, self.high, 0, keepdims=False)
-            return add(total, self.swap(sent, 8), hold=hold)
-        quarter = 2 * self.low + self.high
+    def halve(self, total, axis):
+        sent = lax.dynamic_index_in_dim(total, 1 - self.half, axis, keepdims=False)
+        kept = lax.dynamic_index_in_dim(total, self.half, axis, keepdims=False)
+        return kept + self.swap(sent, 2)
+
+    def scatter(self, total):
+        if self.rows_when:
+            total = total.reshape(total.shape[0], 2, -1, total.shape[-1])
+        if self.rows_when == "before":
+            total = self.halve(total, 1)
         pieces = [
-            lax.dynamic_index_in_dim(total, quarter ^ x, 0, keepdims=False) for x in range(4)
+            lax.dynamic_index_in_dim(total, self.quarter ^ x, 0, keepdims=False)
+            for x in range(4)
         ]
-        pieces = pieces[:1] + [self.swap(pieces[x], s) for x, s in ((1, 8), (2, 4), (3, 12))]
-        return add(*pieces, hold=hold)
-
-    def spread(self, part, hold):
+        part = pieces[0]
+        for x, stride in ((1, 8), (2, 4), (3, 12)):
+            part = part + self.swap(pieces[x], stride)
+        if self.rows_when == "after":
+            part = self.halve(part, 0)
         for stride in self.others:
-            part = add(part, self.swap(part, stride), hold=hold)
+            part = part + self.swap(part, stride)
         return part
 
-    def gather_near(self, part):
-        return jnp.stack([part, self.swap(part, 8)]) if self.deep else part
-
-    def gather_far(self, part):
-        if self.deep:
-            return jnp.concatenate([part, self.swap(part, 4)])
-        return jnp.stack([part] + [self.swap(part, stride) for stride in (8, 4, 12)])
-
-
-def add_kernel(*refs):
-    *ins, _, out = refs
-    total = ins[0][...]
-    for more in ins[1:]:
-        total = total + more[...]
-    out[...] = total
-
-
-def add(*blocks, hold):
-    if hold is None:
-        return sum(blocks[1:], blocks[0])
-    with jax.named_scope("add"):
-        return pl.pallas_call(
-            add_kernel,
-            out_shape=jax.ShapeDtypeStruct(blocks[0].shape, jnp.float32),
-            in_specs=[VMEM] * len(blocks) + [ANY],
-            out_specs=VMEM,
-            compiler_params=params(),
-            cost_estimate=cost(0.3),
-        )(*blocks, hold)
+    def gather(self, part, shape):
+        total = jnp.stack([part] + [self.swap(part, stride) for stride in (8, 4, 12)])
+        if self.rows_when:
+            theirs = self.swap(total, 2)
+            first = self.half == 0
+            total = jnp.stack(
+                [jnp.where(first, total, theirs), jnp.where(first, theirs, total)], 1
+            )
+        return total.reshape(shape)
 
 
 def per_device(
@@ -587,8 +569,7 @@
         far = lax.ppermute(far, "slab", far_pairs)
         near = near_swap(near)
         if not first:
-            early = Sharing(slabs, DEEP[k - 1])
-            part = early.scatter(mine + near_swap(other), None)
+            before = mine, other
         samples = [f32(monitors, d, rows, width)] * 2
         edge = f32(2, 3, 2 * d + 1, height, width)
         with jax.named_scope(f"inner{k}"):
@@ -624,11 +605,15 @@
             operands += [tables]
             specs += [SMEM]
         else:
-            operands += [ghosts, below]
-            specs += [VMEM, HBM]
+            operands += [ghosts, below, *before]
+            specs += [VMEM, HBM, ANY, ANY]
         outs = [f32(2, 3, 2 * d, height, width)] + samples
         kinds = [VMEM] * 3
         aliases = {}
+        if not first:
+            aliases = {len(operands) - 2: 3, len(operands) - 1: 4}
+            outs += [f32(*before[0].shape)] * 2
+            kinds += [ANY] * 2
         if nxt:
             outs = state + samples
             kinds = [HBM] * 2 + [VMEM] * 2
@@ -656,7 +641,9 @@
             if first:
                 ghosts = results[7]
         else:
-            fresh, mine, other = results
+            fresh, mine, other, *before = results
+            early = Sharing(slabs, ROWS_WHEN[k - 1])
+            part = early.scatter(before[0] + near_swap(before[1]))
     with jax.named_scope("merge"):
         e, h = pl.pallas_call(
             functools.partial(merge_kernel, d, depth),
@@ -668,12 +655,12 @@
             compiler_params=params(),
             cost_estimate=cost(1),
         )(e, h, fresh)
-    late = Sharing(slabs, DEEP[-1])
-    part = early.gather_far(early.gather_near(early.spread(part, None)))
-    chunks = [(part, near_swap(part))]
-    total = late.spread(late.scatter(mine + near_swap(other), None), None)
-    total = late.gather_far(late.gather_near(total))
-    chunks.append((total, near_swap(total)))
+    late = Sharing(slabs, ROWS_WHEN[-1])
+    total = mine + near_swap(other)
+    chunks = []
+    for sharing, block in ((early, part), (late, late.scatter(total))):
+        block = sharing.gather(block, total.shape)
+        chunks.append((block, near_swap(block)))
 
     done = 0
     sums = None

time: 96.2 us -> 91.5 us (0.951)
  waiting for transfers between devices: 16.5 us -> 10.6 us
  starting transfers between devices: 44.8 us -> 46 us
    ppermute x14 -> x15, waiting for transfers between devices: 16.5 us -> 9.17 us  [swap(): lax.ppermute(block, 'slab', [(i, i ^ stride) for i in range(self.slabs)])]
    ppermute x6, waiting for transfers between devices: 0.02 us -> 1.41 us  [near_swap(): return lax.ppermute(block, 'slab', near_pairs)]
    ppermute x14 -> x15, starting transfers between devices: 22.2 us -> 23.2 us  [swap(): lax.ppermute(block, 'slab', [(i, i ^ stride) for i in range(self.slabs)])]
  transfers between devices with their start and end apart: 22 -> 23, of which waited for: 4 -> 7; matrix products, arithmetic and copies ran while one was open for 2% -> 2% of each run, Pallas kernels for 20% -> 17%
where the time goes in v4:
time: 91.5 us; the launch traced here: 91.2 us
  starting transfers between devices  46 us (50%)
  Pallas kernels  30.9 us (34%)
  waiting for transfers between devices  10.6 us (12%)
  other arithmetic  1.48 us (2%)
  local copies, waits for them, and re-layouts  1.23 us (1%)
  between operations  1.1 us (1%)
    ppermute x15, starting transfers between devices, swap(): lax.ppermute(block, 'slab', [(i, i ^ stride) for i in range(self.slabs)])  23.2 us
    ppermute x6, starting transfers between devices, near_swap(): return lax.ppermute(block, 'slab', near_pairs)  20.5 us
    ppermute x15, waiting for transfers between devices, swap(): lax.ppermute(block, 'slab', [(i, i ^ stride) for i in range(self.slabs)])  9.17 us
    pallas_call x2, Pallas kernels, per_device(): pl.pallas_call(functools.partial(edge_kernel, d, nxt, first, depth, monit...  8.73 us
    pallas_call x1, Pallas kernels, per_device(): pl.pallas_call(kernel, out_shape=state + samples + [edge], in_specs=[SMEM...  7.19 us
    pallas_call x1, Pallas kernels, per_device(): pl.pallas_call(kernel, out_shape=state + samples + [edge, f32(2, depth, h...  5.91 us
    pallas_call x1, Pallas kernels, per_device(): pl.pallas_call(functools.partial(spectrum_kernel, ROUNDS[-1], done, monit...  3.3 us
    pallas_call x1, Pallas kernels, per_device(): pl.pallas_call(functools.partial(first_pack_kernel, d, mats, depth), out_...  2.94 us
  transfers between devices with their start and end apart: 23, of which 7 were waited for; matrix products, arithmetic and copies ran while one was open for 2% of the time, Pallas kernels for 17%

profile of v4, /device:TPU:0, one launch (start us, length us, event | category | flops | bytes accessed | tf_op | source)
XLA Modules:
  0.0 91.2 jit_solution(3765848849901334137)
XLA Ops:
  0.6 0.0 copy-start
  0.7 2.9 %first_pack.1 = (f32[26,64,128]{2,1,0:T(8,128)}, f32[26,64,128]{2,1,0:T(8,128)}) custom-call(f32[3,16,64,128]{3,2,1,0:T(8,128)} %e_ref.1, f32[3,16,64,128]{3,2,1,0:T(8,128)} %h_ref.1, s32[16,64,128]{2,1,0:T(8,128)} %m_ref.1), custom_call_target="tpu_custom_call" | custom-call | bytes 6000000 | tf_op jit(solution)/shard_map/first_pack/pallas_call | solution.py:548
  3.6 1.6 %collective-permute-start = (f32[1664,128]{1,0:T(8,128)}, f32[1664,128]{1,0:T(8,128)}, u32[]{:S(2)}, u32[]{:S(2)}) collective-permute-start(f32[1664,128]{1,0:T(8,128)} %bitcast.77), channel_id=1, source_target_pairs={{1,2},{2,1},{3,4},{4,3},{5,6},{6,5},{7,8},{8,7},{9,10},{10,9},{11,... | collective-permute-start | bytes 2555912 | tf_op jit(solution)/shard_map/ppermute | solution.py:569
  5.2 3.5 %collective-permute-start.1 = (f32[1664,128]{1,0:T(8,128)}, f32[1664,128]{1,0:T(8,128)}, u32[]{:S(2)}, u32[]{:S(2)}) collective-permute-start(f32[1664,128]{1,0:T(8,128)} %bitcast.76), channel_id=1, source_target_pairs={{0,1},{1,0},{2,3},{3,2},{4,5},{5,4},{6,7},{7,6},{8,9},{9,8},{10,11... | collective-permute-start | bytes 2555912 | tf_op jit(solution)/shard_map/ppermute | solution.py:530
  8.7 0.1 concatenate.6.info
  8.8 0.0 copy-done.6
  8.9 0.0 copy-start.2
  8.9 1.0 %copy-done.2 = s32[16,64,128]{2,1,0:T(8,128)S(1)} copy-done((s32[16,64,128]{2,1,0:T(8,128)S(1)}, s32[16,64,128]{2,1,0:T(8,128)}, u32[]{:S(2)}) %copy-start.2) | copy-done | bytes 524312
  9.9 5.9 %inner0.1 = (f32[3,16,64,128]{3,2,1,0:T(8,128)}, f32[3,16,64,128]{3,2,1,0:T(8,128)}, f32[4,4,48,128]{3,2,1,0:T(8,128)S(1)}, f32[4,4,48,128]{3,2,1,0:T(8,128)S(1)...) custom-call(s32[16]{0:T(128)S(1)} %concatenate.6.info, ...), custom_call_target="tpu_custom_call" | custom-call | bytes 15000000 | tf_op jit(solution)/shard_map/inner0/pallas_call | solution.py:578
  15.8 0.0 collective-permute-done.refs_4_
  15.8 0.0 collective-permute-done.1.refs_5_
  15.8 5.3 %edge0.1 = (f32[3,16,64,128]{3,2,1,0:T(8,128)}, f32[3,16,64,128]{3,2,1,0:T(8,128)}, f32[4,4,48,128]{3,2,1,0:T(8,128)S(1)}, f32[4,4,48,128]{3,2,1,0:T(8,128)S(1)}...) custom-call(s32[16]{0:T(128)S(1)} %concatenate.6.info, ...), custom_call_target="tpu_custom_call", output_to_operand_aliasing={{0}: (8, {}), {1}: (9, {})} | custom-call | bytes 12000000 | tf_op jit(solution)/shard_map/edge0/pallas_call | solution.py:629
  21.1 0.7 collective-permute-start.2
  21.8 15.6 %collective-permute-start.3 = (f32[1280,128]{1,0:T(8,128)S(1)}, f32[1280,128]{1,0:T(8,128)S(1)}, u32[]{:S(2)}, u32[]{:S(2)}) collective-permute-start(f32[1280,128]{1,0:T(8,128)S(1)} %get-tuple-element.47), channel_id=1, source_target_pairs={{0,1},{1,0},{2,3},{3,2},{4,5},{5,4},{6,7},{7,6},{8,9},{9,8},{10,11... | collective-permute-start | bytes 1966088 | tf_op jit(solution)/shard_map/ppermute | solution.py:530
  37.4 7.2 %inner1.1 = (f32[3,16,64,128]{3,2,1,0:T(8,128)}, f32[3,16,64,128]{3,2,1,0:T(8,128)}, f32[4,4,48,128]{3,2,1,0:T(8,128)S(1)}, f32[4,4,48,128]{3,2,1,0:T(8,128)S(1)}, f32[2,3,9,64,128]{4,3,2,1,0:T(8,128)S(1)}) custom-call(s32[16]{0:T(128)S(1)} %concatenate.6.info, ...), custom_call_target="tpu_custom_call", output_to_operand_aliasing={{0}: (1, {}), {1}: (2, {})} | custom-call | bytes 15000000 | tf_op jit(solution)/shard_map/inner1/pallas_call | solution.py:592
  44.6 0.0 collective-permute-done.2.refs_4_
  44.7 0.0 collective-permute-done.3.refs_5_
  44.7 3.4 %edge1.1 = (f32[2,3,8,64,128]{4,3,2,1,0:T(8,128)S(1)}, f32[4,4,48,128]{3,2,1,0:T(8,128)S(1)}, f32[4,4,48,128]{3,2,1,0:T(8,128)S(1)}, f32[4,4,48,128]{3,2,1,0:T(8,128)S(1)}, f32[4,4,48,128]{3,2,1,0:T(8,128)S(1)}) custom-call(s32[16]{0:T(128)S(1)} %concatenate.6.info, ...), custom_call_target="tpu_custom_call", output_to_operand_aliasing={{3}: (9, {}), {4}: (10, {})} | custom-call | bytes 12000000 | tf_op jit(solution)/shard_map/edge1/pallas_call | solution.py:629
  48.1 1.0 %collective-permute-start.13 = (f32[4,4,48,128]{3,2,1,0:T(8,128)S(1)}, f32[4,4,48,128]{3,2,1,0:T(8,128)}, u32[]{:S(2)}, u32[]{:S(2)}) collective-permute-start(f32[4,4,48,128]{3,2,1,0:T(8,128)S(1)} %get-tuple-element.58), channel_id=1, source_target_pairs={{0,1},{1,0},{2,3},{3,2},{4,5},{5,4},{6,7},{7,6},{8,9},{9,8},{10,11... | collective-permute-start | bytes 1179656 | tf_op jit(solution)/shard_map/ppermute | solution.py:530
  49.1 0.1 collective-permute-start.4
  49.2 1.4 %collective-permute-done.13 = f32[4,4,48,128]{3,2,1,0:T(8,128)} collective-permute-done((f32[4,4,48,128]{3,2,1,0:T(8,128)S(1)}, f32[4,4,48,128]{3,2,1,0:T(8,128)}, u32[]{:S(2)}, u32[]{:S(2)}) %collective-permute-start.13) | collective-permute-done | bytes 393248 | tf_op jit(solution)/shard_map/ppermute | solution.py:530
  50.6 1.0 %add.110 = f32[4,4,48,128]{3,2,1,0:T(8,128)S(1)} add(f32[4,4,48,128]{3,2,1,0:T(8,128)S(1)} %get-tuple-element.57, f32[4,4,48,128]{3,2,1,0:T(8,128)} %collective-permute-done.13) | non-fusion elementwise | flops 98304 | bytes 1179648 | tf_op jit(solution)/shard_map/add | solution.py:659
  51.7 2.1 %collective-permute-start.14 = (f32[4,96,128]{2,1,0:T(8,128)S(1)}, f32[4,96,128]{2,1,0:T(8,128)S(1)}, u32[]{:S(2)}, u32[]{:S(2)}) collective-permute-start(f32[4,96,128]{2,1,0:T(8,128)S(1)} %dynamic-slice_bitcast_fusion), channel_id=1, source_target_pairs={{0,2},{1,3},{2,0},{3,1},{4,6},{5,7},{6,4},{7,5},{8,10},{9,11},{10,... | collective-permute-start | bytes 589832 | tf_op jit(solution)/shard_map/ppermute | solution.py:458
  53.8 0.0 collective-permute-done.4
  53.8 0.1 add.100
  53.9 2.6 %collective-permute-start.5 = (f32[4,48,128]{2,1,0:T(8,128)S(1)}, f32[4,48,128]{2,1,0:T(8,128)S(1)}, u32[]{:S(2)}, u32[]{:S(2)}) collective-permute-start(f32[4,48,128]{2,1,0:T(8,128)S(1)} %get-tuple-element.61), channel_id=1, source_target_pairs={{0,8},{1,9},{2,10},{3,11},{4,12},{5,13},{6,14},{7,15},{8,0},{9,1},... | collective-permute-start | bytes 294920 | tf_op jit(solution)/shard_map/ppermute | solution.py:458
  56.5 0.0 collective-permute-start.6
  56.5 1.8 %collective-permute-start.7 = (f32[4,48,128]{2,1,0:T(8,128)S(1)}, f32[4,48,128]{2,1,0:T(8,128)S(1)}, u32[]{:S(2)}, u32[]{:S(2)}) collective-permute-start(f32[4,48,128]{2,1,0:T(8,128)S(1)} %get-tuple-element.62), channel_id=1, source_target_pairs={{0,12},{1,13},{2,14},{3,15},{4,8},{5,9},{6,10},{7,11},{8,4},{9,5},... | collective-permute-start | bytes 294920 | tf_op jit(solution)/shard_map/ppermute | solution.py:458
  58.3 0.7 collective-permute-done.14
  59.0 2.6 %collective-permute-start.15 = (f32[96,128]{1,0:T(8,128)S(1)}, f32[96,128]{1,0:T(8,128)S(1)}, u32[]{:S(2)}, u32[]{:S(2)}) collective-permute-start(f32[96,128]{1,0:T(8,128)S(1)} %get-tuple-element.64), channel_id=1, source_target_pairs={{0,8},{1,9},{2,10},{3,11},{4,12},{5,13},{6,14},{7,15},{8,0},{9,1},... | collective-permute-start | bytes 147464 | tf_op jit(solution)/shard_map/ppermute | solution.py:458
  61.7 1.6 %collective-permute-start.16 = (f32[96,128]{1,0:T(8,128)S(1)}, f32[96,128]{1,0:T(8,128)S(1)}, u32[]{:S(2)}, u32[]{:S(2)}) collective-permute-start(f32[96,128]{1,0:T(8,128)S(1)} %get-tuple-element.66), channel_id=1, source_target_pairs={{0,4},{1,5},{2,6},{3,7},{4,0},{5,1},{6,2},{7,3},{8,12},{9,13},{10,... | collective-permute-start | bytes 147464 | tf_op jit(solution)/shard_map/ppermute | solution.py:458
  63.2 0.0 collective-permute-done.5
  63.2 1.5 %collective-permute-start.17 = (f32[96,128]{1,0:T(8,128)S(1)}, f32[96,128]{1,0:T(8,128)S(1)}, u32[]{:S(2)}, u32[]{:S(2)}) collective-permute-start(f32[96,128]{1,0:T(8,128)S(1)} %get-tuple-element.65), channel_id=1, source_target_pairs={{0,12},{1,13},{2,14},{3,15},{4,8},{5,9},{6,10},{7,11},{8,4},{9,5},... | collective-permute-start | bytes 147464 | tf_op jit(solution)/shard_map/ppermute | solution.py:458
  64.8 0.0 collective-permute-done.6
  64.8 0.9 %collective-permute-done.7 = f32[4,48,128]{2,1,0:T(8,128)S(1)} collective-permute-done((f32[4,48,128]{2,1,0:T(8,128)S(1)}, f32[4,48,128]{2,1,0:T(8,128)S(1)}, u32[]{:S(2)}, u32[]{:S(2)}) %collective-permute-start.7) | collective-permute-done | bytes 98336 | tf_op jit(solution)/shard_map/ppermute | solution.py:458
  65.7 0.6 collective-permute-start.8
  66.3 3.1 %collective-permute-done.15 = f32[96,128]{1,0:T(8,128)S(1)} collective-permute-done((f32[96,128]{1,0:T(8,128)S(1)}, f32[96,128]{1,0:T(8,128)S(1)}, u32[]{:S(2)}, u32[]{:S(2)}) %collective-permute-start.15) | collective-permute-done | bytes 49184 | tf_op jit(solution)/shard_map/ppermute | solution.py:458
  69.4 0.0 collective-permute-done.16
  69.4 0.0 collective-permute-done.17
  69.4 0.0 copy-start.4
  69.4 1.9 %collective-permute-start.18 = (f32[96,128]{1,0:T(8,128)S(1)}, f32[96,128]{1,0:T(8,128)S(1)}, u32[]{:S(2)}, u32[]{:S(2)}) collective-permute-start(f32[96,128]{1,0:T(8,128)S(1)} %fusion.3), channel_id=1, source_target_pairs={{0,8},{1,9},{2,10},{3,11},{4,12},{5,13},{6,14},{7,15},{8,0},{9,1},... | collective-permute-start | bytes 147464 | tf_op jit(solution)/shard_map/ppermute | solution.py:458
  71.3 0.9 %collective-permute-start.19 = (f32[96,128]{1,0:T(8,128)S(1)}, f32[96,128]{1,0:T(8,128)S(1)}, u32[]{:S(2)}, u32[]{:S(2)}) collective-permute-start(f32[96,128]{1,0:T(8,128)S(1)} %fusion.3), channel_id=1, source_target_pairs={{0,4},{1,5},{2,6},{3,7},{4,0},{5,1},{6,2},{7,3},{8,12},{9,13},{10,... | collective-permute-start | bytes 147464 | tf_op jit(solution)/shard_map/ppermute | solution.py:458
  72.2 1.7 %collective-permute-start.20 = (f32[96,128]{1,0:T(8,128)S(1)}, f32[96,128]{1,0:T(8,128)S(1)}, u32[]{:S(2)}, u32[]{:S(2)}) collective-permute-start(f32[96,128]{1,0:T(8,128)S(1)} %fusion.3), channel_id=1, source_target_pairs={{0,12},{1,13},{2,14},{3,15},{4,8},{5,9},{6,10},{7,11},{8,4},{9,5},... | collective-permute-start | bytes 147464 | tf_op jit(solution)/shard_map/ppermute | solution.py:458
  73.9 0.0 collective-permute-done.8
  73.9 1.0 %collective-permute-start.9 = (f32[4,48,128]{2,1,0:T(8,128)S(1)}, f32[4,48,128]{2,1,0:T(8,128)S(1)}, u32[]{:S(2)}, u32[]{:S(2)}) collective-permute-start(f32[4,48,128]{2,1,0:T(8,128)S(1)} %add.108), channel_id=1, source_target_pairs={{0,8},{1,9},{2,10},{3,11},{4,12},{5,13},{6,14},{7,15},{8,0},{9,1},... | collective-permute-start | bytes 294920 | tf_op jit(solution)/shard_map/ppermute | solution.py:458
  74.9 1.8 %collective-permute-start.10 = (f32[4,48,128]{2,1,0:T(8,128)S(1)}, f32[4,48,128]{2,1,0:T(8,128)S(1)}, u32[]{:S(2)}, u32[]{:S(2)}) collective-permute-start(f32[4,48,128]{2,1,0:T(8,128)S(1)} %add.108), channel_id=1, source_target_pairs={{0,4},{1,5},{2,6},{3,7},{4,0},{5,1},{6,2},{7,3},{8,12},{9,13},{10,... | collective-permute-start | bytes 294920 | tf_op jit(solution)/shard_map/ppermute | solution.py:458
  76.7 0.0 collective-permute-done.18
  76.7 1.9 %collective-permute-start.11 = (f32[4,48,128]{2,1,0:T(8,128)S(1)}, f32[4,48,128]{2,1,0:T(8,128)S(1)}, u32[]{:S(2)}, u32[]{:S(2)}) collective-permute-start(f32[4,48,128]{2,1,0:T(8,128)S(1)} %add.108), channel_id=1, source_target_pairs={{0,12},{1,13},{2,14},{3,15},{4,8},{5,9},{6,10},{7,11},{8,4},{9,5},... | collective-permute-start | bytes 294920 | tf_op jit(solution)/shard_map/ppermute | solution.py:458
  78.6 0.0 collective-permute-done.19
  78.6 0.1 collective-permute-done.20
  78.7 1.3 %collective-permute-start.21 = (f32[4,96,128]{2,1,0:T(8,128)S(1)}, f32[4,96,128]{2,1,0:T(8,128)S(1)}, u32[]{:S(2)}, u32[]{:S(2)}) collective-permute-start(f32[4,96,128]{2,1,0:T(8,128)S(1)} %pad_maximum_fusion.2), channel_id=1, source_target_pairs={{0,2},{1,3},{2,0},{3,1},{4,6},{5,7},{6,4},{7,5},{8,10},{9,11},{10,... | collective-permute-start | bytes 589832 | tf_op jit(solution)/shard_map/ppermute | solution.py:458
  80.0 4.0 %collective-permute-done.9 = f32[4,48,128]{2,1,0:T(8,128)S(1)} collective-permute-done((f32[4,48,128]{2,1,0:T(8,128)S(1)}, f32[4,48,128]{2,1,0:T(8,128)S(1)}, u32[]{:S(2)}, u32[]{:S(2)}) %collective-permute-start.9) | collective-permute-done | bytes 98336 | tf_op jit(solution)/shard_map/ppermute | solution.py:458
  84.0 0.0 collective-permute-done.10
  84.0 0.0 collective-permute-done.11
  84.0 0.1 collective-permute-start.12
  84.1 0.4 collective-permute-done.21
  84.5 0.2 collective-permute-start.22
  84.7 0.1 fusion.7
  84.8 0.1 pad_maximum_fusion.3.table
  84.9 1.2 %merge.1 = (f32[3,16,64,128]{3,2,1,0:T(8,128)}, f32[3,16,64,128]{3,2,1,0:T(8,128)}) custom-call(f32[3,16,64,128]{3,2,1,0:T(8,128)} %get-tuple-element.41.e_in, f32[3,16,64,128]{3,2,1,0:T(8,128)} %get-tuple-element.42.h_in, f32[2,3,8,64,128]{4,3,2,1,0:T(8,128)S(1)} %get-tuple-element.52.fresh), custom_call_target="tpu_custom_call", output_to_operand_aliasing={{0}: (0, {}), {1}: (1, {})} | custom-call | bytes 3000000 | tf_op jit(solution)/shard_map/merge/pallas_call | solution.py:648
  86.1 0.0 collective-permute-done.12.other
  86.1 1.6 %partial0.1.before = f32[8,2,4,2,48,128]{5,4,3,2,1,0:T(8,128)S(1)} custom-call(s32[16]{0:T(128)S(1)} %concatenate.6.info, f32[8,16]{1,0:T(8,128)S(1)} %pad_maximum_fusion.3.table, f32[4,4,48,128]{3,2,1,0:T(8,128)S(1)} %pad_maximum_fusion.mine, f32[4,4,48,128]{3,2,1,0:T(8,128)S(1)} %collective-permute-done.12.other), custom_call_target="tpu_custom_call" | custom-call | bytes 9000000 | tf_op jit(solution)/shard_map/partial0/pallas_call | solution.py:669
  87.7 0.0 collective-permute-done.22.other
  87.7 3.3 %spectrum.1 = f32[8,2,4,2,64,128]{5,4,3,2,1,0:T(8,128)} custom-call(s32[16]{0:T(128)S(1)} %concatenate.6.info, f32[8,16]{1,0:T(8,128)S(1)} %pad_maximum_fusion.3.table, f32[8,2,4,2,48,128]{5,4,3,2,1,0:T(8,128)S(1)} %partial0.1.before, f32[4,4,48,128]{3,2,1,0:T(8,128)S(1)} %bitcast.59, f32[4,4,48,128]{3,2,1,0:T(8,128)S(1)} %collective-permute-done.22.other), custom_call_target="tpu_custom_call" | custom-call | bytes 12000000 | tf_op jit(solution)/shard_map/spectrum/pallas_call | solution.py:681
  (26 shorter events, 0.3 us)
Async XLA Ops:
  0.6 8.2 %copy-start = (f32[3,16,64,128]{3,2,1,0:T(8,128)S(1)}, f32[3,16,64,128]{3,2,1,0:T(8,128)}, u32[]{:S(2)}) copy-start(f32[3,16,64,128]{3,2,1,0:T(8,128)} %e_ref.1) | copy-start | bytes 4718596
  0.6 8.2 %copy-start.1 = (f32[3,16,64,128]{3,2,1,0:T(8,128)S(1)}, f32[3,16,64,128]{3,2,1,0:T(8,128)}, u32[]{:S(2)}) copy-start(f32[3,16,64,128]{3,2,1,0:T(8,128)} %h_ref.1) | copy-start | bytes 4718596
  0.7 8.1 %copy-start.3 = (s32[4,2]{0,1:T(2,128)S(1)}, s32[4,2]{0,1:T(2,128)}, u32[]{:S(2)}) copy-start(s32[4,2]{0,1:T(2,128)} %param.14) | copy-start | bytes 100
  0.7 8.1 %copy-start.5 = (s32[4]{0:T(128)S(1)}, s32[4]{0:T(128)}, u32[]{:S(2)}) copy-start(s32[4]{0:T(128)} %param.13) | copy-start | bytes 52
  0.7 8.1 %copy-start.7 = (f32[4]{0:T(128)S(1)}, f32[4]{0:T(128)}, u32[]{:S(2)}) copy-start(f32[4]{0:T(128)} %param.11) | copy-start | bytes 52
  0.7 8.1 %copy-start.6 = (f32[4]{0:T(128)S(1)}, f32[4]{0:T(128)}, u32[]{:S(2)}) copy-start(f32[4]{0:T(128)} %param.12) | copy-start | bytes 52
  3.6 12.2 %collective-permute-start = (f32[1664,128]{1,0:T(8,128)}, f32[1664,128]{1,0:T(8,128)}, u32[]{:S(2)}, u32[]{:S(2)}) collective-permute-start(f32[1664,128]{1,0:T(8,128)} %bitcast.77), channel_id=1, source_target_pairs={{1,2},{2,1},{3,4},{4,3},{5,6},{6,5},{7,8},{8,7},{9,10},{10,9},{11,... | collective-permute-start | bytes 2555912 | tf_op jit(solution)/shard_map/ppermute | solution.py:569
  5.2 10.6 %collective-permute-start.1 = (f32[1664,128]{1,0:T(8,128)}, f32[1664,128]{1,0:T(8,128)}, u32[]{:S(2)}, u32[]{:S(2)}) collective-permute-start(f32[1664,128]{1,0:T(8,128)} %bitcast.76), channel_id=1, source_target_pairs={{0,1},{1,0},{2,3},{3,2},{4,5},{5,4},{6,7},{7,6},{8,9},{9,8},{10,11... | collective-permute-start | bytes 2555912 | tf_op jit(solution)/shard_map/ppermute | solution.py:530
  8.9 1.0 %copy-start.2 = (s32[16,64,128]{2,1,0:T(8,128)S(1)}, s32[16,64,128]{2,1,0:T(8,128)}, u32[]{:S(2)}) copy-start(s32[16,64,128]{2,1,0:T(8,128)} %m_ref.1) | copy-start | bytes 1572868
  21.1 23.5 %collective-permute-start.2 = (f32[1280,128]{1,0:T(8,128)S(1)}, f32[1280,128]{1,0:T(8,128)S(1)}, u32[]{:S(2)}, u32[]{:S(2)}) collective-permute-start(f32[1280,128]{1,0:T(8,128)S(1)} %get-tuple-element.46), channel_id=1, source_target_pairs={{1,2},{2,1},{3,4},{4,3},{5,6},{6,5},{7,8},{8,7},{9,10},{10,9},{11,... | collective-permute-start | bytes 1966088 | tf_op jit(solution)/shard_map/ppermute | solution.py:569
  21.8 22.8 %collective-permute-start.3 = (f32[1280,128]{1,0:T(8,128)S(1)}, f32[1280,128]{1,0:T(8,128)S(1)}, u32[]{:S(2)}, u32[]{:S(2)}) collective-permute-start(f32[1280,128]{1,0:T(8,128)S(1)} %get-tuple-element.47), channel_id=1, source_target_pairs={{0,1},{1,0},{2,3},{3,2},{4,5},{5,4},{6,7},{7,6},{8,9},{9,8},{10,11... | collective-permute-start | bytes 1966088 | tf_op jit(solution)/shard_map/ppermute | solution.py:530
  48.1 2.5 %collective-permute-start.13 = (f32[4,4,48,128]{3,2,1,0:T(8,128)S(1)}, f32[4,4,48,128]{3,2,1,0:T(8,128)}, u32[]{:S(2)}, u32[]{:S(2)}) collective-permute-start(f32[4,4,48,128]{3,2,1,0:T(8,128)S(1)} %get-tuple-element.58), channel_id=1, source_target_pairs={{0,1},{1,0},{2,3},{3,2},{4,5},{5,4},{6,7},{7,6},{8,9},{9,8},{10,11... | collective-permute-start | bytes 1179656 | tf_op jit(solution)/shard_map/ppermute | solution.py:530
  49.1 4.6 %collective-permute-start.4 = (f32[4,4,48,128]{3,2,1,0:T(8,128)S(1)}, f32[4,4,48,128]{3,2,1,0:T(8,128)S(1)}, u32[]{:S(2)}, u32[]{:S(2)}) collective-permute-start(f32[4,4,48,128]{3,2,1,0:T(8,128)S(1)} %get-tuple-element.56), channel_id=1, source_target_pairs={{0,1},{1,0},{2,3},{3,2},{4,5},{5,4},{6,7},{7,6},{8,9},{9,8},{10,11... | collective-permute-start | bytes 1179656 | tf_op jit(solution)/shard_map/ppermute | solution.py:530
  51.7 7.3 %collective-permute-start.14 = (f32[4,96,128]{2,1,0:T(8,128)S(1)}, f32[4,96,128]{2,1,0:T(8,128)S(1)}, u32[]{:S(2)}, u32[]{:S(2)}) collective-permute-start(f32[4,96,128]{2,1,0:T(8,128)S(1)} %dynamic-slice_bitcast_fusion), channel_id=1, source_target_pairs={{0,2},{1,3},{2,0},{3,1},{4,6},{5,7},{6,4},{7,5},{8,10},{9,11},{10,... | collective-permute-start | bytes 589832 | tf_op jit(solution)/shard_map/ppermute | solution.py:458
  53.9 9.4 %collective-permute-start.5 = (f32[4,48,128]{2,1,0:T(8,128)S(1)}, f32[4,48,128]{2,1,0:T(8,128)S(1)}, u32[]{:S(2)}, u32[]{:S(2)}) collective-permute-start(f32[4,48,128]{2,1,0:T(8,128)S(1)} %get-tuple-element.61), channel_id=1, source_target_pairs={{0,8},{1,9},{2,10},{3,11},{4,12},{5,13},{6,14},{7,15},{8,0},{9,1},... | collective-permute-start | bytes 294920 | tf_op jit(solution)/shard_map/ppermute | solution.py:458
  56.5 8.3 %collective-permute-start.6 = (f32[4,48,128]{2,1,0:T(8,128)S(1)}, f32[4,48,128]{2,1,0:T(8,128)S(1)}, u32[]{:S(2)}, u32[]{:S(2)}) collective-permute-start(f32[4,48,128]{2,1,0:T(8,128)S(1)} %get-tuple-element.63), channel_id=1, source_target_pairs={{0,4},{1,5},{2,6},{3,7},{4,0},{5,1},{6,2},{7,3},{8,12},{9,13},{10,... | collective-permute-start | bytes 294920 | tf_op jit(solution)/shard_map/ppermute | solution.py:458
  56.5 9.2 %collective-permute-start.7 = (f32[4,48,128]{2,1,0:T(8,128)S(1)}, f32[4,48,128]{2,1,0:T(8,128)S(1)}, u32[]{:S(2)}, u32[]{:S(2)}) collective-permute-start(f32[4,48,128]{2,1,0:T(8,128)S(1)} %get-tuple-element.62), channel_id=1, source_target_pairs={{0,12},{1,13},{2,14},{3,15},{4,8},{5,9},{6,10},{7,11},{8,4},{9,5},... | collective-permute-start | bytes 294920 | tf_op jit(solution)/shard_map/ppermute | solution.py:458
  59.0 10.4 %collective-permute-start.15 = (f32[96,128]{1,0:T(8,128)S(1)}, f32[96,128]{1,0:T(8,128)S(1)}, u32[]{:S(2)}, u32[]{:S(2)}) collective-permute-start(f32[96,128]{1,0:T(8,128)S(1)} %get-tuple-element.64), channel_id=1, source_target_pairs={{0,8},{1,9},{2,10},{3,11},{4,12},{5,13},{6,14},{7,15},{8,0},{9,1},... | collective-permute-start | bytes 147464 | tf_op jit(solution)/shard_map/ppermute | solution.py:458
  61.7 7.7 %collective-permute-start.16 = (f32[96,128]{1,0:T(8,128)S(1)}, f32[96,128]{1,0:T(8,128)S(1)}, u32[]{:S(2)}, u32[]{:S(2)}) collective-permute-start(f32[96,128]{1,0:T(8,128)S(1)} %get-tuple-element.66), channel_id=1, source_target_pairs={{0,4},{1,5},{2,6},{3,7},{4,0},{5,1},{6,2},{7,3},{8,12},{9,13},{10,... | collective-permute-start | bytes 147464 | tf_op jit(solution)/shard_map/ppermute | solution.py:458
  63.2 6.2 %collective-permute-start.17 = (f32[96,128]{1,0:T(8,128)S(1)}, f32[96,128]{1,0:T(8,128)S(1)}, u32[]{:S(2)}, u32[]{:S(2)}) collective-permute-start(f32[96,128]{1,0:T(8,128)S(1)} %get-tuple-element.65), channel_id=1, source_target_pairs={{0,12},{1,13},{2,14},{3,15},{4,8},{5,9},{6,10},{7,11},{8,4},{9,5},... | collective-permute-start | bytes 147464 | tf_op jit(solution)/shard_map/ppermute | solution.py:458
  65.7 8.2 %collective-permute-start.8 = (f32[4,48,128]{2,1,0:T(8,128)S(1)}, f32[4,48,128]{2,1,0:T(8,128)S(1)}, u32[]{:S(2)}, u32[]{:S(2)}) collective-permute-start(f32[4,48,128]{2,1,0:T(8,128)S(1)} %fusion.1), channel_id=1, source_target_pairs={{0,2},{1,3},{2,0},{3,1},{4,6},{5,7},{6,4},{7,5},{8,10},{9,11},{10,... | collective-permute-start | bytes 294920 | tf_op jit(solution)/shard_map/ppermute | solution.py:458
  69.4 15.3 %copy-start.4 = (s32[8]{0:T(128)S(1)}, s32[8]{0:T(128)}, u32[]{:S(2)}) copy-start(s32[8]{0:T(128)} %param.15) | copy-start | bytes 100
  69.4 7.3 %collective-permute-start.18 = (f32[96,128]{1,0:T(8,128)S(1)}, f32[96,128]{1,0:T(8,128)S(1)}, u32[]{:S(2)}, u32[]{:S(2)}) collective-permute-start(f32[96,128]{1,0:T(8,128)S(1)} %fusion.3), channel_id=1, source_target_pairs={{0,8},{1,9},{2,10},{3,11},{4,12},{5,13},{6,14},{7,15},{8,0},{9,1},... | collective-permute-start | bytes 147464 | tf_op jit(solution)/shard_map/ppermute | solution.py:458
  71.3 7.3 %collective-permute-start.19 = (f32[96,128]{1,0:T(8,128)S(1)}, f32[96,128]{1,0:T(8,128)S(1)}, u32[]{:S(2)}, u32[]{:S(2)}) collective-permute-start(f32[96,128]{1,0:T(8,128)S(1)} %fusion.3), channel_id=1, source_target_pairs={{0,4},{1,5},{2,6},{3,7},{4,0},{5,1},{6,2},{7,3},{8,12},{9,13},{10,... | collective-permute-start | bytes 147464 | tf_op jit(solution)/shard_map/ppermute | solution.py:458
  72.2 6.5 %collective-permute-start.20 = (f32[96,128]{1,0:T(8,128)S(1)}, f32[96,128]{1,0:T(8,128)S(1)}, u32[]{:S(2)}, u32[]{:S(2)}) collective-permute-start(f32[96,128]{1,0:T(8,128)S(1)} %fusion.3), channel_id=1, source_target_pairs={{0,12},{1,13},{2,14},{3,15},{4,8},{5,9},{6,10},{7,11},{8,4},{9,5},... | collective-permute-start | bytes 147464 | tf_op jit(solution)/shard_map/ppermute | solution.py:458
  73.9 10.1 %collective-permute-start.9 = (f32[4,48,128]{2,1,0:T(8,128)S(1)}, f32[4,48,128]{2,1,0:T(8,128)S(1)}, u32[]{:S(2)}, u32[]{:S(2)}) collective-permute-start(f32[4,48,128]{2,1,0:T(8,128)S(1)} %add.108), channel_id=1, source_target_pairs={{0,8},{1,9},{2,10},{3,11},{4,12},{5,13},{6,14},{7,15},{8,0},{9,1},... | collective-permute-start | bytes 294920 | tf_op jit(solution)/shard_map/ppermute | solution.py:458
  74.9 9.1 %collective-permute-start.10 = (f32[4,48,128]{2,1,0:T(8,128)S(1)}, f32[4,48,128]{2,1,0:T(8,128)S(1)}, u32[]{:S(2)}, u32[]{:S(2)}) collective-permute-start(f32[4,48,128]{2,1,0:T(8,128)S(1)} %add.108), channel_id=1, source_target_pairs={{0,4},{1,5},{2,6},{3,7},{4,0},{5,1},{6,2},{7,3},{8,12},{9,13},{10,... | collective-permute-start | bytes 294920 | tf_op jit(solution)/shard_map/ppermute | solution.py:458
  76.7 7.3 %collective-permute-start.11 = (f32[4,48,128]{2,1,0:T(8,128)S(1)}, f32[4,48,128]{2,1,0:T(8,128)S(1)}, u32[]{:S(2)}, u32[]{:S(2)}) collective-permute-start(f32[4,48,128]{2,1,0:T(8,128)S(1)} %add.108), channel_id=1, source_target_pairs={{0,12},{1,13},{2,14},{3,15},{4,8},{5,9},{6,10},{7,11},{8,4},{9,5},... | collective-permute-start | bytes 294920 | tf_op jit(solution)/shard_map/ppermute | solution.py:458
  78.7 5.7 %collective-permute-start.21 = (f32[4,96,128]{2,1,0:T(8,128)S(1)}, f32[4,96,128]{2,1,0:T(8,128)S(1)}, u32[]{:S(2)}, u32[]{:S(2)}) collective-permute-start(f32[4,96,128]{2,1,0:T(8,128)S(1)} %pad_maximum_fusion.2), channel_id=1, source_target_pairs={{0,2},{1,3},{2,0},{3,1},{4,6},{5,7},{6,4},{7,5},{8,10},{9,11},{10,... | collective-permute-start | bytes 589832 | tf_op jit(solution)/shard_map/ppermute | solution.py:458
  84.0 2.1 %collective-permute-start.12 = (f32[4,4,48,128]{3,2,1,0:T(8,128)S(1)}, f32[4,4,48,128]{3,2,1,0:T(8,128)S(1)}, u32[]{:S(2)}, u32[]{:S(2)}) collective-permute-start(f32[4,4,48,128]{3,2,1,0:T(8,128)S(1)} %pad_maximum_fusion.mine), channel_id=1, source_target_pairs={{0,1},{1,0},{2,3},{3,2},{4,5},{5,4},{6,7},{7,6},{8,9},{9,8},{10,11... | collective-permute-start | bytes 1179656 | tf_op jit(solution)/shard_map/ppermute | solution.py:530
  84.5 3.2 %collective-permute-start.22 = (f32[4,4,48,128]{3,2,1,0:T(8,128)S(1)}, f32[4,4,48,128]{3,2,1,0:T(8,128)S(1)}, u32[]{:S(2)}, u32[]{:S(2)}) collective-permute-start(f32[4,4,48,128]{3,2,1,0:T(8,128)S(1)} %bitcast.58), channel_id=1, source_target_pairs={{0,1},{1,0},{2,3},{3,2},{4,5},{5,4},{6,7},{7,6},{8,9},{9,8},{10,11... | collective-permute-start | bytes 1179656 | tf_op jit(solution)/shard_map/ppermute | solution.py:530

commit v5 on v4

--- a/solution.py
+++ b/solution.py
@@ -19,7 +19,6 @@
 ANY = pl.BlockSpec(memory_space=pl.ANY)
 HBM = pl.BlockSpec(memory_space=pltpu.HBM)
 LIMIT = 12 * 1024 * 1024
-PACK_LIMIT = 58 * 1024 * 1024
 PAD = 8
 
 
@@ -262,13 +261,13 @@
     if first:
         tables, *refs = refs
     else:
-        ghosts_in, below_in, _, _, *refs = refs
+        ghosts_in, below_in, _, *refs = refs
     if nxt:
         _, _, e_out, h_out, mine_out, other_out, below_out, far_out, near_out, *refs = refs
         if first:
             ghosts_out, *refs = refs
     else:
-        fresh_out, mine_out, other_out, _, _, *refs = refs
+        fresh_out, mine_out, other_out, _, *refs = refs
     e, h, coefs, sem = refs
     height, width = edge_in.shape[3:]
     g = GHOST
@@ -532,6 +531,15 @@
     def f32(*shape):
         return jax.ShapeDtypeStruct(shape, jnp.float32)
 
+    def vmem(*shape):
+        return pltpu.VMEM(shape, jnp.float32)
+
+    def in_hbm(*arrays):
+        return [pltpu.with_memory_space_constraint(x, pltpu.HBM) for x in arrays]
+
+    def in_vmem(*arrays):
+        return [pltpu.with_memory_space_constraint(x, pltpu.VMEM) for x in arrays]
+
     def scratch(ghosts):
         planes = depth + 2 * ghosts
         padded = (3, planes, height + 2 * PAD, width)
@@ -547,16 +555,16 @@
     with jax.named_scope("first_pack"):
         far, near = pl.pallas_call(
             functools.partial(first_pack_kernel, d, mats, depth),
-            out_shape=[f32(size, height, width)] * 2,
+            out_shape=[vmem(size, height, width)] * 2,
             in_specs=[HBM] * 3,
             out_specs=[VMEM] * 2,
             scratch_shapes=[
                 pltpu.VMEM((2, mats, height, width), jnp.int32),
                 pltpu.SemaphoreType.DMA((copies,)),
             ],
-            compiler_params=params(PACK_LIMIT),
+            compiler_params=params(),
             cost_estimate=cost(2),
-        )(e_start, h_start, material)
+        )(*in_hbm(e_start, h_start, material))
     far, near = far.reshape(-1, width), near.reshape(-1, width)
 
     state = [f32(*e_start.shape), f32(*h_start.shape)]
@@ -569,15 +577,15 @@
         far = lax.ppermute(far, "slab", far_pairs)
         near = near_swap(near)
         if not first:
-            before = mine, other
-        samples = [f32(monitors, d, rows, width)] * 2
-        edge = f32(2, 3, 2 * d + 1, height, width)
+            before = mine + near_swap(other)
+        samples = [vmem(monitors, d, rows, width)] * 2
+        edge = vmem(2, 3, 2 * d + 1, height, width)
         with jax.named_scope(f"inner{k}"):
             kernel = functools.partial(inner_kernel, d, first, depth, monitors, rows)
             if first:
                 e, h, mine, other, edge, coefs = pl.pallas_call(
                     kernel,
-                    out_shape=state + samples + [edge, f32(2, depth, height, width)],
+                    out_shape=state + samples + [edge, vmem(2, depth, height, width)],
                     in_specs=[SMEM, SMEM, HBM, HBM, HBM],
                     out_specs=[HBM] * 2 + [VMEM] * 3 + [ANY],
                     scratch_shapes=scratch(1)
@@ -587,7 +595,7 @@
                     ],
                     compiler_params=params(),
                     cost_estimate=cost(5),
-                )(info, tables, e, h, material)
+                )(info, tables, *in_hbm(e, h, material))
             else:
                 e, h, mine, other, edge = pl.pallas_call(
                     kernel,
@@ -598,22 +606,22 @@
                     scratch_shapes=scratch(1) + [pltpu.SemaphoreType.DMA((12,))],
                     compiler_params=params(),
                     cost_estimate=cost(5),
-                )(info, e, h, coefs)
-        operands = [info, edge, coefs, mine, other, far, near]
+                )(info, *in_hbm(e, h), *in_vmem(coefs))
+        operands = [info, *in_vmem(edge, coefs, mine, other, far, near)]
         specs = [SMEM, VMEM, ANY] + [VMEM] * 4
         if first:
             operands += [tables]
             specs += [SMEM]
         else:
-            operands += [ghosts, below, *before]
-            specs += [VMEM, HBM, ANY, ANY]
-        outs = [f32(2, 3, 2 * d, height, width)] + samples
+            operands += in_vmem(ghosts, below, before)
+            specs += [VMEM, VMEM, ANY]
+        outs = [vmem(2, 3, 2 * d, height, width)] + samples
         kinds = [VMEM] * 3
         aliases = {}
         if not first:
-            aliases = {len(operands) - 2: 3, len(operands) - 1: 4}
-            outs += [f32(*before[0].shape)] * 2
-            kinds += [ANY] * 2
+            aliases = {len(operands) - 1: 3}
+            outs += [vmem(*before.shape)]
+            kinds += [ANY]
         if nxt:
             outs = state + samples
             kinds = [HBM] * 2 + [VMEM] * 2
@@ -621,10 +629,10 @@
             operands += [e, h]
             specs += [HBM] * 2
             size = message_size(nxt, 0, depth, False) * height
-            outs += [f32(3, height, width), f32(size, width), f32(size, width)]
-            kinds += [HBM]
+            outs += [vmem(3, height, width), vmem(size, width), vmem(size, width)]
+            kinds += [VMEM]
             if first:
-                outs += [f32(2, 2 * mats, height, width)]
+                outs += [vmem(2, 2 * mats, height, width)]
         with jax.named_scope(f"edge{k}"):
             results = pl.pallas_call(
                 functools.partial(edge_kernel, d, nxt, first, depth, monitors, rows),
@@ -641,9 +649,9 @@
             if first:
                 ghosts = results[7]
         else:
-            fresh, mine, other, *before = results
+            fresh, mine, other, before = results
             early = Sharing(slabs, ROWS_WHEN[k - 1])
-            part = early.scatter(before[0] + near_swap(before[1]))
+            part = early.scatter(before)
     with jax.named_scope("merge"):
         e, h = pl.pallas_call(
             functools.partial(merge_kernel, d, depth),
@@ -654,7 +662,7 @@
             scratch_shapes=[pltpu.SemaphoreType.DMA((4,))],
             compiler_params=params(),
             cost_estimate=cost(1),
-        )(e, h, fresh)
+        )(*in_hbm(e, h), *in_vmem(fresh))
     late = Sharing(slabs, ROWS_WHEN[-1])
     total = mine + near_swap(other)
     chunks = []
@@ -668,13 +676,13 @@
         with jax.named_scope(f"partial{k}"):
             sums = pl.pallas_call(
                 functools.partial(partial_kernel, d, done, monitors),
-                out_shape=f32(freqs, 2, monitors, 2, rows, width),
+                out_shape=vmem(freqs, 2, monitors, 2, rows, width),
                 grid=(freqs,),
                 in_specs=[SMEM, SMEM] + [VMEM] * 2,
                 out_specs=VMEM,
                 compiler_params=params(),
                 cost_estimate=cost(3),
-            )(info, phase_table, *chunks[k])
+            )(info, phase_table, *in_vmem(*chunks[k]))
         done += d
     with jax.named_scope("spectrum"):
         block = (2, monitors, 2, height, width)
@@ -689,7 +697,7 @@
             ],
             compiler_params=params(),
             cost_estimate=cost(4),
-        )(info, phase_table, sums, *chunks[-1])
+        )(info, phase_table, *in_vmem(sums, *chunks[-1]))
     return e, h, spectrum
 
 

time: 91.5 us -> 88.8 us (0.970)
  local copies, waits for them, and re-layouts: 1.23 us -> 0.17 us
  starting transfers between devices: 46 us -> 45 us
  other arithmetic: 1.48 us -> 0.49 us
    pallas_call x1, Pallas kernels: 5.91 us -> 7.61 us  [per_device(): pl.pallas_call(kernel, out_shape=state + samples + [edge, vmem(2, depth,...]
    unnamed x16 -> x10, local copies, waits for them, and re-layouts: 1.07 us -> 0.03 us
    add x1, other arithmetic: 1.04 us -> 0.05 us  [per_device(): total = mine + near_swap(other)]
  transfers between devices with their start and end apart: 23 -> 23, of which waited for: 7 -> 7; matrix products, arithmetic and copies ran while one was open for 2% -> 1% of each run, Pallas kernels for 17% -> 20%
where the time goes in v5:
time: 88.8 us; the launch traced here: 88.6 us
  starting transfers between devices  45 us (51%)
  Pallas kernels  31.3 us (35%)
  waiting for transfers between devices  10.6 us (12%)
  between operations  1.06 us (1%)
    ppermute x15, starting transfers between devices, swap(): lax.ppermute(block, 'slab', [(i, i ^ stride) for i in range(self.slabs)])  23.2 us
    ppermute x6, starting transfers between devices, near_swap(): return lax.ppermute(block, 'slab', near_pairs)  20.4 us
    ppermute x15, waiting for transfers between devices, swap(): lax.ppermute(block, 'slab', [(i, i ^ stride) for i in range(self.slabs)])  9.2 us
    pallas_call x2, Pallas kernels, per_device(): pl.pallas_call(functools.partial(edge_kernel, d, nxt, first, depth, monit...  7.86 us
    pallas_call x1, Pallas kernels, per_device(): pl.pallas_call(kernel, out_shape=state + samples + [edge, vmem(2, depth,...  7.61 us
    pallas_call x1, Pallas kernels, per_device(): pl.pallas_call(kernel, out_shape=state + samples + [edge], in_specs=[SMEM...  7.19 us
    pallas_call x1, Pallas kernels, per_device(): pl.pallas_call(functools.partial(spectrum_kernel, ROUNDS[-1], done, monit...  3.3 us
    pallas_call x1, Pallas kernels, per_device(): pl.pallas_call(functools.partial(first_pack_kernel, d, mats, depth), out_...  2.51 us
  transfers between devices with their start and end apart: 23, of which 7 were waited for; matrix products, arithmetic and copies ran while one was open for 1% of the time, Pallas kernels for 20%

profile of v5, /device:TPU:0, one launch (start us, length us, event | category | flops | bytes accessed | tf_op | source)
XLA Modules:
  0.0 88.6 jit_solution(16209813533059450111)
XLA Ops:
  0.6 0.0 copy-start
  0.6 0.0 copy-start.2
  0.7 0.0 copy-start.4
  0.7 2.5 %first_pack.1 = (f32[26,64,128]{2,1,0:T(8,128)}, f32[26,64,128]{2,1,0:T(8,128)S(1)}) custom-call(f32[3,16,64,128]{3,2,1,0:T(8,128)} %e_ref.1, f32[3,16,64,128]{3,2,1,0:T(8,128)} %h_ref.1, s32[16,64,128]{2,1,0:T(8,128)} %m_ref.1), custom_call_target="tpu_custom_call" | custom-call | bytes 6000000 | tf_op jit(solution)/shard_map/first_pack/pallas_call | solution.py:556
  3.2 0.7 collective-permute-start
  3.9 4.3 %collective-permute-start.1 = (f32[1664,128]{1,0:T(8,128)S(1)}, f32[1664,128]{1,0:T(8,128)S(1)}, u32[]{:S(2)}, u32[]{:S(2)}) collective-permute-start(f32[1664,128]{1,0:T(8,128)S(1)} %bitcast.60), channel_id=1, source_target_pairs={{0,1},{1,0},{2,3},{3,2},{4,5},{5,4},{6,7},{7,6},{8,9},{9,8},{10,11... | collective-permute-start | bytes 2555912 | tf_op jit(solution)/shard_map/ppermute | solution.py:529
  8.3 0.1 concatenate.6.info
  8.4 0.0 copy-done.3
  8.4 7.6 %inner0.1 = (f32[3,16,64,128]{3,2,1,0:T(8,128)}, f32[3,16,64,128]{3,2,1,0:T(8,128)}, f32[4,4,48,128]{3,2,1,0:T(8,128)S(1)}, f32[4,4,48,128]{3,2,1,0:T(8,128)S(1)...) custom-call(s32[16]{0:T(128)S(1)} %concatenate.6.info, ...), custom_call_target="tpu_custom_call" | custom-call | bytes 15000000 | tf_op jit(solution)/shard_map/inner0/pallas_call | solution.py:586
  16.0 0.0 collective-permute-done.refs_4_
  16.0 0.0 collective-permute-done.1.refs_5_
  16.0 4.4 %edge0.1 = (f32[3,16,64,128]{3,2,1,0:T(8,128)}, f32[3,16,64,128]{3,2,1,0:T(8,128)}, f32[4,4,48,128]{3,2,1,0:T(8,128)S(1)}, f32[4,4,48,128]{3,2,1,0:T(8,128)S(1)}...) custom-call(s32[16]{0:T(128)S(1)} %concatenate.6.info, ...), custom_call_target="tpu_custom_call", output_to_operand_aliasing={{0}: (8, {}), {1}: (9, {})} | custom-call | bytes 12000000 | tf_op jit(solution)/shard_map/edge0/pallas_call | solution.py:637
  20.4 0.7 collective-permute-start.2
  21.2 14.9 %collective-permute-start.3 = (f32[1280,128]{1,0:T(8,128)S(1)}, f32[1280,128]{1,0:T(8,128)S(1)}, u32[]{:S(2)}, u32[]{:S(2)}) collective-permute-start(f32[1280,128]{1,0:T(8,128)S(1)} %get-tuple-element.46), channel_id=1, source_target_pairs={{0,1},{1,0},{2,3},{3,2},{4,5},{5,4},{6,7},{7,6},{8,9},{9,8},{10,11... | collective-permute-start | bytes 1966088 | tf_op jit(solution)/shard_map/ppermute | solution.py:529
  36.0 0.1 collective-permute-start.4
  36.1 7.2 %inner1.1 = (f32[3,16,64,128]{3,2,1,0:T(8,128)}, f32[3,16,64,128]{3,2,1,0:T(8,128)}, f32[4,4,48,128]{3,2,1,0:T(8,128)S(1)}, f32[4,4,48,128]{3,2,1,0:T(8,128)S(1)}, f32[2,3,9,64,128]{4,3,2,1,0:T(8,128)S(1)}) custom-call(s32[16]{0:T(128)S(1)} %concatenate.6.info, ...), custom_call_target="tpu_custom_call", output_to_operand_aliasing={{0}: (1, {}), {1}: (2, {})} | custom-call | bytes 15000000 | tf_op jit(solution)/shard_map/inner1/pallas_call | solution.py:600
  43.3 0.0 collective-permute-done.4
  43.3 0.1 add.98.refs_8_
  43.4 0.0 collective-permute-done.2.refs_4_
  43.4 0.0 collective-permute-done.3.refs_5_
  43.4 3.4 %edge1.1 = (f32[2,3,8,64,128]{4,3,2,1,0:T(8,128)S(1)}, f32[4,4,48,128]{3,2,1,0:T(8,128)S(1)}, f32[4,4,48,128]{3,2,1,0:T(8,128)S(1)}, f32[4,4,48,128]{3,2,1,0:T(8,128)S(1)}) custom-call(s32[16]{0:T(128)S(1)} %concatenate.6.info, f32[2,3,9,64,128]{4,3,2,1,0:T(8,128)S(1)} %get-tuple-element.42.refs_0_, ...), custom_call_target="tpu_custom_call", output_to_operand_aliasing={{3}: (9, {})} | custom-call | bytes 12000000 | tf_op jit(solution)/shard_map/edge1/pallas_call | solution.py:637
  46.8 0.9 %collective-permute-start.13 = (f32[4,4,48,128]{3,2,1,0:T(8,128)S(1)}, f32[4,4,48,128]{3,2,1,0:T(8,128)S(1)}, u32[]{:S(2)}, u32[]{:S(2)}) collective-permute-start(f32[4,4,48,128]{3,2,1,0:T(8,128)S(1)} %get-tuple-element.56), channel_id=1, source_target_pairs={{0,1},{1,0},{2,3},{3,2},{4,5},{5,4},{6,7},{7,6},{8,9},{9,8},{10,11... | collective-permute-start | bytes 1179656 | tf_op jit(solution)/shard_map/ppermute | solution.py:529
  47.7 1.3 %collective-permute-done.13 = f32[4,4,48,128]{3,2,1,0:T(8,128)S(1)} collective-permute-done((f32[4,4,48,128]{3,2,1,0:T(8,128)S(1)}, f32[4,4,48,128]{3,2,1,0:T(8,128)S(1)}, u32[]{:S(2)}, u32[]{:S(2)}) %collective-permute-start.13) | collective-permute-done | bytes 393248 | tf_op jit(solution)/shard_map/ppermute | solution.py:529
  49.1 0.1 add.110
  49.2 2.1 %collective-permute-start.14 = (f32[4,96,128]{2,1,0:T(8,128)S(1)}, f32[4,96,128]{2,1,0:T(8,128)S(1)}, u32[]{:S(2)}, u32[]{:S(2)}) collective-permute-start(f32[4,96,128]{2,1,0:T(8,128)S(1)} %dynamic-slice_bitcast_fusion), channel_id=1, source_target_pairs={{0,2},{1,3},{2,0},{3,1},{4,6},{5,7},{6,4},{7,5},{8,10},{9,11},{10,... | collective-permute-start | bytes 589832 | tf_op jit(solution)/shard_map/ppermute | solution.py:457
  51.2 2.6 %collective-permute-start.5 = (f32[4,48,128]{2,1,0:T(8,128)S(1)}, f32[4,48,128]{2,1,0:T(8,128)S(1)}, u32[]{:S(2)}, u32[]{:S(2)}) collective-permute-start(f32[4,48,128]{2,1,0:T(8,128)S(1)} %get-tuple-element.59), channel_id=1, source_target_pairs={{0,8},{1,9},{2,10},{3,11},{4,12},{5,13},{6,14},{7,15},{8,0},{9,1},... | collective-permute-start | bytes 294920 | tf_op jit(solution)/shard_map/ppermute | solution.py:457
  53.9 0.0 collective-permute-start.6
  53.9 1.8 %collective-permute-start.7 = (f32[4,48,128]{2,1,0:T(8,128)S(1)}, f32[4,48,128]{2,1,0:T(8,128)S(1)}, u32[]{:S(2)}, u32[]{:S(2)}) collective-permute-start(f32[4,48,128]{2,1,0:T(8,128)S(1)} %get-tuple-element.60), channel_id=1, source_target_pairs={{0,12},{1,13},{2,14},{3,15},{4,8},{5,9},{6,10},{7,11},{8,4},{9,5},... | collective-permute-start | bytes 294920 | tf_op jit(solution)/shard_map/ppermute | solution.py:457
  55.7 0.7 collective-permute-done.14
  56.5 2.6 %collective-permute-start.15 = (f32[96,128]{1,0:T(8,128)S(1)}, f32[96,128]{1,0:T(8,128)S(1)}, u32[]{:S(2)}, u32[]{:S(2)}) collective-permute-start(f32[96,128]{1,0:T(8,128)S(1)} %get-tuple-element.62), channel_id=1, source_target_pairs={{0,8},{1,9},{2,10},{3,11},{4,12},{5,13},{6,14},{7,15},{8,0},{9,1},... | collective-permute-start | bytes 147464 | tf_op jit(solution)/shard_map/ppermute | solution.py:457
  59.1 1.6 %collective-permute-start.16 = (f32[96,128]{1,0:T(8,128)S(1)}, f32[96,128]{1,0:T(8,128)S(1)}, u32[]{:S(2)}, u32[]{:S(2)}) collective-permute-start(f32[96,128]{1,0:T(8,128)S(1)} %get-tuple-element.64), channel_id=1, source_target_pairs={{0,4},{1,5},{2,6},{3,7},{4,0},{5,1},{6,2},{7,3},{8,12},{9,13},{10,... | collective-permute-start | bytes 147464 | tf_op jit(solution)/shard_map/ppermute | solution.py:457
  60.7 0.0 collective-permute-done.5
  60.7 1.5 %collective-permute-start.17 = (f32[96,128]{1,0:T(8,128)S(1)}, f32[96,128]{1,0:T(8,128)S(1)}, u32[]{:S(2)}, u32[]{:S(2)}) collective-permute-start(f32[96,128]{1,0:T(8,128)S(1)} %get-tuple-element.63), channel_id=1, source_target_pairs={{0,12},{1,13},{2,14},{3,15},{4,8},{5,9},{6,10},{7,11},{8,4},{9,5},... | collective-permute-start | bytes 147464 | tf_op jit(solution)/shard_map/ppermute | solution.py:457
  62.2 0.0 collective-permute-done.6
  62.2 0.9 collective-permute-done.7
  63.1 0.6 collective-permute-start.8
  63.7 3.1 %collective-permute-done.15 = f32[96,128]{1,0:T(8,128)S(1)} collective-permute-done((f32[96,128]{1,0:T(8,128)S(1)}, f32[96,128]{1,0:T(8,128)S(1)}, u32[]{:S(2)}, u32[]{:S(2)}) %collective-permute-start.15) | collective-permute-done | bytes 49184 | tf_op jit(solution)/shard_map/ppermute | solution.py:457
  66.8 0.0 collective-permute-done.16
  66.8 0.0 collective-permute-done.17
  66.8 0.0 copy-start.1
  66.8 1.9 %collective-permute-start.18 = (f32[96,128]{1,0:T(8,128)S(1)}, f32[96,128]{1,0:T(8,128)S(1)}, u32[]{:S(2)}, u32[]{:S(2)}) collective-permute-start(f32[96,128]{1,0:T(8,128)S(1)} %fusion.3), channel_id=1, source_target_pairs={{0,8},{1,9},{2,10},{3,11},{4,12},{5,13},{6,14},{7,15},{8,0},{9,1},... | collective-permute-start | bytes 147464 | tf_op jit(solution)/shard_map/ppermute | solution.py:457
  68.7 0.9 %collective-permute-start.19 = (f32[96,128]{1,0:T(8,128)S(1)}, f32[96,128]{1,0:T(8,128)S(1)}, u32[]{:S(2)}, u32[]{:S(2)}) collective-permute-start(f32[96,128]{1,0:T(8,128)S(1)} %fusion.3), channel_id=1, source_target_pairs={{0,4},{1,5},{2,6},{3,7},{4,0},{5,1},{6,2},{7,3},{8,12},{9,13},{10,... | collective-permute-start | bytes 147464 | tf_op jit(solution)/shard_map/ppermute | solution.py:457
  69.6 1.7 %collective-permute-start.20 = (f32[96,128]{1,0:T(8,128)S(1)}, f32[96,128]{1,0:T(8,128)S(1)}, u32[]{:S(2)}, u32[]{:S(2)}) collective-permute-start(f32[96,128]{1,0:T(8,128)S(1)} %fusion.3), channel_id=1, source_target_pairs={{0,12},{1,13},{2,14},{3,15},{4,8},{5,9},{6,10},{7,11},{8,4},{9,5},... | collective-permute-start | bytes 147464 | tf_op jit(solution)/shard_map/ppermute | solution.py:457
  71.3 0.0 collective-permute-done.8
  71.3 1.0 %collective-permute-start.9 = (f32[4,48,128]{2,1,0:T(8,128)S(1)}, f32[4,48,128]{2,1,0:T(8,128)S(1)}, u32[]{:S(2)}, u32[]{:S(2)}) collective-permute-start(f32[4,48,128]{2,1,0:T(8,128)S(1)} %add.108), channel_id=1, source_target_pairs={{0,8},{1,9},{2,10},{3,11},{4,12},{5,13},{6,14},{7,15},{8,0},{9,1},... | collective-permute-start | bytes 294920 | tf_op jit(solution)/shard_map/ppermute | solution.py:457
  72.2 1.8 %collective-permute-start.10 = (f32[4,48,128]{2,1,0:T(8,128)S(1)}, f32[4,48,128]{2,1,0:T(8,128)S(1)}, u32[]{:S(2)}, u32[]{:S(2)}) collective-permute-start(f32[4,48,128]{2,1,0:T(8,128)S(1)} %add.108), channel_id=1, source_target_pairs={{0,4},{1,5},{2,6},{3,7},{4,0},{5,1},{6,2},{7,3},{8,12},{9,13},{10,... | collective-permute-start | bytes 294920 | tf_op jit(solution)/shard_map/ppermute | solution.py:457
  74.1 0.0 collective-permute-done.18
  74.1 1.9 %collective-permute-start.11 = (f32[4,48,128]{2,1,0:T(8,128)S(1)}, f32[4,48,128]{2,1,0:T(8,128)S(1)}, u32[]{:S(2)}, u32[]{:S(2)}) collective-permute-start(f32[4,48,128]{2,1,0:T(8,128)S(1)} %add.108), channel_id=1, source_target_pairs={{0,12},{1,13},{2,14},{3,15},{4,8},{5,9},{6,10},{7,11},{8,4},{9,5},... | collective-permute-start | bytes 294920 | tf_op jit(solution)/shard_map/ppermute | solution.py:457
  75.9 0.0 collective-permute-done.19
  75.9 0.1 collective-permute-done.20
  76.1 1.3 %collective-permute-start.21 = (f32[4,96,128]{2,1,0:T(8,128)S(1)}, f32[4,96,128]{2,1,0:T(8,128)S(1)}, u32[]{:S(2)}, u32[]{:S(2)}) collective-permute-start(f32[4,96,128]{2,1,0:T(8,128)S(1)} %pad_maximum_fusion.2), channel_id=1, source_target_pairs={{0,2},{1,3},{2,0},{3,1},{4,6},{5,7},{6,4},{7,5},{8,10},{9,11},{10,... | collective-permute-start | bytes 589832 | tf_op jit(solution)/shard_map/ppermute | solution.py:457
  77.4 4.0 %collective-permute-done.9 = f32[4,48,128]{2,1,0:T(8,128)S(1)} collective-permute-done((f32[4,48,128]{2,1,0:T(8,128)S(1)}, f32[4,48,128]{2,1,0:T(8,128)S(1)}, u32[]{:S(2)}, u32[]{:S(2)}) %collective-permute-start.9) | collective-permute-done | bytes 98336 | tf_op jit(solution)/shard_map/ppermute | solution.py:457
  81.3 0.0 collective-permute-done.10
  81.3 0.0 collective-permute-done.11
  81.4 0.1 collective-permute-start.12
  81.5 0.4 collective-permute-done.21
  81.9 0.2 collective-permute-start.22
  82.1 0.1 fusion.7
  82.2 0.1 pad_maximum_fusion.3.table
  82.3 1.2 %merge.1 = (f32[3,16,64,128]{3,2,1,0:T(8,128)}, f32[3,16,64,128]{3,2,1,0:T(8,128)}) custom-call(f32[3,16,64,128]{3,2,1,0:T(8,128)} %get-tuple-element.40.e_in, f32[3,16,64,128]{3,2,1,0:T(8,128)} %get-tuple-element.41.h_in, f32[2,3,8,64,128]{4,3,2,1,0:T(8,128)S(1)} %get-tuple-element.51.fresh), custom_call_target="tpu_custom_call", output_to_operand_aliasing={{0}: (0, {}), {1}: (1, {})} | custom-call | bytes 3000000 | tf_op jit(solution)/shard_map/merge/pallas_call | solution.py:656
  83.5 0.0 collective-permute-done.12.other
  83.5 1.6 %partial0.1.before = f32[8,2,4,2,48,128]{5,4,3,2,1,0:T(8,128)S(1)} custom-call(s32[16]{0:T(128)S(1)} %concatenate.6.info, f32[8,16]{1,0:T(8,128)S(1)} %pad_maximum_fusion.3.table, f32[4,4,48,128]{3,2,1,0:T(8,128)S(1)} %pad_maximum_fusion.mine, f32[4,4,48,128]{3,2,1,0:T(8,128)S(1)} %collective-permute-done.12.other), custom_call_target="tpu_custom_call" | custom-call | bytes 9000000 | tf_op jit(solution)/shard_map/partial0/pallas_call | solution.py:677
  85.1 0.0 collective-permute-done.22.other
  85.1 3.3 %spectrum.1 = f32[8,2,4,2,64,128]{5,4,3,2,1,0:T(8,128)} custom-call(s32[16]{0:T(128)S(1)} %concatenate.6.info, f32[8,16]{1,0:T(8,128)S(1)} %pad_maximum_fusion.3.table, f32[8,2,4,2,48,128]{5,4,3,2,1,0:T(8,128)S(1)} %partial0.1.before, f32[4,4,48,128]{3,2,1,0:T(8,128)S(1)} %bitcast.59, f32[4,4,48,128]{3,2,1,0:T(8,128)S(1)} %collective-permute-done.22.other), custom_call_target="tpu_custom_call" | custom-call | bytes 12000000 | tf_op jit(solution)/shard_map/spectrum/pallas_call | solution.py:689
  (20 shorter events, 0.3 us)
Async XLA Ops:
  0.6 7.6 %copy-start = (s32[4,2]{0,1:T(2,128)S(1)}, s32[4,2]{0,1:T(2,128)}, u32[]{:S(2)}) copy-start(s32[4,2]{0,1:T(2,128)} %param.14) | copy-start | bytes 100
  0.6 7.6 %copy-start.2 = (s32[4]{0:T(128)S(1)}, s32[4]{0:T(128)}, u32[]{:S(2)}) copy-start(s32[4]{0:T(128)} %param.13) | copy-start | bytes 52
  0.7 7.7 %copy-start.4 = (f32[4]{0:T(128)S(1)}, f32[4]{0:T(128)}, u32[]{:S(2)}) copy-start(f32[4]{0:T(128)} %param.11) | copy-start | bytes 52
  0.7 7.7 %copy-start.3 = (f32[4]{0:T(128)S(1)}, f32[4]{0:T(128)}, u32[]{:S(2)}) copy-start(f32[4]{0:T(128)} %param.12) | copy-start | bytes 52
  3.2 12.8 %collective-permute-start = (f32[1664,128]{1,0:T(8,128)}, f32[1664,128]{1,0:T(8,128)S(1)}, u32[]{:S(2)}, u32[]{:S(2)}) collective-permute-start(f32[1664,128]{1,0:T(8,128)} %bitcast.8), channel_id=1, source_target_pairs={{1,2},{2,1},{3,4},{4,3},{5,6},{6,5},{7,8},{8,7},{9,10},{10,9},{11,... | collective-permute-start | bytes 2555912 | tf_op jit(solution)/shard_map/ppermute | solution.py:577
  3.9 12.1 %collective-permute-start.1 = (f32[1664,128]{1,0:T(8,128)S(1)}, f32[1664,128]{1,0:T(8,128)S(1)}, u32[]{:S(2)}, u32[]{:S(2)}) collective-permute-start(f32[1664,128]{1,0:T(8,128)S(1)} %bitcast.60), channel_id=1, source_target_pairs={{0,1},{1,0},{2,3},{3,2},{4,5},{5,4},{6,7},{7,6},{8,9},{9,8},{10,11... | collective-permute-start | bytes 2555912 | tf_op jit(solution)/shard_map/ppermute | solution.py:529
  20.4 22.9 %collective-permute-start.2 = (f32[1280,128]{1,0:T(8,128)S(1)}, f32[1280,128]{1,0:T(8,128)S(1)}, u32[]{:S(2)}, u32[]{:S(2)}) collective-permute-start(f32[1280,128]{1,0:T(8,128)S(1)} %get-tuple-element.45), channel_id=1, source_target_pairs={{1,2},{2,1},{3,4},{4,3},{5,6},{6,5},{7,8},{8,7},{9,10},{10,9},{11,... | collective-permute-start | bytes 1966088 | tf_op jit(solution)/shard_map/ppermute | solution.py:577
  21.2 22.2 %collective-permute-start.3 = (f32[1280,128]{1,0:T(8,128)S(1)}, f32[1280,128]{1,0:T(8,128)S(1)}, u32[]{:S(2)}, u32[]{:S(2)}) collective-permute-start(f32[1280,128]{1,0:T(8,128)S(1)} %get-tuple-element.46), channel_id=1, source_target_pairs={{0,1},{1,0},{2,3},{3,2},{4,5},{5,4},{6,7},{7,6},{8,9},{9,8},{10,11... | collective-permute-start | bytes 1966088 | tf_op jit(solution)/shard_map/ppermute | solution.py:529
  36.0 7.3 %collective-permute-start.4 = (f32[4,4,48,128]{3,2,1,0:T(8,128)S(1)}, f32[4,4,48,128]{3,2,1,0:T(8,128)S(1)}, u32[]{:S(2)}, u32[]{:S(2)}) collective-permute-start(f32[4,4,48,128]{3,2,1,0:T(8,128)S(1)} %get-tuple-element.50), channel_id=1, source_target_pairs={{0,1},{1,0},{2,3},{3,2},{4,5},{5,4},{6,7},{7,6},{8,9},{9,8},{10,11... | collective-permute-start | bytes 1179656 | tf_op jit(solution)/shard_map/ppermute | solution.py:529
  46.8 2.2 %collective-permute-start.13 = (f32[4,4,48,128]{3,2,1,0:T(8,128)S(1)}, f32[4,4,48,128]{3,2,1,0:T(8,128)S(1)}, u32[]{:S(2)}, u32[]{:S(2)}) collective-permute-start(f32[4,4,48,128]{3,2,1,0:T(8,128)S(1)} %get-tuple-element.56), channel_id=1, source_target_pairs={{0,1},{1,0},{2,3},{3,2},{4,5},{5,4},{6,7},{7,6},{8,9},{9,8},{10,11... | collective-permute-start | bytes 1179656 | tf_op jit(solution)/shard_map/ppermute | solution.py:529
  49.2 7.3 %collective-permute-start.14 = (f32[4,96,128]{2,1,0:T(8,128)S(1)}, f32[4,96,128]{2,1,0:T(8,128)S(1)}, u32[]{:S(2)}, u32[]{:S(2)}) collective-permute-start(f32[4,96,128]{2,1,0:T(8,128)S(1)} %dynamic-slice_bitcast_fusion), channel_id=1, source_target_pairs={{0,2},{1,3},{2,0},{3,1},{4,6},{5,7},{6,4},{7,5},{8,10},{9,11},{10,... | collective-permute-start | bytes 589832 | tf_op jit(solution)/shard_map/ppermute | solution.py:457
  51.2 9.4 %collective-permute-start.5 = (f32[4,48,128]{2,1,0:T(8,128)S(1)}, f32[4,48,128]{2,1,0:T(8,128)S(1)}, u32[]{:S(2)}, u32[]{:S(2)}) collective-permute-start(f32[4,48,128]{2,1,0:T(8,128)S(1)} %get-tuple-element.59), channel_id=1, source_target_pairs={{0,8},{1,9},{2,10},{3,11},{4,12},{5,13},{6,14},{7,15},{8,0},{9,1},... | collective-permute-start | bytes 294920 | tf_op jit(solution)/shard_map/ppermute | solution.py:457
  53.9 8.3 %collective-permute-start.6 = (f32[4,48,128]{2,1,0:T(8,128)S(1)}, f32[4,48,128]{2,1,0:T(8,128)S(1)}, u32[]{:S(2)}, u32[]{:S(2)}) collective-permute-start(f32[4,48,128]{2,1,0:T(8,128)S(1)} %get-tuple-element.61), channel_id=1, source_target_pairs={{0,4},{1,5},{2,6},{3,7},{4,0},{5,1},{6,2},{7,3},{8,12},{9,13},{10,... | collective-permute-start | bytes 294920 | tf_op jit(solution)/shard_map/ppermute | solution.py:457
  53.9 9.2 %collective-permute-start.7 = (f32[4,48,128]{2,1,0:T(8,128)S(1)}, f32[4,48,128]{2,1,0:T(8,128)S(1)}, u32[]{:S(2)}, u32[]{:S(2)}) collective-permute-start(f32[4,48,128]{2,1,0:T(8,128)S(1)} %get-tuple-element.60), channel_id=1, source_target_pairs={{0,12},{1,13},{2,14},{3,15},{4,8},{5,9},{6,10},{7,11},{8,4},{9,5},... | collective-permute-start | bytes 294920 | tf_op jit(solution)/shard_map/ppermute | solution.py:457
  56.5 10.3 %collective-permute-start.15 = (f32[96,128]{1,0:T(8,128)S(1)}, f32[96,128]{1,0:T(8,128)S(1)}, u32[]{:S(2)}, u32[]{:S(2)}) collective-permute-start(f32[96,128]{1,0:T(8,128)S(1)} %get-tuple-element.62), channel_id=1, source_target_pairs={{0,8},{1,9},{2,10},{3,11},{4,12},{5,13},{6,14},{7,15},{8,0},{9,1},... | collective-permute-start | bytes 147464 | tf_op jit(solution)/shard_map/ppermute | solution.py:457
  59.1 7.6 %collective-permute-start.16 = (f32[96,128]{1,0:T(8,128)S(1)}, f32[96,128]{1,0:T(8,128)S(1)}, u32[]{:S(2)}, u32[]{:S(2)}) collective-permute-start(f32[96,128]{1,0:T(8,128)S(1)} %get-tuple-element.64), channel_id=1, source_target_pairs={{0,4},{1,5},{2,6},{3,7},{4,0},{5,1},{6,2},{7,3},{8,12},{9,13},{10,... | collective-permute-start | bytes 147464 | tf_op jit(solution)/shard_map/ppermute | solution.py:457
  60.7 6.1 %collective-permute-start.17 = (f32[96,128]{1,0:T(8,128)S(1)}, f32[96,128]{1,0:T(8,128)S(1)}, u32[]{:S(2)}, u32[]{:S(2)}) collective-permute-start(f32[96,128]{1,0:T(8,128)S(1)} %get-tuple-element.63), channel_id=1, source_target_pairs={{0,12},{1,13},{2,14},{3,15},{4,8},{5,9},{6,10},{7,11},{8,4},{9,5},... | collective-permute-start | bytes 147464 | tf_op jit(solution)/shard_map/ppermute | solution.py:457
  63.1 8.2 %collective-permute-start.8 = (f32[4,48,128]{2,1,0:T(8,128)S(1)}, f32[4,48,128]{2,1,0:T(8,128)S(1)}, u32[]{:S(2)}, u32[]{:S(2)}) collective-permute-start(f32[4,48,128]{2,1,0:T(8,128)S(1)} %fusion.1), channel_id=1, source_target_pairs={{0,2},{1,3},{2,0},{3,1},{4,6},{5,7},{6,4},{7,5},{8,10},{9,11},{10,... | collective-permute-start | bytes 294920 | tf_op jit(solution)/shard_map/ppermute | solution.py:457
  66.8 15.3 %copy-start.1 = (s32[8]{0:T(128)S(1)}, s32[8]{0:T(128)}, u32[]{:S(2)}) copy-start(s32[8]{0:T(128)} %param.15) | copy-start | bytes 100
  66.8 7.3 %collective-permute-start.18 = (f32[96,128]{1,0:T(8,128)S(1)}, f32[96,128]{1,0:T(8,128)S(1)}, u32[]{:S(2)}, u32[]{:S(2)}) collective-permute-start(f32[96,128]{1,0:T(8,128)S(1)} %fusion.3), channel_id=1, source_target_pairs={{0,8},{1,9},{2,10},{3,11},{4,12},{5,13},{6,14},{7,15},{8,0},{9,1},... | collective-permute-start | bytes 147464 | tf_op jit(solution)/shard_map/ppermute | solution.py:457
  68.7 7.3 %collective-permute-start.19 = (f32[96,128]{1,0:T(8,128)S(1)}, f32[96,128]{1,0:T(8,128)S(1)}, u32[]{:S(2)}, u32[]{:S(2)}) collective-permute-start(f32[96,128]{1,0:T(8,128)S(1)} %fusion.3), channel_id=1, source_target_pairs={{0,4},{1,5},{2,6},{3,7},{4,0},{5,1},{6,2},{7,3},{8,12},{9,13},{10,... | collective-permute-start | bytes 147464 | tf_op jit(solution)/shard_map/ppermute | solution.py:457
  69.6 6.5 %collective-permute-start.20 = (f32[96,128]{1,0:T(8,128)S(1)}, f32[96,128]{1,0:T(8,128)S(1)}, u32[]{:S(2)}, u32[]{:S(2)}) collective-permute-start(f32[96,128]{1,0:T(8,128)S(1)} %fusion.3), channel_id=1, source_target_pairs={{0,12},{1,13},{2,14},{3,15},{4,8},{5,9},{6,10},{7,11},{8,4},{9,5},... | collective-permute-start | bytes 147464 | tf_op jit(solution)/shard_map/ppermute | solution.py:457
  71.3 10.1 %collective-permute-start.9 = (f32[4,48,128]{2,1,0:T(8,128)S(1)}, f32[4,48,128]{2,1,0:T(8,128)S(1)}, u32[]{:S(2)}, u32[]{:S(2)}) collective-permute-start(f32[4,48,128]{2,1,0:T(8,128)S(1)} %add.108), channel_id=1, source_target_pairs={{0,8},{1,9},{2,10},{3,11},{4,12},{5,13},{6,14},{7,15},{8,0},{9,1},... | collective-permute-start | bytes 294920 | tf_op jit(solution)/shard_map/ppermute | solution.py:457
  72.2 9.1 %collective-permute-start.10 = (f32[4,48,128]{2,1,0:T(8,128)S(1)}, f32[4,48,128]{2,1,0:T(8,128)S(1)}, u32[]{:S(2)}, u32[]{:S(2)}) collective-permute-start(f32[4,48,128]{2,1,0:T(8,128)S(1)} %add.108), channel_id=1, source_target_pairs={{0,4},{1,5},{2,6},{3,7},{4,0},{5,1},{6,2},{7,3},{8,12},{9,13},{10,... | collective-permute-start | bytes 294920 | tf_op jit(solution)/shard_map/ppermute | solution.py:457
  74.1 7.3 %collective-permute-start.11 = (f32[4,48,128]{2,1,0:T(8,128)S(1)}, f32[4,48,128]{2,1,0:T(8,128)S(1)}, u32[]{:S(2)}, u32[]{:S(2)}) collective-permute-start(f32[4,48,128]{2,1,0:T(8,128)S(1)} %add.108), channel_id=1, source_target_pairs={{0,12},{1,13},{2,14},{3,15},{4,8},{5,9},{6,10},{7,11},{8,4},{9,5},... | collective-permute-start | bytes 294920 | tf_op jit(solution)/shard_map/ppermute | solution.py:457
  76.1 5.7 %collective-permute-start.21 = (f32[4,96,128]{2,1,0:T(8,128)S(1)}, f32[4,96,128]{2,1,0:T(8,128)S(1)}, u32[]{:S(2)}, u32[]{:S(2)}) collective-permute-start(f32[4,96,128]{2,1,0:T(8,128)S(1)} %pad_maximum_fusion.2), channel_id=1, source_target_pairs={{0,2},{1,3},{2,0},{3,1},{4,6},{5,7},{6,4},{7,5},{8,10},{9,11},{10,... | collective-permute-start | bytes 589832 | tf_op jit(solution)/shard_map/ppermute | solution.py:457
  81.4 2.1 %collective-permute-start.12 = (f32[4,4,48,128]{3,2,1,0:T(8,128)S(1)}, f32[4,4,48,128]{3,2,1,0:T(8,128)S(1)}, u32[]{:S(2)}, u32[]{:S(2)}) collective-permute-start(f32[4,4,48,128]{3,2,1,0:T(8,128)S(1)} %pad_maximum_fusion.mine), channel_id=1, source_target_pairs={{0,1},{1,0},{2,3},{3,2},{4,5},{5,4},{6,7},{7,6},{8,9},{9,8},{10,11... | collective-permute-start | bytes 1179656 | tf_op jit(solution)/shard_map/ppermute | solution.py:529
  81.9 3.2 %collective-permute-start.22 = (f32[4,4,48,128]{3,2,1,0:T(8,128)S(1)}, f32[4,4,48,128]{3,2,1,0:T(8,128)S(1)}, u32[]{:S(2)}, u32[]{:S(2)}) collective-permute-start(f32[4,4,48,128]{3,2,1,0:T(8,128)S(1)} %bitcast.58), channel_id=1, source_target_pairs={{0,1},{1,0},{2,3},{3,2},{4,5},{5,4},{6,7},{7,6},{8,9},{9,8},{10,11... | collective-permute-start | bytes 1179656 | tf_op jit(solution)/shard_map/ppermute | solution.py:529

commit v6 on v5

--- a/solution.py
+++ b/solution.py
@@ -391,57 +391,47 @@
         copy.wait()
 
 
-def merge_kernel(d, depth, e_in, h_in, fresh, e_out, h_out, sem):
-    moves = []
-    for k, x_out in enumerate((e_out, h_out)):
-        for j, plane in enumerate((0, depth - d)):
-            moves.append((fresh.at[k, :, pl.ds(j * d, d)], x_out.at[:, pl.ds(plane, d)]))
-    for copy in start_all(moves, sem):
-        copy.wait()
-
-
-def partial_kernel(d, at_step, monitors, info, table, mine, other, out):
-    f = pl.program_id(0)
-    steps = table.shape[1] // 2
-    for m in range(monitors):
-        at = jnp.bitwise_xor(m, info[3])
-        for side, samples in enumerate((mine, other)):
-            planes = [samples[at, t] for t in range(d)]
-            for part in range(2):
-                total = planes[0] * table[f, part * steps + at_step]
-                for t in range(1, d):
-                    total = total + planes[t] * table[f, part * steps + at_step + t]
-                out[f, part, m, side] = total
-
-
-def spectrum_kernel(
-    d, at_step, monitors, freqs, info, table, before, mine, other, out, blocks, sem
-):
-    rows, width = mine.shape[2:]
-    height = blocks.shape[4]
-    steps = table.shape[1] // 2
-    pad = jnp.zeros((height - rows, width), jnp.float32)
+def spectrum_kernel(side, chunks, monitors, freqs, info, table, *refs):
+    samples, (blocks, sem) = refs[: len(chunks)], refs[-2:]
+    if side == 0:
+        fresh, _, _, out, *state = refs[len(chunks) : -2]
+        edge = fresh.shape[2] // 2
+        moves = []
+        for k, x_out in enumerate(state):
+            for j, plane in enumerate((0, x_out.shape[1] - edge)):
+                moves.append(
+                    (fresh.at[k, :, pl.ds(j * edge, edge)], x_out.at[:, pl.ds(plane, edge)])
+                )
+        copies = start_all(moves, sem)
+    else:
+        out = refs[-3]
+        copies = []
+    rows, width = samples[0].shape[2:]
+    steps = sum(chunks)
+    blocks[...] = jnp.zeros(blocks.shape, jnp.float32)
+    c = info[0] if side == 0 else 1 - info[0]
+
+    def copy(f):
+        return pltpu.make_async_copy(blocks.at[f], out.at[f, :, :, c], sem.at[4 + f])
 
     def body(f, _):
         for m in range(monitors):
             start = monitor_info(info, m, monitors)[1]
             at = jnp.bitwise_xor(m, info[3])
-            for side, samples in enumerate((mine, other)):
-                c = info[0] if side == 0 else 1 - info[0]
-                planes = [samples[at, t] for t in range(d)]
-                for part in range(2):
-                    total = before[f, part, m, side]
-                    for t in range(d):
-                        total = total + planes[t] * table[f, part * steps + at_step + t]
-                    blocks[f, part, m, c] = pltpu.roll(
-                        jnp.concatenate([total, pad], 0), start, 0
-                    )
-        pltpu.make_async_copy(blocks.at[f], out.at[f], sem.at[f]).start()
+            planes = [chunk[at, t] for chunk, d in zip(samples, chunks) for t in range(d)]
+            for part in range(2):
+                total = planes[0] * table[f, part * steps]
+                for t in range(1, steps):
+                    total = total + planes[t] * table[f, part * steps + t]
+                blocks[f, part, m, pl.ds(start, rows)] = total
+        copy(f).start()
         return 0
 
     lax.fori_loop(0, freqs, body, 0)
     for f in range(freqs):
-        pltpu.make_async_copy(blocks.at[f], out.at[f], sem.at[f]).wait()
+        copy(f).wait()
+    for move in copies:
+        move.wait()
 
 
 class Sharing:
@@ -652,52 +642,39 @@
             fresh, mine, other, before = results
             early = Sharing(slabs, ROWS_WHEN[k - 1])
             part = early.scatter(before)
-    with jax.named_scope("merge"):
-        e, h = pl.pallas_call(
-            functools.partial(merge_kernel, d, depth),
-            out_shape=state,
-            in_specs=[ANY, ANY, VMEM],
-            out_specs=[ANY, ANY],
-            input_output_aliases={0: 0, 1: 1},
-            scratch_shapes=[pltpu.SemaphoreType.DMA((4,))],
-            compiler_params=params(),
-            cost_estimate=cost(1),
-        )(*in_hbm(e, h), *in_vmem(fresh))
     late = Sharing(slabs, ROWS_WHEN[-1])
     total = mine + near_swap(other)
-    chunks = []
+    sums = []
     for sharing, block in ((early, part), (late, late.scatter(total))):
-        block = sharing.gather(block, total.shape)
-        chunks.append((block, near_swap(block)))
-
-    done = 0
-    sums = None
-    for k, d in enumerate(ROUNDS[:-1]):
-        with jax.named_scope(f"partial{k}"):
-            sums = pl.pallas_call(
-                functools.partial(partial_kernel, d, done, monitors),
-                out_shape=vmem(freqs, 2, monitors, 2, rows, width),
-                grid=(freqs,),
-                in_specs=[SMEM, SMEM] + [VMEM] * 2,
-                out_specs=VMEM,
+        sums.append(sharing.gather(block, total.shape))
+    spectrum = []
+    for side, chunks in enumerate((sums, [near_swap(block) for block in sums])):
+        operands = [info, phase_table, *in_vmem(*chunks)]
+        if side == 0:
+            operands += in_vmem(fresh) + in_hbm(e, h)
+        else:
+            operands += in_hbm(*spectrum)
+        last = len(operands)
+        with jax.named_scope(f"spectrum{side}"):
+            results = pl.pallas_call(
+                functools.partial(spectrum_kernel, side, ROUNDS, monitors, freqs),
+                out_shape=[f32(freqs, 2, monitors, 2, height, width)] + state * (1 - side),
+                in_specs=[SMEM, SMEM]
+                + [VMEM] * (len(chunks) + 1 - side)
+                + [HBM] * (2 - side),
+                out_specs=[HBM] * (3 - 2 * side),
+                input_output_aliases={last - 1: 0} if side else {last - 2: 1, last - 1: 2},
+                scratch_shapes=[
+                    pltpu.VMEM((freqs, 2, monitors, height, width), jnp.float32),
+                    pltpu.SemaphoreType.DMA((4 + freqs,)),
+                ],
                 compiler_params=params(),
-                cost_estimate=cost(3),
-            )(info, phase_table, *in_vmem(*chunks[k]))
-        done += d
-    with jax.named_scope("spectrum"):
-        block = (2, monitors, 2, height, width)
-        spectrum = pl.pallas_call(
-            functools.partial(spectrum_kernel, ROUNDS[-1], done, monitors, freqs),
-            out_shape=f32(freqs, *block),
-            in_specs=[SMEM, SMEM] + [VMEM] * 3,
-            out_specs=HBM,
-            scratch_shapes=[
-                pltpu.VMEM((freqs, *block), jnp.float32),
-                pltpu.SemaphoreType.DMA((freqs,)),
-            ],
-            compiler_params=params(),
-            cost_estimate=cost(4),
-        )(info, phase_table, *in_vmem(sums, *chunks[-1]))
+                cost_estimate=cost(2),
+            )(*operands)
+        spectrum = results[:1]
+        if side == 0:
+            e, h = results[1:]
+    (spectrum,) = spectrum
     return e, h, spectrum
 
 

time: 88.8 us -> 87.8 us (0.989)
  Pallas kernels: 31.3 us -> 30.3 us
    pallas_call x3 -> x2, Pallas kernels: 6.09 us -> 5.1 us  [per_device(): pl.pallas_call(functools.partial(spectrum_kernel, side, ROUNDS, monitors,...]
where the time goes in v6:
time: 87.8 us; the launch traced here: 87.6 us
  starting transfers between devices  44.9 us (51%)
  Pallas kernels  30.3 us (35%)
  waiting for transfers between devices  10.7 us (12%)
  between operations  1.05 us (1%)
    ppermute x15, starting transfers between devices, swap(): lax.ppermute(block, 'slab', [(i, i ^ stride) for i in range(self.slabs)])  23.2 us
    ppermute x6, starting transfers between devices, near_swap(): return lax.ppermute(block, 'slab', near_pairs)  20.4 us
    ppermute x15, waiting for transfers between devices, swap(): lax.ppermute(block, 'slab', [(i, i ^ stride) for i in range(self.slabs)])  9.28 us
    pallas_call x2, Pallas kernels, per_device(): pl.pallas_call(functools.partial(edge_kernel, d, nxt, first, depth, monit...  7.86 us
    pallas_call x1, Pallas kernels, per_device(): pl.pallas_call(kernel, out_shape=state + samples + [edge, vmem(2, depth,...  7.61 us
    pallas_call x1, Pallas kernels, per_device(): pl.pallas_call(kernel, out_shape=state + samples + [edge], in_specs=[SMEM...  7.19 us
    pallas_call x2, Pallas kernels, per_device(): pl.pallas_call(functools.partial(spectrum_kernel, side, ROUNDS, monitors,...  5.1 us
    pallas_call x1, Pallas kernels, per_device(): pl.pallas_call(functools.partial(first_pack_kernel, d, mats, depth), out_...  2.51 us
  transfers between devices with their start and end apart: 23, of which 7 were waited for; matrix products, arithmetic and copies ran while one was open for 1% of the time, Pallas kernels for 20%

profile of v6, /device:TPU:0, one launch (start us, length us, event | category | flops | bytes accessed | tf_op | source)
XLA Modules:
  0.0 87.6 jit_solution(17467871508441282456)
XLA Ops:
  0.6 0.0 copy-start
  0.6 0.0 copy-start.2
  0.7 0.0 copy-start.4
  0.7 0.0 copy-start.3
  0.7 2.5 %first_pack.1 = (f32[26,64,128]{2,1,0:T(8,128)}, f32[26,64,128]{2,1,0:T(8,128)S(1)}) custom-call(f32[3,16,64,128]{3,2,1,0:T(8,128)} %e_ref.1, f32[3,16,64,128]{3,2,1,0:T(8,128)} %h_ref.1, s32[16,64,128]{2,1,0:T(8,128)} %m_ref.1), custom_call_target="tpu_custom_call" | custom-call | bytes 6000000 | tf_op jit(solution)/shard_map/first_pack/pallas_call | solution.py:546
  3.2 0.7 collective-permute-start
  3.9 4.3 %collective-permute-start.1 = (f32[1664,128]{1,0:T(8,128)S(1)}, f32[1664,128]{1,0:T(8,128)S(1)}, u32[]{:S(2)}, u32[]{:S(2)}) collective-permute-start(f32[1664,128]{1,0:T(8,128)S(1)} %bitcast.60), channel_id=1, source_target_pairs={{0,1},{1,0},{2,3},{3,2},{4,5},{5,4},{6,7},{7,6},{8,9},{9,8},{10,11... | collective-permute-start | bytes 2555912 | tf_op jit(solution)/shard_map/ppermute | solution.py:519
  8.3 0.1 concatenate.6.info
  8.4 0.0 copy-done.3
  8.4 7.6 %inner0.1 = (f32[3,16,64,128]{3,2,1,0:T(8,128)}, f32[3,16,64,128]{3,2,1,0:T(8,128)}, f32[4,4,48,128]{3,2,1,0:T(8,128)S(1)}, f32[4,4,48,128]{3,2,1,0:T(8,128)S(1)...) custom-call(s32[16]{0:T(128)S(1)} %concatenate.6.info, ...), custom_call_target="tpu_custom_call" | custom-call | bytes 15000000 | tf_op jit(solution)/shard_map/inner0/pallas_call | solution.py:576
  16.0 0.0 collective-permute-done.refs_4_
  16.0 0.0 collective-permute-done.1.refs_5_
  16.0 4.4 %edge0.1 = (f32[3,16,64,128]{3,2,1,0:T(8,128)}, f32[3,16,64,128]{3,2,1,0:T(8,128)}, f32[4,4,48,128]{3,2,1,0:T(8,128)S(1)}, f32[4,4,48,128]{3,2,1,0:T(8,128)S(1)}...) custom-call(s32[16]{0:T(128)S(1)} %concatenate.6.info, ...), custom_call_target="tpu_custom_call", output_to_operand_aliasing={{0}: (8, {}), {1}: (9, {})} | custom-call | bytes 12000000 | tf_op jit(solution)/shard_map/edge0/pallas_call | solution.py:627
  20.4 0.7 collective-permute-start.2
  21.2 14.9 %collective-permute-start.3 = (f32[1280,128]{1,0:T(8,128)S(1)}, f32[1280,128]{1,0:T(8,128)S(1)}, u32[]{:S(2)}, u32[]{:S(2)}) collective-permute-start(f32[1280,128]{1,0:T(8,128)S(1)} %get-tuple-element.45), channel_id=1, source_target_pairs={{0,1},{1,0},{2,3},{3,2},{4,5},{5,4},{6,7},{7,6},{8,9},{9,8},{10,11... | collective-permute-start | bytes 1966088 | tf_op jit(solution)/shard_map/ppermute | solution.py:519
  36.0 0.1 collective-permute-start.4
  36.1 7.2 %inner1.1 = (f32[3,16,64,128]{3,2,1,0:T(8,128)}, f32[3,16,64,128]{3,2,1,0:T(8,128)}, f32[4,4,48,128]{3,2,1,0:T(8,128)S(1)}, f32[4,4,48,128]{3,2,1,0:T(8,128)S(1)}, f32[2,3,9,64,128]{4,3,2,1,0:T(8,128)S(1)}) custom-call(s32[16]{0:T(128)S(1)} %concatenate.6.info, ...), custom_call_target="tpu_custom_call", output_to_operand_aliasing={{0}: (1, {}), {1}: (2, {})} | custom-call | bytes 15000000 | tf_op jit(solution)/shard_map/inner1/pallas_call | solution.py:590
  43.3 0.0 collective-permute-done.4
  43.3 0.1 add.100.refs_8_
  43.4 0.0 collective-permute-done.2.refs_4_
  43.4 0.0 collective-permute-done.3.refs_5_
  43.4 3.4 %edge1.1 = (f32[2,3,8,64,128]{4,3,2,1,0:T(8,128)S(1)}, f32[4,4,48,128]{3,2,1,0:T(8,128)S(1)}, f32[4,4,48,128]{3,2,1,0:T(8,128)S(1)}, f32[4,4,48,128]{3,2,1,0:T(8,128)S(1)}) custom-call(s32[16]{0:T(128)S(1)} %concatenate.6.info, f32[2,3,9,64,128]{4,3,2,1,0:T(8,128)S(1)} %get-tuple-element.41.refs_0_, ...), custom_call_target="tpu_custom_call", output_to_operand_aliasing={{3}: (9, {})} | custom-call | bytes 12000000 | tf_op jit(solution)/shard_map/edge1/pallas_call | solution.py:627
  46.8 0.9 %collective-permute-start.12 = (f32[4,4,48,128]{3,2,1,0:T(8,128)S(1)}, f32[4,4,48,128]{3,2,1,0:T(8,128)S(1)}, u32[]{:S(2)}, u32[]{:S(2)}) collective-permute-start(f32[4,4,48,128]{3,2,1,0:T(8,128)S(1)} %get-tuple-element.52), channel_id=1, source_target_pairs={{0,1},{1,0},{2,3},{3,2},{4,5},{5,4},{6,7},{7,6},{8,9},{9,8},{10,11... | collective-permute-start | bytes 1179656 | tf_op jit(solution)/shard_map/ppermute | solution.py:519
  47.7 1.3 %collective-permute-done.12 = f32[4,4,48,128]{3,2,1,0:T(8,128)S(1)} collective-permute-done((f32[4,4,48,128]{3,2,1,0:T(8,128)S(1)}, f32[4,4,48,128]{3,2,1,0:T(8,128)S(1)}, u32[]{:S(2)}, u32[]{:S(2)}) %collective-permute-start.12) | collective-permute-done | bytes 393248 | tf_op jit(solution)/shard_map/ppermute | solution.py:519
  49.1 0.1 add.110
  49.2 2.1 %collective-permute-start.13 = (f32[4,96,128]{2,1,0:T(8,128)S(1)}, f32[4,96,128]{2,1,0:T(8,128)S(1)}, u32[]{:S(2)}, u32[]{:S(2)}) collective-permute-start(f32[4,96,128]{2,1,0:T(8,128)S(1)} %dynamic-slice_bitcast_fusion), channel_id=1, source_target_pairs={{0,2},{1,3},{2,0},{3,1},{4,6},{5,7},{6,4},{7,5},{8,10},{9,11},{10,... | collective-permute-start | bytes 589832 | tf_op jit(solution)/shard_map/ppermute | solution.py:447
  51.2 2.6 %collective-permute-start.5 = (f32[4,48,128]{2,1,0:T(8,128)S(1)}, f32[4,48,128]{2,1,0:T(8,128)S(1)}, u32[]{:S(2)}, u32[]{:S(2)}) collective-permute-start(f32[4,48,128]{2,1,0:T(8,128)S(1)} %get-tuple-element.61), channel_id=1, source_target_pairs={{0,8},{1,9},{2,10},{3,11},{4,12},{5,13},{6,14},{7,15},{8,0},{9,1},... | collective-permute-start | bytes 294920 | tf_op jit(solution)/shard_map/ppermute | solution.py:447
  53.9 0.0 collective-permute-start.6
  53.9 1.8 %collective-permute-start.7 = (f32[4,48,128]{2,1,0:T(8,128)S(1)}, f32[4,48,128]{2,1,0:T(8,128)S(1)}, u32[]{:S(2)}, u32[]{:S(2)}) collective-permute-start(f32[4,48,128]{2,1,0:T(8,128)S(1)} %get-tuple-element.62), channel_id=1, source_target_pairs={{0,12},{1,13},{2,14},{3,15},{4,8},{5,9},{6,10},{7,11},{8,4},{9,5},... | collective-permute-start | bytes 294920 | tf_op jit(solution)/shard_map/ppermute | solution.py:447
  55.7 0.7 collective-permute-done.13
  56.5 2.6 %collective-permute-start.14 = (f32[96,128]{1,0:T(8,128)S(1)}, f32[96,128]{1,0:T(8,128)S(1)}, u32[]{:S(2)}, u32[]{:S(2)}) collective-permute-start(f32[96,128]{1,0:T(8,128)S(1)} %get-tuple-element.64), channel_id=1, source_target_pairs={{0,8},{1,9},{2,10},{3,11},{4,12},{5,13},{6,14},{7,15},{8,0},{9,1},... | collective-permute-start | bytes 147464 | tf_op jit(solution)/shard_map/ppermute | solution.py:447
  59.1 1.6 %collective-permute-start.15 = (f32[96,128]{1,0:T(8,128)S(1)}, f32[96,128]{1,0:T(8,128)S(1)}, u32[]{:S(2)}, u32[]{:S(2)}) collective-permute-start(f32[96,128]{1,0:T(8,128)S(1)} %get-tuple-element.66), channel_id=1, source_target_pairs={{0,4},{1,5},{2,6},{3,7},{4,0},{5,1},{6,2},{7,3},{8,12},{9,13},{10,... | collective-permute-start | bytes 147464 | tf_op jit(solution)/shard_map/ppermute | solution.py:447
  60.7 0.0 collective-permute-done.5
  60.7 1.5 %collective-permute-start.16 = (f32[96,128]{1,0:T(8,128)S(1)}, f32[96,128]{1,0:T(8,128)S(1)}, u32[]{:S(2)}, u32[]{:S(2)}) collective-permute-start(f32[96,128]{1,0:T(8,128)S(1)} %get-tuple-element.65), channel_id=1, source_target_pairs={{0,12},{1,13},{2,14},{3,15},{4,8},{5,9},{6,10},{7,11},{8,4},{9,5},... | collective-permute-start | bytes 147464 | tf_op jit(solution)/shard_map/ppermute | solution.py:447
  62.2 0.0 collective-permute-done.6
  62.2 0.9 collective-permute-done.7
  63.1 0.6 collective-permute-start.8
  63.7 3.1 %collective-permute-done.14 = f32[96,128]{1,0:T(8,128)S(1)} collective-permute-done((f32[96,128]{1,0:T(8,128)S(1)}, f32[96,128]{1,0:T(8,128)S(1)}, u32[]{:S(2)}, u32[]{:S(2)}) %collective-permute-start.14) | collective-permute-done | bytes 49184 | tf_op jit(solution)/shard_map/ppermute | solution.py:447
  66.8 0.0 collective-permute-done.15
  66.8 0.0 collective-permute-done.16
  66.8 0.0 copy-start.1
  66.8 1.9 %collective-permute-start.17 = (f32[96,128]{1,0:T(8,128)S(1)}, f32[96,128]{1,0:T(8,128)S(1)}, u32[]{:S(2)}, u32[]{:S(2)}) collective-permute-start(f32[96,128]{1,0:T(8,128)S(1)} %fusion.3), channel_id=1, source_target_pairs={{0,8},{1,9},{2,10},{3,11},{4,12},{5,13},{6,14},{7,15},{8,0},{9,1},... | collective-permute-start | bytes 147464 | tf_op jit(solution)/shard_map/ppermute | solution.py:447
  68.7 0.9 %collective-permute-start.18 = (f32[96,128]{1,0:T(8,128)S(1)}, f32[96,128]{1,0:T(8,128)S(1)}, u32[]{:S(2)}, u32[]{:S(2)}) collective-permute-start(f32[96,128]{1,0:T(8,128)S(1)} %fusion.3), channel_id=1, source_target_pairs={{0,4},{1,5},{2,6},{3,7},{4,0},{5,1},{6,2},{7,3},{8,12},{9,13},{10,... | collective-permute-start | bytes 147464 | tf_op jit(solution)/shard_map/ppermute | solution.py:447
  69.6 1.7 %collective-permute-start.19 = (f32[96,128]{1,0:T(8,128)S(1)}, f32[96,128]{1,0:T(8,128)S(1)}, u32[]{:S(2)}, u32[]{:S(2)}) collective-permute-start(f32[96,128]{1,0:T(8,128)S(1)} %fusion.3), channel_id=1, source_target_pairs={{0,12},{1,13},{2,14},{3,15},{4,8},{5,9},{6,10},{7,11},{8,4},{9,5},... | collective-permute-start | bytes 147464 | tf_op jit(solution)/shard_map/ppermute | solution.py:447
  71.3 0.0 collective-permute-done.8
  71.3 1.0 %collective-permute-start.9 = (f32[4,48,128]{2,1,0:T(8,128)S(1)}, f32[4,48,128]{2,1,0:T(8,128)S(1)}, u32[]{:S(2)}, u32[]{:S(2)}) collective-permute-start(f32[4,48,128]{2,1,0:T(8,128)S(1)} %add.108), channel_id=1, source_target_pairs={{0,8},{1,9},{2,10},{3,11},{4,12},{5,13},{6,14},{7,15},{8,0},{9,1},... | collective-permute-start | bytes 294920 | tf_op jit(solution)/shard_map/ppermute | solution.py:447
  72.2 1.8 %collective-permute-start.10 = (f32[4,48,128]{2,1,0:T(8,128)S(1)}, f32[4,48,128]{2,1,0:T(8,128)S(1)}, u32[]{:S(2)}, u32[]{:S(2)}) collective-permute-start(f32[4,48,128]{2,1,0:T(8,128)S(1)} %add.108), channel_id=1, source_target_pairs={{0,4},{1,5},{2,6},{3,7},{4,0},{5,1},{6,2},{7,3},{8,12},{9,13},{10,... | collective-permute-start | bytes 294920 | tf_op jit(solution)/shard_map/ppermute | solution.py:447
  74.1 0.0 collective-permute-done.17
  74.1 1.9 %collective-permute-start.11 = (f32[4,48,128]{2,1,0:T(8,128)S(1)}, f32[4,48,128]{2,1,0:T(8,128)S(1)}, u32[]{:S(2)}, u32[]{:S(2)}) collective-permute-start(f32[4,48,128]{2,1,0:T(8,128)S(1)} %add.108), channel_id=1, source_target_pairs={{0,12},{1,13},{2,14},{3,15},{4,8},{5,9},{6,10},{7,11},{8,4},{9,5},... | collective-permute-start | bytes 294920 | tf_op jit(solution)/shard_map/ppermute | solution.py:447
  75.9 0.0 collective-permute-done.18
  76.0 0.2 collective-permute-done.19
  76.2 1.2 %collective-permute-start.20 = (f32[4,96,128]{2,1,0:T(8,128)S(1)}, f32[4,96,128]{2,1,0:T(8,128)S(1)}, u32[]{:S(2)}, u32[]{:S(2)}) collective-permute-start(f32[4,96,128]{2,1,0:T(8,128)S(1)} %pad_maximum_fusion.2), channel_id=1, source_target_pairs={{0,2},{1,3},{2,0},{3,1},{4,6},{5,7},{6,4},{7,5},{8,10},{9,11},{10,... | collective-permute-start | bytes 589832 | tf_op jit(solution)/shard_map/ppermute | solution.py:447
  77.4 4.0 %collective-permute-done.9 = f32[4,48,128]{2,1,0:T(8,128)S(1)} collective-permute-done((f32[4,48,128]{2,1,0:T(8,128)S(1)}, f32[4,48,128]{2,1,0:T(8,128)S(1)}, u32[]{:S(2)}, u32[]{:S(2)}) %collective-permute-start.9) | collective-permute-done | bytes 98336 | tf_op jit(solution)/shard_map/ppermute | solution.py:447
  81.3 0.0 collective-permute-done.10
  81.3 0.0 collective-permute-done.11
  81.4 0.1 collective-permute-start.21
  81.5 0.4 collective-permute-done.20
  82.0 0.1 collective-permute-start.22
  82.1 0.1 fusion.7
  82.2 0.1 pad_maximum_fusion.3.table
  82.3 2.6 %spectrum0.1 = (f32[8,2,4,2,64,128]{5,4,3,2,1,0:T(8,128)}, f32[3,16,64,128]{3,2,1,0:T(8,128)}, f32[3,16,64,128]{3,2,1,0:T(8,128)}) custom-call(s32[16]{0:T(128)S(1)} %concatenate.6.info, f32[8,16]{1,0:T(8,128)S(1)} %pad_maximum_fusion.3.table, f32[4,4,48,128]{3,2,1,0:T(8,128)S(1)} %pad_maximum_fusion.refs_0_, ...), custom_call_target="tpu_custom_call", output_to_operand_aliasing={{1}: (5, {}), {2}: (6, {})} | custom-call | bytes 6000000 | tf_op jit(solution)/shard_map/spectrum0/pallas_call | solution.py:659
  84.9 0.0 collective-permute-done.21.refs_0_
  84.9 0.0 collective-permute-done.22.refs_1_
  84.9 2.5 %spectrum1.1 = f32[8,2,4,2,64,128]{5,4,3,2,1,0:T(8,128)} custom-call(s32[16]{0:T(128)S(1)} %concatenate.6.info, f32[8,16]{1,0:T(8,128)S(1)} %pad_maximum_fusion.3.table, f32[4,4,48,128]{3,2,1,0:T(8,128)S(1)} %collective-permute-done.21.refs_0_, f32[4,4,48,128]{3,2,1,0:T(8,128)S(1)} %collective-permute-done.22.refs_1_, ...), custom_call_target="tpu_custom_call", output_to_operand_aliasing={{}: (4, {})} | custom-call | bytes 6000000 | tf_op jit(solution)/shard_map/spectrum1/pallas_call | solution.py:659
  (19 shorter events, 0.3 us)
Async XLA Ops:
  0.6 7.6 %copy-start = (s32[4,2]{0,1:T(2,128)S(1)}, s32[4,2]{0,1:T(2,128)}, u32[]{:S(2)}) copy-start(s32[4,2]{0,1:T(2,128)} %param.14) | copy-start | bytes 100
  0.6 7.6 %copy-start.2 = (s32[4]{0:T(128)S(1)}, s32[4]{0:T(128)}, u32[]{:S(2)}) copy-start(s32[4]{0:T(128)} %param.13) | copy-start | bytes 52
  0.7 7.7 %copy-start.4 = (f32[4]{0:T(128)S(1)}, f32[4]{0:T(128)}, u32[]{:S(2)}) copy-start(f32[4]{0:T(128)} %param.11) | copy-start | bytes 52
  0.7 7.7 %copy-start.3 = (f32[4]{0:T(128)S(1)}, f32[4]{0:T(128)}, u32[]{:S(2)}) copy-start(f32[4]{0:T(128)} %param.12) | copy-start | bytes 52
  3.2 12.8 %collective-permute-start = (f32[1664,128]{1,0:T(8,128)}, f32[1664,128]{1,0:T(8,128)S(1)}, u32[]{:S(2)}, u32[]{:S(2)}) collective-permute-start(f32[1664,128]{1,0:T(8,128)} %bitcast.8), channel_id=1, source_target_pairs={{1,2},{2,1},{3,4},{4,3},{5,6},{6,5},{7,8},{8,7},{9,10},{10,9},{11,... | collective-permute-start | bytes 2555912 | tf_op jit(solution)/shard_map/ppermute | solution.py:567
  3.9 12.1 %collective-permute-start.1 = (f32[1664,128]{1,0:T(8,128)S(1)}, f32[1664,128]{1,0:T(8,128)S(1)}, u32[]{:S(2)}, u32[]{:S(2)}) collective-permute-start(f32[1664,128]{1,0:T(8,128)S(1)} %bitcast.60), channel_id=1, source_target_pairs={{0,1},{1,0},{2,3},{3,2},{4,5},{5,4},{6,7},{7,6},{8,9},{9,8},{10,11... | collective-permute-start | bytes 2555912 | tf_op jit(solution)/shard_map/ppermute | solution.py:519
  20.4 22.9 %collective-permute-start.2 = (f32[1280,128]{1,0:T(8,128)S(1)}, f32[1280,128]{1,0:T(8,128)S(1)}, u32[]{:S(2)}, u32[]{:S(2)}) collective-permute-start(f32[1280,128]{1,0:T(8,128)S(1)} %get-tuple-element.44), channel_id=1, source_target_pairs={{1,2},{2,1},{3,4},{4,3},{5,6},{6,5},{7,8},{8,7},{9,10},{10,9},{11,... | collective-permute-start | bytes 1966088 | tf_op jit(solution)/shard_map/ppermute | solution.py:567
  21.2 22.2 %collective-permute-start.3 = (f32[1280,128]{1,0:T(8,128)S(1)}, f32[1280,128]{1,0:T(8,128)S(1)}, u32[]{:S(2)}, u32[]{:S(2)}) collective-permute-start(f32[1280,128]{1,0:T(8,128)S(1)} %get-tuple-element.45), channel_id=1, source_target_pairs={{0,1},{1,0},{2,3},{3,2},{4,5},{5,4},{6,7},{7,6},{8,9},{9,8},{10,11... | collective-permute-start | bytes 1966088 | tf_op jit(solution)/shard_map/ppermute | solution.py:519
  36.0 7.3 %collective-permute-start.4 = (f32[4,4,48,128]{3,2,1,0:T(8,128)S(1)}, f32[4,4,48,128]{3,2,1,0:T(8,128)S(1)}, u32[]{:S(2)}, u32[]{:S(2)}) collective-permute-start(f32[4,4,48,128]{3,2,1,0:T(8,128)S(1)} %get-tuple-element.49), channel_id=1, source_target_pairs={{0,1},{1,0},{2,3},{3,2},{4,5},{5,4},{6,7},{7,6},{8,9},{9,8},{10,11... | collective-permute-start | bytes 1179656 | tf_op jit(solution)/shard_map/ppermute | solution.py:519
  46.8 2.2 %collective-permute-start.12 = (f32[4,4,48,128]{3,2,1,0:T(8,128)S(1)}, f32[4,4,48,128]{3,2,1,0:T(8,128)S(1)}, u32[]{:S(2)}, u32[]{:S(2)}) collective-permute-start(f32[4,4,48,128]{3,2,1,0:T(8,128)S(1)} %get-tuple-element.52), channel_id=1, source_target_pairs={{0,1},{1,0},{2,3},{3,2},{4,5},{5,4},{6,7},{7,6},{8,9},{9,8},{10,11... | collective-permute-start | bytes 1179656 | tf_op jit(solution)/shard_map/ppermute | solution.py:519
  49.2 7.3 %collective-permute-start.13 = (f32[4,96,128]{2,1,0:T(8,128)S(1)}, f32[4,96,128]{2,1,0:T(8,128)S(1)}, u32[]{:S(2)}, u32[]{:S(2)}) collective-permute-start(f32[4,96,128]{2,1,0:T(8,128)S(1)} %dynamic-slice_bitcast_fusion), channel_id=1, source_target_pairs={{0,2},{1,3},{2,0},{3,1},{4,6},{5,7},{6,4},{7,5},{8,10},{9,11},{10,... | collective-permute-start | bytes 589832 | tf_op jit(solution)/shard_map/ppermute | solution.py:447
  51.2 9.4 %collective-permute-start.5 = (f32[4,48,128]{2,1,0:T(8,128)S(1)}, f32[4,48,128]{2,1,0:T(8,128)S(1)}, u32[]{:S(2)}, u32[]{:S(2)}) collective-permute-start(f32[4,48,128]{2,1,0:T(8,128)S(1)} %get-tuple-element.61), channel_id=1, source_target_pairs={{0,8},{1,9},{2,10},{3,11},{4,12},{5,13},{6,14},{7,15},{8,0},{9,1},... | collective-permute-start | bytes 294920 | tf_op jit(solution)/shard_map/ppermute | solution.py:447
  53.9 8.3 %collective-permute-start.6 = (f32[4,48,128]{2,1,0:T(8,128)S(1)}, f32[4,48,128]{2,1,0:T(8,128)S(1)}, u32[]{:S(2)}, u32[]{:S(2)}) collective-permute-start(f32[4,48,128]{2,1,0:T(8,128)S(1)} %get-tuple-element.63), channel_id=1, source_target_pairs={{0,4},{1,5},{2,6},{3,7},{4,0},{5,1},{6,2},{7,3},{8,12},{9,13},{10,... | collective-permute-start | bytes 294920 | tf_op jit(solution)/shard_map/ppermute | solution.py:447
  53.9 9.1 %collective-permute-start.7 = (f32[4,48,128]{2,1,0:T(8,128)S(1)}, f32[4,48,128]{2,1,0:T(8,128)S(1)}, u32[]{:S(2)}, u32[]{:S(2)}) collective-permute-start(f32[4,48,128]{2,1,0:T(8,128)S(1)} %get-tuple-element.62), channel_id=1, source_target_pairs={{0,12},{1,13},{2,14},{3,15},{4,8},{5,9},{6,10},{7,11},{8,4},{9,5},... | collective-permute-start | bytes 294920 | tf_op jit(solution)/shard_map/ppermute | solution.py:447
  56.5 10.3 %collective-permute-start.14 = (f32[96,128]{1,0:T(8,128)S(1)}, f32[96,128]{1,0:T(8,128)S(1)}, u32[]{:S(2)}, u32[]{:S(2)}) collective-permute-start(f32[96,128]{1,0:T(8,128)S(1)} %get-tuple-element.64), channel_id=1, source_target_pairs={{0,8},{1,9},{2,10},{3,11},{4,12},{5,13},{6,14},{7,15},{8,0},{9,1},... | collective-permute-start | bytes 147464 | tf_op jit(solution)/shard_map/ppermute | solution.py:447
  59.1 7.6 %collective-permute-start.15 = (f32[96,128]{1,0:T(8,128)S(1)}, f32[96,128]{1,0:T(8,128)S(1)}, u32[]{:S(2)}, u32[]{:S(2)}) collective-permute-start(f32[96,128]{1,0:T(8,128)S(1)} %get-tuple-element.66), channel_id=1, source_target_pairs={{0,4},{1,5},{2,6},{3,7},{4,0},{5,1},{6,2},{7,3},{8,12},{9,13},{10,... | collective-permute-start | bytes 147464 | tf_op jit(solution)/shard_map/ppermute | solution.py:447
  60.7 6.1 %collective-permute-start.16 = (f32[96,128]{1,0:T(8,128)S(1)}, f32[96,128]{1,0:T(8,128)S(1)}, u32[]{:S(2)}, u32[]{:S(2)}) collective-permute-start(f32[96,128]{1,0:T(8,128)S(1)} %get-tuple-element.65), channel_id=1, source_target_pairs={{0,12},{1,13},{2,14},{3,15},{4,8},{5,9},{6,10},{7,11},{8,4},{9,5},... | collective-permute-start | bytes 147464 | tf_op jit(solution)/shard_map/ppermute | solution.py:447
  63.1 8.2 %collective-permute-start.8 = (f32[4,48,128]{2,1,0:T(8,128)S(1)}, f32[4,48,128]{2,1,0:T(8,128)S(1)}, u32[]{:S(2)}, u32[]{:S(2)}) collective-permute-start(f32[4,48,128]{2,1,0:T(8,128)S(1)} %fusion.1), channel_id=1, source_target_pairs={{0,2},{1,3},{2,0},{3,1},{4,6},{5,7},{6,4},{7,5},{8,10},{9,11},{10,... | collective-permute-start | bytes 294920 | tf_op jit(solution)/shard_map/ppermute | solution.py:447
  66.8 15.3 %copy-start.1 = (s32[8]{0:T(128)S(1)}, s32[8]{0:T(128)}, u32[]{:S(2)}) copy-start(s32[8]{0:T(128)} %param.15) | copy-start | bytes 100
  66.8 7.3 %collective-permute-start.17 = (f32[96,128]{1,0:T(8,128)S(1)}, f32[96,128]{1,0:T(8,128)S(1)}, u32[]{:S(2)}, u32[]{:S(2)}) collective-permute-start(f32[96,128]{1,0:T(8,128)S(1)} %fusion.3), channel_id=1, source_target_pairs={{0,8},{1,9},{2,10},{3,11},{4,12},{5,13},{6,14},{7,15},{8,0},{9,1},... | collective-permute-start | bytes 147464 | tf_op jit(solution)/shard_map/ppermute | solution.py:447
  68.7 7.3 %collective-permute-start.18 = (f32[96,128]{1,0:T(8,128)S(1)}, f32[96,128]{1,0:T(8,128)S(1)}, u32[]{:S(2)}, u32[]{:S(2)}) collective-permute-start(f32[96,128]{1,0:T(8,128)S(1)} %fusion.3), channel_id=1, source_target_pairs={{0,4},{1,5},{2,6},{3,7},{4,0},{5,1},{6,2},{7,3},{8,12},{9,13},{10,... | collective-permute-start | bytes 147464 | tf_op jit(solution)/shard_map/ppermute | solution.py:447
  69.6 6.5 %collective-permute-start.19 = (f32[96,128]{1,0:T(8,128)S(1)}, f32[96,128]{1,0:T(8,128)S(1)}, u32[]{:S(2)}, u32[]{:S(2)}) collective-permute-start(f32[96,128]{1,0:T(8,128)S(1)} %fusion.3), channel_id=1, source_target_pairs={{0,12},{1,13},{2,14},{3,15},{4,8},{5,9},{6,10},{7,11},{8,4},{9,5},... | collective-permute-start | bytes 147464 | tf_op jit(solution)/shard_map/ppermute | solution.py:447
  71.3 10.1 %collective-permute-start.9 = (f32[4,48,128]{2,1,0:T(8,128)S(1)}, f32[4,48,128]{2,1,0:T(8,128)S(1)}, u32[]{:S(2)}, u32[]{:S(2)}) collective-permute-start(f32[4,48,128]{2,1,0:T(8,128)S(1)} %add.108), channel_id=1, source_target_pairs={{0,8},{1,9},{2,10},{3,11},{4,12},{5,13},{6,14},{7,15},{8,0},{9,1},... | collective-permute-start | bytes 294920 | tf_op jit(solution)/shard_map/ppermute | solution.py:447
  72.2 9.1 %collective-permute-start.10 = (f32[4,48,128]{2,1,0:T(8,128)S(1)}, f32[4,48,128]{2,1,0:T(8,128)S(1)}, u32[]{:S(2)}, u32[]{:S(2)}) collective-permute-start(f32[4,48,128]{2,1,0:T(8,128)S(1)} %add.108), channel_id=1, source_target_pairs={{0,4},{1,5},{2,6},{3,7},{4,0},{5,1},{6,2},{7,3},{8,12},{9,13},{10,... | collective-permute-start | bytes 294920 | tf_op jit(solution)/shard_map/ppermute | solution.py:447
  74.1 7.3 %collective-permute-start.11 = (f32[4,48,128]{2,1,0:T(8,128)S(1)}, f32[4,48,128]{2,1,0:T(8,128)S(1)}, u32[]{:S(2)}, u32[]{:S(2)}) collective-permute-start(f32[4,48,128]{2,1,0:T(8,128)S(1)} %add.108), channel_id=1, source_target_pairs={{0,12},{1,13},{2,14},{3,15},{4,8},{5,9},{6,10},{7,11},{8,4},{9,5},... | collective-permute-start | bytes 294920 | tf_op jit(solution)/shard_map/ppermute | solution.py:447
  76.2 5.7 %collective-permute-start.20 = (f32[4,96,128]{2,1,0:T(8,128)S(1)}, f32[4,96,128]{2,1,0:T(8,128)S(1)}, u32[]{:S(2)}, u32[]{:S(2)}) collective-permute-start(f32[4,96,128]{2,1,0:T(8,128)S(1)} %pad_maximum_fusion.2), channel_id=1, source_target_pairs={{0,2},{1,3},{2,0},{3,1},{4,6},{5,7},{6,4},{7,5},{8,10},{9,11},{10,... | collective-permute-start | bytes 589832 | tf_op jit(solution)/shard_map/ppermute | solution.py:447
  81.4 3.5 %collective-permute-start.21 = (f32[4,4,48,128]{3,2,1,0:T(8,128)S(1)}, f32[4,4,48,128]{3,2,1,0:T(8,128)S(1)}, u32[]{:S(2)}, u32[]{:S(2)}) collective-permute-start(f32[4,4,48,128]{3,2,1,0:T(8,128)S(1)} %pad_maximum_fusion.refs_0_), channel_id=1, source_target_pairs={{0,1},{1,0},{2,3},{3,2},{4,5},{5,4},{6,7},{7,6},{8,9},{9,8},{10,11... | collective-permute-start | bytes 1179656 | tf_op jit(solution)/shard_map/ppermute | solution.py:519
  82.0 2.9 %collective-permute-start.22 = (f32[4,4,48,128]{3,2,1,0:T(8,128)S(1)}, f32[4,4,48,128]{3,2,1,0:T(8,128)S(1)}, u32[]{:S(2)}, u32[]{:S(2)}) collective-permute-start(f32[4,4,48,128]{3,2,1,0:T(8,128)S(1)} %bitcast.58), channel_id=1, source_target_pairs={{0,1},{1,0},{2,3},{3,2},{4,5},{5,4},{6,7},{7,6},{8,9},{9,8},{10,11... | collective-permute-start | bytes 1179656 | tf_op jit(solution)/shard_map/ppermute | solution.py:519

commit v7 on v6

--- a/solution.py
+++ b/solution.py
@@ -244,14 +244,16 @@
 
     moves = []
     for k, (x, x_out) in enumerate(((e, e_out), (h, h_out))):
-        moves.append((x.at[:, pl.ds(g, d), inside], edge_out.at[k, :, pl.ds(0, d)]))
-        moves.append(
-            (x.at[:, pl.ds(g + depth - 1 - d, d + 1), inside], edge_out.at[k, :, pl.ds(d, d + 1)])
-        )
         moves += [(x.at[c, own, inside], x_out.at[c]) for c in range(3)]
+    copies = start_all(moves, sem)
+    for k, x in enumerate((e, h)):
+        for c in range(3):
+            edge_out[k, c, pl.ds(0, d)] = x[c, pl.ds(g, d), inside]
+            edge_out[k, c, pl.ds(d, d + 1)] = x[c, pl.ds(g + depth - 1 - d, d + 1), inside]
     if first:
-        moves += [(coefs.at[k, own], coefs_out.at[k]) for k in range(2)]
-    for copy in start_all(moves, sem):
+        for k in range(2):
+            coefs_out[k] = coefs[k, own]
+    for copy in copies:
         copy.wait()
 
 
@@ -275,18 +277,17 @@
     even = info[0] == 0
     below, above = info[1], info[2]
 
-    moves = []
+    yee = Yee(e, h, coefs, height, width, g, below)
     for k, x in enumerate((e, h)):
         for source, planes, at in ((0, d, 0), (d, d + 1, depth - 1 - d)):
-            moves.append(
-                (edge_in.at[k, :, pl.ds(source, planes)], x.at[:, pl.ds(g + at, planes), inside])
-            )
+            for c in range(3):
+                part = edge_in[k, c, pl.ds(source, planes)]
+                x[c, pl.ds(g + at, planes), inside] = part
     for plane in (0, depth - d):
-        moves.append((coefs_in.at[:, pl.ds(plane, d)], coefs.at[:, pl.ds(g + plane, d)]))
+        for k in range(2):
+            coefs[k, pl.ds(g + plane, d)] = coefs_in[k, pl.ds(plane, d)]
     if not first:
-        moves.append((below_in, h.at[:, g - 1, inside]))
-    copies = start_all(moves, sem)
-    yee = Yee(e, h, coefs, height, width, g, below)
+        h[:, g - 1, inside] = below_in[...]
 
     sides = (
         (-depth, up_pieces(d, mats if first else 0, depth, first)),
@@ -328,8 +329,6 @@
     else:
         for k, at in enumerate(ghost_planes):
             coefs[:, at] = ghosts_in[:, k]
-    for copy in copies:
-        copy.wait()
 
     mine, other = info[0], 1 - info[0]
     for s in range(1, d + 1):
@@ -356,18 +355,22 @@
             )
             other_out[m, s - 1] = fresh
 
-    moves = []
-    for k, x in enumerate((e, h)):
-        for j, plane in enumerate((0, depth - d)):
-            source = x.at[:, pl.ds(g + plane, d), inside]
-            if nxt:
-                moves.append((source, (e_out, h_out)[k].at[:, pl.ds(plane, d)]))
-            else:
-                moves.append((source, fresh_out.at[k, :, pl.ds(j * d, d)]))
+    copies = []
     if nxt:
-        moves.append((h.at[:, g - 1, inside], below_out))
-    copies = start_all(moves, sem)
+        moves = []
+        for x, x_out in ((e, e_out), (h, h_out)):
+            for plane in (0, depth - d):
+                source = x.at[:, pl.ds(g + plane, d), inside]
+                moves.append((source, x_out.at[:, pl.ds(plane, d)]))
+        copies = start_all(moves, sem)
+    else:
+        for k, x in enumerate((e, h)):
+            for j, plane in enumerate((0, depth - d)):
+                for c in range(3):
+                    part = x[c, pl.ds(g + plane, d), inside]
+                    fresh_out[k, c, pl.ds(j * d, d)] = part
     if nxt:
+        below_out[...] = h[:, g - 1, inside]
 
         def pack(down_ref, up_ref):
             for pieces, out in (
@@ -408,7 +411,6 @@
         copies = []
     rows, width = samples[0].shape[2:]
     steps = sum(chunks)
-    blocks[...] = jnp.zeros(blocks.shape, jnp.float32)
     c = info[0] if side == 0 else 1 - info[0]
 
     def copy(f):
@@ -423,6 +425,8 @@
                 total = planes[0] * table[f, part * steps]
                 for t in range(1, steps):
                     total = total + planes[t] * table[f, part * steps + t]
+                blocks[f, part, m, pl.ds(0, (blocks.shape[3] - rows))] = jnp.zeros(((blocks.shape[3] - rows), width), jnp.float32)
+                blocks[f, part, m, pl.ds(rows, (blocks.shape[3] - rows))] = jnp.zeros(((blocks.shape[3] - rows), width), jnp.float32)
                 blocks[f, part, m, pl.ds(start, rows)] = total
         copy(f).start()
         return 0
@@ -577,7 +581,7 @@
                     kernel,
                     out_shape=state + samples + [edge, vmem(2, depth, height, width)],
                     in_specs=[SMEM, SMEM, HBM, HBM, HBM],
-                    out_specs=[HBM] * 2 + [VMEM] * 3 + [ANY],
+                    out_specs=[HBM] * 2 + [VMEM] * 4,
                     scratch_shapes=scratch(1)
                     + [
                         pltpu.VMEM((depth, height, width), jnp.int32),
@@ -598,7 +602,7 @@
                     cost_estimate=cost(5),
                 )(info, *in_hbm(e, h), *in_vmem(coefs))
         operands = [info, *in_vmem(edge, coefs, mine, other, far, near)]
-        specs = [SMEM, VMEM, ANY] + [VMEM] * 4
+        specs = [SMEM] + [VMEM] * 6
         if first:
             operands += [tables]
             specs += [SMEM]

time: 87.8 us -> 87.4 us (level)
  no operation moved by 1% of the time
where the time goes in v7:
time: 87.4 us; the launch traced here: 87.2 us
  starting transfers between devices  45.2 us (52%)
  Pallas kernels  29.6 us (34%)
  waiting for transfers between devices  10.7 us (12%)
  between operations  1.05 us (1%)
    ppermute x15, starting transfers between devices, swap(): lax.ppermute(block, 'slab', [(i, i ^ stride) for i in range(self.slabs)])  23.2 us
    ppermute x6, starting transfers between devices, near_swap(): return lax.ppermute(block, 'slab', near_pairs)  20.6 us
    ppermute x15, waiting for transfers between devices, swap(): lax.ppermute(block, 'slab', [(i, i ^ stride) for i in range(self.slabs)])  9.29 us
    pallas_call x2, Pallas kernels, per_device(): pl.pallas_call(functools.partial(edge_kernel, d, nxt, first, depth, monit...  7.54 us
    pallas_call x1, Pallas kernels, per_device(): pl.pallas_call(kernel, out_shape=state + samples + [edge, vmem(2, depth,...  7.49 us
    pallas_call x1, Pallas kernels, per_device(): pl.pallas_call(kernel, out_shape=state + samples + [edge], in_specs=[SMEM...  7.07 us
    pallas_call x2, Pallas kernels, per_device(): pl.pallas_call(functools.partial(spectrum_kernel, side, ROUNDS, monitors,...  5.01 us
    pallas_call x1, Pallas kernels, per_device(): pl.pallas_call(functools.partial(first_pack_kernel, d, mats, depth), out_...  2.51 us
  transfers between devices with their start and end apart: 23, of which 7 were waited for; matrix products, arithmetic and copies ran while one was open for 1% of the time, Pallas kernels for 20%

profile of v7, /device:TPU:0, one launch (start us, length us, event | category | flops | bytes accessed | tf_op | source)
XLA Modules:
  0.0 87.2 jit_solution(18384380494864924885)
XLA Ops:
  0.6 0.0 copy-start
  0.6 0.0 copy-start.2
  0.7 0.0 copy-start.4
  0.7 0.0 copy-start.3
  0.7 2.5 %first_pack.1 = (f32[26,64,128]{2,1,0:T(8,128)}, f32[26,64,128]{2,1,0:T(8,128)S(1)}) custom-call(f32[3,16,64,128]{3,2,1,0:T(8,128)} %e_ref.1, f32[3,16,64,128]{3,2,1,0:T(8,128)} %h_ref.1, s32[16,64,128]{2,1,0:T(8,128)} %m_ref.1), custom_call_target="tpu_custom_call" | custom-call | bytes 6000000 | tf_op jit(solution)/shard_map/first_pack/pallas_call | solution.py:550
  3.2 0.7 collective-permute-start
  3.9 4.3 %collective-permute-start.1 = (f32[1664,128]{1,0:T(8,128)S(1)}, f32[1664,128]{1,0:T(8,128)S(1)}, u32[]{:S(2)}, u32[]{:S(2)}) collective-permute-start(f32[1664,128]{1,0:T(8,128)S(1)} %bitcast.60), channel_id=1, source_target_pairs={{0,1},{1,0},{2,3},{3,2},{4,5},{5,4},{6,7},{7,6},{8,9},{9,8},{10,11... | collective-permute-start | bytes 2555912 | tf_op jit(solution)/shard_map/ppermute | solution.py:523
  8.3 0.1 concatenate.6.info
  8.4 0.0 copy-done.3
  8.4 7.5 %inner0.1 = (f32[3,16,64,128]{3,2,1,0:T(8,128)}, f32[3,16,64,128]{3,2,1,0:T(8,128)}, f32[4,4,48,128]{3,2,1,0:T(8,128)S(1)}, f32[4,4,48,128]{3,2,1,0:T(8,128)S(1)...) custom-call(s32[16]{0:T(128)S(1)} %concatenate.6.info, ...), custom_call_target="tpu_custom_call" | custom-call | bytes 15000000 | tf_op jit(solution)/shard_map/inner0/pallas_call | solution.py:580
  15.9 0.0 collective-permute-done.refs_4_
  15.9 0.0 collective-permute-done.1.refs_5_
  15.9 4.3 %edge0.1 = (f32[3,16,64,128]{3,2,1,0:T(8,128)}, f32[3,16,64,128]{3,2,1,0:T(8,128)}, f32[4,4,48,128]{3,2,1,0:T(8,128)S(1)}, f32[4,4,48,128]{3,2,1,0:T(8,128)S(1)}...) custom-call(s32[16]{0:T(128)S(1)} %concatenate.6.info, ...), custom_call_target="tpu_custom_call", output_to_operand_aliasing={{0}: (8, {}), {1}: (9, {})} | custom-call | bytes 12000000 | tf_op jit(solution)/shard_map/edge0/pallas_call | solution.py:631
  20.2 0.7 collective-permute-start.2
  20.9 15.0 %collective-permute-start.3 = (f32[1280,128]{1,0:T(8,128)S(1)}, f32[1280,128]{1,0:T(8,128)S(1)}, u32[]{:S(2)}, u32[]{:S(2)}) collective-permute-start(f32[1280,128]{1,0:T(8,128)S(1)} %get-tuple-element.45), channel_id=1, source_target_pairs={{0,1},{1,0},{2,3},{3,2},{4,5},{5,4},{6,7},{7,6},{8,9},{9,8},{10,11... | collective-permute-start | bytes 1966088 | tf_op jit(solution)/shard_map/ppermute | solution.py:523
  35.9 0.1 collective-permute-start.4
  36.0 7.1 %inner1.1 = (f32[3,16,64,128]{3,2,1,0:T(8,128)}, f32[3,16,64,128]{3,2,1,0:T(8,128)}, f32[4,4,48,128]{3,2,1,0:T(8,128)S(1)}, f32[4,4,48,128]{3,2,1,0:T(8,128)S(1)}, f32[2,3,9,64,128]{4,3,2,1,0:T(8,128)S(1)}) custom-call(s32[16]{0:T(128)S(1)} %concatenate.6.info, ...), custom_call_target="tpu_custom_call", output_to_operand_aliasing={{0}: (1, {}), {1}: (2, {})} | custom-call | bytes 15000000 | tf_op jit(solution)/shard_map/inner1/pallas_call | solution.py:594
  43.0 0.0 collective-permute-done.4
  43.1 0.1 add.100.refs_8_
  43.1 0.0 collective-permute-done.2.refs_4_
  43.1 0.0 collective-permute-done.3.refs_5_
  43.1 3.3 %edge1.1 = (f32[2,3,8,64,128]{4,3,2,1,0:T(8,128)S(1)}, f32[4,4,48,128]{3,2,1,0:T(8,128)S(1)}, f32[4,4,48,128]{3,2,1,0:T(8,128)S(1)}, f32[4,4,48,128]{3,2,1,0:T(8,128)S(1)}) custom-call(s32[16]{0:T(128)S(1)} %concatenate.6.info, f32[2,3,9,64,128]{4,3,2,1,0:T(8,128)S(1)} %get-tuple-element.41.refs_0_, ...), custom_call_target="tpu_custom_call", output_to_operand_aliasing={{3}: (9, {})} | custom-call | bytes 12000000 | tf_op jit(solution)/shard_map/edge1/pallas_call | solution.py:631
  46.4 1.0 %collective-permute-start.12 = (f32[4,4,48,128]{3,2,1,0:T(8,128)S(1)}, f32[4,4,48,128]{3,2,1,0:T(8,128)S(1)}, u32[]{:S(2)}, u32[]{:S(2)}) collective-permute-start(f32[4,4,48,128]{3,2,1,0:T(8,128)S(1)} %get-tuple-element.52), channel_id=1, source_target_pairs={{0,1},{1,0},{2,3},{3,2},{4,5},{5,4},{6,7},{7,6},{8,9},{9,8},{10,11... | collective-permute-start | bytes 1179656 | tf_op jit(solution)/shard_map/ppermute | solution.py:523
  47.4 1.3 %collective-permute-done.12 = f32[4,4,48,128]{3,2,1,0:T(8,128)S(1)} collective-permute-done((f32[4,4,48,128]{3,2,1,0:T(8,128)S(1)}, f32[4,4,48,128]{3,2,1,0:T(8,128)S(1)}, u32[]{:S(2)}, u32[]{:S(2)}) %collective-permute-start.12) | collective-permute-done | bytes 393248 | tf_op jit(solution)/shard_map/ppermute | solution.py:523
  48.7 0.1 add.110
  48.8 2.1 %collective-permute-start.13 = (f32[4,96,128]{2,1,0:T(8,128)S(1)}, f32[4,96,128]{2,1,0:T(8,128)S(1)}, u32[]{:S(2)}, u32[]{:S(2)}) collective-permute-start(f32[4,96,128]{2,1,0:T(8,128)S(1)} %dynamic-slice_bitcast_fusion), channel_id=1, source_target_pairs={{0,2},{1,3},{2,0},{3,1},{4,6},{5,7},{6,4},{7,5},{8,10},{9,11},{10,... | collective-permute-start | bytes 589832 | tf_op jit(solution)/shard_map/ppermute | solution.py:451
  50.9 2.7 %collective-permute-start.5 = (f32[4,48,128]{2,1,0:T(8,128)S(1)}, f32[4,48,128]{2,1,0:T(8,128)S(1)}, u32[]{:S(2)}, u32[]{:S(2)}) collective-permute-start(f32[4,48,128]{2,1,0:T(8,128)S(1)} %get-tuple-element.61), channel_id=1, source_target_pairs={{0,8},{1,9},{2,10},{3,11},{4,12},{5,13},{6,14},{7,15},{8,0},{9,1},... | collective-permute-start | bytes 294920 | tf_op jit(solution)/shard_map/ppermute | solution.py:451
  53.6 0.0 collective-permute-start.6
  53.6 1.8 %collective-permute-start.7 = (f32[4,48,128]{2,1,0:T(8,128)S(1)}, f32[4,48,128]{2,1,0:T(8,128)S(1)}, u32[]{:S(2)}, u32[]{:S(2)}) collective-permute-start(f32[4,48,128]{2,1,0:T(8,128)S(1)} %get-tuple-element.62), channel_id=1, source_target_pairs={{0,12},{1,13},{2,14},{3,15},{4,8},{5,9},{6,10},{7,11},{8,4},{9,5},... | collective-permute-start | bytes 294920 | tf_op jit(solution)/shard_map/ppermute | solution.py:451
  55.4 0.7 collective-permute-done.13
  56.2 2.7 %collective-permute-start.14 = (f32[96,128]{1,0:T(8,128)S(1)}, f32[96,128]{1,0:T(8,128)S(1)}, u32[]{:S(2)}, u32[]{:S(2)}) collective-permute-start(f32[96,128]{1,0:T(8,128)S(1)} %get-tuple-element.64), channel_id=1, source_target_pairs={{0,8},{1,9},{2,10},{3,11},{4,12},{5,13},{6,14},{7,15},{8,0},{9,1},... | collective-permute-start | bytes 147464 | tf_op jit(solution)/shard_map/ppermute | solution.py:451
  58.8 1.6 %collective-permute-start.15 = (f32[96,128]{1,0:T(8,128)S(1)}, f32[96,128]{1,0:T(8,128)S(1)}, u32[]{:S(2)}, u32[]{:S(2)}) collective-permute-start(f32[96,128]{1,0:T(8,128)S(1)} %get-tuple-element.66), channel_id=1, source_target_pairs={{0,4},{1,5},{2,6},{3,7},{4,0},{5,1},{6,2},{7,3},{8,12},{9,13},{10,... | collective-permute-start | bytes 147464 | tf_op jit(solution)/shard_map/ppermute | solution.py:451
  60.4 0.0 collective-permute-done.5
  60.4 1.5 %collective-permute-start.16 = (f32[96,128]{1,0:T(8,128)S(1)}, f32[96,128]{1,0:T(8,128)S(1)}, u32[]{:S(2)}, u32[]{:S(2)}) collective-permute-start(f32[96,128]{1,0:T(8,128)S(1)} %get-tuple-element.65), channel_id=1, source_target_pairs={{0,12},{1,13},{2,14},{3,15},{4,8},{5,9},{6,10},{7,11},{8,4},{9,5},... | collective-permute-start | bytes 147464 | tf_op jit(solution)/shard_map/ppermute | solution.py:451
  61.9 0.0 collective-permute-done.6
  61.9 0.9 collective-permute-done.7
  62.8 0.6 collective-permute-start.8
  63.4 3.1 %collective-permute-done.14 = f32[96,128]{1,0:T(8,128)S(1)} collective-permute-done((f32[96,128]{1,0:T(8,128)S(1)}, f32[96,128]{1,0:T(8,128)S(1)}, u32[]{:S(2)}, u32[]{:S(2)}) %collective-permute-start.14) | collective-permute-done | bytes 49184 | tf_op jit(solution)/shard_map/ppermute | solution.py:451
  66.4 0.0 collective-permute-done.15
  66.4 0.0 collective-permute-done.16
  66.5 0.0 copy-start.1
  66.5 1.9 %collective-permute-start.17 = (f32[96,128]{1,0:T(8,128)S(1)}, f32[96,128]{1,0:T(8,128)S(1)}, u32[]{:S(2)}, u32[]{:S(2)}) collective-permute-start(f32[96,128]{1,0:T(8,128)S(1)} %fusion.3), channel_id=1, source_target_pairs={{0,8},{1,9},{2,10},{3,11},{4,12},{5,13},{6,14},{7,15},{8,0},{9,1},... | collective-permute-start | bytes 147464 | tf_op jit(solution)/shard_map/ppermute | solution.py:451
  68.3 0.9 %collective-permute-start.18 = (f32[96,128]{1,0:T(8,128)S(1)}, f32[96,128]{1,0:T(8,128)S(1)}, u32[]{:S(2)}, u32[]{:S(2)}) collective-permute-start(f32[96,128]{1,0:T(8,128)S(1)} %fusion.3), channel_id=1, source_target_pairs={{0,4},{1,5},{2,6},{3,7},{4,0},{5,1},{6,2},{7,3},{8,12},{9,13},{10,... | collective-permute-start | bytes 147464 | tf_op jit(solution)/shard_map/ppermute | solution.py:451
  69.3 1.6 %collective-permute-start.19 = (f32[96,128]{1,0:T(8,128)S(1)}, f32[96,128]{1,0:T(8,128)S(1)}, u32[]{:S(2)}, u32[]{:S(2)}) collective-permute-start(f32[96,128]{1,0:T(8,128)S(1)} %fusion.3), channel_id=1, source_target_pairs={{0,12},{1,13},{2,14},{3,15},{4,8},{5,9},{6,10},{7,11},{8,4},{9,5},... | collective-permute-start | bytes 147464 | tf_op jit(solution)/shard_map/ppermute | solution.py:451
  70.9 0.0 collective-permute-done.8
  71.0 1.0 %collective-permute-start.9 = (f32[4,48,128]{2,1,0:T(8,128)S(1)}, f32[4,48,128]{2,1,0:T(8,128)S(1)}, u32[]{:S(2)}, u32[]{:S(2)}) collective-permute-start(f32[4,48,128]{2,1,0:T(8,128)S(1)} %add.108), channel_id=1, source_target_pairs={{0,8},{1,9},{2,10},{3,11},{4,12},{5,13},{6,14},{7,15},{8,0},{9,1},... | collective-permute-start | bytes 294920 | tf_op jit(solution)/shard_map/ppermute | solution.py:451
  71.9 1.8 %collective-permute-start.10 = (f32[4,48,128]{2,1,0:T(8,128)S(1)}, f32[4,48,128]{2,1,0:T(8,128)S(1)}, u32[]{:S(2)}, u32[]{:S(2)}) collective-permute-start(f32[4,48,128]{2,1,0:T(8,128)S(1)} %add.108), channel_id=1, source_target_pairs={{0,4},{1,5},{2,6},{3,7},{4,0},{5,1},{6,2},{7,3},{8,12},{9,13},{10,... | collective-permute-start | bytes 294920 | tf_op jit(solution)/shard_map/ppermute | solution.py:451
  73.8 0.0 collective-permute-done.17
  73.8 1.9 %collective-permute-start.11 = (f32[4,48,128]{2,1,0:T(8,128)S(1)}, f32[4,48,128]{2,1,0:T(8,128)S(1)}, u32[]{:S(2)}, u32[]{:S(2)}) collective-permute-start(f32[4,48,128]{2,1,0:T(8,128)S(1)} %add.108), channel_id=1, source_target_pairs={{0,12},{1,13},{2,14},{3,15},{4,8},{5,9},{6,10},{7,11},{8,4},{9,5},... | collective-permute-start | bytes 294920 | tf_op jit(solution)/shard_map/ppermute | solution.py:451
  75.6 0.0 collective-permute-done.18
  75.6 0.2 collective-permute-done.19
  75.8 1.2 %collective-permute-start.20 = (f32[4,96,128]{2,1,0:T(8,128)S(1)}, f32[4,96,128]{2,1,0:T(8,128)S(1)}, u32[]{:S(2)}, u32[]{:S(2)}) collective-permute-start(f32[4,96,128]{2,1,0:T(8,128)S(1)} %pad_maximum_fusion.2), channel_id=1, source_target_pairs={{0,2},{1,3},{2,0},{3,1},{4,6},{5,7},{6,4},{7,5},{8,10},{9,11},{10,... | collective-permute-start | bytes 589832 | tf_op jit(solution)/shard_map/ppermute | solution.py:451
  77.1 4.0 %collective-permute-done.9 = f32[4,48,128]{2,1,0:T(8,128)S(1)} collective-permute-done((f32[4,48,128]{2,1,0:T(8,128)S(1)}, f32[4,48,128]{2,1,0:T(8,128)S(1)}, u32[]{:S(2)}, u32[]{:S(2)}) %collective-permute-start.9) | collective-permute-done | bytes 98336 | tf_op jit(solution)/shard_map/ppermute | solution.py:451
  81.0 0.0 collective-permute-done.10
  81.0 0.0 collective-permute-done.11
  81.1 0.1 collective-permute-start.21
  81.1 0.5 collective-permute-done.20
  81.7 0.1 collective-permute-start.22
  81.8 0.1 fusion.7
  81.9 0.1 pad_maximum_fusion.3.table
  82.0 2.5 %spectrum0.1 = (f32[8,2,4,2,64,128]{5,4,3,2,1,0:T(8,128)}, f32[3,16,64,128]{3,2,1,0:T(8,128)}, f32[3,16,64,128]{3,2,1,0:T(8,128)}) custom-call(s32[16]{0:T(128)S(1)} %concatenate.6.info, f32[8,16]{1,0:T(8,128)S(1)} %pad_maximum_fusion.3.table, f32[4,4,48,128]{3,2,1,0:T(8,128)S(1)} %pad_maximum_fusion.refs_0_, ...), custom_call_target="tpu_custom_call", output_to_operand_aliasing={{1}: (5, {}), {2}: (6, {})} | custom-call | bytes 6000000 | tf_op jit(solution)/shard_map/spectrum0/pallas_call | solution.py:663
  84.5 0.0 collective-permute-done.21.refs_0_
  84.5 0.0 collective-permute-done.22.refs_1_
  84.5 2.5 %spectrum1.1 = f32[8,2,4,2,64,128]{5,4,3,2,1,0:T(8,128)} custom-call(s32[16]{0:T(128)S(1)} %concatenate.6.info, f32[8,16]{1,0:T(8,128)S(1)} %pad_maximum_fusion.3.table, f32[4,4,48,128]{3,2,1,0:T(8,128)S(1)} %collective-permute-done.21.refs_0_, f32[4,4,48,128]{3,2,1,0:T(8,128)S(1)} %collective-permute-done.22.refs_1_, ...), custom_call_target="tpu_custom_call", output_to_operand_aliasing={{}: (4, {})} | custom-call | bytes 6000000 | tf_op jit(solution)/shard_map/spectrum1/pallas_call | solution.py:663
  (19 shorter events, 0.3 us)
Async XLA Ops:
  0.6 7.6 %copy-start = (s32[4,2]{0,1:T(2,128)S(1)}, s32[4,2]{0,1:T(2,128)}, u32[]{:S(2)}) copy-start(s32[4,2]{0,1:T(2,128)} %param.14) | copy-start | bytes 100
  0.6 7.6 %copy-start.2 = (s32[4]{0:T(128)S(1)}, s32[4]{0:T(128)}, u32[]{:S(2)}) copy-start(s32[4]{0:T(128)} %param.13) | copy-start | bytes 52
  0.7 7.7 %copy-start.4 = (f32[4]{0:T(128)S(1)}, f32[4]{0:T(128)}, u32[]{:S(2)}) copy-start(f32[4]{0:T(128)} %param.11) | copy-start | bytes 52
  0.7 7.7 %copy-start.3 = (f32[4]{0:T(128)S(1)}, f32[4]{0:T(128)}, u32[]{:S(2)}) copy-start(f32[4]{0:T(128)} %param.12) | copy-start | bytes 52
  3.2 12.7 %collective-permute-start = (f32[1664,128]{1,0:T(8,128)}, f32[1664,128]{1,0:T(8,128)S(1)}, u32[]{:S(2)}, u32[]{:S(2)}) collective-permute-start(f32[1664,128]{1,0:T(8,128)} %bitcast.8), channel_id=1, source_target_pairs={{1,2},{2,1},{3,4},{4,3},{5,6},{6,5},{7,8},{8,7},{9,10},{10,9},{11,... | collective-permute-start | bytes 2555912 | tf_op jit(solution)/shard_map/ppermute | solution.py:571
  3.9 12.0 %collective-permute-start.1 = (f32[1664,128]{1,0:T(8,128)S(1)}, f32[1664,128]{1,0:T(8,128)S(1)}, u32[]{:S(2)}, u32[]{:S(2)}) collective-permute-start(f32[1664,128]{1,0:T(8,128)S(1)} %bitcast.60), channel_id=1, source_target_pairs={{0,1},{1,0},{2,3},{3,2},{4,5},{5,4},{6,7},{7,6},{8,9},{9,8},{10,11... | collective-permute-start | bytes 2555912 | tf_op jit(solution)/shard_map/ppermute | solution.py:523
  20.2 22.9 %collective-permute-start.2 = (f32[1280,128]{1,0:T(8,128)S(1)}, f32[1280,128]{1,0:T(8,128)S(1)}, u32[]{:S(2)}, u32[]{:S(2)}) collective-permute-start(f32[1280,128]{1,0:T(8,128)S(1)} %get-tuple-element.44), channel_id=1, source_target_pairs={{1,2},{2,1},{3,4},{4,3},{5,6},{6,5},{7,8},{8,7},{9,10},{10,9},{11,... | collective-permute-start | bytes 1966088 | tf_op jit(solution)/shard_map/ppermute | solution.py:571
  20.9 22.2 %collective-permute-start.3 = (f32[1280,128]{1,0:T(8,128)S(1)}, f32[1280,128]{1,0:T(8,128)S(1)}, u32[]{:S(2)}, u32[]{:S(2)}) collective-permute-start(f32[1280,128]{1,0:T(8,128)S(1)} %get-tuple-element.45), channel_id=1, source_target_pairs={{0,1},{1,0},{2,3},{3,2},{4,5},{5,4},{6,7},{7,6},{8,9},{9,8},{10,11... | collective-permute-start | bytes 1966088 | tf_op jit(solution)/shard_map/ppermute | solution.py:523
  35.9 7.2 %collective-permute-start.4 = (f32[4,4,48,128]{3,2,1,0:T(8,128)S(1)}, f32[4,4,48,128]{3,2,1,0:T(8,128)S(1)}, u32[]{:S(2)}, u32[]{:S(2)}) collective-permute-start(f32[4,4,48,128]{3,2,1,0:T(8,128)S(1)} %get-tuple-element.49), channel_id=1, source_target_pairs={{0,1},{1,0},{2,3},{3,2},{4,5},{5,4},{6,7},{7,6},{8,9},{9,8},{10,11... | collective-permute-start | bytes 1179656 | tf_op jit(solution)/shard_map/ppermute | solution.py:523
  46.4 2.4 %collective-permute-start.12 = (f32[4,4,48,128]{3,2,1,0:T(8,128)S(1)}, f32[4,4,48,128]{3,2,1,0:T(8,128)S(1)}, u32[]{:S(2)}, u32[]{:S(2)}) collective-permute-start(f32[4,4,48,128]{3,2,1,0:T(8,128)S(1)} %get-tuple-element.52), channel_id=1, source_target_pairs={{0,1},{1,0},{2,3},{3,2},{4,5},{5,4},{6,7},{7,6},{8,9},{9,8},{10,11... | collective-permute-start | bytes 1179656 | tf_op jit(solution)/shard_map/ppermute | solution.py:523
  48.8 7.3 %collective-permute-start.13 = (f32[4,96,128]{2,1,0:T(8,128)S(1)}, f32[4,96,128]{2,1,0:T(8,128)S(1)}, u32[]{:S(2)}, u32[]{:S(2)}) collective-permute-start(f32[4,96,128]{2,1,0:T(8,128)S(1)} %dynamic-slice_bitcast_fusion), channel_id=1, source_target_pairs={{0,2},{1,3},{2,0},{3,1},{4,6},{5,7},{6,4},{7,5},{8,10},{9,11},{10,... | collective-permute-start | bytes 589832 | tf_op jit(solution)/shard_map/ppermute | solution.py:451
  50.9 9.5 %collective-permute-start.5 = (f32[4,48,128]{2,1,0:T(8,128)S(1)}, f32[4,48,128]{2,1,0:T(8,128)S(1)}, u32[]{:S(2)}, u32[]{:S(2)}) collective-permute-start(f32[4,48,128]{2,1,0:T(8,128)S(1)} %get-tuple-element.61), channel_id=1, source_target_pairs={{0,8},{1,9},{2,10},{3,11},{4,12},{5,13},{6,14},{7,15},{8,0},{9,1},... | collective-permute-start | bytes 294920 | tf_op jit(solution)/shard_map/ppermute | solution.py:451
  53.6 8.3 %collective-permute-start.6 = (f32[4,48,128]{2,1,0:T(8,128)S(1)}, f32[4,48,128]{2,1,0:T(8,128)S(1)}, u32[]{:S(2)}, u32[]{:S(2)}) collective-permute-start(f32[4,48,128]{2,1,0:T(8,128)S(1)} %get-tuple-element.63), channel_id=1, source_target_pairs={{0,4},{1,5},{2,6},{3,7},{4,0},{5,1},{6,2},{7,3},{8,12},{9,13},{10,... | collective-permute-start | bytes 294920 | tf_op jit(solution)/shard_map/ppermute | solution.py:451
  53.6 9.1 %collective-permute-start.7 = (f32[4,48,128]{2,1,0:T(8,128)S(1)}, f32[4,48,128]{2,1,0:T(8,128)S(1)}, u32[]{:S(2)}, u32[]{:S(2)}) collective-permute-start(f32[4,48,128]{2,1,0:T(8,128)S(1)} %get-tuple-element.62), channel_id=1, source_target_pairs={{0,12},{1,13},{2,14},{3,15},{4,8},{5,9},{6,10},{7,11},{8,4},{9,5},... | collective-permute-start | bytes 294920 | tf_op jit(solution)/shard_map/ppermute | solution.py:451
  56.2 10.3 %collective-permute-start.14 = (f32[96,128]{1,0:T(8,128)S(1)}, f32[96,128]{1,0:T(8,128)S(1)}, u32[]{:S(2)}, u32[]{:S(2)}) collective-permute-start(f32[96,128]{1,0:T(8,128)S(1)} %get-tuple-element.64), channel_id=1, source_target_pairs={{0,8},{1,9},{2,10},{3,11},{4,12},{5,13},{6,14},{7,15},{8,0},{9,1},... | collective-permute-start | bytes 147464 | tf_op jit(solution)/shard_map/ppermute | solution.py:451
  58.8 7.6 %collective-permute-start.15 = (f32[96,128]{1,0:T(8,128)S(1)}, f32[96,128]{1,0:T(8,128)S(1)}, u32[]{:S(2)}, u32[]{:S(2)}) collective-permute-start(f32[96,128]{1,0:T(8,128)S(1)} %get-tuple-element.66), channel_id=1, source_target_pairs={{0,4},{1,5},{2,6},{3,7},{4,0},{5,1},{6,2},{7,3},{8,12},{9,13},{10,... | collective-permute-start | bytes 147464 | tf_op jit(solution)/shard_map/ppermute | solution.py:451
  60.4 6.1 %collective-permute-start.16 = (f32[96,128]{1,0:T(8,128)S(1)}, f32[96,128]{1,0:T(8,128)S(1)}, u32[]{:S(2)}, u32[]{:S(2)}) collective-permute-start(f32[96,128]{1,0:T(8,128)S(1)} %get-tuple-element.65), channel_id=1, source_target_pairs={{0,12},{1,13},{2,14},{3,15},{4,8},{5,9},{6,10},{7,11},{8,4},{9,5},... | collective-permute-start | bytes 147464 | tf_op jit(solution)/shard_map/ppermute | solution.py:451
  62.8 8.2 %collective-permute-start.8 = (f32[4,48,128]{2,1,0:T(8,128)S(1)}, f32[4,48,128]{2,1,0:T(8,128)S(1)}, u32[]{:S(2)}, u32[]{:S(2)}) collective-permute-start(f32[4,48,128]{2,1,0:T(8,128)S(1)} %fusion.1), channel_id=1, source_target_pairs={{0,2},{1,3},{2,0},{3,1},{4,6},{5,7},{6,4},{7,5},{8,10},{9,11},{10,... | collective-permute-start | bytes 294920 | tf_op jit(solution)/shard_map/ppermute | solution.py:451
  66.5 15.3 %copy-start.1 = (s32[8]{0:T(128)S(1)}, s32[8]{0:T(128)}, u32[]{:S(2)}) copy-start(s32[8]{0:T(128)} %param.15) | copy-start | bytes 100
  66.5 7.3 %collective-permute-start.17 = (f32[96,128]{1,0:T(8,128)S(1)}, f32[96,128]{1,0:T(8,128)S(1)}, u32[]{:S(2)}, u32[]{:S(2)}) collective-permute-start(f32[96,128]{1,0:T(8,128)S(1)} %fusion.3), channel_id=1, source_target_pairs={{0,8},{1,9},{2,10},{3,11},{4,12},{5,13},{6,14},{7,15},{8,0},{9,1},... | collective-permute-start | bytes 147464 | tf_op jit(solution)/shard_map/ppermute | solution.py:451
  68.3 7.3 %collective-permute-start.18 = (f32[96,128]{1,0:T(8,128)S(1)}, f32[96,128]{1,0:T(8,128)S(1)}, u32[]{:S(2)}, u32[]{:S(2)}) collective-permute-start(f32[96,128]{1,0:T(8,128)S(1)} %fusion.3), channel_id=1, source_target_pairs={{0,4},{1,5},{2,6},{3,7},{4,0},{5,1},{6,2},{7,3},{8,12},{9,13},{10,... | collective-permute-start | bytes 147464 | tf_op jit(solution)/shard_map/ppermute | solution.py:451
  69.3 6.5 %collective-permute-start.19 = (f32[96,128]{1,0:T(8,128)S(1)}, f32[96,128]{1,0:T(8,128)S(1)}, u32[]{:S(2)}, u32[]{:S(2)}) collective-permute-start(f32[96,128]{1,0:T(8,128)S(1)} %fusion.3), channel_id=1, source_target_pairs={{0,12},{1,13},{2,14},{3,15},{4,8},{5,9},{6,10},{7,11},{8,4},{9,5},... | collective-permute-start | bytes 147464 | tf_op jit(solution)/shard_map/ppermute | solution.py:451
  71.0 10.1 %collective-permute-start.9 = (f32[4,48,128]{2,1,0:T(8,128)S(1)}, f32[4,48,128]{2,1,0:T(8,128)S(1)}, u32[]{:S(2)}, u32[]{:S(2)}) collective-permute-start(f32[4,48,128]{2,1,0:T(8,128)S(1)} %add.108), channel_id=1, source_target_pairs={{0,8},{1,9},{2,10},{3,11},{4,12},{5,13},{6,14},{7,15},{8,0},{9,1},... | collective-permute-start | bytes 294920 | tf_op jit(solution)/shard_map/ppermute | solution.py:451
  71.9 9.1 %collective-permute-start.10 = (f32[4,48,128]{2,1,0:T(8,128)S(1)}, f32[4,48,128]{2,1,0:T(8,128)S(1)}, u32[]{:S(2)}, u32[]{:S(2)}) collective-permute-start(f32[4,48,128]{2,1,0:T(8,128)S(1)} %add.108), channel_id=1, source_target_pairs={{0,4},{1,5},{2,6},{3,7},{4,0},{5,1},{6,2},{7,3},{8,12},{9,13},{10,... | collective-permute-start | bytes 294920 | tf_op jit(solution)/shard_map/ppermute | solution.py:451
  73.8 7.2 %collective-permute-start.11 = (f32[4,48,128]{2,1,0:T(8,128)S(1)}, f32[4,48,128]{2,1,0:T(8,128)S(1)}, u32[]{:S(2)}, u32[]{:S(2)}) collective-permute-start(f32[4,48,128]{2,1,0:T(8,128)S(1)} %add.108), channel_id=1, source_target_pairs={{0,12},{1,13},{2,14},{3,15},{4,8},{5,9},{6,10},{7,11},{8,4},{9,5},... | collective-permute-start | bytes 294920 | tf_op jit(solution)/shard_map/ppermute | solution.py:451
  75.8 5.7 %collective-permute-start.20 = (f32[4,96,128]{2,1,0:T(8,128)S(1)}, f32[4,96,128]{2,1,0:T(8,128)S(1)}, u32[]{:S(2)}, u32[]{:S(2)}) collective-permute-start(f32[4,96,128]{2,1,0:T(8,128)S(1)} %pad_maximum_fusion.2), channel_id=1, source_target_pairs={{0,2},{1,3},{2,0},{3,1},{4,6},{5,7},{6,4},{7,5},{8,10},{9,11},{10,... | collective-permute-start | bytes 589832 | tf_op jit(solution)/shard_map/ppermute | solution.py:451
  81.1 3.5 %collective-permute-start.21 = (f32[4,4,48,128]{3,2,1,0:T(8,128)S(1)}, f32[4,4,48,128]{3,2,1,0:T(8,128)S(1)}, u32[]{:S(2)}, u32[]{:S(2)}) collective-permute-start(f32[4,4,48,128]{3,2,1,0:T(8,128)S(1)} %pad_maximum_fusion.refs_0_), channel_id=1, source_target_pairs={{0,1},{1,0},{2,3},{3,2},{4,5},{5,4},{6,7},{7,6},{8,9},{9,8},{10,11... | collective-permute-start | bytes 1179656 | tf_op jit(solution)/shard_map/ppermute | solution.py:523
  81.7 2.9 %collective-permute-start.22 = (f32[4,4,48,128]{3,2,1,0:T(8,128)S(1)}, f32[4,4,48,128]{3,2,1,0:T(8,128)S(1)}, u32[]{:S(2)}, u32[]{:S(2)}) collective-permute-start(f32[4,4,48,128]{3,2,1,0:T(8,128)S(1)} %bitcast.58), channel_id=1, source_target_pairs={{0,1},{1,0},{2,3},{3,2},{4,5},{5,4},{6,7},{7,6},{8,9},{9,8},{10,11... | collective-permute-start | bytes 1179656 | tf_op jit(solution)/shard_map/ppermute | solution.py:523

commit v8 on v7

--- a/solution.py
+++ b/solution.py
@@ -601,7 +601,8 @@
                     compiler_params=params(),
                     cost_estimate=cost(5),
                 )(info, *in_hbm(e, h), *in_vmem(coefs))
-        operands = [info, *in_vmem(edge, coefs, mine, other, far, near)]
+        operands = [info, *in_vmem(edge, coefs, mine, other)]
+        operands += (in_hbm(far) if first else in_vmem(far)) + in_vmem(near)
         specs = [SMEM] + [VMEM] * 6
         if first:
             operands += [tables]

time: 87.4 us -> 87 us (level)
    ppermute x6, starting transfers between devices: 20.6 us -> 19.7 us  [near_swap(): return lax.ppermute(block, 'slab', near_pairs)]
    pallas_call x1, Pallas kernels: 2.51 us -> 1.61 us  [per_device(): pl.pallas_call(functools.partial(first_pack_kernel, d, mats, depth), out_...]
    ppermute x2, starting transfers between devices: 1.42 us -> 2.3 us  [per_device(): far = lax.ppermute(far, 'slab', far_pairs)]
where the time goes in v8:
time: 87 us; the launch traced here: 86.8 us
  starting transfers between devices  45.2 us (52%)
  Pallas kernels  29.3 us (34%)
  waiting for transfers between devices  10.6 us (12%)
  between operations  1.05 us (1%)
    ppermute x15, starting transfers between devices, swap(): lax.ppermute(block, 'slab', [(i, i ^ stride) for i in range(self.slabs)])  23.2 us
    ppermute x6, starting transfers between devices, near_swap(): return lax.ppermute(block, 'slab', near_pairs)  19.7 us
    ppermute x15, waiting for transfers between devices, swap(): lax.ppermute(block, 'slab', [(i, i ^ stride) for i in range(self.slabs)])  9.2 us
    pallas_call x2, Pallas kernels, per_device(): pl.pallas_call(functools.partial(edge_kernel, d, nxt, first, depth, monit...  8.16 us
    pallas_call x1, Pallas kernels, per_device(): pl.pallas_call(kernel, out_shape=state + samples + [edge, vmem(2, depth,...  7.49 us
    pallas_call x1, Pallas kernels, per_device(): pl.pallas_call(kernel, out_shape=state + samples + [edge], in_specs=[SMEM...  7.07 us
    pallas_call x2, Pallas kernels, per_device(): pl.pallas_call(functools.partial(spectrum_kernel, side, ROUNDS, monitors,...  5.01 us
    ppermute x2, starting transfers between devices, per_device(): far = lax.ppermute(far, 'slab', far_pairs)  2.3 us
  transfers between devices with their start and end apart: 23, of which 7 were waited for; matrix products, arithmetic and copies ran while one was open for 1% of the time, Pallas kernels for 20%

profile of v8, /device:TPU:0, one launch (start us, length us, event | category | flops | bytes accessed | tf_op | source)
XLA Modules:
  0.0 86.8 jit_solution(18325539303844528487)
XLA Ops:
  0.6 0.0 copy-start
  0.6 0.0 copy-start.2
  0.7 0.0 copy-start.4
  0.7 0.0 copy-start.3
  0.7 1.6 %first_pack.1 = (f32[26,64,128]{2,1,0:T(8,128)S(1)}, f32[26,64,128]{2,1,0:T(8,128)S(1)}) custom-call(f32[3,16,64,128]{3,2,1,0:T(8,128)} %e_ref.1, f32[3,16,64,128]{3,2,1,0:T(8,128)} %h_ref.1, s32[16,64,128]{2,1,0:T(8,128)} %m_ref.1), custom_call_target="tpu_custom_call" | custom-call | bytes 6000000 | tf_op jit(solution)/shard_map/first_pack/pallas_call | solution.py:550
  2.3 1.6 %collective-permute-start = (f32[1664,128]{1,0:T(8,128)S(1)}, f32[1664,128]{1,0:T(8,128)}, u32[]{:S(2)}, u32[]{:S(2)}) collective-permute-start(f32[1664,128]{1,0:T(8,128)S(1)} %bitcast.61), channel_id=1, source_target_pairs={{1,2},{2,1},{3,4},{4,3},{5,6},{6,5},{7,8},{8,7},{9,10},{10,9},{11,... | collective-permute-start | bytes 2555912 | tf_op jit(solution)/shard_map/ppermute | solution.py:571
  3.9 3.5 %collective-permute-start.1 = (f32[1664,128]{1,0:T(8,128)S(1)}, f32[1664,128]{1,0:T(8,128)S(1)}, u32[]{:S(2)}, u32[]{:S(2)}) collective-permute-start(f32[1664,128]{1,0:T(8,128)S(1)} %bitcast.60), channel_id=1, source_target_pairs={{0,1},{1,0},{2,3},{3,2},{4,5},{5,4},{6,7},{7,6},{8,9},{9,8},{10,11... | collective-permute-start | bytes 2555912 | tf_op jit(solution)/shard_map/ppermute | solution.py:523
  7.4 0.1 concatenate.6.info
  7.5 0.0 copy-done.3
  7.5 7.5 %inner0.1 = (f32[3,16,64,128]{3,2,1,0:T(8,128)}, f32[3,16,64,128]{3,2,1,0:T(8,128)}, f32[4,4,48,128]{3,2,1,0:T(8,128)S(1)}, f32[4,4,48,128]{3,2,1,0:T(8,128)S(1)...) custom-call(s32[16]{0:T(128)S(1)} %concatenate.6.info, ...), custom_call_target="tpu_custom_call" | custom-call | bytes 15000000 | tf_op jit(solution)/shard_map/inner0/pallas_call | solution.py:580
  15.0 0.0 collective-permute-done.refs_4_
  15.0 0.0 collective-permute-done.1.refs_5_
  15.0 4.9 %edge0.1 = (f32[3,16,64,128]{3,2,1,0:T(8,128)}, f32[3,16,64,128]{3,2,1,0:T(8,128)}, f32[4,4,48,128]{3,2,1,0:T(8,128)S(1)}, f32[4,4,48,128]{3,2,1,0:T(8,128)S(1)}...) custom-call(s32[16]{0:T(128)S(1)} %concatenate.6.info, ...), custom_call_target="tpu_custom_call", output_to_operand_aliasing={{0}: (8, {}), {1}: (9, {})} | custom-call | bytes 12000000 | tf_op jit(solution)/shard_map/edge0/pallas_call | solution.py:632
  19.9 0.7 collective-permute-start.2
  20.6 14.9 %collective-permute-start.3 = (f32[1280,128]{1,0:T(8,128)S(1)}, f32[1280,128]{1,0:T(8,128)S(1)}, u32[]{:S(2)}, u32[]{:S(2)}) collective-permute-start(f32[1280,128]{1,0:T(8,128)S(1)} %get-tuple-element.45), channel_id=1, source_target_pairs={{0,1},{1,0},{2,3},{3,2},{4,5},{5,4},{6,7},{7,6},{8,9},{9,8},{10,11... | collective-permute-start | bytes 1966088 | tf_op jit(solution)/shard_map/ppermute | solution.py:523
  35.5 0.1 collective-permute-start.4
  35.6 7.1 %inner1.1 = (f32[3,16,64,128]{3,2,1,0:T(8,128)}, f32[3,16,64,128]{3,2,1,0:T(8,128)}, f32[4,4,48,128]{3,2,1,0:T(8,128)S(1)}, f32[4,4,48,128]{3,2,1,0:T(8,128)S(1)}, f32[2,3,9,64,128]{4,3,2,1,0:T(8,128)S(1)}) custom-call(s32[16]{0:T(128)S(1)} %concatenate.6.info, ...), custom_call_target="tpu_custom_call", output_to_operand_aliasing={{0}: (1, {}), {1}: (2, {})} | custom-call | bytes 15000000 | tf_op jit(solution)/shard_map/inner1/pallas_call | solution.py:594
  42.7 0.0 collective-permute-done.4
  42.7 0.1 add.100.refs_8_
  42.7 0.0 collective-permute-done.2.refs_4_
  42.7 0.0 collective-permute-done.3.refs_5_
  42.7 3.3 %edge1.1 = (f32[2,3,8,64,128]{4,3,2,1,0:T(8,128)S(1)}, f32[4,4,48,128]{3,2,1,0:T(8,128)S(1)}, f32[4,4,48,128]{3,2,1,0:T(8,128)S(1)}, f32[4,4,48,128]{3,2,1,0:T(8,128)S(1)}) custom-call(s32[16]{0:T(128)S(1)} %concatenate.6.info, f32[2,3,9,64,128]{4,3,2,1,0:T(8,128)S(1)} %get-tuple-element.41.refs_0_, ...), custom_call_target="tpu_custom_call", output_to_operand_aliasing={{3}: (9, {})} | custom-call | bytes 12000000 | tf_op jit(solution)/shard_map/edge1/pallas_call | solution.py:632
  46.0 1.0 %collective-permute-start.12 = (f32[4,4,48,128]{3,2,1,0:T(8,128)S(1)}, f32[4,4,48,128]{3,2,1,0:T(8,128)S(1)}, u32[]{:S(2)}, u32[]{:S(2)}) collective-permute-start(f32[4,4,48,128]{3,2,1,0:T(8,128)S(1)} %get-tuple-element.52), channel_id=1, source_target_pairs={{0,1},{1,0},{2,3},{3,2},{4,5},{5,4},{6,7},{7,6},{8,9},{9,8},{10,11... | collective-permute-start | bytes 1179656 | tf_op jit(solution)/shard_map/ppermute | solution.py:523
  47.0 1.3 %collective-permute-done.12 = f32[4,4,48,128]{3,2,1,0:T(8,128)S(1)} collective-permute-done((f32[4,4,48,128]{3,2,1,0:T(8,128)S(1)}, f32[4,4,48,128]{3,2,1,0:T(8,128)S(1)}, u32[]{:S(2)}, u32[]{:S(2)}) %collective-permute-start.12) | collective-permute-done | bytes 393248 | tf_op jit(solution)/shard_map/ppermute | solution.py:523
  48.4 0.1 add.110
  48.4 2.1 %collective-permute-start.13 = (f32[4,96,128]{2,1,0:T(8,128)S(1)}, f32[4,96,128]{2,1,0:T(8,128)S(1)}, u32[]{:S(2)}, u32[]{:S(2)}) collective-permute-start(f32[4,96,128]{2,1,0:T(8,128)S(1)} %dynamic-slice_bitcast_fusion), channel_id=1, source_target_pairs={{0,2},{1,3},{2,0},{3,1},{4,6},{5,7},{6,4},{7,5},{8,10},{9,11},{10,... | collective-permute-start | bytes 589832 | tf_op jit(solution)/shard_map/ppermute | solution.py:451
  50.5 2.7 %collective-permute-start.5 = (f32[4,48,128]{2,1,0:T(8,128)S(1)}, f32[4,48,128]{2,1,0:T(8,128)S(1)}, u32[]{:S(2)}, u32[]{:S(2)}) collective-permute-start(f32[4,48,128]{2,1,0:T(8,128)S(1)} %get-tuple-element.61), channel_id=1, source_target_pairs={{0,8},{1,9},{2,10},{3,11},{4,12},{5,13},{6,14},{7,15},{8,0},{9,1},... | collective-permute-start | bytes 294920 | tf_op jit(solution)/shard_map/ppermute | solution.py:451
  53.2 0.0 collective-permute-start.6
  53.2 1.8 %collective-permute-start.7 = (f32[4,48,128]{2,1,0:T(8,128)S(1)}, f32[4,48,128]{2,1,0:T(8,128)S(1)}, u32[]{:S(2)}, u32[]{:S(2)}) collective-permute-start(f32[4,48,128]{2,1,0:T(8,128)S(1)} %get-tuple-element.62), channel_id=1, source_target_pairs={{0,12},{1,13},{2,14},{3,15},{4,8},{5,9},{6,10},{7,11},{8,4},{9,5},... | collective-permute-start | bytes 294920 | tf_op jit(solution)/shard_map/ppermute | solution.py:451
  55.0 0.7 collective-permute-done.13
  55.8 2.7 %collective-permute-start.14 = (f32[96,128]{1,0:T(8,128)S(1)}, f32[96,128]{1,0:T(8,128)S(1)}, u32[]{:S(2)}, u32[]{:S(2)}) collective-permute-start(f32[96,128]{1,0:T(8,128)S(1)} %get-tuple-element.64), channel_id=1, source_target_pairs={{0,8},{1,9},{2,10},{3,11},{4,12},{5,13},{6,14},{7,15},{8,0},{9,1},... | collective-permute-start | bytes 147464 | tf_op jit(solution)/shard_map/ppermute | solution.py:451
  58.4 1.6 %collective-permute-start.15 = (f32[96,128]{1,0:T(8,128)S(1)}, f32[96,128]{1,0:T(8,128)S(1)}, u32[]{:S(2)}, u32[]{:S(2)}) collective-permute-start(f32[96,128]{1,0:T(8,128)S(1)} %get-tuple-element.66), channel_id=1, source_target_pairs={{0,4},{1,5},{2,6},{3,7},{4,0},{5,1},{6,2},{7,3},{8,12},{9,13},{10,... | collective-permute-start | bytes 147464 | tf_op jit(solution)/shard_map/ppermute | solution.py:451
  60.0 0.0 collective-permute-done.5
  60.0 1.5 %collective-permute-start.16 = (f32[96,128]{1,0:T(8,128)S(1)}, f32[96,128]{1,0:T(8,128)S(1)}, u32[]{:S(2)}, u32[]{:S(2)}) collective-permute-start(f32[96,128]{1,0:T(8,128)S(1)} %get-tuple-element.65), channel_id=1, source_target_pairs={{0,12},{1,13},{2,14},{3,15},{4,8},{5,9},{6,10},{7,11},{8,4},{9,5},... | collective-permute-start | bytes 147464 | tf_op jit(solution)/shard_map/ppermute | solution.py:451
  61.5 0.0 collective-permute-done.6
  61.5 0.9 %collective-permute-done.7 = f32[4,48,128]{2,1,0:T(8,128)S(1)} collective-permute-done((f32[4,48,128]{2,1,0:T(8,128)S(1)}, f32[4,48,128]{2,1,0:T(8,128)S(1)}, u32[]{:S(2)}, u32[]{:S(2)}) %collective-permute-start.7) | collective-permute-done | bytes 98336 | tf_op jit(solution)/shard_map/ppermute | solution.py:451
  62.4 0.6 collective-permute-start.8
  63.0 3.1 %collective-permute-done.14 = f32[96,128]{1,0:T(8,128)S(1)} collective-permute-done((f32[96,128]{1,0:T(8,128)S(1)}, f32[96,128]{1,0:T(8,128)S(1)}, u32[]{:S(2)}, u32[]{:S(2)}) %collective-permute-start.14) | collective-permute-done | bytes 49184 | tf_op jit(solution)/shard_map/ppermute | solution.py:451
  66.1 0.0 collective-permute-done.15
  66.1 0.0 collective-permute-done.16
  66.1 0.0 copy-start.1
  66.1 1.9 %collective-permute-start.17 = (f32[96,128]{1,0:T(8,128)S(1)}, f32[96,128]{1,0:T(8,128)S(1)}, u32[]{:S(2)}, u32[]{:S(2)}) collective-permute-start(f32[96,128]{1,0:T(8,128)S(1)} %fusion.3), channel_id=1, source_target_pairs={{0,8},{1,9},{2,10},{3,11},{4,12},{5,13},{6,14},{7,15},{8,0},{9,1},... | collective-permute-start | bytes 147464 | tf_op jit(solution)/shard_map/ppermute | solution.py:451
  68.0 0.9 %collective-permute-start.18 = (f32[96,128]{1,0:T(8,128)S(1)}, f32[96,128]{1,0:T(8,128)S(1)}, u32[]{:S(2)}, u32[]{:S(2)}) collective-permute-start(f32[96,128]{1,0:T(8,128)S(1)} %fusion.3), channel_id=1, source_target_pairs={{0,4},{1,5},{2,6},{3,7},{4,0},{5,1},{6,2},{7,3},{8,12},{9,13},{10,... | collective-permute-start | bytes 147464 | tf_op jit(solution)/shard_map/ppermute | solution.py:451
  68.9 1.6 %collective-permute-start.19 = (f32[96,128]{1,0:T(8,128)S(1)}, f32[96,128]{1,0:T(8,128)S(1)}, u32[]{:S(2)}, u32[]{:S(2)}) collective-permute-start(f32[96,128]{1,0:T(8,128)S(1)} %fusion.3), channel_id=1, source_target_pairs={{0,12},{1,13},{2,14},{3,15},{4,8},{5,9},{6,10},{7,11},{8,4},{9,5},... | collective-permute-start | bytes 147464 | tf_op jit(solution)/shard_map/ppermute | solution.py:451
  70.6 0.0 collective-permute-done.8
  70.6 1.0 %collective-permute-start.9 = (f32[4,48,128]{2,1,0:T(8,128)S(1)}, f32[4,48,128]{2,1,0:T(8,128)S(1)}, u32[]{:S(2)}, u32[]{:S(2)}) collective-permute-start(f32[4,48,128]{2,1,0:T(8,128)S(1)} %add.108), channel_id=1, source_target_pairs={{0,8},{1,9},{2,10},{3,11},{4,12},{5,13},{6,14},{7,15},{8,0},{9,1},... | collective-permute-start | bytes 294920 | tf_op jit(solution)/shard_map/ppermute | solution.py:451
  71.5 1.8 %collective-permute-start.10 = (f32[4,48,128]{2,1,0:T(8,128)S(1)}, f32[4,48,128]{2,1,0:T(8,128)S(1)}, u32[]{:S(2)}, u32[]{:S(2)}) collective-permute-start(f32[4,48,128]{2,1,0:T(8,128)S(1)} %add.108), channel_id=1, source_target_pairs={{0,4},{1,5},{2,6},{3,7},{4,0},{5,1},{6,2},{7,3},{8,12},{9,13},{10,... | collective-permute-start | bytes 294920 | tf_op jit(solution)/shard_map/ppermute | solution.py:451
  73.4 0.0 collective-permute-done.17
  73.4 1.9 %collective-permute-start.11 = (f32[4,48,128]{2,1,0:T(8,128)S(1)}, f32[4,48,128]{2,1,0:T(8,128)S(1)}, u32[]{:S(2)}, u32[]{:S(2)}) collective-permute-start(f32[4,48,128]{2,1,0:T(8,128)S(1)} %add.108), channel_id=1, source_target_pairs={{0,12},{1,13},{2,14},{3,15},{4,8},{5,9},{6,10},{7,11},{8,4},{9,5},... | collective-permute-start | bytes 294920 | tf_op jit(solution)/shard_map/ppermute | solution.py:451
  75.2 0.0 collective-permute-done.18
  75.2 0.1 collective-permute-done.19
  75.4 1.3 %collective-permute-start.20 = (f32[4,96,128]{2,1,0:T(8,128)S(1)}, f32[4,96,128]{2,1,0:T(8,128)S(1)}, u32[]{:S(2)}, u32[]{:S(2)}) collective-permute-start(f32[4,96,128]{2,1,0:T(8,128)S(1)} %pad_maximum_fusion.2), channel_id=1, source_target_pairs={{0,2},{1,3},{2,0},{3,1},{4,6},{5,7},{6,4},{7,5},{8,10},{9,11},{10,... | collective-permute-start | bytes 589832 | tf_op jit(solution)/shard_map/ppermute | solution.py:451
  76.7 4.0 %collective-permute-done.9 = f32[4,48,128]{2,1,0:T(8,128)S(1)} collective-permute-done((f32[4,48,128]{2,1,0:T(8,128)S(1)}, f32[4,48,128]{2,1,0:T(8,128)S(1)}, u32[]{:S(2)}, u32[]{:S(2)}) %collective-permute-start.9) | collective-permute-done | bytes 98336 | tf_op jit(solution)/shard_map/ppermute | solution.py:451
  80.6 0.0 collective-permute-done.10
  80.6 0.0 collective-permute-done.11
  80.7 0.1 collective-permute-start.21
  80.7 0.4 collective-permute-done.20
  81.2 0.2 collective-permute-start.22
  81.4 0.1 fusion.7
  81.5 0.1 pad_maximum_fusion.3.table
  81.6 2.5 %spectrum0.1 = (f32[8,2,4,2,64,128]{5,4,3,2,1,0:T(8,128)}, f32[3,16,64,128]{3,2,1,0:T(8,128)}, f32[3,16,64,128]{3,2,1,0:T(8,128)}) custom-call(s32[16]{0:T(128)S(1)} %concatenate.6.info, f32[8,16]{1,0:T(8,128)S(1)} %pad_maximum_fusion.3.table, f32[4,4,48,128]{3,2,1,0:T(8,128)S(1)} %pad_maximum_fusion.refs_0_, ...), custom_call_target="tpu_custom_call", output_to_operand_aliasing={{1}: (5, {}), {2}: (6, {})} | custom-call | bytes 6000000 | tf_op jit(solution)/shard_map/spectrum0/pallas_call | solution.py:664
  84.1 0.0 collective-permute-done.21.refs_0_
  84.1 0.0 collective-permute-done.22.refs_1_
  84.2 2.5 %spectrum1.1 = f32[8,2,4,2,64,128]{5,4,3,2,1,0:T(8,128)} custom-call(s32[16]{0:T(128)S(1)} %concatenate.6.info, f32[8,16]{1,0:T(8,128)S(1)} %pad_maximum_fusion.3.table, f32[4,4,48,128]{3,2,1,0:T(8,128)S(1)} %collective-permute-done.21.refs_0_, f32[4,4,48,128]{3,2,1,0:T(8,128)S(1)} %collective-permute-done.22.refs_1_, ...), custom_call_target="tpu_custom_call", output_to_operand_aliasing={{}: (4, {})} | custom-call | bytes 6000000 | tf_op jit(solution)/shard_map/spectrum1/pallas_call | solution.py:664
  (19 shorter events, 0.3 us)
Async XLA Ops:
  0.6 6.7 %copy-start = (s32[4,2]{0,1:T(2,128)S(1)}, s32[4,2]{0,1:T(2,128)}, u32[]{:S(2)}) copy-start(s32[4,2]{0,1:T(2,128)} %param.14) | copy-start | bytes 100
  0.6 6.7 %copy-start.2 = (s32[4]{0:T(128)S(1)}, s32[4]{0:T(128)}, u32[]{:S(2)}) copy-start(s32[4]{0:T(128)} %param.13) | copy-start | bytes 52
  0.7 6.8 %copy-start.4 = (f32[4]{0:T(128)S(1)}, f32[4]{0:T(128)}, u32[]{:S(2)}) copy-start(f32[4]{0:T(128)} %param.11) | copy-start | bytes 52
  0.7 6.8 %copy-start.3 = (f32[4]{0:T(128)S(1)}, f32[4]{0:T(128)}, u32[]{:S(2)}) copy-start(f32[4]{0:T(128)} %param.12) | copy-start | bytes 52
  2.3 12.7 %collective-permute-start = (f32[1664,128]{1,0:T(8,128)S(1)}, f32[1664,128]{1,0:T(8,128)}, u32[]{:S(2)}, u32[]{:S(2)}) collective-permute-start(f32[1664,128]{1,0:T(8,128)S(1)} %bitcast.61), channel_id=1, source_target_pairs={{1,2},{2,1},{3,4},{4,3},{5,6},{6,5},{7,8},{8,7},{9,10},{10,9},{11,... | collective-permute-start | bytes 2555912 | tf_op jit(solution)/shard_map/ppermute | solution.py:571
  3.9 11.1 %collective-permute-start.1 = (f32[1664,128]{1,0:T(8,128)S(1)}, f32[1664,128]{1,0:T(8,128)S(1)}, u32[]{:S(2)}, u32[]{:S(2)}) collective-permute-start(f32[1664,128]{1,0:T(8,128)S(1)} %bitcast.60), channel_id=1, source_target_pairs={{0,1},{1,0},{2,3},{3,2},{4,5},{5,4},{6,7},{7,6},{8,9},{9,8},{10,11... | collective-permute-start | bytes 2555912 | tf_op jit(solution)/shard_map/ppermute | solution.py:523
  19.9 22.8 %collective-permute-start.2 = (f32[1280,128]{1,0:T(8,128)S(1)}, f32[1280,128]{1,0:T(8,128)S(1)}, u32[]{:S(2)}, u32[]{:S(2)}) collective-permute-start(f32[1280,128]{1,0:T(8,128)S(1)} %get-tuple-element.44), channel_id=1, source_target_pairs={{1,2},{2,1},{3,4},{4,3},{5,6},{6,5},{7,8},{8,7},{9,10},{10,9},{11,... | collective-permute-start | bytes 1966088 | tf_op jit(solution)/shard_map/ppermute | solution.py:571
  20.6 22.1 %collective-permute-start.3 = (f32[1280,128]{1,0:T(8,128)S(1)}, f32[1280,128]{1,0:T(8,128)S(1)}, u32[]{:S(2)}, u32[]{:S(2)}) collective-permute-start(f32[1280,128]{1,0:T(8,128)S(1)} %get-tuple-element.45), channel_id=1, source_target_pairs={{0,1},{1,0},{2,3},{3,2},{4,5},{5,4},{6,7},{7,6},{8,9},{9,8},{10,11... | collective-permute-start | bytes 1966088 | tf_op jit(solution)/shard_map/ppermute | solution.py:523
  35.5 7.2 %collective-permute-start.4 = (f32[4,4,48,128]{3,2,1,0:T(8,128)S(1)}, f32[4,4,48,128]{3,2,1,0:T(8,128)S(1)}, u32[]{:S(2)}, u32[]{:S(2)}) collective-permute-start(f32[4,4,48,128]{3,2,1,0:T(8,128)S(1)} %get-tuple-element.49), channel_id=1, source_target_pairs={{0,1},{1,0},{2,3},{3,2},{4,5},{5,4},{6,7},{7,6},{8,9},{9,8},{10,11... | collective-permute-start | bytes 1179656 | tf_op jit(solution)/shard_map/ppermute | solution.py:523
  46.0 2.4 %collective-permute-start.12 = (f32[4,4,48,128]{3,2,1,0:T(8,128)S(1)}, f32[4,4,48,128]{3,2,1,0:T(8,128)S(1)}, u32[]{:S(2)}, u32[]{:S(2)}) collective-permute-start(f32[4,4,48,128]{3,2,1,0:T(8,128)S(1)} %get-tuple-element.52), channel_id=1, source_target_pairs={{0,1},{1,0},{2,3},{3,2},{4,5},{5,4},{6,7},{7,6},{8,9},{9,8},{10,11... | collective-permute-start | bytes 1179656 | tf_op jit(solution)/shard_map/ppermute | solution.py:523
  48.4 7.3 %collective-permute-start.13 = (f32[4,96,128]{2,1,0:T(8,128)S(1)}, f32[4,96,128]{2,1,0:T(8,128)S(1)}, u32[]{:S(2)}, u32[]{:S(2)}) collective-permute-start(f32[4,96,128]{2,1,0:T(8,128)S(1)} %dynamic-slice_bitcast_fusion), channel_id=1, source_target_pairs={{0,2},{1,3},{2,0},{3,1},{4,6},{5,7},{6,4},{7,5},{8,10},{9,11},{10,... | collective-permute-start | bytes 589832 | tf_op jit(solution)/shard_map/ppermute | solution.py:451
  50.5 9.4 %collective-permute-start.5 = (f32[4,48,128]{2,1,0:T(8,128)S(1)}, f32[4,48,128]{2,1,0:T(8,128)S(1)}, u32[]{:S(2)}, u32[]{:S(2)}) collective-permute-start(f32[4,48,128]{2,1,0:T(8,128)S(1)} %get-tuple-element.61), channel_id=1, source_target_pairs={{0,8},{1,9},{2,10},{3,11},{4,12},{5,13},{6,14},{7,15},{8,0},{9,1},... | collective-permute-start | bytes 294920 | tf_op jit(solution)/shard_map/ppermute | solution.py:451
  53.2 8.3 %collective-permute-start.6 = (f32[4,48,128]{2,1,0:T(8,128)S(1)}, f32[4,48,128]{2,1,0:T(8,128)S(1)}, u32[]{:S(2)}, u32[]{:S(2)}) collective-permute-start(f32[4,48,128]{2,1,0:T(8,128)S(1)} %get-tuple-element.63), channel_id=1, source_target_pairs={{0,4},{1,5},{2,6},{3,7},{4,0},{5,1},{6,2},{7,3},{8,12},{9,13},{10,... | collective-permute-start | bytes 294920 | tf_op jit(solution)/shard_map/ppermute | solution.py:451
  53.2 9.1 %collective-permute-start.7 = (f32[4,48,128]{2,1,0:T(8,128)S(1)}, f32[4,48,128]{2,1,0:T(8,128)S(1)}, u32[]{:S(2)}, u32[]{:S(2)}) collective-permute-start(f32[4,48,128]{2,1,0:T(8,128)S(1)} %get-tuple-element.62), channel_id=1, source_target_pairs={{0,12},{1,13},{2,14},{3,15},{4,8},{5,9},{6,10},{7,11},{8,4},{9,5},... | collective-permute-start | bytes 294920 | tf_op jit(solution)/shard_map/ppermute | solution.py:451
  55.8 10.3 %collective-permute-start.14 = (f32[96,128]{1,0:T(8,128)S(1)}, f32[96,128]{1,0:T(8,128)S(1)}, u32[]{:S(2)}, u32[]{:S(2)}) collective-permute-start(f32[96,128]{1,0:T(8,128)S(1)} %get-tuple-element.64), channel_id=1, source_target_pairs={{0,8},{1,9},{2,10},{3,11},{4,12},{5,13},{6,14},{7,15},{8,0},{9,1},... | collective-permute-start | bytes 147464 | tf_op jit(solution)/shard_map/ppermute | solution.py:451
  58.4 7.6 %collective-permute-start.15 = (f32[96,128]{1,0:T(8,128)S(1)}, f32[96,128]{1,0:T(8,128)S(1)}, u32[]{:S(2)}, u32[]{:S(2)}) collective-permute-start(f32[96,128]{1,0:T(8,128)S(1)} %get-tuple-element.66), channel_id=1, source_target_pairs={{0,4},{1,5},{2,6},{3,7},{4,0},{5,1},{6,2},{7,3},{8,12},{9,13},{10,... | collective-permute-start | bytes 147464 | tf_op jit(solution)/shard_map/ppermute | solution.py:451
  60.0 6.1 %collective-permute-start.16 = (f32[96,128]{1,0:T(8,128)S(1)}, f32[96,128]{1,0:T(8,128)S(1)}, u32[]{:S(2)}, u32[]{:S(2)}) collective-permute-start(f32[96,128]{1,0:T(8,128)S(1)} %get-tuple-element.65), channel_id=1, source_target_pairs={{0,12},{1,13},{2,14},{3,15},{4,8},{5,9},{6,10},{7,11},{8,4},{9,5},... | collective-permute-start | bytes 147464 | tf_op jit(solution)/shard_map/ppermute | solution.py:451
  62.4 8.2 %collective-permute-start.8 = (f32[4,48,128]{2,1,0:T(8,128)S(1)}, f32[4,48,128]{2,1,0:T(8,128)S(1)}, u32[]{:S(2)}, u32[]{:S(2)}) collective-permute-start(f32[4,48,128]{2,1,0:T(8,128)S(1)} %fusion.1), channel_id=1, source_target_pairs={{0,2},{1,3},{2,0},{3,1},{4,6},{5,7},{6,4},{7,5},{8,10},{9,11},{10,... | collective-permute-start | bytes 294920 | tf_op jit(solution)/shard_map/ppermute | solution.py:451
  66.1 15.3 %copy-start.1 = (s32[8]{0:T(128)S(1)}, s32[8]{0:T(128)}, u32[]{:S(2)}) copy-start(s32[8]{0:T(128)} %param.15) | copy-start | bytes 100
  66.1 7.3 %collective-permute-start.17 = (f32[96,128]{1,0:T(8,128)S(1)}, f32[96,128]{1,0:T(8,128)S(1)}, u32[]{:S(2)}, u32[]{:S(2)}) collective-permute-start(f32[96,128]{1,0:T(8,128)S(1)} %fusion.3), channel_id=1, source_target_pairs={{0,8},{1,9},{2,10},{3,11},{4,12},{5,13},{6,14},{7,15},{8,0},{9,1},... | collective-permute-start | bytes 147464 | tf_op jit(solution)/shard_map/ppermute | solution.py:451
  68.0 7.3 %collective-permute-start.18 = (f32[96,128]{1,0:T(8,128)S(1)}, f32[96,128]{1,0:T(8,128)S(1)}, u32[]{:S(2)}, u32[]{:S(2)}) collective-permute-start(f32[96,128]{1,0:T(8,128)S(1)} %fusion.3), channel_id=1, source_target_pairs={{0,4},{1,5},{2,6},{3,7},{4,0},{5,1},{6,2},{7,3},{8,12},{9,13},{10,... | collective-permute-start | bytes 147464 | tf_op jit(solution)/shard_map/ppermute | solution.py:451
  68.9 6.5 %collective-permute-start.19 = (f32[96,128]{1,0:T(8,128)S(1)}, f32[96,128]{1,0:T(8,128)S(1)}, u32[]{:S(2)}, u32[]{:S(2)}) collective-permute-start(f32[96,128]{1,0:T(8,128)S(1)} %fusion.3), channel_id=1, source_target_pairs={{0,12},{1,13},{2,14},{3,15},{4,8},{5,9},{6,10},{7,11},{8,4},{9,5},... | collective-permute-start | bytes 147464 | tf_op jit(solution)/shard_map/ppermute | solution.py:451
  70.6 10.1 %collective-permute-start.9 = (f32[4,48,128]{2,1,0:T(8,128)S(1)}, f32[4,48,128]{2,1,0:T(8,128)S(1)}, u32[]{:S(2)}, u32[]{:S(2)}) collective-permute-start(f32[4,48,128]{2,1,0:T(8,128)S(1)} %add.108), channel_id=1, source_target_pairs={{0,8},{1,9},{2,10},{3,11},{4,12},{5,13},{6,14},{7,15},{8,0},{9,1},... | collective-permute-start | bytes 294920 | tf_op jit(solution)/shard_map/ppermute | solution.py:451
  71.5 9.1 %collective-permute-start.10 = (f32[4,48,128]{2,1,0:T(8,128)S(1)}, f32[4,48,128]{2,1,0:T(8,128)S(1)}, u32[]{:S(2)}, u32[]{:S(2)}) collective-permute-start(f32[4,48,128]{2,1,0:T(8,128)S(1)} %add.108), channel_id=1, source_target_pairs={{0,4},{1,5},{2,6},{3,7},{4,0},{5,1},{6,2},{7,3},{8,12},{9,13},{10,... | collective-permute-start | bytes 294920 | tf_op jit(solution)/shard_map/ppermute | solution.py:451
  73.4 7.3 %collective-permute-start.11 = (f32[4,48,128]{2,1,0:T(8,128)S(1)}, f32[4,48,128]{2,1,0:T(8,128)S(1)}, u32[]{:S(2)}, u32[]{:S(2)}) collective-permute-start(f32[4,48,128]{2,1,0:T(8,128)S(1)} %add.108), channel_id=1, source_target_pairs={{0,12},{1,13},{2,14},{3,15},{4,8},{5,9},{6,10},{7,11},{8,4},{9,5},... | collective-permute-start | bytes 294920 | tf_op jit(solution)/shard_map/ppermute | solution.py:451
  75.4 5.7 %collective-permute-start.20 = (f32[4,96,128]{2,1,0:T(8,128)S(1)}, f32[4,96,128]{2,1,0:T(8,128)S(1)}, u32[]{:S(2)}, u32[]{:S(2)}) collective-permute-start(f32[4,96,128]{2,1,0:T(8,128)S(1)} %pad_maximum_fusion.2), channel_id=1, source_target_pairs={{0,2},{1,3},{2,0},{3,1},{4,6},{5,7},{6,4},{7,5},{8,10},{9,11},{10,... | collective-permute-start | bytes 589832 | tf_op jit(solution)/shard_map/ppermute | solution.py:451
  80.7 3.5 %collective-permute-start.21 = (f32[4,4,48,128]{3,2,1,0:T(8,128)S(1)}, f32[4,4,48,128]{3,2,1,0:T(8,128)S(1)}, u32[]{:S(2)}, u32[]{:S(2)}) collective-permute-start(f32[4,4,48,128]{3,2,1,0:T(8,128)S(1)} %pad_maximum_fusion.refs_0_), channel_id=1, source_target_pairs={{0,1},{1,0},{2,3},{3,2},{4,5},{5,4},{6,7},{7,6},{8,9},{9,8},{10,11... | collective-permute-start | bytes 1179656 | tf_op jit(solution)/shard_map/ppermute | solution.py:523
  81.2 2.9 %collective-permute-start.22 = (f32[4,4,48,128]{3,2,1,0:T(8,128)S(1)}, f32[4,4,48,128]{3,2,1,0:T(8,128)S(1)}, u32[]{:S(2)}, u32[]{:S(2)}) collective-permute-start(f32[4,4,48,128]{3,2,1,0:T(8,128)S(1)} %bitcast.58), channel_id=1, source_target_pairs={{0,1},{1,0},{2,3},{3,2},{4,5},{5,4},{6,7},{7,6},{8,9},{9,8},{10,11... | collective-permute-start | bytes 1179656 | tf_op jit(solution)/shard_map/ppermute | solution.py:523
